TPU v7x, 32 devices: a whole 2x2x4 slice. The times are simulated.
32 devices in a mesh: group: 1, ctx: 8 (over z, y), exp: 4 (over x, core).
Axes of the slice: x: 2, y: 2, z: 4, core: 2. Of those that a mesh axis runs over, the one named last changes fastest.
Arguments:
- hidden: bfloat16 [1536, 2048], P(('group', 'ctx', 'exp')), may hold values from -6 to 6
- queries: bfloat16 [1536, 512], P(('group', 'ctx'), 'exp'), may hold values from -6 to 6
- keys: bfloat16 [1536, 256], P(('group', 'ctx')), may hold values from -6 to 6
- values: bfloat16 [1536, 256], P(('group', 'ctx')), may hold values from -6 to 6
- positions: int32 [1536], P(('group', 'ctx')), may hold values from 0 to 191, as said below
- out_weight: bfloat16 [512, 2048], P('exp'), may hold values from -0.25 to 0.25
- ffn_gain: float32 [2048], replicated, may hold values from 0.1 to 1.9
- router_weight: bfloat16 [2048, 16], replicated, may hold values from -0.125 to 0.125
- routes: int32 [1536, 8], P(('group', 'ctx', 'exp')), may hold values from 0 to 15, all different within a row; in each aligned block of 48 rows (0 to 47, 48 to 95, ...) at most 36 rows name the same one
- expert_in: bfloat16 [8, 4, 2048, 384], P('ctx', 'exp'), may hold values from -0.125 to 0.125
- expert_out: bfloat16 [8, 4, 192, 2048], P('ctx', 'exp'), may hold values from -0.3125 to 0.3125
- rollout_logits: float32 [1536, 16], P(('group', 'ctx', 'exp')), may hold values from -12 to 12
Outputs:
- layer_out: bfloat16 [1536, 2048], P(('group', 'ctx', 'exp'))
- router_kl: float32 [1536], P(('group', 'ctx', 'exp'))
Inputs may be any that keep to these rules, and one draw needn't show every extreme that they name: `positions`: documents are runs of consecutive tokens, each of at most 192 tokens; the offset is 0 at a document's first token and rises by one to its last; at least one document has exactly 192 tokens. `routes`: each row names 8 different experts. Within the rows of one device no expert is named by more than 36 rows, a bound that some block reaches.
All inputs are finite; a program needn't handle non-finite values.
Results may differ from a plain program's by a relative error of at most 0.013.
Values may be sent and summed in bfloat16 or wider, within the bound.
No kernel may reach another device: no remote copies, remote signals or barrier semaphores. Data moves between devices by JAX's collectives and lax.ppermute only.
A program may use at most 64 MiB of HBM per device.

v0:
```python
import jax
import jax.numpy as jnp
from jax import lax
from jax.sharding import PartitionSpec as P

eps = 1e-06
theta = 1000000.0


def passed_along(value, axis, steps):
    count = lax.axis_size(axis)
    initial, last = (max(0, -steps), min(count, count - steps))
    return lax.ppermute(value, axis, [(source, source + steps) for source in range(initial, last)])


def frequencies(head_dim):
    return theta ** (-jnp.arange(head_dim // 2, dtype=jnp.float32) * 2.0 / head_dim)


def head_norm(values_in):
    widened = values_in.astype(jnp.float32)
    return widened / jnp.sqrt(jnp.mean(widened * widened, axis=-1, keepdims=True) + eps)


def rotate(vectors, angle):
    middle = vectors.shape[-1] // 2
    cosine = jnp.cos(angle)
    sine_part = jnp.sin(angle)
    leading = vectors[..., :middle]
    trailing = vectors[..., middle:]
    return jnp.concatenate(
        [leading * cosine - trailing * sine_part, trailing * cosine + leading * sine_part], axis=-1
    )


def activate(act):
    inner = act.shape[1] // 2
    return (jax.nn.silu(act[:, :inner]) * act[:, inner:]).astype(jnp.bfloat16)


def body(
    hidden,
    queries,
    keys,
    values,
    positions,
    out_weight,
    ffn_gain,
    router_weight,
    routes,
    expert_in,
    expert_out,
    rollout_logits,
):
    block_rows = queries.shape[0]
    head_dim = queries.shape[1]
    width = hidden.shape[1]
    token_rows = hidden.shape[0]
    top_count = routes.shape[1]
    experts_total = router_weight.shape[1]
    ctx_index = lax.axis_index("ctx")
    exp_index = lax.axis_index("exp")
    ctx_count = lax.axis_size("ctx")
    exp_count = lax.axis_size("exp")
    kv_heads = keys.shape[1] // head_dim
    kv_group = exp_index // (exp_count // kv_heads)
    angle = positions.astype(jnp.float32)[:, None] * frequencies(head_dim)[None, :]
    query_rot = rotate(head_norm(queries), angle).astype(jnp.bfloat16)
    key_own = rotate(
        head_norm(lax.dynamic_slice_in_dim(keys, kv_group * head_dim, head_dim, 1)), angle
    ).astype(jnp.bfloat16)
    value_own = lax.dynamic_slice_in_dim(values, kv_group * head_dim, head_dim, 1)
    key_before, value_before = passed_along((key_own, value_own), "ctx", 1)
    key_window = jnp.concatenate([key_before, key_own], axis=0)
    value_window = jnp.concatenate([value_before, value_own], axis=0)
    scores = lax.dot_general(
        query_rot, key_window, (((1,), (1,)), ((), ())), preferred_element_type=jnp.float32
    )
    scores = scores / jnp.sqrt(jnp.float32(head_dim))
    query_at = ctx_index * block_rows + jnp.arange(block_rows, dtype=jnp.int32)
    key_at = ctx_index * block_rows - block_rows + jnp.arange(2 * block_rows, dtype=jnp.int32)
    allowed = (key_at[None, :] <= query_at[:, None]) & (
        key_at[None, :] >= (query_at - positions)[:, None]
    )
    raw = jnp.where(allowed, jnp.exp(scores), 0.0)
    weights = (raw / jnp.sum(raw, axis=1, keepdims=True)).astype(jnp.bfloat16)
    head_out = jnp.dot(weights, value_window, preferred_element_type=jnp.float32).astype(
        jnp.bfloat16
    )
    term = jnp.dot(head_out, out_weight, preferred_element_type=jnp.float32).astype(jnp.bfloat16)
    summed = lax.psum_scatter(
        lax.optimization_barrier(term).astype(jnp.float32).astype(jnp.bfloat16),
        "exp",
        scatter_dimension=0,
        tiled=True,
    ).astype(jnp.float32)
    attended = (hidden.astype(jnp.float32) + summed).astype(jnp.bfloat16)
    widened = attended.astype(jnp.float32)
    moe_in = (
        widened
        / jnp.sqrt(jnp.mean(widened * widened, axis=1, keepdims=True) + eps)
        * ffn_gain[None, :]
    ).astype(jnp.bfloat16)
    router_logits = jnp.dot(moe_in, router_weight, preferred_element_type=jnp.float32)
    current_logprob = router_logits - jnp.log(
        jnp.sum(jnp.exp(router_logits), axis=1, keepdims=True)
    )
    rollout_logprob = rollout_logits - jnp.log(
        jnp.sum(jnp.exp(rollout_logits), axis=1, keepdims=True)
    )
    router_kl = jnp.sum(jnp.exp(rollout_logprob) * (rollout_logprob - current_logprob), axis=1)
    expert_ids = jnp.arange(experts_total, dtype=jnp.int32)
    picked = routes[:, :, None] == expert_ids[None, None, :]
    chosen_logits = jnp.sum(jnp.where(picked, router_logits[:, None, :], 0.0), axis=2)
    gate_raw = jnp.exp(chosen_logits)
    gates = (gate_raw / jnp.sum(gate_raw, axis=1, keepdims=True)).astype(jnp.bfloat16)
    capacity = min(token_rows, max(2, 3 * token_rows * top_count // (2 * experts_total)))
    per_column = experts_total // exp_count
    slots_total = experts_total * capacity
    flat_routes = routes.reshape(-1)
    member = (flat_routes[:, None] == expert_ids[None, :]).astype(jnp.int32)
    earlier = jnp.cumsum(member, axis=0) - member
    slot_rank = jnp.sum(earlier * member, axis=1)
    target = (
        flat_routes % per_column * exp_count + flat_routes // per_column
    ) * capacity + slot_rank
    target_grid = target.reshape(token_rows, top_count)
    slot_ids = jnp.arange(slots_total, dtype=jnp.int32)
    placing = jnp.any(target_grid[None, :, :] == slot_ids[:, None, None], axis=2).astype(
        jnp.bfloat16
    )
    gate_grid = jnp.where(
        target_grid[:, :, None] == slot_ids[None, None, :], gates[:, :, None], jnp.bfloat16(0)
    )
    combining = jnp.sum(gate_grid.astype(jnp.float32), axis=1).astype(jnp.bfloat16)
    weight_in = expert_in[0, 0]
    weight_out = expert_out[0, 0]
    packed = jnp.dot(placing, moe_in, preferred_element_type=jnp.float32).astype(jnp.bfloat16)
    packed = packed.reshape(per_column, 1, exp_count, capacity, width)
    doubled = jnp.broadcast_to(packed, (per_column, 2, exp_count, capacity, width)).reshape(
        ctx_count, exp_count, capacity, width
    )
    arrived = lax.all_to_all(
        lax.all_to_all(doubled, "ctx", split_axis=0, concat_axis=0, tiled=True),
        "exp",
        split_axis=1,
        concat_axis=1,
        tiled=True,
    )
    act = jnp.dot(arrived.reshape(-1, width), weight_in, preferred_element_type=jnp.float32)
    partial_value = jnp.dot(activate(act), weight_out, preferred_element_type=jnp.float32).astype(
        jnp.bfloat16
    )
    returned = lax.all_to_all(
        lax.all_to_all(
            partial_value.reshape(ctx_count, exp_count, capacity, width),
            "ctx",
            split_axis=0,
            concat_axis=0,
            tiled=True,
        ),
        "exp",
        split_axis=1,
        concat_axis=1,
        tiled=True,
    )
    paired = returned.reshape(per_column, 2, exp_count * capacity, width).astype(jnp.float32)
    expert_output = (paired[:, 0] + paired[:, 1]).astype(jnp.bfloat16).reshape(slots_total, width)
    moe_out = jnp.dot(combining, expert_output, preferred_element_type=jnp.float32)
    layer_out = (attended.astype(jnp.float32) + moe_out).astype(jnp.bfloat16)
    return (layer_out, router_kl)


def solution(mesh):
    return jax.shard_map(
        body,
        mesh=mesh,
        in_specs=(
            P(("group", "ctx", "exp"), None),
            P(("group", "ctx"), "exp"),
            P(("group", "ctx"), None),
            P(("group", "ctx"), None),
            P(("group", "ctx")),
            P("exp", None),
            P(),
            P(),
            P(("group", "ctx", "exp"), None),
            P("ctx", "exp", None, None),
            P("ctx", "exp", None, None),
            P(("group", "ctx", "exp"), None),
        ),
        out_specs=(P(("group", "ctx", "exp"), None), P(("group", "ctx", "exp"))),
        check_vma=False,
    )
```

profile of v0, /device:TPU:0, one launch (start us, length us, event | category | flops | bytes accessed | tf_op | source)
XLA Modules:
  0.0 477.2 jit_solution(11053212332906591154)
XLA Ops:
  7.3 0.9 constant_dynamic-slice_fusion
  8.2 4.9 %collective-permute-start.1 = (bf16[192,128]{1,0:T(8,128)(2,1)S(1)}, bf16[192,128]{1,0:T(8,128)(2,1)S(1)}, u32[]{:S(2)}, u32[]{:S(2)}) collective-permute-start(bf16[192,128]{1,0:T(8,128)(2,1)S(1)} %constant_dynamic-slice_fusion), channel_id=1, source_target_pairs={{0,4},{4,8},{8,12},{12,16},{16,20},{20,24},{24,28},{1,5},{5,9},{9,... | collective-permute-start | bytes 147464 | tf_op jit(solution)/shard_map/ppermute | solution.py:13
  13.1 0.9 fusion.26
  14.0 0.9 fusion.27
  14.9 0.9 convert_divide_fusion.1
  18.1 3.4 collective-permute-start
  21.6 1.7 collective-permute-done
  23.7 2.5 convolution_convert_fusion.2
  28.2 23.4 %reduce-scatter.2.cloned.1.call-done = bf16[48,2048]{1,0:T(8,128)(2,1)} async-done(((bf16[192,2048]{1,0:T(8,128)(2,1)}), bf16[48,2048]{1,0:T(8,128)(2,1)}) %reduce-scatter.2.cloned.1.call-update) | async-done | bytes 196624 | tf_op jit(solution)/shard_map/reduce_scatter | solution.py:91
  51.6 1.1 fusion.13
  52.7 1.0 fusion.15
  53.8 2.3 convolution_convert_fusion.1
  56.0 4.1 broadcast_in_dim.33
  60.1 3.6 copy.76
  63.7 2.9 broadcast_in_dim.34
  66.6 109.7 %all_to_all.20 = bf16[8,4,36,2048]{3,1,2,0:T(4,128)(2,1)S(1)} all-to-all(bf16[8,4,36,2048]{3,1,2,0:T(4,128)(2,1)S(1)} %bitcast.40), channel_id=1, replica_groups=mesh['group'=1,'ctx'=8,'exp'=4] {'ctx'}, dimensions={0} | all-to-all | bytes 9437184 | tf_op jit(solution)/shard_map/all_to_all | solution.py:144
  176.3 2.6 copy.77
  178.9 56.4 %all_to_all.21 = bf16[8,4,36,2048]{3,0,2,1:T(8,128)(2,1)S(1)} all-to-all(bf16[8,4,36,2048]{3,0,2,1:T(8,128)(2,1)S(1)} %copy.77), channel_id=1, replica_groups=mesh['group'=1,'ctx'=8,'exp'=4] {'exp'}, dimensions={1} | all-to-all | bytes 9437184 | tf_op jit(solution)/shard_map/all_to_all | solution.py:143
  235.3 4.9 %copy.78 = bf16[8,4,36,2048]{3,2,1,0:T(8,128)(2,1)} copy(bf16[8,4,36,2048]{3,0,2,1:T(8,128)(2,1)S(1)} %all_to_all.21) | data formatting | bytes 9437184 | tf_op jit(solution)/shard_map/all_to_all | solution.py:143
  240.2 7.2 %reshape.183 = bf16[1152,2048]{1,0:T(8,128)(2,1)} reshape(bf16[8,4,36,2048]{3,2,1,0:T(8,128)(2,1)} %copy.78) | data formatting | bytes 9437184 | tf_op jit(solution)/shard_map/reshape | solution.py:150
  247.4 4.7 fusion.2
  252.2 3.6 convolution_convert_fusion
  255.8 7.2 %reshape.184 = bf16[8,4,36,2048]{3,2,1,0:T(8,128)(2,1)} reshape(bf16[1152,2048]{1,0:T(8,128)(2,1)} %convolution_convert_fusion) | data formatting | bytes 9437184 | tf_op jit(solution)/shard_map/reshape | solution.py:156
  263.0 6.2 %copy.79 = bf16[8,4,36,2048]{3,1,2,0:T(4,128)(2,1)S(1)} copy(bf16[8,4,36,2048]{3,2,1,0:T(8,128)(2,1)} %reshape.184) | data formatting | bytes 9437184 | tf_op jit(solution)/shard_map/reshape | solution.py:156
  269.2 107.7 %all_to_all.22 = bf16[8,4,36,2048]{3,1,2,0:T(4,128)(2,1)S(1)} all-to-all(bf16[8,4,36,2048]{3,1,2,0:T(4,128)(2,1)S(1)} %copy.79), channel_id=1, replica_groups=mesh['group'=1,'ctx'=8,'exp'=4] {'ctx'}, dimensions={0} | all-to-all | bytes 9437184 | tf_op jit(solution)/shard_map/all_to_all | solution.py:155
  376.8 4.7 copy.80
  381.6 5.1 %all-to-all-start.3 = ((bf16[8,4,36,2048]{3,0,2,1:T(8,128)(2,1)}), bf16[8,4,36,2048]{3,0,2,1:T(8,128)(2,1)}, u32[]{:S(2)}, u32[]{:S(2)}) async-start(bf16[8,4,36,2048]{3,0,2,1:T(8,128)(2,1)} %copy.80), calls=%async_computation.4 | async-start | bytes 9437184 | tf_op jit(solution)/shard_map/all_to_all | solution.py:154
  388.0 52.5 %all-to-all-done.3 = bf16[8,4,36,2048]{3,0,2,1:T(8,128)(2,1)} async-done(((bf16[8,4,36,2048]{3,0,2,1:T(8,128)(2,1)}), bf16[8,4,36,2048]{3,0,2,1:T(8,128)(2,1)}, u32[]{:S(2)}, u32[]{:S(2)}) %all-to-all-start.3) | async-done | bytes 4718624 | tf_op jit(solution)/shard_map/all_to_all | solution.py:154
  440.5 11.0 %reshape.185 = f32[4,2,144,2048]{3,1,0,2:T(2,128)} reshape(bf16[8,4,36,2048]{3,0,2,1:T(8,128)(2,1)} %all-to-all-done.3) | data formatting | bytes 14155776 | tf_op jit(solution)/shard_map/convert_element_type | solution.py:167
  451.5 12.3 %fusion.67 = (f32[4,1,144,2048]{3,1,0,2:T(1,128)S(1)}, f32[4,1,144,2048]{3,1,0,2:T(1,128)S(1)}) fusion(f32[4,2,144,2048]{3,1,0,2:T(2,128)} %reshape.185), kind=kLoop, calls=%fused_computation.107 | loop fusion | bytes 18874368 | tf_op jit(solution)/shard_map/slice | solution.py:168
  463.8 5.2 %fusion = bf16[4,1,144,2048]{3,2,1,0:T(8,128)(2,1)S(1)} fusion(f32[4,1,144,2048]{3,1,0,2:T(1,128)S(1)} %get-tuple-element.3, f32[4,1,144,2048]{3,1,0,2:T(1,128)S(1)} %get-tuple-element.2), kind=kLoop, calls=%fused_computation.2 | loop fusion | flops 2359296 | bytes 11796480 | tf_op jit(solution)/shard_map/convert_element_type | solution.py:168
  469.1 1.2 fusion.1
  (53 shorter events, 6.0 us)
Async XLA Ops:
  7.2 240.3 %copy-start = (bf16[1,1,2048,384]{3,2,1,0:T(8,128)(2,1)S(1)}, bf16[1,1,2048,384]{3,2,1,0:T(8,128)(2,1)}, u32[]{:S(2)}) copy-start(bf16[1,1,2048,384]{3,2,1,0:T(8,128)(2,1)} %param.21) | copy-start | bytes 4718596
  7.2 19.0 %copy-start.6 = (s32[48,8]{0,1:T(8,128)S(1)}, s32[48,8]{0,1:T(8,128)}, u32[]{:S(2)}) copy-start(s32[48,8]{0,1:T(8,128)} %param.20) | copy-start | bytes 4612
  7.2 44.4 %copy-start.2 = (bf16[48,2048]{1,0:T(8,128)(2,1)S(1)}, bf16[48,2048]{1,0:T(8,128)(2,1)}, u32[]{:S(2)}) copy-start(bf16[48,2048]{1,0:T(8,128)(2,1)} %param.12) | copy-start | bytes 589828
  7.2 45.5 %copy-start.7 = (f32[2048]{0:T(1024)S(1)}, f32[2048]{0:T(1024)}, u32[]{:S(2)}) copy-start(f32[2048]{0:T(1024)} %param.18) | copy-start | bytes 24580
  7.2 44.4 %reduce-scatter.2.cloned.1.call-start = ((), (), s32[]{:S(2)}) async-start(), calls=%async_computation.5 | async-start | bytes 983040 | tf_op jit(solution)/shard_map/reduce_scatter | solution.py:91
  8.2 15.5 %collective-permute-start.1 = (bf16[192,128]{1,0:T(8,128)(2,1)S(1)}, bf16[192,128]{1,0:T(8,128)(2,1)S(1)}, u32[]{:S(2)}, u32[]{:S(2)}) collective-permute-start(bf16[192,128]{1,0:T(8,128)(2,1)S(1)} %constant_dynamic-slice_fusion), channel_id=1, source_target_pairs={{0,4},{4,8},{8,12},{12,16},{16,20},{20,24},{24,28},{1,5},{5,9},{9,... | collective-permute-start | bytes 147464 | tf_op jit(solution)/shard_map/ppermute | solution.py:13
  18.1 5.2 %collective-permute-start = (bf16[192,128]{1,0:T(8,128)(2,1)S(1)}, bf16[192,128]{1,0:T(8,128)(2,1)S(1)}, u32[]{:S(2)}, u32[]{:S(2)}) collective-permute-start(bf16[192,128]{1,0:T(8,128)(2,1)S(1)} %pad_maximum_fusion), channel_id=1, source_target_pairs={{0,4},{4,8},{8,12},{12,16},{16,20},{20,24},{24,28},{1,5},{5,9},{9,... | collective-permute-start | bytes 147464 | tf_op jit(solution)/shard_map/ppermute | solution.py:13
  247.4 4.7 copy-start.8
  381.6 5.1 %copy-start.5 = (f32[48,16]{0,1:T(8,128)S(1)}, f32[48,16]{0,1:T(8,128)}, u32[]{:S(2)}) copy-start(f32[48,16]{0,1:T(8,128)} %param.23) | copy-start | bytes 9220
  381.6 5.1 %copy-start.4 = (bf16[2048,16]{0,1:T(8,128)(2,1)S(1)}, bf16[2048,16]{0,1:T(8,128)(2,1)}, u32[]{:S(2)}) copy-start(bf16[2048,16]{0,1:T(8,128)(2,1)} %param.19) | copy-start | bytes 196612
  381.6 58.9 %all-to-all-start.3 = ((bf16[8,4,36,2048]{3,0,2,1:T(8,128)(2,1)}), bf16[8,4,36,2048]{3,0,2,1:T(8,128)(2,1)}, u32[]{:S(2)}, u32[]{:S(2)}) async-start(bf16[8,4,36,2048]{3,0,2,1:T(8,128)(2,1)} %copy.80), calls=%async_computation.4 | async-start | bytes 9437184 | tf_op jit(solution)/shard_map/all_to_all | solution.py:154
  463.8 6.5 %copy-start.1 = (bf16[1,1,2048,384]{3,2,1,0:T(8,128)(2,1)S(1)}, bf16[1,1,2048,384]{3,2,1,0:T(8,128)(2,1)}, u32[]{:S(2)}) copy-start(bf16[1,1,2048,384]{3,2,1,0:T(8,128)(2,1)} %param.21) | copy-start | bytes 4718596
  463.8 5.2 %copy-start.3 = (bf16[48,2048]{1,0:T(8,128)(2,1)S(1)}, bf16[48,2048]{1,0:T(8,128)(2,1)}, u32[]{:S(2)}) copy-start(bf16[48,2048]{1,0:T(8,128)(2,1)} %reduce-scatter.2.cloned.1.call-done) | copy-start | bytes 589828
Sparse Core Ops, SparseCore 0:
  26.3 25.2 reduce-scatter.1
where the time goes:
time: 479 us; the launch traced here: 477 us
  blocking collectives  274 us (57%)
  waiting for transfers between devices  77.6 us (16%)
  local copies, waits for them, and re-layouts  68.4 us (14%)
  matrix products  14.9 us (3%)
  other arithmetic  14.8 us (3%)
  between operations  14.4 us (3%)
  starting transfers between devices  13.4 us (3%)
    all_to_all x1, blocking collectives, body(): lax.all_to_all(doubled, 'ctx', split_axis=0, concat_axis=0, tiled=True)  110 us
    all_to_all x1, blocking collectives, body(): lax.all_to_all(partial_value.reshape(ctx_count, exp_count, capacity, widt...  108 us
    all_to_all x1, blocking collectives, body(): lax.all_to_all(lax.all_to_all(doubled, 'ctx', split_axis=0, concat_axis=0...  56.4 us
    all_to_all x1, waiting for transfers between devices, body(): lax.all_to_all(lax.all_to_all(partial_value.reshape(ctx_count, exp_count,...  52.5 us
    reduce_scatter x1, waiting for transfers between devices, body(): lax.psum_scatter(lax.optimization_barrier(term).astype(jnp.float32).astyp...  23.4 us
    reshape x2, local copies, waits for them, and re-layouts, body(): partial_value.reshape(ctx_count, exp_count, capacity, width)  13.4 us
    slice x1, local copies, waits for them, and re-layouts, body(): paired[:, 0] + paired[:, 1]  12.3 us
    convert_element_type x1, local copies, waits for them, and re-layouts, body(): returned.reshape(per_column, 2, exp_count * capacity, width)  11 us
  transfers between devices with their start and end apart: 4, of which 3 were waited for; matrix products, arithmetic and copies ran while one was open for 2% of the time, Pallas kernels for 0%

commit v1 on v0

--- a/solution.py
+++ b/solution.py
@@ -38,7 +38,7 @@
     return (jax.nn.silu(act[:, :inner]) * act[:, inner:]).astype(jnp.bfloat16)
 
 
-def body(
+def sparse_body(
     hidden,
     queries,
     keys,
@@ -171,6 +171,161 @@
     return (layer_out, router_kl)
 
 
+def swapped(value, axis, mask):
+    count = lax.axis_size(axis)
+    return lax.ppermute(value, axis, [(source, source ^ mask) for source in range(count)])
+
+
+def dense_body(
+    hidden,
+    queries,
+    keys,
+    values,
+    positions,
+    out_weight,
+    ffn_gain,
+    router_weight,
+    routes,
+    expert_in,
+    expert_out,
+    rollout_logits,
+):
+    block_rows = queries.shape[0]
+    head_dim = queries.shape[1]
+    width = hidden.shape[1]
+    token_rows = hidden.shape[0]
+    experts_total = router_weight.shape[1]
+    ctx_index = lax.axis_index("ctx")
+    exp_index = lax.axis_index("exp")
+    exp_count = lax.axis_size("exp")
+    kv_heads = keys.shape[1] // head_dim
+    per_column = experts_total // exp_count
+    share = exp_count // kv_heads
+    bits = []
+    step = exp_count // 2
+    while step:
+        bits.append(step)
+        step //= 2
+
+    weight_in = expert_in[0, 0]
+    weight_out = expert_out[0, 0]
+    kv_own = jnp.concatenate([keys, values], axis=1)
+    kv_before = passed_along(kv_own, "ctx", 1)
+    query_rows = lax.all_to_all(queries, "exp", split_axis=0, concat_axis=1, tiled=True)
+    other_in = swapped(weight_in, "ctx", 1)
+    other_out = swapped(weight_out, "ctx", 1)
+    out_rows = out_weight
+    for bit in bits:
+        out_rows = jnp.concatenate([out_rows, swapped(out_rows, "exp", bit)], axis=0)
+    head_order = [0]
+    for bit in bits:
+        head_order = head_order + [h ^ bit for h in head_order]
+
+    row_start = exp_index * token_rows
+    own_positions = lax.dynamic_slice_in_dim(positions, row_start, token_rows, 0)
+    spectrum = frequencies(head_dim)
+    key_positions = jnp.concatenate(
+        [positions[0] - block_rows + jnp.arange(block_rows, dtype=jnp.int32), positions]
+    )
+    key_angle = key_positions.astype(jnp.float32)[:, None] * spectrum[None, :]
+    query_angle = own_positions.astype(jnp.float32)[:, None] * spectrum[None, :]
+    kv_window = jnp.concatenate([kv_before, kv_own], axis=0)
+    query_at = row_start + jnp.arange(token_rows, dtype=jnp.int32)
+    key_at = jnp.arange(2 * block_rows, dtype=jnp.int32) - block_rows
+    allowed = (key_at[None, :] <= query_at[:, None]) & (
+        key_at[None, :] >= (query_at - own_positions)[:, None]
+    )
+    heads = []
+    key_rots = [
+        rotate(head_norm(kv_window[:, g * head_dim : (g + 1) * head_dim]), key_angle).astype(jnp.bfloat16)
+        for g in range(kv_heads)
+    ]
+    for h in range(exp_count):
+        g = h // share
+        query_rot = rotate(
+            head_norm(query_rows[:, h * head_dim : (h + 1) * head_dim]), query_angle
+        ).astype(jnp.bfloat16)
+        scores = lax.dot_general(
+            query_rot, key_rots[g], (((1,), (1,)), ((), ())), preferred_element_type=jnp.float32
+        ) / jnp.sqrt(jnp.float32(head_dim))
+        raw = jnp.where(allowed, jnp.exp(scores), 0.0)
+        weights = (raw / jnp.sum(raw, axis=1, keepdims=True)).astype(jnp.bfloat16)
+        value_cols = kv_window[:, (kv_heads + g) * head_dim : (kv_heads + g + 1) * head_dim]
+        heads.append(
+            jnp.dot(weights, value_cols, preferred_element_type=jnp.float32).astype(jnp.bfloat16)
+        )
+    stacked = jnp.stack(heads)
+    head_out = jnp.concatenate(
+        [lax.dynamic_index_in_dim(stacked, exp_index ^ h, 0, keepdims=False) for h in head_order], axis=1
+    )
+    summed = jnp.dot(head_out, out_rows, preferred_element_type=jnp.float32)
+    attended = (hidden.astype(jnp.float32) + summed).astype(jnp.bfloat16)
+    widened = attended.astype(jnp.float32)
+    moe_in = (
+        widened
+        / jnp.sqrt(jnp.mean(widened * widened, axis=1, keepdims=True) + eps)
+        * ffn_gain[None, :]
+    ).astype(jnp.bfloat16)
+    router_logits = jnp.dot(moe_in, router_weight, preferred_element_type=jnp.float32)
+    current_logprob = router_logits - jnp.log(
+        jnp.sum(jnp.exp(router_logits), axis=1, keepdims=True)
+    )
+    rollout_logprob = rollout_logits - jnp.log(
+        jnp.sum(jnp.exp(rollout_logits), axis=1, keepdims=True)
+    )
+    router_kl = jnp.sum(jnp.exp(rollout_logprob) * (rollout_logprob - current_logprob), axis=1)
+    expert_ids = jnp.arange(experts_total, dtype=jnp.int32)
+    picked = jnp.any(routes[:, :, None] == expert_ids[None, None, :], axis=1)
+    gate_raw = jnp.where(picked, jnp.exp(router_logits), 0.0)
+    gates = (gate_raw / jnp.sum(gate_raw, axis=1, keepdims=True)).astype(jnp.bfloat16)
+    lanes = -(-experts_total // 128) * 128
+    payload = jnp.concatenate(
+        [moe_in, jnp.pad(gates, ((0, 0), (0, lanes - experts_total)))], axis=1
+    )
+
+    gathered = jnp.stack([payload] + [swapped(payload, "ctx", 2 * k) for k in range(1, per_column)])
+    for bit in bits:
+        gathered = jnp.stack([gathered, swapped(gathered, "exp", bit)])
+    flat = gathered.reshape(-1, width + lanes)
+    tokens = flat[:, :width]
+    gate = lax.dynamic_slice_in_dim(
+        flat[:, width:], exp_index * per_column + ctx_index // 2, 1, 1
+    ).astype(jnp.float32)
+    inner = jnp.concatenate(
+        [
+            activate(jnp.dot(tokens, weight_in, preferred_element_type=jnp.float32)),
+            activate(jnp.dot(tokens, other_in, preferred_element_type=jnp.float32)),
+        ],
+        axis=1,
+    )
+    partial = jnp.dot(
+        inner, jnp.concatenate([weight_out, other_out], axis=0), preferred_element_type=jnp.float32
+    )
+    partial = (partial * gate).astype(jnp.bfloat16)
+    for bit in reversed(bits):
+        halves = partial.reshape(2, -1, width)
+        partial = (
+            halves[0].astype(jnp.float32) + swapped(halves[1], "exp", bit).astype(jnp.float32)
+        ).astype(jnp.bfloat16)
+    blocks = partial.reshape(per_column, token_rows, width)
+    moe_out = blocks[0].astype(jnp.float32)
+    for k in range(1, per_column):
+        moe_out = moe_out + swapped(blocks[k], "ctx", 2 * k).astype(jnp.float32)
+    layer_out = (attended.astype(jnp.float32) + moe_out).astype(jnp.bfloat16)
+    return (layer_out, router_kl)
+
+
+def powers_of_two(*counts):
+    return all(count & (count - 1) == 0 for count in counts)
+
+
+def body(*arrays):
+    experts_total = arrays[7].shape[1]
+    exp_count, ctx_count = lax.axis_size("exp"), lax.axis_size("ctx")
+    dense = experts_total <= 2 * arrays[8].shape[1] and powers_of_two(exp_count, ctx_count)
+    return (dense_body if dense else sparse_body)(*arrays)
+
+
 def solution(mesh):
     return jax.shard_map(
         body,

time: 479 us -> 174 us (0.36)
  blocking collectives: 274 us -> 0 us
  local copies, waits for them, and re-layouts: 68.4 us -> 4.62 us
  waiting for transfers between devices: 77.6 us -> 117 us
  starting transfers between devices: 13.4 us -> 28.1 us
  between operations: 14.4 us -> 1.74 us
  other arithmetic: 14.8 us -> 8.71 us
    all_to_all x3 -> x0, blocking collectives: 274 us -> none  [the longest x1 110 us: body(): lax.all_to_all(doubled, 'ctx', split_axis=0, concat_axis=0, tiled=True)]
    ppermute x0 -> x14, waiting for transfers between devices: none -> 117 us  [swapped(): lax.ppermute(value, axis, [(source, source ^ mask) for source in range(co...]
    all_to_all x1, waiting for transfers between devices: 52.5 us -> 0.01 us  [dense_body(): lax.all_to_all(queries, 'exp', split_axis=0, concat_axis=1, tiled=True)]
    reduce_scatter x1 -> x0, waiting for transfers between devices: 23.4 us -> none  [body(): lax.psum_scatter(lax.optimization_barrier(term).astype(jnp.float32).astyp...]
    reshape x3 -> x0, local copies, waits for them, and re-layouts: 20.6 us -> none  [the longest x2 13.4 us: body(): partial_value.reshape(ctx_count, exp_count, capacity, width)]
    ppermute x0 -> x14, starting transfers between devices: none -> 19.7 us  [swapped(): lax.ppermute(value, axis, [(source, source ^ mask) for source in range(co...]
    all_to_all x3 -> x1, local copies, waits for them, and re-layouts: 12.2 us -> 0.01 us  [dense_body(): lax.all_to_all(queries, 'exp', split_axis=0, concat_axis=1, tiled=True)]
    convert_element_type x2 -> x0, local copies, waits for them, and re-layouts: 11.1 us -> none  [the longest x1 11 us: body(): returned.reshape(per_column, 2, exp_count * capacity, width)]
  transfers between devices with their start and end apart: 4 -> 16, of which waited for: 3 -> 12; matrix products, arithmetic and copies ran while one was open for 2% -> 11% of each run, Pallas kernels for 0% -> 0%
where the time goes in v1:
time: 174 us; the launch traced here: 173 us
  waiting for transfers between devices  117 us (67%)
  starting transfers between devices  28.1 us (16%)
  matrix products  12.7 us (7%)
  other arithmetic  8.71 us (5%)
  local copies, waits for them, and re-layouts  4.62 us (3%)
  between operations  1.74 us (1%)
    ppermute x14, waiting for transfers between devices, swapped(): lax.ppermute(value, axis, [(source, source ^ mask) for source in range(co...  117 us
    ppermute x14, starting transfers between devices, swapped(): lax.ppermute(value, axis, [(source, source ^ mask) for source in range(co...  19.7 us
    all_to_all x1, starting transfers between devices, dense_body(): lax.all_to_all(queries, 'exp', split_axis=0, concat_axis=1, tiled=True)  4.35 us
    ppermute x1, starting transfers between devices, passed_along(): lax.ppermute(value, axis, [(source, source + steps) for source in range(i...  3.96 us
    dot_general x1, matrix products, dense_body(): jnp.dot(tokens, weight_in, preferred_element_type=jnp.float32)  3.78 us
  transfers between devices with their start and end apart: 16, of which 12 were waited for; matrix products, arithmetic and copies ran while one was open for 11% of the time, Pallas kernels for 0%

profile of v1, /device:TPU:0, one launch (start us, length us, event | category | flops | bytes accessed | tf_op | source)
XLA Modules:
  0.0 173.2 jit_solution(16908108203952472361)
XLA Ops:
  0.6 4.4 %all-to-all-start = ((bf16[4,48,128]{2,1,0:T(8,128)(2,1)}), bf16[4,48,128]{2,1,0:T(8,128)(2,1)S(1)}, u32[]{:S(2)}, u32[]{:S(2)}) async-start(bf16[4,48,128]{2,1,0:T(8,128)(2,1)} %bitcast.50), calls=%async_computation | async-start | bytes 98304 | tf_op jit(solution)/shard_map/all_to_all | solution.py:214
  5.0 1.0 copy.29
  6.0 1.0 copy.30
  7.0 4.0 %collective-permute-start = (bf16[192,512]{0,1:T(8,128)(2,1)S(1)}, bf16[192,512]{0,1:T(8,128)(2,1)S(1)}, u32[]{:S(2)}, u32[]{:S(2)}) collective-permute-start(bf16[192,512]{0,1:T(8,128)(2,1)S(1)} %pad_maximum_fusion.4), channel_id=1, source_target_pairs={{0,4},{4,8},{8,12},{12,16},{16,20},{20,24},{24,28},{1,5},{5,9},{9,... | collective-permute-start | bytes 589832 | tf_op jit(solution)/shard_map/ppermute | solution.py:13
  11.0 2.1 %collective-permute-start.1 = (bf16[128,2048]{1,0:T(8,128)(2,1)}, bf16[128,2048]{1,0:T(8,128)(2,1)S(1)}, u32[]{:S(2)}, u32[]{:S(2)}) collective-permute-start(bf16[128,2048]{1,0:T(8,128)(2,1)} %param.17), channel_id=1, source_target_pairs={{0,2},{1,3},{2,0},{3,1},{4,6},{5,7},{6,4},{7,5},{8,10},{9,11},{10,... | collective-permute-start | bytes 1572872 | tf_op jit(solution)/shard_map/ppermute | solution.py:176
  13.1 1.2 slice.120
  15.7 0.8 add_convert_fusion.3
  19.4 5.9 %collective-permute-done.1 = bf16[128,2048]{1,0:T(8,128)(2,1)S(1)} collective-permute-done((bf16[128,2048]{1,0:T(8,128)(2,1)}, bf16[128,2048]{1,0:T(8,128)(2,1)S(1)}, u32[]{:S(2)}, u32[]{:S(2)}) %collective-permute-start.1) | collective-permute-done | bytes 524320 | tf_op jit(solution)/shard_map/ppermute | solution.py:176
  26.8 1.3 collective-permute-done.2
  30.1 1.6 collective-permute-start.3
  31.8 2.6 %collective-permute-start.4 = (bf16[48,2176]{1,0:T(8,128)(2,1)S(1)}, bf16[48,2176]{1,0:T(8,128)(2,1)S(1)}, u32[]{:S(2)}, u32[]{:S(2)}) collective-permute-start(bf16[48,2176]{1,0:T(8,128)(2,1)S(1)} %get-tuple-element.20), channel_id=1, source_target_pairs={{0,16},{4,20},{8,24},{12,28},{16,0},{20,4},{24,8},{28,12},{1,17},{... | collective-permute-start | bytes 626696 | tf_op jit(solution)/shard_map/ppermute | solution.py:176
  34.6 6.7 %collective-permute-done.3 = bf16[48,2176]{1,0:T(8,128)(2,1)S(1)} collective-permute-done((bf16[48,2176]{1,0:T(8,128)(2,1)S(1)}, bf16[48,2176]{1,0:T(8,128)(2,1)S(1)}, u32[]{:S(2)}, u32[]{:S(2)}) %collective-permute-start.3) | collective-permute-done | bytes 208928 | tf_op jit(solution)/shard_map/ppermute | solution.py:176
  41.3 8.4 %collective-permute-done.4 = bf16[48,2176]{1,0:T(8,128)(2,1)S(1)} collective-permute-done((bf16[48,2176]{1,0:T(8,128)(2,1)S(1)}, bf16[48,2176]{1,0:T(8,128)(2,1)S(1)}, u32[]{:S(2)}, u32[]{:S(2)}) %collective-permute-start.4) | collective-permute-done | bytes 208928 | tf_op jit(solution)/shard_map/ppermute | solution.py:176
  49.8 1.7 %collective-permute-start.6 = (bf16[4,48,2176]{2,1,0:T(8,128)(2,1)S(1)}, bf16[4,48,2176]{2,1,0:T(8,128)(2,1)S(1)}, u32[]{:S(2)}, u32[]{:S(2)}) collective-permute-start(bf16[4,48,2176]{2,1,0:T(8,128)(2,1)S(1)} %get-tuple-element.13), channel_id=1, source_target_pairs={{0,2},{1,3},{2,0},{3,1},{4,6},{5,7},{6,4},{7,5},{8,10},{9,11},{10,... | collective-permute-start | bytes 2506760 | tf_op jit(solution)/shard_map/ppermute | solution.py:176
  51.5 16.9 %collective-permute-done.6 = bf16[4,48,2176]{2,1,0:T(8,128)(2,1)S(1)} collective-permute-done((bf16[4,48,2176]{2,1,0:T(8,128)(2,1)S(1)}, bf16[4,48,2176]{2,1,0:T(8,128)(2,1)S(1)}, u32[]{:S(2)}, u32[]{:S(2)}) %collective-permute-start.6) | collective-permute-done | bytes 835616 | tf_op jit(solution)/shard_map/ppermute | solution.py:176
  68.8 1.6 collective-permute-start.8
  70.8 1.6 collective-permute-done.7
  72.4 1.8 %pad_maximum_fusion = bf16[2,2,4,48,2176]{4,3,2,1,0:T(8,128)(2,1)S(1)} fusion(bf16[1,2,4,48,2176]{4,3,2,1,0:T(8,128)(2,1)} %bitcast.18, bf16[1,2,4,48,2176]{4,3,2,1,0:T(8,128)(2,1)S(1)} %get-tuple-element.10), kind=kLoop, calls=%fused_computation.1 | loop fusion | flops 1671168 | bytes 6684672 | tf_op jit(solution)/shard_map/stack | solution.py:288
  74.2 32.1 %collective-permute-done.8 = bf16[2048,384]{1,0:T(8,128)(2,1)} collective-permute-done((bf16[2048,384]{1,0:T(8,128)(2,1)}, bf16[2048,384]{1,0:T(8,128)(2,1)}, u32[]{:S(2)}, u32[]{:S(2)}) %collective-permute-start.8) | collective-permute-done | bytes 1572896 | tf_op jit(solution)/shard_map/ppermute | solution.py:176
  106.3 2.9 %fusion = f32[768,384]{0,1:T(8,128)S(1)} fusion(bf16[2048,384]{1,0:T(8,128)(2,1)} %collective-permute-done.8, bf16[768,2176]{1,0:T(8,128)(2,1)S(1)} %bitcast.44), kind=kOutput, calls=%fused_computation.3 | convolution fusion | flops 1207959552 | bytes 5898240 | tf_op jit(solution)/shard_map/dot_general | solution.py:297
  109.7 3.8 %fusion.2 = f32[768,384]{0,1:T(8,128)S(1)} fusion(bf16[768,2176]{1,0:T(8,128)(2,1)} %bitcast.45, bf16[1,1,2048,384]{3,2,1,0:T(8,128)(2,1)} %param.21), kind=kOutput, calls=%fused_computation.5 | convolution fusion | flops 1207959552 | bytes 5898240 | tf_op jit(solution)/shard_map/dot_general | solution.py:296
  113.7 9.1 %collective-permute-done.9 = bf16[192,2048]{1,0:T(8,128)(2,1)} collective-permute-done((bf16[192,2048]{1,0:T(8,128)(2,1)}, bf16[192,2048]{1,0:T(8,128)(2,1)}, u32[]{:S(2)}, u32[]{:S(2)}) %collective-permute-start.9) | collective-permute-done | bytes 786464 | tf_op jit(solution)/shard_map/ppermute | solution.py:176
  122.7 3.2 %multiply_convert_fusion = bf16[768,2048]{1,0:T(8,128)(2,1)S(1)} fusion(f32[768]{0:T(1024)S(1)} %convert_reduce_fusion, bf16[192,2048]{1,0:T(8,128)(2,1)} %collective-permute-done.9, bf16[192,2048]{1,0:T(8,128)(2,1)} %bitcast.21, bf16[768,192]{0,1:T(8,128)(2,1)S(1)} %fusion.26, bf16[768,192]{0,1:T(8,128)(2,1)S(1)} %fusion.27), kind=kOutput, calls=%fused_computation | convolution fusion | flops 1215430656 | bytes 5311488 | tf_op jit(solution)/shard_map/dot_general | solution.py:301
  126.1 3.4 %collective-permute-done.10 = bf16[384,2048]{1,0:T(8,128)(2,1)S(1)} collective-permute-done((bf16[384,2048]{1,0:T(8,128)(2,1)S(1)}, bf16[384,2048]{1,0:T(8,128)(2,1)S(1)}, u32[]{:S(2)}, u32[]{:S(2)}) %collective-permute-start.10) | collective-permute-done | bytes 1572896 | tf_op jit(solution)/shard_map/ppermute | solution.py:176
  130.2 1.7 collective-permute-start.11
  132.0 17.9 %collective-permute-done.11 = bf16[192,2048]{1,0:T(8,128)(2,1)S(1)} collective-permute-done((bf16[192,2048]{1,0:T(8,128)(2,1)S(1)}, bf16[192,2048]{1,0:T(8,128)(2,1)S(1)}, u32[]{:S(2)}, u32[]{:S(2)}) %collective-permute-start.11) | collective-permute-done | bytes 786464 | tf_op jit(solution)/shard_map/ppermute | solution.py:176
  150.2 5.0 %collective-permute-start.12 = (bf16[48,2048]{1,0:T(8,128)(2,1)S(1)}, bf16[48,2048]{1,0:T(8,128)(2,1)S(1)}, u32[]{:S(2)}, u32[]{:S(2)}) collective-permute-start(bf16[48,2048]{1,0:T(8,128)(2,1)S(1)} %get-tuple-element.14), channel_id=1, source_target_pairs={{0,8},{4,12},{8,0},{12,4},{16,24},{20,28},{24,16},{28,20},{1,9},{5... | collective-permute-start | bytes 589832 | tf_op jit(solution)/shard_map/ppermute | solution.py:176
  155.2 1.1 collective-permute-start.13
  156.3 1.4 collective-permute-start.14
  158.3 4.2 %collective-permute-done.12 = bf16[48,2048]{1,0:T(8,128)(2,1)S(1)} collective-permute-done((bf16[48,2048]{1,0:T(8,128)(2,1)S(1)}, bf16[48,2048]{1,0:T(8,128)(2,1)S(1)}, u32[]{:S(2)}, u32[]{:S(2)}) %collective-permute-start.12) | collective-permute-done | bytes 196640 | tf_op jit(solution)/shard_map/ppermute | solution.py:176
  162.4 9.9 %collective-permute-done.13 = bf16[48,2048]{1,0:T(8,128)(2,1)S(1)} collective-permute-done((bf16[48,2048]{1,0:T(8,128)(2,1)S(1)}, bf16[48,2048]{1,0:T(8,128)(2,1)S(1)}, u32[]{:S(2)}, u32[]{:S(2)}) %collective-permute-start.13) | collective-permute-done | bytes 196640 | tf_op jit(solution)/shard_map/ppermute | solution.py:176
  172.4 0.8 add_convert_fusion.2
  (79 shorter events, 10.6 us)
Async XLA Ops:
  0.6 29.0 %copy-start = (bf16[2048,16]{0,1:T(8,128)(2,1)S(1)}, bf16[2048,16]{0,1:T(8,128)(2,1)}, u32[]{:S(2)}) copy-start(bf16[2048,16]{0,1:T(8,128)(2,1)} %param.19) | copy-start | bytes 196612
  0.6 16.6 %all-to-all-start = ((bf16[4,48,128]{2,1,0:T(8,128)(2,1)}), bf16[4,48,128]{2,1,0:T(8,128)(2,1)S(1)}, u32[]{:S(2)}, u32[]{:S(2)}) async-start(bf16[4,48,128]{2,1,0:T(8,128)(2,1)} %bitcast.50), calls=%async_computation | async-start | bytes 98304 | tf_op jit(solution)/shard_map/all_to_all | solution.py:214
  7.0 10.8 %collective-permute-start = (bf16[192,512]{0,1:T(8,128)(2,1)S(1)}, bf16[192,512]{0,1:T(8,128)(2,1)S(1)}, u32[]{:S(2)}, u32[]{:S(2)}) collective-permute-start(bf16[192,512]{0,1:T(8,128)(2,1)S(1)} %pad_maximum_fusion.4), channel_id=1, source_target_pairs={{0,4},{4,8},{8,12},{12,16},{16,20},{20,24},{24,28},{1,5},{5,9},{9,... | collective-permute-start | bytes 589832 | tf_op jit(solution)/shard_map/ppermute | solution.py:13
  11.0 14.3 %collective-permute-start.1 = (bf16[128,2048]{1,0:T(8,128)(2,1)}, bf16[128,2048]{1,0:T(8,128)(2,1)S(1)}, u32[]{:S(2)}, u32[]{:S(2)}) collective-permute-start(bf16[128,2048]{1,0:T(8,128)(2,1)} %param.17), channel_id=1, source_target_pairs={{0,2},{1,3},{2,0},{3,1},{4,6},{5,7},{6,4},{7,5},{8,10},{9,11},{10,... | collective-permute-start | bytes 1572872 | tf_op jit(solution)/shard_map/ppermute | solution.py:176
  17.8 7.5 %copy-start.4 = (bf16[128,2048]{1,0:T(8,128)(2,1)S(1)}, bf16[128,2048]{1,0:T(8,128)(2,1)}, u32[]{:S(2)}) copy-start(bf16[128,2048]{1,0:T(8,128)(2,1)} %param.17) | copy-start | bytes 1572868
  19.4 8.7 %copy-start.7 = (bf16[48,2048]{1,0:T(8,128)(2,1)S(1)}, bf16[48,2048]{1,0:T(8,128)(2,1)}, u32[]{:S(2)}) copy-start(bf16[48,2048]{1,0:T(8,128)(2,1)} %param.12) | copy-start | bytes 589828
  25.4 2.7 %collective-permute-start.2 = (bf16[256,2048]{1,0:T(8,128)(2,1)S(1)}, bf16[256,2048]{1,0:T(8,128)(2,1)S(1)}, u32[]{:S(2)}, u32[]{:S(2)}) collective-permute-start(bf16[256,2048]{1,0:T(8,128)(2,1)S(1)} %pad_maximum_fusion.2), channel_id=1, source_target_pairs={{0,1},{1,0},{2,3},{3,2},{4,5},{5,4},{6,7},{7,6},{8,9},{9,8},{10,11... | collective-permute-start | bytes 3145736 | tf_op jit(solution)/shard_map/ppermute | solution.py:176
  28.1 1.4 copy-start.6
  28.7 0.8 copy-start.2
  30.1 11.1 %collective-permute-start.3 = (bf16[48,2176]{1,0:T(8,128)(2,1)S(1)}, bf16[48,2176]{1,0:T(8,128)(2,1)S(1)}, u32[]{:S(2)}, u32[]{:S(2)}) collective-permute-start(bf16[48,2176]{1,0:T(8,128)(2,1)S(1)} %get-tuple-element.20), channel_id=1, source_target_pairs={{0,8},{4,12},{8,0},{12,4},{16,24},{20,28},{24,16},{28,20},{1,9},{5... | collective-permute-start | bytes 626696 | tf_op jit(solution)/shard_map/ppermute | solution.py:176
  31.8 17.9 %collective-permute-start.4 = (bf16[48,2176]{1,0:T(8,128)(2,1)S(1)}, bf16[48,2176]{1,0:T(8,128)(2,1)S(1)}, u32[]{:S(2)}, u32[]{:S(2)}) collective-permute-start(bf16[48,2176]{1,0:T(8,128)(2,1)S(1)} %get-tuple-element.20), channel_id=1, source_target_pairs={{0,16},{4,20},{8,24},{12,28},{16,0},{20,4},{24,8},{28,12},{1,17},{... | collective-permute-start | bytes 626696 | tf_op jit(solution)/shard_map/ppermute | solution.py:176
  34.3 15.3 %collective-permute-start.5 = (bf16[48,2176]{1,0:T(8,128)(2,1)S(1)}, bf16[48,2176]{1,0:T(8,128)(2,1)S(1)}, u32[]{:S(2)}, u32[]{:S(2)}) collective-permute-start(bf16[48,2176]{1,0:T(8,128)(2,1)S(1)} %get-tuple-element.20), channel_id=1, source_target_pairs={{0,24},{4,28},{8,16},{12,20},{16,8},{20,12},{24,0},{28,4},{1,25},{... | collective-permute-start | bytes 626696 | tf_op jit(solution)/shard_map/ppermute | solution.py:176
  49.8 18.6 %collective-permute-start.6 = (bf16[4,48,2176]{2,1,0:T(8,128)(2,1)S(1)}, bf16[4,48,2176]{2,1,0:T(8,128)(2,1)S(1)}, u32[]{:S(2)}, u32[]{:S(2)}) collective-permute-start(bf16[4,48,2176]{2,1,0:T(8,128)(2,1)S(1)} %get-tuple-element.13), channel_id=1, source_target_pairs={{0,2},{1,3},{2,0},{3,1},{4,6},{5,7},{6,4},{7,5},{8,10},{9,11},{10,... | collective-permute-start | bytes 2506760 | tf_op jit(solution)/shard_map/ppermute | solution.py:176
  68.7 3.7 %collective-permute-start.7 = (bf16[2,4,48,2176]{3,2,1,0:T(8,128)(2,1)S(1)}, bf16[2,4,48,2176]{3,2,1,0:T(8,128)(2,1)}, u32[]{:S(2)}, u32[]{:S(2)}) collective-permute-start(bf16[2,4,48,2176]{3,2,1,0:T(8,128)(2,1)S(1)} %get-tuple-element.11), channel_id=1, source_target_pairs={{0,1},{1,0},{2,3},{3,2},{4,5},{5,4},{6,7},{7,6},{8,9},{9,8},{10,11... | collective-permute-start | bytes 5013512 | tf_op jit(solution)/shard_map/ppermute | solution.py:176
  68.8 37.6 %collective-permute-start.8 = (bf16[2048,384]{1,0:T(8,128)(2,1)}, bf16[2048,384]{1,0:T(8,128)(2,1)}, u32[]{:S(2)}, u32[]{:S(2)}) collective-permute-start(bf16[2048,384]{1,0:T(8,128)(2,1)} %bitcast.20), channel_id=1, source_target_pairs={{0,4},{4,0},{8,12},{12,8},{16,20},{20,16},{24,28},{28,24},{1,5},{5... | collective-permute-start | bytes 4718600 | tf_op jit(solution)/shard_map/ppermute | solution.py:176
  70.3 52.4 %collective-permute-start.9 = (bf16[192,2048]{1,0:T(8,128)(2,1)}, bf16[192,2048]{1,0:T(8,128)(2,1)}, u32[]{:S(2)}, u32[]{:S(2)}) collective-permute-start(bf16[192,2048]{1,0:T(8,128)(2,1)} %bitcast.21), channel_id=1, source_target_pairs={{0,4},{4,0},{8,12},{12,8},{16,20},{20,16},{24,28},{28,24},{1,5},{5... | collective-permute-start | bytes 2359304 | tf_op jit(solution)/shard_map/ppermute | solution.py:176
  74.2 35.0 %copy-start.1 = (bf16[2,2,4,48,2176]{4,3,2,1,0:T(8,128)(2,1)}, bf16[2,2,4,48,2176]{4,3,2,1,0:T(8,128)(2,1)S(1)}, u32[]{:S(2)}) copy-start(bf16[2,2,4,48,2176]{4,3,2,1,0:T(8,128)(2,1)S(1)} %pad_maximum_fusion) | copy-start | bytes 10027012
  126.1 3.5 %collective-permute-start.10 = (bf16[384,2048]{1,0:T(8,128)(2,1)S(1)}, bf16[384,2048]{1,0:T(8,128)(2,1)S(1)}, u32[]{:S(2)}, u32[]{:S(2)}) collective-permute-start(bf16[384,2048]{1,0:T(8,128)(2,1)S(1)} %slice.177), channel_id=1, source_target_pairs={{0,1},{1,0},{2,3},{3,2},{4,5},{5,4},{6,7},{7,6},{8,9},{9,8},{10,11... | collective-permute-start | bytes 4718600 | tf_op jit(solution)/shard_map/ppermute | solution.py:176
  130.2 27.5 %copy-start.5 = (f32[48,16]{0,1:T(8,128)S(1)}, f32[48,16]{0,1:T(8,128)}, u32[]{:S(2)}) copy-start(f32[48,16]{0,1:T(8,128)} %param.23) | copy-start | bytes 9220
  130.2 42.2 %copy-start.3 = (f32[48,2048]{1,0:T(8,128)S(1)}, f32[48,2048]{1,0:T(8,128)}, u32[]{:S(2)}) copy-start(f32[48,2048]{1,0:T(8,128)} %copy-done.2) | copy-start | bytes 1179652
  130.2 19.6 %collective-permute-start.11 = (bf16[192,2048]{1,0:T(8,128)(2,1)S(1)}, bf16[192,2048]{1,0:T(8,128)(2,1)S(1)}, u32[]{:S(2)}, u32[]{:S(2)}) collective-permute-start(bf16[192,2048]{1,0:T(8,128)(2,1)S(1)} %slice.179), channel_id=1, source_target_pairs={{0,2},{1,3},{2,0},{3,1},{4,6},{5,7},{6,4},{7,5},{8,10},{9,11},{10,... | collective-permute-start | bytes 2359304 | tf_op jit(solution)/shard_map/ppermute | solution.py:176
  150.2 12.2 %collective-permute-start.12 = (bf16[48,2048]{1,0:T(8,128)(2,1)S(1)}, bf16[48,2048]{1,0:T(8,128)(2,1)S(1)}, u32[]{:S(2)}, u32[]{:S(2)}) collective-permute-start(bf16[48,2048]{1,0:T(8,128)(2,1)S(1)} %get-tuple-element.14), channel_id=1, source_target_pairs={{0,8},{4,12},{8,0},{12,4},{16,24},{20,28},{24,16},{28,20},{1,9},{5... | collective-permute-start | bytes 589832 | tf_op jit(solution)/shard_map/ppermute | solution.py:176
  155.2 17.2 %collective-permute-start.13 = (bf16[48,2048]{1,0:T(8,128)(2,1)S(1)}, bf16[48,2048]{1,0:T(8,128)(2,1)S(1)}, u32[]{:S(2)}, u32[]{:S(2)}) collective-permute-start(bf16[48,2048]{1,0:T(8,128)(2,1)S(1)} %get-tuple-element.16), channel_id=1, source_target_pairs={{0,16},{4,20},{8,24},{12,28},{16,0},{20,4},{24,8},{28,12},{1,17},{... | collective-permute-start | bytes 589832 | tf_op jit(solution)/shard_map/ppermute | solution.py:176
  156.3 16.1 %collective-permute-start.14 = (bf16[48,2048]{1,0:T(8,128)(2,1)S(1)}, bf16[48,2048]{1,0:T(8,128)(2,1)S(1)}, u32[]{:S(2)}, u32[]{:S(2)}) collective-permute-start(bf16[48,2048]{1,0:T(8,128)(2,1)S(1)} %get-tuple-element.15), channel_id=1, source_target_pairs={{0,24},{4,28},{8,16},{12,20},{16,8},{20,12},{24,0},{28,4},{1,25},{... | collective-permute-start | bytes 589832 | tf_op jit(solution)/shard_map/ppermute | solution.py:176

commit v2 on v1

--- a/solution.py
+++ b/solution.py
@@ -1,6 +1,10 @@
+import functools
+
 import jax
 import jax.numpy as jnp
 from jax import lax
+from jax.experimental import pallas as pl
+from jax.experimental.pallas import tpu as pltpu
 from jax.sharding import PartitionSpec as P
 
 eps = 1e-06
@@ -176,6 +180,52 @@
     return lax.ppermute(value, axis, [(source, source ^ mask) for source in range(count)])
 
 
+def expert_kernel(parts, width, index_ref, *refs):
+    token_refs, refs = refs[:parts], refs[parts:]
+    own_in, first, second, own_out, other_out, keep_ref, send_ref, tokens, gates = refs
+    rows = token_refs[0].shape[0]
+    lanes = token_refs[0].shape[1] - width
+    for p, ref in enumerate(token_refs):
+        tokens[p * rows : (p + 1) * rows, :] = ref[:, :width]
+        picked = lax.broadcasted_iota(jnp.int32, (rows, lanes), 1) == index_ref[0]
+        gates[p * rows : (p + 1) * rows, :] = jnp.sum(
+            jnp.where(picked, ref[:, width:].astype(jnp.float32), 0.0), axis=1, keepdims=True
+        )
+    depth = width // 2
+    own = jnp.dot(tokens[...], own_in[...], preferred_element_type=jnp.float32)
+    other = jnp.dot(tokens[:, :depth], first[...], preferred_element_type=jnp.float32) + jnp.dot(
+        tokens[:, depth:], second[...], preferred_element_type=jnp.float32
+    )
+    out = jnp.dot(activate(own), own_out[...], preferred_element_type=jnp.float32) + jnp.dot(
+        activate(other), other_out[...], preferred_element_type=jnp.float32
+    )
+    out = (out * gates[...]).astype(jnp.bfloat16)
+    half = keep_ref.shape[0]
+    keep_ref[...] = out[:half]
+    send_ref[...] = out[half:]
+
+
+def expert_block(index, tokens, own_in, own_out, other_in, other_out, width):
+    parts = len(tokens)
+    rows = parts * tokens[0].shape[0]
+    half = jax.ShapeDtypeStruct((rows // 2, width), jnp.bfloat16)
+    vmem = pl.BlockSpec(memory_space=pltpu.VMEM)
+    return pl.pallas_call(
+        functools.partial(expert_kernel, parts, width),
+        out_shape=(half, half),
+        in_specs=[pl.BlockSpec(memory_space=pltpu.SMEM)] + [vmem] * (parts + 5),
+        out_specs=(vmem, vmem),
+        scratch_shapes=[
+            pltpu.VMEM((rows, width), jnp.bfloat16),
+            pltpu.VMEM((rows, 1), jnp.float32),
+        ],
+        compiler_params=pltpu.CompilerParams(vmem_limit_bytes=40 * 1024 * 1024),
+        cost_estimate=pl.CostEstimate(
+            flops=2 * rows * 3 * width * own_in.shape[1], bytes_accessed=8 << 20, transcendentals=0
+        ),
+    )(index, *tokens, own_in, other_in[0], other_in[1], own_out, other_out)
+
+
 def dense_body(
     hidden,
     queries,
@@ -212,8 +262,6 @@
     kv_own = jnp.concatenate([keys, values], axis=1)
     kv_before = passed_along(kv_own, "ctx", 1)
     query_rows = lax.all_to_all(queries, "exp", split_axis=0, concat_axis=1, tiled=True)
-    other_in = swapped(weight_in, "ctx", 1)
-    other_out = swapped(weight_out, "ctx", 1)
     out_rows = out_weight
     for bit in bits:
         out_rows = jnp.concatenate([out_rows, swapped(out_rows, "exp", bit)], axis=0)
@@ -283,34 +331,32 @@
         [moe_in, jnp.pad(gates, ((0, 0), (0, lanes - experts_total)))], axis=1
     )
 
-    gathered = jnp.stack([payload] + [swapped(payload, "ctx", 2 * k) for k in range(1, per_column)])
-    for bit in bits:
-        gathered = jnp.stack([gathered, swapped(gathered, "exp", bit)])
-    flat = gathered.reshape(-1, width + lanes)
-    tokens = flat[:, :width]
-    gate = lax.dynamic_slice_in_dim(
-        flat[:, width:], exp_index * per_column + ctx_index // 2, 1, 1
-    ).astype(jnp.float32)
-    inner = jnp.concatenate(
-        [
-            activate(jnp.dot(tokens, weight_in, preferred_element_type=jnp.float32)),
-            activate(jnp.dot(tokens, other_in, preferred_element_type=jnp.float32)),
-        ],
-        axis=1,
-    )
-    partial = jnp.dot(
-        inner, jnp.concatenate([weight_out, other_out], axis=0), preferred_element_type=jnp.float32
-    )
-    partial = (partial * gate).astype(jnp.bfloat16)
-    for bit in reversed(bits):
-        halves = partial.reshape(2, -1, width)
-        partial = (
-            halves[0].astype(jnp.float32) + swapped(halves[1], "exp", bit).astype(jnp.float32)
-        ).astype(jnp.bfloat16)
-    blocks = partial.reshape(per_column, token_rows, width)
-    moe_out = blocks[0].astype(jnp.float32)
-    for k in range(1, per_column):
-        moe_out = moe_out + swapped(blocks[k], "ctx", 2 * k).astype(jnp.float32)
+    first, second = weight_in[: width // 2], weight_in[width // 2 :]
+    other_first = swapped(first, "ctx", 1)
+    payload, other_first, second = lax.optimization_barrier((payload, other_first, second))
+    other_second = swapped(second, "ctx", 1)
+    blocks = [payload] + [swapped(payload, "ctx", 2 * k) for k in range(1, per_column)]
+    gathered = []
+    for k, block in enumerate(blocks):
+        parts = [block]
+        for bit in bits:
+            parts = parts + [swapped(part, "exp", bit) for part in parts]
+        gathered.append(parts)
+    expert_index = (exp_index * per_column + ctx_index // 2).reshape(1).astype(jnp.int32)
+    other_second, weight_out_late = lax.optimization_barrier((other_second, weight_out))
+    other_out = swapped(weight_out_late, "ctx", 1)
+    returned = {}
+    for k in sorted(range(per_column), key=lambda k: -min(k, 2.5)):
+        keep, send = expert_block(
+            expert_index, gathered[k], weight_in, weight_out, (other_first, other_second), other_out, width
+        )
+        for bit in reversed(bits):
+            total = keep.astype(jnp.float32) + swapped(send, "exp", bit).astype(jnp.float32)
+            total = total.astype(jnp.bfloat16)
+            half = total.shape[0] // 2
+            keep, send = total[:half], total[half:]
+        returned[k] = total if k == 0 else swapped(total, "ctx", 2 * k)
+    moe_out = sum(returned[k].astype(jnp.float32) for k in range(per_column))
     layer_out = (attended.astype(jnp.float32) + moe_out).astype(jnp.bfloat16)
     return (layer_out, router_kl)
 

time: 174 us -> 132 us (0.76)
  waiting for transfers between devices: 117 us -> 53.5 us
  starting transfers between devices: 28.1 us -> 40.2 us
  Pallas kernels: 0 us -> 11.6 us
  local copies, waits for them, and re-layouts: 4.62 us -> 15.5 us
  matrix products: 12.7 us -> 4.02 us
  other arithmetic: 8.71 us -> 4.71 us
    ppermute x14 -> x31, waiting for transfers between devices: 117 us -> 53.5 us  [swapped(): lax.ppermute(value, axis, [(source, source ^ mask) for source in range(co...]
    ppermute x14 -> x31, starting transfers between devices: 19.7 us -> 33.5 us  [swapped(): lax.ppermute(value, axis, [(source, source ^ mask) for source in range(co...]
    pallas_call x0 -> x4, Pallas kernels: none -> 11.6 us  [expert_block(): pl.pallas_call(functools.partial(expert_kernel, parts, width), out_shape=...]
    dot_general x3 -> x0, matrix products: 9.87 us -> none  [the longest x1 3.78 us: dense_body(): jnp.dot(tokens, weight_in, preferred_element_type=jnp.float32)]
    unnamed x19 -> x48, local copies, waits for them, and re-layouts: 2.88 us -> 12 us
    slice x4 -> x5, local copies, waits for them, and re-layouts: 0.22 us -> 2.79 us  [the longest x1 2.73 us: dense_body(): first, second = (weight_in[:width // 2], weight_in[width // 2:])]
    another operation x6 -> x2, other arithmetic: 2.85 us -> 0.66 us  [the longest x3 2.15 us: dense_body(): gathered = jnp.stack([gathered, swapped(gathered, 'exp', bit)])]
  transfers between devices with their start and end apart: 16 -> 33, of which waited for: 12 -> 12; matrix products, arithmetic and copies ran while one was open for 11% -> 10% of each run, Pallas kernels for 0% -> 9%
where the time goes in v2:
time: 132 us; the launch traced here: 131 us
  waiting for transfers between devices  53.5 us (41%)
  starting transfers between devices  40.2 us (30%)
  local copies, waits for them, and re-layouts  15.5 us (12%)
  Pallas kernels  11.6 us (9%)
  other arithmetic  4.71 us (4%)
  matrix products  4.02 us (3%)
  between operations  1.81 us (1%)
    ppermute x31, waiting for transfers between devices, swapped(): lax.ppermute(value, axis, [(source, source ^ mask) for source in range(co...  53.5 us
    ppermute x31, starting transfers between devices, swapped(): lax.ppermute(value, axis, [(source, source ^ mask) for source in range(co...  33.5 us
    unnamed x48, local copies, waits for them, and re-layouts  12 us
    pallas_call x4, Pallas kernels, expert_block(): pl.pallas_call(functools.partial(expert_kernel, parts, width), out_shape=...  11.6 us
    ppermute x1, starting transfers between devices, passed_along(): lax.ppermute(value, axis, [(source, source + steps) for source in range(i...  3.44 us
    all_to_all x1, starting transfers between devices, dense_body(): lax.all_to_all(queries, 'exp', split_axis=0, concat_axis=1, tiled=True)  3.29 us
    slice x1, local copies, waits for them, and re-layouts, dense_body(): first, second = (weight_in[:width // 2], weight_in[width // 2:])  2.73 us
  transfers between devices with their start and end apart: 33, of which 12 were waited for; matrix products, arithmetic and copies ran while one was open for 10% of the time, Pallas kernels for 9%

profile of v2, /device:TPU:0, one launch (start us, length us, event | category | flops | bytes accessed | tf_op | source)
XLA Modules:
  0.0 131.3 jit_solution(14921240058678635399)
XLA Ops:
  0.6 3.0 %collective-permute-start.1 = (bf16[128,2048]{1,0:T(8,128)(2,1)}, bf16[128,2048]{1,0:T(8,128)(2,1)S(1)}, u32[]{:S(2)}, u32[]{:S(2)}) collective-permute-start(bf16[128,2048]{1,0:T(8,128)(2,1)} %param.17), channel_id=1, source_target_pairs={{0,2},{1,3},{2,0},{3,1},{4,6},{5,7},{6,4},{7,5},{8,10},{9,11},{10,... | collective-permute-start | bytes 1572872 | tf_op jit(solution)/shard_map/ppermute | solution.py:180
  4.6 1.0 copy.26
  5.7 3.4 %collective-permute-start = (bf16[192,512]{0,1:T(8,128)(2,1)S(1)}, bf16[192,512]{0,1:T(8,128)(2,1)S(1)}, u32[]{:S(2)}, u32[]{:S(2)}) collective-permute-start(bf16[192,512]{0,1:T(8,128)(2,1)S(1)} %pad_maximum_fusion.1), channel_id=1, source_target_pairs={{0,4},{4,8},{8,12},{12,16},{16,20},{20,24},{24,28},{1,5},{5,9},{9,... | collective-permute-start | bytes 589832 | tf_op jit(solution)/shard_map/ppermute | solution.py:17
  9.1 3.3 %all-to-all-start = ((bf16[4,48,128]{2,1,0:T(8,128)(2,1)}), bf16[4,48,128]{2,1,0:T(8,128)(2,1)S(1)}, u32[]{:S(2)}, u32[]{:S(2)}) async-start(bf16[4,48,128]{2,1,0:T(8,128)(2,1)} %bitcast.42), calls=%async_computation | async-start | bytes 98304 | tf_op jit(solution)/shard_map/all_to_all | solution.py:264
  12.5 2.7 %slice_bitcast_fusion = (bf16[1024,384]{1,0:T(8,128)(2,1)}, bf16[1024,384]{1,0:T(8,128)(2,1)}) fusion(bf16[1,1,2048,384]{3,2,1,0:T(8,128)(2,1)} %param.21), kind=kLoop, calls=%fused_computation.33 | loop fusion | bytes 3145728 | tf_op jit(solution)/shard_map/slice | solution.py:334
  15.2 1.5 %collective-permute-start.3 = (bf16[1024,384]{1,0:T(8,128)(2,1)}, bf16[1024,384]{1,0:T(8,128)(2,1)S(1)}, u32[]{:S(2)}, u32[]{:S(2)}) collective-permute-start(bf16[1024,384]{1,0:T(8,128)(2,1)} %get-tuple-element.37), channel_id=1, source_target_pairs={{0,4},{4,0},{8,12},{12,8},{16,20},{20,16},{24,28},{28,24},{1,5},{5... | collective-permute-start | bytes 2359304 | tf_op jit(solution)/shard_map/ppermute | solution.py:180
  22.0 1.2 collective-permute-done.2
  23.2 1.8 %multiply_reduce_fusion = (f32[48]{0:T(128)S(1)}, f32[48,2048]{1,0:T(8,128)S(1)}) fusion(bf16[256,2048]{1,0:T(8,128)(2,1)S(1)} %collective-permute-done.2, bf16[128,2048]{1,0:T(8,128)(2,1)} %copy-done.17, bf16[128,2048]{1,0:T(8,128)(2,1)S(1)} %copy-done.16, bf16[48,128]{1,0:T(8,128)(2,1)S(1)} %get-tuple-element.45, ...), kind=kOutput, calls=%fused_computation.44 | convolution fusion | flops 107741136 | bytes 2736320 | tf_op jit(solution)/shard_map/dot_general | solution.py:309
  28.0 7.3 %collective-permute-done.3.refs_5_ = bf16[1024,384]{1,0:T(8,128)(2,1)S(1)} collective-permute-done((bf16[1024,384]{1,0:T(8,128)(2,1)}, bf16[1024,384]{1,0:T(8,128)(2,1)S(1)}, u32[]{:S(2)}, u32[]{:S(2)}) %collective-permute-start.3) | collective-permute-done | bytes 786464 | tf_op jit(solution)/shard_map/ppermute | solution.py:180
  35.3 1.5 %collective-permute-start.7 = (bf16[1024,384]{1,0:T(8,128)(2,1)}, bf16[1024,384]{1,0:T(8,128)(2,1)S(1)}, u32[]{:S(2)}, u32[]{:S(2)}) collective-permute-start(bf16[1024,384]{1,0:T(8,128)(2,1)} %get-tuple-element.17), channel_id=1, source_target_pairs={{0,4},{4,0},{8,12},{12,8},{16,20},{20,16},{24,28},{28,24},{1,5},{5... | collective-permute-start | bytes 2359304 | tf_op jit(solution)/shard_map/ppermute | solution.py:180
  36.8 17.8 %collective-permute-done.7.refs_6_ = bf16[1024,384]{1,0:T(8,128)(2,1)S(1)} collective-permute-done((bf16[1024,384]{1,0:T(8,128)(2,1)}, bf16[1024,384]{1,0:T(8,128)(2,1)S(1)}, u32[]{:S(2)}, u32[]{:S(2)}) %collective-permute-start.7) | collective-permute-done | bytes 786464 | tf_op jit(solution)/shard_map/ppermute | solution.py:180
  55.6 1.5 %collective-permute-start.8 = (bf16[192,2048]{1,0:T(8,128)(2,1)S(1)}, bf16[192,2048]{1,0:T(8,128)(2,1)}, u32[]{:S(2)}, u32[]{:S(2)}) collective-permute-start(bf16[192,2048]{1,0:T(8,128)(2,1)S(1)} %bitcast.37), channel_id=1, source_target_pairs={{0,4},{4,0},{8,12},{12,8},{16,20},{20,16},{24,28},{28,24},{1,5},{5... | collective-permute-start | bytes 2359304 | tf_op jit(solution)/shard_map/ppermute | solution.py:180
  57.1 2.6 %collective-permute-start.25 = (bf16[48,2176]{1,0:T(8,128)(2,1)S(1)}, bf16[48,2176]{1,0:T(8,128)(2,1)S(1)}, u32[]{:S(2)}, u32[]{:S(2)}) collective-permute-start(bf16[48,2176]{1,0:T(8,128)(2,1)S(1)} %fusion.20.refs_0_), channel_id=1, source_target_pairs={{0,24},{4,28},{8,16},{12,20},{16,8},{20,12},{24,0},{28,4},{1,25},{... | collective-permute-start | bytes 626696 | tf_op jit(solution)/shard_map/ppermute | solution.py:180
  60.1 6.7 %collective-permute-done.25.refs_0_ = bf16[48,2176]{1,0:T(8,128)(2,1)S(1)} collective-permute-done((bf16[48,2176]{1,0:T(8,128)(2,1)S(1)}, bf16[48,2176]{1,0:T(8,128)(2,1)S(1)}, u32[]{:S(2)}, u32[]{:S(2)}) %collective-permute-start.25) | collective-permute-done | bytes 208928 | tf_op jit(solution)/shard_map/ppermute | solution.py:180
  67.7 7.3 %collective-permute-start.11 = (bf16[48,2176]{1,0:T(8,128)(2,1)S(1)}, bf16[48,2176]{1,0:T(8,128)(2,1)}, u32[]{:S(2)}, u32[]{:S(2)}) collective-permute-start(bf16[48,2176]{1,0:T(8,128)(2,1)S(1)} %fusion.20.refs_0_), channel_id=1, source_target_pairs={{0,8},{4,12},{8,0},{12,4},{16,24},{20,28},{24,16},{28,20},{1,9},{5... | collective-permute-start | bytes 626696 | tf_op jit(solution)/shard_map/ppermute | solution.py:180
  75.8 1.6 %collective-permute-done.18.refs_0_ = bf16[48,2176]{1,0:T(8,128)(2,1)} collective-permute-done((bf16[48,2176]{1,0:T(8,128)(2,1)S(1)}, bf16[48,2176]{1,0:T(8,128)(2,1)}, u32[]{:S(2)}, u32[]{:S(2)}) %collective-permute-start.18) | collective-permute-done | bytes 208928 | tf_op jit(solution)/shard_map/ppermute | solution.py:180
  79.0 2.7 %collective-permute-done.11.refs_0_ = bf16[48,2176]{1,0:T(8,128)(2,1)} collective-permute-done((bf16[48,2176]{1,0:T(8,128)(2,1)S(1)}, bf16[48,2176]{1,0:T(8,128)(2,1)}, u32[]{:S(2)}, u32[]{:S(2)}) %collective-permute-start.11) | collective-permute-done | bytes 208928 | tf_op jit(solution)/shard_map/ppermute | solution.py:180
  83.3 1.1 collective-permute-start.12
  85.6 1.1 copy-done.4
  90.5 2.7 %shard_map.134 = (bf16[96,2048]{1,0:T(8,128)(2,1)S(1)}, bf16[96,2048]{1,0:T(8,128)(2,1)S(1)}) custom-call(s32[1]{0:T(128)} %bitcast.11.index_ref, bf16[48,2176]{1,0:T(8,128)(2,1)S(1)} %copy-done.6, bf16[48,2176]{1,0:T(8,128)(2,1)S(1)} %copy-done.8, bf16[48,2176]{1,0:T(8,128)(2,1)S(1)} %copy-done.10, bf16[48,2176]{1,0:T(8,128)(2,1)S(1)} %copy-done.12, ...), custom_call_target="tpu_custom_call" | custom-call | flops 905969664 | bytes 8388608 | tf_op jit(solution)/shard_map/pallas_call | solution.py:213
  94.4 3.1 %shard_map.133 = (bf16[96,2048]{1,0:T(8,128)(2,1)S(1)}, bf16[96,2048]{1,0:T(8,128)(2,1)S(1)}) custom-call(s32[1]{0:T(128)} %bitcast.11.index_ref, bf16[48,2176]{1,0:T(8,128)(2,1)} %collective-permute-done.18.refs_0_, bf16[48,2176]{1,0:T(8,128)(2,1)} %collective-permute-done.19.refs_1_, bf16[48,2176]{1,0:T(8,128)(2,1)} %collective-permute-done.20.refs_2_, ...), custom_call_target="tpu_custom_call" | custom-call | flops 905969664 | bytes 8388608 | tf_op jit(solution)/shard_map/pallas_call | solution.py:213
  98.0 2.9 %shard_map.132 = (bf16[96,2048]{1,0:T(8,128)(2,1)S(1)}, bf16[96,2048]{1,0:T(8,128)(2,1)S(1)}) custom-call(s32[1]{0:T(128)} %bitcast.11.index_ref, bf16[48,2176]{1,0:T(8,128)(2,1)} %collective-permute-done.11.refs_0_, bf16[48,2176]{1,0:T(8,128)(2,1)} %collective-permute-done.12.refs_1_, bf16[48,2176]{1,0:T(8,128)(2,1)S(1)} %collective-permute-done.13.refs_2_, ...), custom_call_target="tpu_custom_call" | custom-call | flops 905969664 | bytes 8388608 | tf_op jit(solution)/shard_map/pallas_call | solution.py:213
  101.1 2.8 %shard_map.131 = (bf16[96,2048]{1,0:T(8,128)(2,1)S(1)}, bf16[96,2048]{1,0:T(8,128)(2,1)S(1)}) custom-call(s32[1]{0:T(128)} %bitcast.11.index_ref, bf16[48,2176]{1,0:T(8,128)(2,1)S(1)} %fusion.20.refs_0_, bf16[48,2176]{1,0:T(8,128)(2,1)} %collective-permute-done.4.refs_1_, bf16[48,2176]{1,0:T(8,128)(2,1)S(1)} %collective-permute-done.5.refs_2_, ...), custom_call_target="tpu_custom_call" | custom-call | flops 905969664 | bytes 8388608 | tf_op jit(solution)/shard_map/pallas_call | solution.py:213
  105.7 1.2 collective-permute-start.23
  108.1 1.2 collective-permute-start.10
  109.3 3.1 %collective-permute-done.30 = bf16[48,2048]{1,0:T(8,128)(2,1)S(1)} collective-permute-done((bf16[48,2048]{1,0:T(8,128)(2,1)S(1)}, bf16[48,2048]{1,0:T(8,128)(2,1)S(1)}, u32[]{:S(2)}, u32[]{:S(2)}) %collective-permute-start.30) | collective-permute-done | bytes 196640 | tf_op jit(solution)/shard_map/ppermute | solution.py:180
  112.5 2.6 %collective-permute-start.31 = (bf16[48,2048]{1,0:T(8,128)(2,1)S(1)}, bf16[48,2048]{1,0:T(8,128)(2,1)S(1)}, u32[]{:S(2)}, u32[]{:S(2)}) collective-permute-start(bf16[48,2048]{1,0:T(8,128)(2,1)S(1)} %add_convert_fusion.5), channel_id=1, source_target_pairs={{0,24},{4,28},{8,16},{12,20},{16,8},{20,12},{24,0},{28,4},{1,25},{... | collective-permute-start | bytes 589832 | tf_op jit(solution)/shard_map/ppermute | solution.py:180
  115.1 1.5 %collective-permute-done.23 = bf16[48,2048]{1,0:T(8,128)(2,1)S(1)} collective-permute-done((bf16[48,2048]{1,0:T(8,128)(2,1)S(1)}, bf16[48,2048]{1,0:T(8,128)(2,1)S(1)}, u32[]{:S(2)}, u32[]{:S(2)}) %collective-permute-start.23) | collective-permute-done | bytes 196640 | tf_op jit(solution)/shard_map/ppermute | solution.py:180
  116.7 1.5 %collective-permute-start.24 = (bf16[48,2048]{1,0:T(8,128)(2,1)S(1)}, bf16[48,2048]{1,0:T(8,128)(2,1)S(1)}, u32[]{:S(2)}, u32[]{:S(2)}) collective-permute-start(bf16[48,2048]{1,0:T(8,128)(2,1)S(1)} %add_convert_fusion.6), channel_id=1, source_target_pairs={{0,16},{4,20},{8,24},{12,28},{16,0},{20,4},{24,8},{28,12},{1,17},{... | collective-permute-start | bytes 589832 | tf_op jit(solution)/shard_map/ppermute | solution.py:180
  118.2 2.6 %collective-permute-done.16 = bf16[48,2048]{1,0:T(8,128)(2,1)S(1)} collective-permute-done((bf16[48,2048]{1,0:T(8,128)(2,1)S(1)}, bf16[48,2048]{1,0:T(8,128)(2,1)S(1)}, u32[]{:S(2)}, u32[]{:S(2)}) %collective-permute-start.16) | collective-permute-done | bytes 196640 | tf_op jit(solution)/shard_map/ppermute | solution.py:180
  121.7 2.5 %collective-permute-done.10 = bf16[48,2048]{1,0:T(8,128)(2,1)S(1)} collective-permute-done((bf16[48,2048]{1,0:T(8,128)(2,1)S(1)}, bf16[48,2048]{1,0:T(8,128)(2,1)S(1)}, u32[]{:S(2)}, u32[]{:S(2)}) %collective-permute-start.10) | collective-permute-done | bytes 196640 | tf_op jit(solution)/shard_map/ppermute | solution.py:180
  124.2 6.0 %collective-permute-done.24 = bf16[48,2048]{1,0:T(8,128)(2,1)S(1)} collective-permute-done((bf16[48,2048]{1,0:T(8,128)(2,1)S(1)}, bf16[48,2048]{1,0:T(8,128)(2,1)S(1)}, u32[]{:S(2)}, u32[]{:S(2)}) %collective-permute-start.24) | collective-permute-done | bytes 196640 | tf_op jit(solution)/shard_map/ppermute | solution.py:180
  (142 shorter events, 26.4 us)
Async XLA Ops:
  0.6 19.7 %collective-permute-start.1 = (bf16[128,2048]{1,0:T(8,128)(2,1)}, bf16[128,2048]{1,0:T(8,128)(2,1)S(1)}, u32[]{:S(2)}, u32[]{:S(2)}) collective-permute-start(bf16[128,2048]{1,0:T(8,128)(2,1)} %param.17), channel_id=1, source_target_pairs={{0,2},{1,3},{2,0},{3,1},{4,6},{5,7},{6,4},{7,5},{8,10},{9,11},{10,... | collective-permute-start | bytes 1572872 | tf_op jit(solution)/shard_map/ppermute | solution.py:180
  5.7 13.0 %collective-permute-start = (bf16[192,512]{0,1:T(8,128)(2,1)S(1)}, bf16[192,512]{0,1:T(8,128)(2,1)S(1)}, u32[]{:S(2)}, u32[]{:S(2)}) collective-permute-start(bf16[192,512]{0,1:T(8,128)(2,1)S(1)} %pad_maximum_fusion.1), channel_id=1, source_target_pairs={{0,4},{4,8},{8,12},{12,16},{16,20},{20,24},{24,28},{1,5},{5,9},{9,... | collective-permute-start | bytes 589832 | tf_op jit(solution)/shard_map/ppermute | solution.py:17
  9.1 9.1 %all-to-all-start = ((bf16[4,48,128]{2,1,0:T(8,128)(2,1)}), bf16[4,48,128]{2,1,0:T(8,128)(2,1)S(1)}, u32[]{:S(2)}, u32[]{:S(2)}) async-start(bf16[4,48,128]{2,1,0:T(8,128)(2,1)} %bitcast.42), calls=%async_computation | async-start | bytes 98304 | tf_op jit(solution)/shard_map/all_to_all | solution.py:264
  15.2 20.1 %collective-permute-start.3 = (bf16[1024,384]{1,0:T(8,128)(2,1)}, bf16[1024,384]{1,0:T(8,128)(2,1)S(1)}, u32[]{:S(2)}, u32[]{:S(2)}) collective-permute-start(bf16[1024,384]{1,0:T(8,128)(2,1)} %get-tuple-element.37), channel_id=1, source_target_pairs={{0,4},{4,0},{8,12},{12,8},{16,20},{20,16},{24,28},{28,24},{1,5},{5... | collective-permute-start | bytes 2359304 | tf_op jit(solution)/shard_map/ppermute | solution.py:180
  35.3 19.3 %collective-permute-start.7 = (bf16[1024,384]{1,0:T(8,128)(2,1)}, bf16[1024,384]{1,0:T(8,128)(2,1)S(1)}, u32[]{:S(2)}, u32[]{:S(2)}) collective-permute-start(bf16[1024,384]{1,0:T(8,128)(2,1)} %get-tuple-element.17), channel_id=1, source_target_pairs={{0,4},{4,0},{8,12},{12,8},{16,20},{20,16},{24,28},{28,24},{1,5},{5... | collective-permute-start | bytes 2359304 | tf_op jit(solution)/shard_map/ppermute | solution.py:180
  55.6 30.0 %collective-permute-start.8 = (bf16[192,2048]{1,0:T(8,128)(2,1)S(1)}, bf16[192,2048]{1,0:T(8,128)(2,1)}, u32[]{:S(2)}, u32[]{:S(2)}) collective-permute-start(bf16[192,2048]{1,0:T(8,128)(2,1)S(1)} %bitcast.37), channel_id=1, source_target_pairs={{0,4},{4,0},{8,12},{12,8},{16,20},{20,16},{24,28},{28,24},{1,5},{5... | collective-permute-start | bytes 2359304 | tf_op jit(solution)/shard_map/ppermute | solution.py:180
  57.1 9.7 %collective-permute-start.25 = (bf16[48,2176]{1,0:T(8,128)(2,1)S(1)}, bf16[48,2176]{1,0:T(8,128)(2,1)S(1)}, u32[]{:S(2)}, u32[]{:S(2)}) collective-permute-start(bf16[48,2176]{1,0:T(8,128)(2,1)S(1)} %fusion.20.refs_0_), channel_id=1, source_target_pairs={{0,24},{4,28},{8,16},{12,20},{16,8},{20,12},{24,0},{28,4},{1,25},{... | collective-permute-start | bytes 626696 | tf_op jit(solution)/shard_map/ppermute | solution.py:180
  59.7 17.7 %collective-permute-start.18 = (bf16[48,2176]{1,0:T(8,128)(2,1)S(1)}, bf16[48,2176]{1,0:T(8,128)(2,1)}, u32[]{:S(2)}, u32[]{:S(2)}) collective-permute-start(bf16[48,2176]{1,0:T(8,128)(2,1)S(1)} %fusion.20.refs_0_), channel_id=1, source_target_pairs={{0,16},{4,20},{8,24},{12,28},{16,0},{20,4},{24,8},{28,12},{1,17},{... | collective-permute-start | bytes 626696 | tf_op jit(solution)/shard_map/ppermute | solution.py:180
  66.8 11.4 %collective-permute-start.26 = (bf16[48,2176]{1,0:T(8,128)(2,1)S(1)}, bf16[48,2176]{1,0:T(8,128)(2,1)S(1)}, u32[]{:S(2)}, u32[]{:S(2)}) collective-permute-start(bf16[48,2176]{1,0:T(8,128)(2,1)S(1)} %collective-permute-done.25.refs_0_), channel_id=1, source_target_pairs={{0,2},{1,3},{2,0},{3,1},{4,6},{5,7},{6,4},{7,5},{8,10},{9,11},{10,... | collective-permute-start | bytes 626696 | tf_op jit(solution)/shard_map/ppermute | solution.py:180
  67.7 14.0 %collective-permute-start.11 = (bf16[48,2176]{1,0:T(8,128)(2,1)S(1)}, bf16[48,2176]{1,0:T(8,128)(2,1)}, u32[]{:S(2)}, u32[]{:S(2)}) collective-permute-start(bf16[48,2176]{1,0:T(8,128)(2,1)S(1)} %fusion.20.refs_0_), channel_id=1, source_target_pairs={{0,8},{4,12},{8,0},{12,4},{16,24},{20,28},{24,16},{28,20},{1,9},{5... | collective-permute-start | bytes 626696 | tf_op jit(solution)/shard_map/ppermute | solution.py:180
  75.1 7.5 %collective-permute-start.27 = (bf16[48,2176]{1,0:T(8,128)(2,1)S(1)}, bf16[48,2176]{1,0:T(8,128)(2,1)S(1)}, u32[]{:S(2)}, u32[]{:S(2)}) collective-permute-start(bf16[48,2176]{1,0:T(8,128)(2,1)S(1)} %collective-permute-done.25.refs_0_), channel_id=1, source_target_pairs={{0,1},{1,0},{2,3},{3,2},{4,5},{5,4},{6,7},{7,6},{8,9},{9,8},{10,11... | collective-permute-start | bytes 626696 | tf_op jit(solution)/shard_map/ppermute | solution.py:180
  77.3 7.1 %collective-permute-start.19 = (bf16[48,2176]{1,0:T(8,128)(2,1)}, bf16[48,2176]{1,0:T(8,128)(2,1)}, u32[]{:S(2)}, u32[]{:S(2)}) collective-permute-start(bf16[48,2176]{1,0:T(8,128)(2,1)} %collective-permute-done.18.refs_0_), channel_id=1, source_target_pairs={{0,2},{1,3},{2,0},{3,1},{4,6},{5,7},{6,4},{7,5},{8,10},{9,11},{10,... | collective-permute-start | bytes 626696 | tf_op jit(solution)/shard_map/ppermute | solution.py:180
  78.3 6.2 %collective-permute-start.28 = (bf16[48,2176]{1,0:T(8,128)(2,1)S(1)}, bf16[48,2176]{1,0:T(8,128)(2,1)S(1)}, u32[]{:S(2)}, u32[]{:S(2)}) collective-permute-start(bf16[48,2176]{1,0:T(8,128)(2,1)S(1)} %collective-permute-done.26.refs_1_), channel_id=1, source_target_pairs={{0,1},{1,0},{2,3},{3,2},{4,5},{5,4},{6,7},{7,6},{8,9},{9,8},{10,11... | collective-permute-start | bytes 626696 | tf_op jit(solution)/shard_map/ppermute | solution.py:180
  81.7 11.6 %collective-permute-start.4 = (bf16[48,2176]{1,0:T(8,128)(2,1)S(1)}, bf16[48,2176]{1,0:T(8,128)(2,1)}, u32[]{:S(2)}, u32[]{:S(2)}) collective-permute-start(bf16[48,2176]{1,0:T(8,128)(2,1)S(1)} %fusion.20.refs_0_), channel_id=1, source_target_pairs={{0,2},{1,3},{2,0},{3,1},{4,6},{5,7},{6,4},{7,5},{8,10},{9,11},{10,... | collective-permute-start | bytes 626696 | tf_op jit(solution)/shard_map/ppermute | solution.py:180
  83.3 10.5 %collective-permute-start.12 = (bf16[48,2176]{1,0:T(8,128)(2,1)}, bf16[48,2176]{1,0:T(8,128)(2,1)}, u32[]{:S(2)}, u32[]{:S(2)}) collective-permute-start(bf16[48,2176]{1,0:T(8,128)(2,1)} %collective-permute-done.11.refs_0_), channel_id=1, source_target_pairs={{0,2},{1,3},{2,0},{3,1},{4,6},{5,7},{6,4},{7,5},{8,10},{9,11},{10,... | collective-permute-start | bytes 626696 | tf_op jit(solution)/shard_map/ppermute | solution.py:180
  84.4 9.5 %collective-permute-start.20 = (bf16[48,2176]{1,0:T(8,128)(2,1)}, bf16[48,2176]{1,0:T(8,128)(2,1)}, u32[]{:S(2)}, u32[]{:S(2)}) collective-permute-start(bf16[48,2176]{1,0:T(8,128)(2,1)} %collective-permute-done.18.refs_0_), channel_id=1, source_target_pairs={{0,1},{1,0},{2,3},{3,2},{4,5},{5,4},{6,7},{7,6},{8,9},{9,8},{10,11... | collective-permute-start | bytes 626696 | tf_op jit(solution)/shard_map/ppermute | solution.py:180
  85.1 9.2 %collective-permute-start.21 = (bf16[48,2176]{1,0:T(8,128)(2,1)}, bf16[48,2176]{1,0:T(8,128)(2,1)}, u32[]{:S(2)}, u32[]{:S(2)}) collective-permute-start(bf16[48,2176]{1,0:T(8,128)(2,1)} %collective-permute-done.19.refs_1_), channel_id=1, source_target_pairs={{0,1},{1,0},{2,3},{3,2},{4,5},{5,4},{6,7},{7,6},{8,9},{9,8},{10,11... | collective-permute-start | bytes 626696 | tf_op jit(solution)/shard_map/ppermute | solution.py:180
  93.2 11.2 %collective-permute-start.29 = (bf16[96,2048]{1,0:T(8,128)(2,1)S(1)}, bf16[96,2048]{1,0:T(8,128)(2,1)S(1)}, u32[]{:S(2)}, u32[]{:S(2)}) collective-permute-start(bf16[96,2048]{1,0:T(8,128)(2,1)S(1)} %get-tuple-element.27), channel_id=1, source_target_pairs={{0,1},{1,0},{2,3},{3,2},{4,5},{5,4},{6,7},{7,6},{8,9},{9,8},{10,11... | collective-permute-start | bytes 1179656 | tf_op jit(solution)/shard_map/ppermute | solution.py:180
  93.3 4.2 %collective-permute-start.13 = (bf16[48,2176]{1,0:T(8,128)(2,1)}, bf16[48,2176]{1,0:T(8,128)(2,1)S(1)}, u32[]{:S(2)}, u32[]{:S(2)}) collective-permute-start(bf16[48,2176]{1,0:T(8,128)(2,1)} %collective-permute-done.11.refs_0_), channel_id=1, source_target_pairs={{0,1},{1,0},{2,3},{3,2},{4,5},{5,4},{6,7},{7,6},{8,9},{9,8},{10,11... | collective-permute-start | bytes 626696 | tf_op jit(solution)/shard_map/ppermute | solution.py:180
  93.8 4.2 %collective-permute-start.14 = (bf16[48,2176]{1,0:T(8,128)(2,1)}, bf16[48,2176]{1,0:T(8,128)(2,1)S(1)}, u32[]{:S(2)}, u32[]{:S(2)}) collective-permute-start(bf16[48,2176]{1,0:T(8,128)(2,1)} %collective-permute-done.12.refs_1_), channel_id=1, source_target_pairs={{0,1},{1,0},{2,3},{3,2},{4,5},{5,4},{6,7},{7,6},{8,9},{9,8},{10,11... | collective-permute-start | bytes 626696 | tf_op jit(solution)/shard_map/ppermute | solution.py:180
  93.9 7.2 %collective-permute-start.5 = (bf16[48,2176]{1,0:T(8,128)(2,1)S(1)}, bf16[48,2176]{1,0:T(8,128)(2,1)S(1)}, u32[]{:S(2)}, u32[]{:S(2)}) collective-permute-start(bf16[48,2176]{1,0:T(8,128)(2,1)S(1)} %fusion.20.refs_0_), channel_id=1, source_target_pairs={{0,1},{1,0},{2,3},{3,2},{4,5},{5,4},{6,7},{7,6},{8,9},{9,8},{10,11... | collective-permute-start | bytes 626696 | tf_op jit(solution)/shard_map/ppermute | solution.py:180
  94.3 6.8 %collective-permute-start.6 = (bf16[48,2176]{1,0:T(8,128)(2,1)}, bf16[48,2176]{1,0:T(8,128)(2,1)S(1)}, u32[]{:S(2)}, u32[]{:S(2)}) collective-permute-start(bf16[48,2176]{1,0:T(8,128)(2,1)} %collective-permute-done.4.refs_1_), channel_id=1, source_target_pairs={{0,1},{1,0},{2,3},{3,2},{4,5},{5,4},{6,7},{7,6},{8,9},{9,8},{10,11... | collective-permute-start | bytes 626696 | tf_op jit(solution)/shard_map/ppermute | solution.py:180
  97.5 8.0 %collective-permute-start.22 = (bf16[96,2048]{1,0:T(8,128)(2,1)S(1)}, bf16[96,2048]{1,0:T(8,128)(2,1)S(1)}, u32[]{:S(2)}, u32[]{:S(2)}) collective-permute-start(bf16[96,2048]{1,0:T(8,128)(2,1)S(1)} %get-tuple-element.25), channel_id=1, source_target_pairs={{0,1},{1,0},{2,3},{3,2},{4,5},{5,4},{6,7},{7,6},{8,9},{9,8},{10,11... | collective-permute-start | bytes 1179656 | tf_op jit(solution)/shard_map/ppermute | solution.py:180
  101.0 5.9 %collective-permute-start.15 = (bf16[96,2048]{1,0:T(8,128)(2,1)S(1)}, bf16[96,2048]{1,0:T(8,128)(2,1)S(1)}, u32[]{:S(2)}, u32[]{:S(2)}) collective-permute-start(bf16[96,2048]{1,0:T(8,128)(2,1)S(1)} %get-tuple-element.23), channel_id=1, source_target_pairs={{0,1},{1,0},{2,3},{3,2},{4,5},{5,4},{6,7},{7,6},{8,9},{9,8},{10,11... | collective-permute-start | bytes 1179656 | tf_op jit(solution)/shard_map/ppermute | solution.py:180
  104.0 4.0 %collective-permute-start.9 = (bf16[96,2048]{1,0:T(8,128)(2,1)S(1)}, bf16[96,2048]{1,0:T(8,128)(2,1)S(1)}, u32[]{:S(2)}, u32[]{:S(2)}) collective-permute-start(bf16[96,2048]{1,0:T(8,128)(2,1)S(1)} %get-tuple-element.21), channel_id=1, source_target_pairs={{0,1},{1,0},{2,3},{3,2},{4,5},{5,4},{6,7},{7,6},{8,9},{9,8},{10,11... | collective-permute-start | bytes 1179656 | tf_op jit(solution)/shard_map/ppermute | solution.py:180
  104.6 7.8 %collective-permute-start.30 = (bf16[48,2048]{1,0:T(8,128)(2,1)S(1)}, bf16[48,2048]{1,0:T(8,128)(2,1)S(1)}, u32[]{:S(2)}, u32[]{:S(2)}) collective-permute-start(bf16[48,2048]{1,0:T(8,128)(2,1)S(1)} %slice.161), channel_id=1, source_target_pairs={{0,2},{1,3},{2,0},{3,1},{4,6},{5,7},{6,4},{7,5},{8,10},{9,11},{10,... | collective-permute-start | bytes 589832 | tf_op jit(solution)/shard_map/ppermute | solution.py:180
  105.7 10.9 %collective-permute-start.23 = (bf16[48,2048]{1,0:T(8,128)(2,1)S(1)}, bf16[48,2048]{1,0:T(8,128)(2,1)S(1)}, u32[]{:S(2)}, u32[]{:S(2)}) collective-permute-start(bf16[48,2048]{1,0:T(8,128)(2,1)S(1)} %slice.159), channel_id=1, source_target_pairs={{0,2},{1,3},{2,0},{3,1},{4,6},{5,7},{6,4},{7,5},{8,10},{9,11},{10,... | collective-permute-start | bytes 589832 | tf_op jit(solution)/shard_map/ppermute | solution.py:180
  107.0 13.8 %collective-permute-start.16 = (bf16[48,2048]{1,0:T(8,128)(2,1)S(1)}, bf16[48,2048]{1,0:T(8,128)(2,1)S(1)}, u32[]{:S(2)}, u32[]{:S(2)}) collective-permute-start(bf16[48,2048]{1,0:T(8,128)(2,1)S(1)} %slice.157), channel_id=1, source_target_pairs={{0,2},{1,3},{2,0},{3,1},{4,6},{5,7},{6,4},{7,5},{8,10},{9,11},{10,... | collective-permute-start | bytes 589832 | tf_op jit(solution)/shard_map/ppermute | solution.py:180
  108.1 16.1 %collective-permute-start.10 = (bf16[48,2048]{1,0:T(8,128)(2,1)S(1)}, bf16[48,2048]{1,0:T(8,128)(2,1)S(1)}, u32[]{:S(2)}, u32[]{:S(2)}) collective-permute-start(bf16[48,2048]{1,0:T(8,128)(2,1)S(1)} %slice.155), channel_id=1, source_target_pairs={{0,2},{1,3},{2,0},{3,1},{4,6},{5,7},{6,4},{7,5},{8,10},{9,11},{10,... | collective-permute-start | bytes 589832 | tf_op jit(solution)/shard_map/ppermute | solution.py:180
  112.5 11.7 %collective-permute-start.31 = (bf16[48,2048]{1,0:T(8,128)(2,1)S(1)}, bf16[48,2048]{1,0:T(8,128)(2,1)S(1)}, u32[]{:S(2)}, u32[]{:S(2)}) collective-permute-start(bf16[48,2048]{1,0:T(8,128)(2,1)S(1)} %add_convert_fusion.5), channel_id=1, source_target_pairs={{0,24},{4,28},{8,16},{12,20},{16,8},{20,12},{24,0},{28,4},{1,25},{... | collective-permute-start | bytes 589832 | tf_op jit(solution)/shard_map/ppermute | solution.py:180
  116.7 13.5 %collective-permute-start.24 = (bf16[48,2048]{1,0:T(8,128)(2,1)S(1)}, bf16[48,2048]{1,0:T(8,128)(2,1)S(1)}, u32[]{:S(2)}, u32[]{:S(2)}) collective-permute-start(bf16[48,2048]{1,0:T(8,128)(2,1)S(1)} %add_convert_fusion.6), channel_id=1, source_target_pairs={{0,16},{4,20},{8,24},{12,28},{16,0},{20,4},{24,8},{28,12},{1,17},{... | collective-permute-start | bytes 589832 | tf_op jit(solution)/shard_map/ppermute | solution.py:180
  120.9 9.6 %collective-permute-start.17 = (bf16[48,2048]{1,0:T(8,128)(2,1)S(1)}, bf16[48,2048]{1,0:T(8,128)(2,1)S(1)}, u32[]{:S(2)}, u32[]{:S(2)}) collective-permute-start(bf16[48,2048]{1,0:T(8,128)(2,1)S(1)} %add_convert_fusion.7), channel_id=1, source_target_pairs={{0,8},{4,12},{8,0},{12,4},{16,24},{20,28},{24,16},{28,20},{1,9},{5... | collective-permute-start | bytes 589832 | tf_op jit(solution)/shard_map/ppermute | solution.py:180
  (24 other events, 187.1 us)

commit v3 on v0

--- a/solution.py
+++ b/solution.py
@@ -1,6 +1,12 @@
+import functools
+import math
+
 import jax
 import jax.numpy as jnp
+import numpy as np
 from jax import lax
+from jax.experimental import pallas as pl
+from jax.experimental.pallas import tpu as pltpu
 from jax.sharding import PartitionSpec as P
 
 eps = 1e-06
@@ -38,7 +44,7 @@
     return (jax.nn.silu(act[:, :inner]) * act[:, inner:]).astype(jnp.bfloat16)
 
 
-def body(
+def sparse_body(
     hidden,
     queries,
     keys,
@@ -171,6 +177,324 @@
     return (layer_out, router_kl)
 
 
+def swapped(value, axis, mask):
+    count = lax.axis_size(axis)
+    return lax.ppermute(value, axis, [(source, source ^ mask) for source in range(count)])
+
+
+def attention_kernel(share, index_ref, spectrum_ref, pos_ref, q_ref, *refs):
+    before_ref, own_k, own_v, out_ref, cos_ref, sin_ref, pos_col = refs
+    heads, rows, size = out_ref.shape
+    block = own_k.shape[0]
+    start = pl.multiple_of(index_ref[0] * rows, 16)
+    pos_row = pos_ref[...].astype(jnp.float32)
+    along = lax.broadcasted_iota(jnp.int32, (block, block), 0)
+    across = lax.broadcasted_iota(jnp.int32, (block, block), 1)
+    pos_col[...] = jnp.sum(jnp.where(along == across, pos_row, 0.0), axis=1, keepdims=True)
+    opening = jnp.sum(jnp.where(across[:1] == 0, pos_row, 0.0), axis=1, keepdims=True)
+    earlier = opening - block + along[:, :1].astype(jnp.float32)
+    lane = lax.broadcasted_iota(jnp.int32, (1, size), 1)
+    lower = lane < size // 2
+    phase = jnp.where(lower, 0.0, math.pi / 2)
+    for half, at in enumerate((earlier, pos_col[...])):
+        turn = jnp.cos(at * spectrum_ref[...] - phase)
+        swap = pltpu.roll(turn, size // 2, 1)
+        cos_ref[half * block : (half + 1) * block, :] = jnp.where(lower, turn, swap)
+        sin_ref[half * block : (half + 1) * block, :] = jnp.where(lower, -swap, turn)
+
+    def turned(vectors, cosine, sine):
+        wide = vectors.astype(jnp.float32)
+        wide = wide * lax.rsqrt(jnp.mean(wide * wide, axis=1, keepdims=True) + eps)
+        return (wide * cosine + pltpu.roll(wide, size // 2, 1) * sine).astype(jnp.bfloat16)
+
+    own = pl.ds(block + start, rows)
+    query_at = start + lax.broadcasted_iota(jnp.int32, (rows, 2 * block), 0)
+    key_at = lax.broadcasted_iota(jnp.int32, (rows, 2 * block), 1) - block
+    reach = pos_col[pl.ds(start, rows), :].astype(jnp.int32)
+    allowed = (key_at <= query_at) & (key_at >= query_at - reach)
+    for group in range(heads // share):
+        columns = slice(group * size, (group + 1) * size)
+        keys = jnp.concatenate(
+            [
+                turned(before_ref[:, columns], cos_ref[:block, :], sin_ref[:block, :]),
+                turned(own_k[:, columns], cos_ref[block:, :], sin_ref[block:, :]),
+            ],
+            axis=0,
+        )
+        values = jnp.concatenate([before_ref[:, own_k.shape[1] + group * size :][:, :size], own_v[:, columns]], axis=0)
+        for h in range(group * share, (group + 1) * share):
+            query = turned(q_ref[:, h * size : (h + 1) * size], cos_ref[own, :], sin_ref[own, :])
+            scores = lax.dot_general(
+                query, keys, (((1,), (1,)), ((), ())), preferred_element_type=jnp.float32
+            ) * (1.0 / math.sqrt(size))
+            raw = jnp.where(allowed, jnp.exp(scores), 0.0)
+            weights = (raw / jnp.sum(raw, axis=1, keepdims=True)).astype(jnp.bfloat16)
+            out_ref[h] = jnp.dot(weights, values, preferred_element_type=jnp.float32).astype(
+                jnp.bfloat16
+            )
+
+
+def router_kernel(order, index_ref, heads_ref, *refs):
+    parts, refs = refs[: len(order)], refs[len(order) :]
+    hidden_ref, gain_ref, router_ref, routes_ref, rollout_ref, attended_ref, payload_ref, kl_ref = refs
+    width = hidden_ref.shape[1]
+    experts, rows = rollout_ref.shape
+    total = hidden_ref[...].astype(jnp.float32)
+    for part, h in zip(parts, order):
+        total = total + jnp.dot(
+            heads_ref[index_ref[0] ^ h], part[...], preferred_element_type=jnp.float32
+        )
+    attended = total.astype(jnp.bfloat16)
+    attended_ref[...] = attended
+    wide = attended.astype(jnp.float32)
+    moe_in = (
+        wide * lax.rsqrt(jnp.mean(wide * wide, axis=1, keepdims=True) + eps) * gain_ref[...]
+    ).astype(jnp.bfloat16)
+    payload_ref[:, :width] = moe_in
+    logits = lax.dot_general(
+        router_ref[...], moe_in, (((1,), (1,)), ((), ())), preferred_element_type=jnp.float32
+    )
+    raised = jnp.exp(logits)
+    rollout = rollout_ref[...]
+    current_log = logits - jnp.log(jnp.sum(raised, axis=0, keepdims=True))
+    rollout_log = rollout - jnp.log(jnp.sum(jnp.exp(rollout), axis=0, keepdims=True))
+    kl_ref[...] = jnp.sum(jnp.exp(rollout_log) * (rollout_log - current_log), axis=0, keepdims=True)
+    ids = lax.broadcasted_iota(jnp.int32, (experts, rows), 0)
+    picked = jnp.zeros((experts, rows), jnp.float32)
+    for k in range(routes_ref.shape[0]):
+        picked = picked + jnp.where(routes_ref[k : k + 1, :] == ids, 1.0, 0.0)
+    chosen = jnp.where(picked > 0.0, raised, 0.0)
+    gates = (chosen / jnp.sum(chosen, axis=0, keepdims=True)).astype(jnp.bfloat16)
+    lanes = payload_ref.shape[1] - width
+    spread = (
+        lax.broadcasted_iota(jnp.int32, (experts, lanes), 0)
+        == lax.broadcasted_iota(jnp.int32, (experts, lanes), 1)
+    ).astype(jnp.float32).astype(jnp.bfloat16)
+    payload_ref[:, width:] = lax.dot_general(
+        gates, spread, (((0,), (0,)), ((), ())), preferred_element_type=jnp.float32
+    ).astype(jnp.bfloat16)
+
+
+VMEM = pl.BlockSpec(memory_space=pltpu.VMEM)
+SMEM = pl.BlockSpec(memory_space=pltpu.SMEM)
+
+
+HBM = pl.BlockSpec(memory_space=pltpu.HBM)
+
+
+def fetching(kernel, count, stored, index_ref, *refs):
+    inputs, refs = refs[:count], refs[count:]
+    outputs, refs = refs[: len(stored)], refs[len(stored) :]
+    held, refs = refs[:count], refs[count:]
+    sent, refs = refs[: sum(stored)], refs[sum(stored) :]
+    arrived, left, scratch = refs[0], refs[1], refs[2:]
+    copies = [
+        pltpu.make_async_copy(source, target, arrived.at[i])
+        for i, (source, target) in enumerate(zip(inputs, held))
+    ]
+    for copy in copies:
+        copy.start()
+    for copy in copies:
+        copy.wait()
+    sent = iter(sent)
+    built, copies = [], []
+    for output, far in zip(outputs, stored):
+        built.append(next(sent) if far else output)
+        if far:
+            copies.append(pltpu.make_async_copy(built[-1], output, left.at[len(copies)]))
+    kernel(index_ref, *held, *built, *scratch)
+    for copy in copies:
+        copy.start()
+    for copy in copies:
+        copy.wait()
+
+
+def small_kernel(kernel, out_shape, inputs, stored, scratch=(), flops=0):
+    held = [pltpu.VMEM(array.shape, array.dtype) for array in inputs[1:]]
+    sent = [pltpu.VMEM(leaf.shape, leaf.dtype) for leaf, far in zip(out_shape, stored) if far]
+    return pl.pallas_call(
+        functools.partial(fetching, kernel, len(held), stored),
+        out_shape=out_shape,
+        in_specs=[SMEM] + [HBM] * len(held),
+        out_specs=tuple(HBM if far else VMEM for far in stored),
+        scratch_shapes=[
+            *held,
+            *sent,
+            pltpu.SemaphoreType.DMA((len(held),)),
+            pltpu.SemaphoreType.DMA((max(1, len(sent)),)),
+            *scratch,
+        ],
+        compiler_params=pltpu.CompilerParams(vmem_limit_bytes=16 * 1024 * 1024),
+        cost_estimate=pl.CostEstimate(flops=flops, bytes_accessed=1 << 20, transcendentals=0),
+    )(*inputs)
+
+
+def expert_kernel(parts, width, index_ref, *refs):
+    token_refs, refs = refs[:parts], refs[parts:]
+    own_in, other_in, own_out, other_out, keep_ref, send_ref, tokens, arrived = refs
+    rows = token_refs[0].shape[0]
+    lanes = token_refs[0].shape[1] - width
+    copies = [
+        pltpu.make_async_copy(ref, tokens.at[pl.ds(p * rows, rows), :], arrived.at[p])
+        for p, ref in enumerate(token_refs)
+    ]
+    for copy in copies:
+        copy.start()
+    for copy in copies:
+        copy.wait()
+    picked = lax.broadcasted_iota(jnp.int32, (parts * rows, lanes), 1) == index_ref[0]
+    gate = jnp.sum(
+        jnp.where(picked, tokens[:, width:].astype(jnp.float32), 0.0), axis=1, keepdims=True
+    )
+    own = jnp.dot(tokens[:, :width], own_in[...], preferred_element_type=jnp.float32)
+    other = jnp.dot(tokens[:, :width], other_in[...], preferred_element_type=jnp.float32)
+    out = jnp.dot(activate(own), own_out[...], preferred_element_type=jnp.float32) + jnp.dot(
+        activate(other), other_out[...], preferred_element_type=jnp.float32
+    )
+    out = (out * gate).astype(jnp.bfloat16)
+    half = keep_ref.shape[0]
+    keep_ref[...] = out[:half]
+    send_ref[...] = out[half:]
+
+
+def expert_block(index, tokens, own_in, own_out, other_in, other_out, width):
+    parts = len(tokens)
+    rows = parts * tokens[0].shape[0]
+    half = jax.ShapeDtypeStruct((rows // 2, width), jnp.bfloat16)
+    return pl.pallas_call(
+        functools.partial(expert_kernel, parts, width),
+        out_shape=(half, half),
+        in_specs=[SMEM] + [HBM] * parts + [VMEM] * 4,
+        out_specs=(VMEM, VMEM),
+        scratch_shapes=[
+            pltpu.VMEM((rows, tokens[0].shape[1]), jnp.bfloat16),
+            pltpu.SemaphoreType.DMA((parts,)),
+        ],
+        compiler_params=pltpu.CompilerParams(vmem_limit_bytes=16 * 1024 * 1024),
+        cost_estimate=pl.CostEstimate(
+            flops=2 * rows * 3 * width * own_in.shape[1], bytes_accessed=8 << 20, transcendentals=0
+        ),
+    )(index, *tokens, own_in, other_in, own_out, other_out)
+
+
+def dense_body(
+    hidden,
+    queries,
+    keys,
+    values,
+    positions,
+    out_weight,
+    ffn_gain,
+    router_weight,
+    routes,
+    expert_in,
+    expert_out,
+    rollout_logits,
+):
+    block_rows = queries.shape[0]
+    head_dim = queries.shape[1]
+    width = hidden.shape[1]
+    token_rows = hidden.shape[0]
+    experts_total = router_weight.shape[1]
+    ctx_index = lax.axis_index("ctx")
+    exp_index = lax.axis_index("exp")
+    exp_count = lax.axis_size("exp")
+    kv_heads = keys.shape[1] // head_dim
+    per_column = experts_total // exp_count
+    share = exp_count // kv_heads
+    bits = []
+    step = exp_count // 2
+    while step:
+        bits.append(step)
+        step //= 2
+
+    weight_in = expert_in[0, 0]
+    weight_out = expert_out[0, 0]
+    before = passed_along(jnp.concatenate([keys, values], axis=1), "ctx", 1)
+    query_rows = lax.all_to_all(queries, "exp", split_axis=0, concat_axis=1, tiled=True)
+    before, weight_in, weight_out = lax.optimization_barrier((before, weight_in, weight_out))
+    other_out = swapped(weight_out, "ctx", 1)
+    other_in = swapped(weight_in, "ctx", 1)
+
+    index = exp_index.reshape(1).astype(jnp.int32)
+    spectrum = np.float32(theta) ** (-np.arange(head_dim // 2, dtype=np.float32) * 2.0 / head_dim)
+    spectrum = jnp.asarray(np.concatenate([spectrum, spectrum])[None, :].astype(np.float32))
+    table = pltpu.VMEM((2 * block_rows, head_dim), jnp.float32)
+    (head_out,) = small_kernel(
+        functools.partial(attention_kernel, exp_count // kv_heads),
+        (jax.ShapeDtypeStruct((exp_count, token_rows, head_dim), jnp.bfloat16),),
+        (index, spectrum, positions[None, :], query_rows, before, keys, values),
+        (True,),
+        (table, table, pltpu.VMEM((block_rows, 1), jnp.float32)),
+        8 * block_rows * token_rows * queries.shape[1],
+    )
+    out_parts, head_order = [out_weight], [0]
+    for bit in bits[:-1]:
+        out_parts = out_parts + [swapped(part, "exp", bit) for part in out_parts]
+        head_order = head_order + [h ^ bit for h in head_order]
+    head_out, *late = lax.optimization_barrier((head_out, *out_parts[1:]))
+    out_parts = out_parts[:1] + late
+    out_parts = out_parts + [swapped(part, "exp", bits[-1]) for part in out_parts]
+    head_order = head_order + [h ^ bits[-1] for h in head_order]
+    lanes = -(-experts_total // 128) * 128
+    attended, payload, router_kl = small_kernel(
+        functools.partial(router_kernel, tuple(head_order)),
+        (
+            jax.ShapeDtypeStruct((token_rows, width), jnp.bfloat16),
+            jax.ShapeDtypeStruct((token_rows, width + lanes), jnp.bfloat16),
+            jax.ShapeDtypeStruct((1, token_rows), jnp.float32),
+        ),
+        (index, head_out, *out_parts, hidden, ffn_gain[None, :], router_weight.T, routes.T, rollout_logits.T),
+        (False, True, False),
+        (),
+        2 * token_rows * width * out_weight.shape[0] * exp_count,
+    )
+    router_kl = router_kl[0]
+    blocks = [payload] + [swapped(payload, "ctx", 2 * k) for k in range(1, per_column)]
+    gathered, passed = [], None
+    for block in blocks:
+        parts = [block]
+        for bit in bits:
+            if passed is not None and bit != bits[-1]:
+                passed, *parts = lax.optimization_barrier((passed, *parts))
+                gathered[-1][1] = passed
+            parts = parts + [swapped(part, "exp", bit) for part in parts]
+            if bit == bits[0]:
+                passed = parts[-1]
+        gathered.append(parts)
+    expert_index = (exp_index * per_column + ctx_index // 2).reshape(1).astype(jnp.int32)
+    returned, passed = {}, None
+    for k in sorted(range(per_column), key=lambda k: -min(k, 2.5)):
+        keep, send = expert_block(
+            expert_index, gathered[k], weight_in, weight_out, other_in, other_out, width
+        )
+        for bit in reversed(bits):
+            if passed is not None and bit == bits[0]:
+                passed, send = lax.optimization_barrier((passed, send))
+            received = swapped(send, "exp", bit)
+            if bit == bits[0]:
+                passed = received
+            total = keep.astype(jnp.float32) + received.astype(jnp.float32)
+            total = total.astype(jnp.bfloat16)
+            half = total.shape[0] // 2
+            keep, send = total[:half], total[half:]
+        returned[k] = total if k == 0 else swapped(total, "ctx", 2 * k)
+    moe_out = sum(returned[k].astype(jnp.float32) for k in range(per_column))
+    layer_out = (attended.astype(jnp.float32) + moe_out).astype(jnp.bfloat16)
+    return (layer_out, router_kl)
+
+
+def powers_of_two(*counts):
+    return all(count & (count - 1) == 0 for count in counts)
+
+
+def body(*arrays):
+    experts_total = arrays[7].shape[1]
+    exp_count, ctx_count = lax.axis_size("exp"), lax.axis_size("ctx")
+    dense = experts_total <= 2 * arrays[8].shape[1] and powers_of_two(exp_count, ctx_count)
+    return (dense_body if dense else sparse_body)(*arrays)
+
+
 def solution(mesh):
     return jax.shard_map(
         body,

time: 479 us -> 118 us (0.25)
  blocking collectives: 274 us -> 0 us
  local copies, waits for them, and re-layouts: 68.4 us -> 14.5 us
  waiting for transfers between devices: 77.6 us -> 39.1 us
  starting transfers between devices: 13.4 us -> 42.5 us
  Pallas kernels: 0 us -> 17.6 us
  matrix products: 14.9 us -> 0 us
  between operations: 14.4 us -> 0.9 us
  other arithmetic: 14.8 us -> 2.31 us
    all_to_all x3 -> x0, blocking collectives: 274 us -> none  [the longest x1 110 us: body(): lax.all_to_all(doubled, 'ctx', split_axis=0, concat_axis=0, tiled=True)]
    all_to_all x1, waiting for transfers between devices: 52.5 us -> 3.53 us  [dense_body(): lax.all_to_all(queries, 'exp', split_axis=0, concat_axis=1, tiled=True)]
    ppermute x0 -> x31, starting transfers between devices: none -> 35.7 us  [swapped(): lax.ppermute(value, axis, [(source, source ^ mask) for source in range(co...]
    ppermute x0 -> x31, waiting for transfers between devices: none -> 31.7 us  [swapped(): lax.ppermute(value, axis, [(source, source ^ mask) for source in range(co...]
    reduce_scatter x1 -> x0, waiting for transfers between devices: 23.4 us -> none  [body(): lax.psum_scatter(lax.optimization_barrier(term).astype(jnp.float32).astyp...]
    reshape x3 -> x0, local copies, waits for them, and re-layouts: 20.6 us -> none  [the longest x2 13.4 us: body(): partial_value.reshape(ctx_count, exp_count, capacity, width)]
    pallas_call x0 -> x6, Pallas kernels: none -> 17.6 us  [the longest x4 11.4 us: expert_block(): pl.pallas_call(functools.partial(expert_kernel, parts, width), out_shape=...]
    dot_general x7 -> x0, matrix products: 14.9 us -> none  [the longest x1 4.69 us: body(): jnp.dot(arrived.reshape(-1, width), weight_in, preferred_element_type=jnp...]
  transfers between devices with their start and end apart: 4 -> 33, of which waited for: 3 -> 15; matrix products, arithmetic and copies ran while one was open for 2% -> 1% of each run, Pallas kernels for 0% -> 15%
where the time goes in v3:
time: 118 us; the launch traced here: 117 us
  starting transfers between devices  42.5 us (36%)
  waiting for transfers between devices  39.1 us (33%)
  Pallas kernels  17.6 us (15%)
  local copies, waits for them, and re-layouts  14.5 us (12%)
  other arithmetic  2.31 us (2%)
    ppermute x31, starting transfers between devices, swapped(): lax.ppermute(value, axis, [(source, source ^ mask) for source in range(co...  35.7 us
    ppermute x31, waiting for transfers between devices, swapped(): lax.ppermute(value, axis, [(source, source ^ mask) for source in range(co...  31.7 us
    unnamed x44, local copies, waits for them, and re-layouts  14.4 us
    pallas_call x4, Pallas kernels, expert_block(): pl.pallas_call(functools.partial(expert_kernel, parts, width), out_shape=...  11.4 us
    pallas_call x2, Pallas kernels, small_kernel(): pl.pallas_call(functools.partial(fetching, kernel, len(held), stored), ou...  6.25 us
    ppermute x1, waiting for transfers between devices, passed_along(): lax.ppermute(value, axis, [(source, source + steps) for source in range(i...  3.85 us
    all_to_all x1, waiting for transfers between devices, dense_body(): lax.all_to_all(queries, 'exp', split_axis=0, concat_axis=1, tiled=True)  3.53 us
    ppermute x1, starting transfers between devices, passed_along(): lax.ppermute(value, axis, [(source, source + steps) for source in range(i...  3.44 us
  transfers between devices with their start and end apart: 33, of which 15 were waited for; matrix products, arithmetic and copies ran while one was open for 1% of the time, Pallas kernels for 15%

profile of v3, /device:TPU:0, one launch (start us, length us, event | category | flops | bytes accessed | tf_op | source)
XLA Modules:
  0.0 116.9 jit_solution(13391578951963486750)
XLA Ops:
  0.6 3.0 %collective-permute-start.1 = (bf16[128,2048]{1,0:T(8,128)(2,1)}, bf16[128,2048]{1,0:T(8,128)(2,1)}, u32[]{:S(2)}, u32[]{:S(2)}) collective-permute-start(bf16[128,2048]{1,0:T(8,128)(2,1)} %refs_1_.1), channel_id=1, source_target_pairs={{0,2},{1,3},{2,0},{3,1},{4,6},{5,7},{6,4},{7,5},{8,10},{9,11},{10,... | collective-permute-start | bytes 1572872 | tf_op jit(solution)/shard_map/ppermute | solution.py:182
  4.6 3.4 %collective-permute-start = (bf16[192,512]{1,0:T(8,128)(2,1)S(1)}, bf16[192,512]{1,0:T(8,128)(2,1)S(1)}, u32[]{:S(2)}, u32[]{:S(2)}) collective-permute-start(bf16[192,512]{1,0:T(8,128)(2,1)S(1)} %pad_maximum_fusion), channel_id=1, source_target_pairs={{0,4},{4,8},{8,12},{12,16},{16,20},{20,24},{24,28},{1,5},{5,9},{9,... | collective-permute-start | bytes 589832 | tf_op jit(solution)/shard_map/ppermute | solution.py:19
  8.0 3.9 %collective-permute-done.refs_3_ = bf16[192,512]{1,0:T(8,128)(2,1)S(1)} collective-permute-done((bf16[192,512]{1,0:T(8,128)(2,1)S(1)}, bf16[192,512]{1,0:T(8,128)(2,1)S(1)}, u32[]{:S(2)}, u32[]{:S(2)}) %collective-permute-start) | collective-permute-done | bytes 196640 | tf_op jit(solution)/shard_map/ppermute | solution.py:19
  11.9 2.5 %collective-permute-start.8 = (bf16[2048,384]{1,0:T(8,128)(2,1)}, bf16[2048,384]{1,0:T(8,128)(2,1)S(1)}, u32[]{:S(2)}, u32[]{:S(2)}) collective-permute-start(bf16[2048,384]{1,0:T(8,128)(2,1)} %bitcast.17), channel_id=1, source_target_pairs={{0,4},{4,0},{8,12},{12,8},{16,20},{20,16},{24,28},{28,24},{1,5},{5... | collective-permute-start | bytes 4718600 | tf_op jit(solution)/shard_map/ppermute | solution.py:182
  14.4 3.4 %all-to-all-start = ((bf16[4,48,128]{2,1,0:T(8,128)(2,1)}), bf16[4,48,128]{2,1,0:T(8,128)(2,1)S(1)}, u32[]{:S(2)}, u32[]{:S(2)}) async-start(bf16[4,48,128]{2,1,0:T(8,128)(2,1)} %bitcast.32), calls=%async_computation | async-start | bytes 98304 | tf_op jit(solution)/shard_map/all_to_all | solution.py:414
  18.3 3.5 %all-to-all-done = bf16[4,48,128]{2,1,0:T(8,128)(2,1)S(1)} async-done(((bf16[4,48,128]{2,1,0:T(8,128)(2,1)}), bf16[4,48,128]{2,1,0:T(8,128)(2,1)S(1)}, u32[]{:S(2)}, u32[]{:S(2)}) %all-to-all-start) | async-done | bytes 49184 | tf_op jit(solution)/shard_map/all_to_all | solution.py:414
  24.9 2.7 %shard_map.140.refs_0_ = bf16[4,48,128]{2,1,0:T(8,128)(2,1)S(1)} custom-call(s32[1]{0:T(128)} %bitcast.index_ref, f32[1,128]{1,0:T(1,128)S(1)} %copy-done.21, s32[1,192]{1,0:T(1,128)S(1)} %bitcast.31, bf16[48,512]{1,0:T(8,128)(2,1)S(1)} %copy_bitcast_fusion.refs_2_, bf16[192,512]{1,0:T(8,128)(2,1)S(1)} %collective-permute-done.refs_3_, ...), custom_call_target="tpu_custom_call" | custom-call | flops 9437184 | bytes 1048576 | tf_op jit(solution)/shard_map/pallas_call | solution.py:315
  27.8 2.0 %collective-permute-done.3.refs_4_ = bf16[128,2048]{1,0:T(8,128)(2,1)S(1)} collective-permute-done((bf16[128,2048]{1,0:T(8,128)(2,1)}, bf16[128,2048]{1,0:T(8,128)(2,1)S(1)}, u32[]{:S(2)}, u32[]{:S(2)}) %collective-permute-start.3) | collective-permute-done | bytes 524320 | tf_op jit(solution)/shard_map/ppermute | solution.py:182
  34.7 3.5 %shard_map.141 = (bf16[48,2048]{1,0:T(8,128)(2,1)S(1)}, bf16[48,2176]{1,0:T(8,128)(2,1)}, f32[1,48]{1,0:T(1,128)}) custom-call(s32[1]{0:T(128)} %bitcast.index_ref, bf16[4,48,128]{2,1,0:T(8,128)(2,1)S(1)} %shard_map.140.refs_0_, bf16[128,2048]{1,0:T(8,128)(2,1)S(1)} %copy-done.4, bf16[128,2048]{1,0:T(8,128)(2,1)} %collective-permute-done.1.refs_2_, ...), custom_call_target="tpu_custom_call" | custom-call | flops 100663296 | bytes 1048576 | tf_op jit(solution)/shard_map/pallas_call | solution.py:315
  38.4 1.6 %collective-permute-start.5 = (bf16[48,2176]{1,0:T(8,128)(2,1)}, bf16[48,2176]{1,0:T(8,128)(2,1)S(1)}, u32[]{:S(2)}, u32[]{:S(2)}) collective-permute-start(bf16[48,2176]{1,0:T(8,128)(2,1)} %get-tuple-element.31.refs_0_), channel_id=1, source_target_pairs={{0,8},{4,12},{8,0},{12,4},{16,24},{20,28},{24,16},{28,20},{1,9},{5... | collective-permute-start | bytes 626696 | tf_op jit(solution)/shard_map/ppermute | solution.py:182
  40.0 2.6 %collective-permute-start.12 = (bf16[48,2176]{1,0:T(8,128)(2,1)}, bf16[48,2176]{1,0:T(8,128)(2,1)S(1)}, u32[]{:S(2)}, u32[]{:S(2)}) collective-permute-start(bf16[48,2176]{1,0:T(8,128)(2,1)} %get-tuple-element.31.refs_0_), channel_id=1, source_target_pairs={{0,16},{4,20},{8,24},{12,28},{16,0},{20,4},{24,8},{28,12},{1,17},{... | collective-permute-start | bytes 626696 | tf_op jit(solution)/shard_map/ppermute | solution.py:182
  42.6 3.3 %collective-permute-done.4.refs_1_ = bf16[48,2176]{1,0:T(8,128)(2,1)} collective-permute-done((bf16[48,2176]{1,0:T(8,128)(2,1)}, bf16[48,2176]{1,0:T(8,128)(2,1)}, u32[]{:S(2)}, u32[]{:S(2)}) %collective-permute-start.4) | collective-permute-done | bytes 208928 | tf_op jit(solution)/shard_map/ppermute | solution.py:182
  45.8 4.3 %collective-permute-done.5.refs_0_ = bf16[48,2176]{1,0:T(8,128)(2,1)S(1)} collective-permute-done((bf16[48,2176]{1,0:T(8,128)(2,1)}, bf16[48,2176]{1,0:T(8,128)(2,1)S(1)}, u32[]{:S(2)}, u32[]{:S(2)}) %collective-permute-start.5) | collective-permute-done | bytes 208928 | tf_op jit(solution)/shard_map/ppermute | solution.py:182
  50.2 1.7 %collective-permute-start.11 = (bf16[48,2176]{1,0:T(8,128)(2,1)S(1)}, bf16[48,2176]{1,0:T(8,128)(2,1)}, u32[]{:S(2)}, u32[]{:S(2)}) collective-permute-start(bf16[48,2176]{1,0:T(8,128)(2,1)S(1)} %collective-permute-done.5.refs_0_), channel_id=1, source_target_pairs={{0,2},{1,3},{2,0},{3,1},{4,6},{5,7},{6,4},{7,5},{8,10},{9,11},{10,... | collective-permute-start | bytes 626696 | tf_op jit(solution)/shard_map/ppermute | solution.py:182
  51.8 2.5 %collective-permute-start.14 = (bf16[48,2176]{1,0:T(8,128)(2,1)}, bf16[48,2176]{1,0:T(8,128)(2,1)S(1)}, u32[]{:S(2)}, u32[]{:S(2)}) collective-permute-start(bf16[48,2176]{1,0:T(8,128)(2,1)} %get-tuple-element.31.refs_0_), channel_id=1, source_target_pairs={{0,24},{4,28},{8,16},{12,20},{16,8},{20,12},{24,0},{28,4},{1,25},{... | collective-permute-start | bytes 626696 | tf_op jit(solution)/shard_map/ppermute | solution.py:182
  54.3 2.3 %collective-permute-done.11.refs_1_ = bf16[48,2176]{1,0:T(8,128)(2,1)} collective-permute-done((bf16[48,2176]{1,0:T(8,128)(2,1)S(1)}, bf16[48,2176]{1,0:T(8,128)(2,1)}, u32[]{:S(2)}, u32[]{:S(2)}) %collective-permute-start.11) | collective-permute-done | bytes 208928 | tf_op jit(solution)/shard_map/ppermute | solution.py:182
  56.6 1.2 %collective-permute-start.13 = (bf16[48,2176]{1,0:T(8,128)(2,1)S(1)}, bf16[48,2176]{1,0:T(8,128)(2,1)S(1)}, u32[]{:S(2)}, u32[]{:S(2)}) collective-permute-start(bf16[48,2176]{1,0:T(8,128)(2,1)S(1)} %collective-permute-done.12.refs_0_), channel_id=1, source_target_pairs={{0,2},{1,3},{2,0},{3,1},{4,6},{5,7},{6,4},{7,5},{8,10},{9,11},{10,... | collective-permute-start | bytes 626696 | tf_op jit(solution)/shard_map/ppermute | solution.py:182
  59.7 2.7 %collective-permute-done.13.refs_1_ = bf16[48,2176]{1,0:T(8,128)(2,1)S(1)} collective-permute-done((bf16[48,2176]{1,0:T(8,128)(2,1)S(1)}, bf16[48,2176]{1,0:T(8,128)(2,1)S(1)}, u32[]{:S(2)}, u32[]{:S(2)}) %collective-permute-start.13) | collective-permute-done | bytes 208928 | tf_op jit(solution)/shard_map/ppermute | solution.py:182
  62.4 2.3 %collective-permute-done.9.refs_7_ = bf16[192,2048]{1,0:T(8,128)(2,1)S(1)} collective-permute-done((bf16[192,2048]{1,0:T(8,128)(2,1)}, bf16[192,2048]{1,0:T(8,128)(2,1)S(1)}, u32[]{:S(2)}, u32[]{:S(2)}) %collective-permute-start.9) | collective-permute-done | bytes 786464 | tf_op jit(solution)/shard_map/ppermute | solution.py:182
  71.0 3.1 %shard_map.145 = (bf16[96,2048]{1,0:T(8,128)(2,1)S(1)}, bf16[96,2048]{1,0:T(8,128)(2,1)S(1)}) custom-call(s32[1]{0:T(128)} %bitcast.10.index_ref, bf16[48,2176]{1,0:T(8,128)(2,1)S(1)} %copy-done.12, bf16[48,2176]{1,0:T(8,128)(2,1)} %collective-permute-done.11.refs_1_, bf16[48,2176]{1,0:T(8,128)(2,1)S(1)} %copy-done.14, ...), custom_call_target="tpu_custom_call" | custom-call | flops 905969664 | bytes 8388608 | tf_op jit(solution)/shard_map/pallas_call | solution.py:364
  75.4 2.8 %shard_map.142 = (bf16[96,2048]{1,0:T(8,128)(2,1)S(1)}, bf16[96,2048]{1,0:T(8,128)(2,1)S(1)}) custom-call(s32[1]{0:T(128)} %bitcast.10.index_ref, bf16[48,2176]{1,0:T(8,128)(2,1)} %get-tuple-element.31.refs_0_, bf16[48,2176]{1,0:T(8,128)(2,1)} %collective-permute-done.4.refs_1_, bf16[48,2176]{1,0:T(8,128)(2,1)} %collective-permute-done.6.refs_2_, ...), custom_call_target="tpu_custom_call" | custom-call | flops 905969664 | bytes 8388608 | tf_op jit(solution)/shard_map/pallas_call | solution.py:364
  78.7 2.7 %shard_map.144 = (bf16[96,2048]{1,0:T(8,128)(2,1)S(1)}, bf16[96,2048]{1,0:T(8,128)(2,1)S(1)}) custom-call(s32[1]{0:T(128)} %bitcast.10.index_ref, bf16[48,2176]{1,0:T(8,128)(2,1)S(1)} %copy-done.8, bf16[48,2176]{1,0:T(8,128)(2,1)S(1)} %copy-done.10, bf16[48,2176]{1,0:T(8,128)(2,1)S(1)} %collective-permute-done.20.refs_2_, ...), custom_call_target="tpu_custom_call" | custom-call | flops 905969664 | bytes 8388608 | tf_op jit(solution)/shard_map/pallas_call | solution.py:364
  81.6 2.8 %shard_map.143 = (bf16[96,2048]{1,0:T(8,128)(2,1)S(1)}, bf16[96,2048]{1,0:T(8,128)(2,1)S(1)}) custom-call(s32[1]{0:T(128)} %bitcast.10.index_ref, bf16[48,2176]{1,0:T(8,128)(2,1)S(1)} %collective-permute-done.14.refs_0_, bf16[48,2176]{1,0:T(8,128)(2,1)} %collective-permute-done.15.refs_1_, bf16[48,2176]{1,0:T(8,128)(2,1)S(1)} %collective-permute-done.16.refs_2_, ...), custom_call_target="tpu_custom_call" | custom-call | flops 905969664 | bytes 8388608 | tf_op jit(solution)/shard_map/pallas_call | solution.py:364
  86.4 1.6 %collective-permute-start.19 = (bf16[48,2048]{1,0:T(8,128)(2,1)S(1)}, bf16[48,2048]{1,0:T(8,128)(2,1)S(1)}, u32[]{:S(2)}, u32[]{:S(2)}) collective-permute-start(bf16[48,2048]{1,0:T(8,128)(2,1)S(1)} %slice.33), channel_id=1, source_target_pairs={{0,2},{1,3},{2,0},{3,1},{4,6},{5,7},{6,4},{7,5},{8,10},{9,11},{10,... | collective-permute-start | bytes 589832 | tf_op jit(solution)/shard_map/ppermute | solution.py:182
  88.0 5.5 %collective-permute-done.19 = bf16[48,2048]{1,0:T(8,128)(2,1)S(1)} collective-permute-done((bf16[48,2048]{1,0:T(8,128)(2,1)S(1)}, bf16[48,2048]{1,0:T(8,128)(2,1)S(1)}, u32[]{:S(2)}, u32[]{:S(2)}) %collective-permute-start.19) | collective-permute-done | bytes 196640 | tf_op jit(solution)/shard_map/ppermute | solution.py:182
  93.5 1.5 %collective-permute-start.23 = (bf16[48,2048]{1,0:T(8,128)(2,1)S(1)}, bf16[48,2048]{1,0:T(8,128)(2,1)S(1)}, u32[]{:S(2)}, u32[]{:S(2)}) collective-permute-start(bf16[48,2048]{1,0:T(8,128)(2,1)S(1)} %slice.34), channel_id=1, source_target_pairs={{0,2},{1,3},{2,0},{3,1},{4,6},{5,7},{6,4},{7,5},{8,10},{9,11},{10,... | collective-permute-start | bytes 589832 | tf_op jit(solution)/shard_map/ppermute | solution.py:182
  95.1 4.7 %collective-permute-start.31 = (bf16[48,2048]{1,0:T(8,128)(2,1)S(1)}, bf16[48,2048]{1,0:T(8,128)(2,1)S(1)}, u32[]{:S(2)}, u32[]{:S(2)}) collective-permute-start(bf16[48,2048]{1,0:T(8,128)(2,1)S(1)} %add_convert_fusion.5), channel_id=1, source_target_pairs={{0,24},{4,28},{8,16},{12,20},{16,8},{20,12},{24,0},{28,4},{1,25},{... | collective-permute-start | bytes 589832 | tf_op jit(solution)/shard_map/ppermute | solution.py:182
  99.8 1.5 %collective-permute-start.27 = (bf16[48,2048]{1,0:T(8,128)(2,1)S(1)}, bf16[48,2048]{1,0:T(8,128)(2,1)S(1)}, u32[]{:S(2)}, u32[]{:S(2)}) collective-permute-start(bf16[48,2048]{1,0:T(8,128)(2,1)S(1)} %slice.35), channel_id=1, source_target_pairs={{0,2},{1,3},{2,0},{3,1},{4,6},{5,7},{6,4},{7,5},{8,10},{9,11},{10,... | collective-permute-start | bytes 589832 | tf_op jit(solution)/shard_map/ppermute | solution.py:182
  101.3 3.7 %collective-permute-start.30 = (bf16[48,2048]{1,0:T(8,128)(2,1)S(1)}, bf16[48,2048]{1,0:T(8,128)(2,1)S(1)}, u32[]{:S(2)}, u32[]{:S(2)}) collective-permute-start(bf16[48,2048]{1,0:T(8,128)(2,1)S(1)} %add_convert_fusion.6), channel_id=1, source_target_pairs={{0,16},{4,20},{8,24},{12,28},{16,0},{20,4},{24,8},{28,12},{1,17},{... | collective-permute-start | bytes 589832 | tf_op jit(solution)/shard_map/ppermute | solution.py:182
  105.5 2.7 %collective-permute-start.29 = (bf16[48,2048]{1,0:T(8,128)(2,1)S(1)}, bf16[48,2048]{1,0:T(8,128)(2,1)S(1)}, u32[]{:S(2)}, u32[]{:S(2)}) collective-permute-start(bf16[48,2048]{1,0:T(8,128)(2,1)S(1)} %add_convert_fusion.7), channel_id=1, source_target_pairs={{0,8},{4,12},{8,0},{12,4},{16,24},{20,28},{24,16},{28,20},{1,9},{5... | collective-permute-start | bytes 589832 | tf_op jit(solution)/shard_map/ppermute | solution.py:182
  108.2 1.5 %collective-permute-start.28 = (bf16[48,2048]{1,0:T(8,128)(2,1)S(1)}, bf16[48,2048]{1,0:T(8,128)(2,1)S(1)}, u32[]{:S(2)}, u32[]{:S(2)}) collective-permute-start(bf16[48,2048]{1,0:T(8,128)(2,1)S(1)} %slice.36), channel_id=1, source_target_pairs={{0,2},{1,3},{2,0},{3,1},{4,6},{5,7},{6,4},{7,5},{8,10},{9,11},{10,... | collective-permute-start | bytes 589832 | tf_op jit(solution)/shard_map/ppermute | solution.py:182
  109.7 6.2 %collective-permute-done.30 = bf16[48,2048]{1,0:T(8,128)(2,1)S(1)} collective-permute-done((bf16[48,2048]{1,0:T(8,128)(2,1)S(1)}, bf16[48,2048]{1,0:T(8,128)(2,1)S(1)}, u32[]{:S(2)}, u32[]{:S(2)}) %collective-permute-start.30) | collective-permute-done | bytes 196640 | tf_op jit(solution)/shard_map/ppermute | solution.py:182
  (98 shorter events, 23.5 us)
Async XLA Ops:
  0.6 27.0 %collective-permute-start.1 = (bf16[128,2048]{1,0:T(8,128)(2,1)}, bf16[128,2048]{1,0:T(8,128)(2,1)}, u32[]{:S(2)}, u32[]{:S(2)}) collective-permute-start(bf16[128,2048]{1,0:T(8,128)(2,1)} %refs_1_.1), channel_id=1, source_target_pairs={{0,2},{1,3},{2,0},{3,1},{4,6},{5,7},{6,4},{7,5},{8,10},{9,11},{10,... | collective-permute-start | bytes 1572872 | tf_op jit(solution)/shard_map/ppermute | solution.py:182
  4.6 7.3 %collective-permute-start = (bf16[192,512]{1,0:T(8,128)(2,1)S(1)}, bf16[192,512]{1,0:T(8,128)(2,1)S(1)}, u32[]{:S(2)}, u32[]{:S(2)}) collective-permute-start(bf16[192,512]{1,0:T(8,128)(2,1)S(1)} %pad_maximum_fusion), channel_id=1, source_target_pairs={{0,4},{4,8},{8,12},{12,16},{16,20},{20,24},{24,28},{1,5},{5,9},{9,... | collective-permute-start | bytes 589832 | tf_op jit(solution)/shard_map/ppermute | solution.py:19
  11.9 55.0 %collective-permute-start.8 = (bf16[2048,384]{1,0:T(8,128)(2,1)}, bf16[2048,384]{1,0:T(8,128)(2,1)S(1)}, u32[]{:S(2)}, u32[]{:S(2)}) collective-permute-start(bf16[2048,384]{1,0:T(8,128)(2,1)} %bitcast.17), channel_id=1, source_target_pairs={{0,4},{4,0},{8,12},{12,8},{16,20},{20,16},{24,28},{28,24},{1,5},{5... | collective-permute-start | bytes 4718600 | tf_op jit(solution)/shard_map/ppermute | solution.py:182
  14.4 7.4 %all-to-all-start = ((bf16[4,48,128]{2,1,0:T(8,128)(2,1)}), bf16[4,48,128]{2,1,0:T(8,128)(2,1)S(1)}, u32[]{:S(2)}, u32[]{:S(2)}) async-start(bf16[4,48,128]{2,1,0:T(8,128)(2,1)} %bitcast.32), calls=%async_computation | async-start | bytes 98304 | tf_op jit(solution)/shard_map/all_to_all | solution.py:414
  17.8 10.0 %collective-permute-start.2 = (bf16[128,2048]{1,0:T(8,128)(2,1)}, bf16[128,2048]{1,0:T(8,128)(2,1)}, u32[]{:S(2)}, u32[]{:S(2)}) collective-permute-start(bf16[128,2048]{1,0:T(8,128)(2,1)} %refs_1_.1), channel_id=1, source_target_pairs={{0,1},{1,0},{2,3},{3,2},{4,5},{5,4},{6,7},{7,6},{8,9},{9,8},{10,11... | collective-permute-start | bytes 1572872 | tf_op jit(solution)/shard_map/ppermute | solution.py:182
  27.7 2.2 %collective-permute-start.3 = (bf16[128,2048]{1,0:T(8,128)(2,1)}, bf16[128,2048]{1,0:T(8,128)(2,1)S(1)}, u32[]{:S(2)}, u32[]{:S(2)}) collective-permute-start(bf16[128,2048]{1,0:T(8,128)(2,1)} %collective-permute-done.1.refs_2_), channel_id=1, source_target_pairs={{0,1},{1,0},{2,3},{3,2},{4,5},{5,4},{6,7},{7,6},{8,9},{9,8},{10,11... | collective-permute-start | bytes 1572872 | tf_op jit(solution)/shard_map/ppermute | solution.py:182
  27.7 37.0 %collective-permute-start.9 = (bf16[192,2048]{1,0:T(8,128)(2,1)}, bf16[192,2048]{1,0:T(8,128)(2,1)S(1)}, u32[]{:S(2)}, u32[]{:S(2)}) collective-permute-start(bf16[192,2048]{1,0:T(8,128)(2,1)} %bitcast.22), channel_id=1, source_target_pairs={{0,4},{4,0},{8,12},{12,8},{16,20},{20,16},{24,28},{28,24},{1,5},{5... | collective-permute-start | bytes 2359304 | tf_op jit(solution)/shard_map/ppermute | solution.py:182
  38.3 7.6 %collective-permute-start.4 = (bf16[48,2176]{1,0:T(8,128)(2,1)}, bf16[48,2176]{1,0:T(8,128)(2,1)}, u32[]{:S(2)}, u32[]{:S(2)}) collective-permute-start(bf16[48,2176]{1,0:T(8,128)(2,1)} %get-tuple-element.31.refs_0_), channel_id=1, source_target_pairs={{0,2},{1,3},{2,0},{3,1},{4,6},{5,7},{6,4},{7,5},{8,10},{9,11},{10,... | collective-permute-start | bytes 626696 | tf_op jit(solution)/shard_map/ppermute | solution.py:182
  38.4 11.7 %collective-permute-start.5 = (bf16[48,2176]{1,0:T(8,128)(2,1)}, bf16[48,2176]{1,0:T(8,128)(2,1)S(1)}, u32[]{:S(2)}, u32[]{:S(2)}) collective-permute-start(bf16[48,2176]{1,0:T(8,128)(2,1)} %get-tuple-element.31.refs_0_), channel_id=1, source_target_pairs={{0,8},{4,12},{8,0},{12,4},{16,24},{20,28},{24,16},{28,20},{1,9},{5... | collective-permute-start | bytes 626696 | tf_op jit(solution)/shard_map/ppermute | solution.py:182
  40.0 14.3 %collective-permute-start.12 = (bf16[48,2176]{1,0:T(8,128)(2,1)}, bf16[48,2176]{1,0:T(8,128)(2,1)S(1)}, u32[]{:S(2)}, u32[]{:S(2)}) collective-permute-start(bf16[48,2176]{1,0:T(8,128)(2,1)} %get-tuple-element.31.refs_0_), channel_id=1, source_target_pairs={{0,16},{4,20},{8,24},{12,28},{16,0},{20,4},{24,8},{28,12},{1,17},{... | collective-permute-start | bytes 626696 | tf_op jit(solution)/shard_map/ppermute | solution.py:182
  50.2 6.5 %collective-permute-start.11 = (bf16[48,2176]{1,0:T(8,128)(2,1)S(1)}, bf16[48,2176]{1,0:T(8,128)(2,1)}, u32[]{:S(2)}, u32[]{:S(2)}) collective-permute-start(bf16[48,2176]{1,0:T(8,128)(2,1)S(1)} %collective-permute-done.5.refs_0_), channel_id=1, source_target_pairs={{0,2},{1,3},{2,0},{3,1},{4,6},{5,7},{6,4},{7,5},{8,10},{9,11},{10,... | collective-permute-start | bytes 626696 | tf_op jit(solution)/shard_map/ppermute | solution.py:182
  51.8 7.9 %collective-permute-start.14 = (bf16[48,2176]{1,0:T(8,128)(2,1)}, bf16[48,2176]{1,0:T(8,128)(2,1)S(1)}, u32[]{:S(2)}, u32[]{:S(2)}) collective-permute-start(bf16[48,2176]{1,0:T(8,128)(2,1)} %get-tuple-element.31.refs_0_), channel_id=1, source_target_pairs={{0,24},{4,28},{8,16},{12,20},{16,8},{20,12},{24,0},{28,4},{1,25},{... | collective-permute-start | bytes 626696 | tf_op jit(solution)/shard_map/ppermute | solution.py:182
  56.6 5.8 %collective-permute-start.13 = (bf16[48,2176]{1,0:T(8,128)(2,1)S(1)}, bf16[48,2176]{1,0:T(8,128)(2,1)S(1)}, u32[]{:S(2)}, u32[]{:S(2)}) collective-permute-start(bf16[48,2176]{1,0:T(8,128)(2,1)S(1)} %collective-permute-done.12.refs_0_), channel_id=1, source_target_pairs={{0,2},{1,3},{2,0},{3,1},{4,6},{5,7},{6,4},{7,5},{8,10},{9,11},{10,... | collective-permute-start | bytes 626696 | tf_op jit(solution)/shard_map/ppermute | solution.py:182
  57.8 7.8 %collective-permute-start.24 = (bf16[48,2176]{1,0:T(8,128)(2,1)S(1)}, bf16[48,2176]{1,0:T(8,128)(2,1)S(1)}, u32[]{:S(2)}, u32[]{:S(2)}) collective-permute-start(bf16[48,2176]{1,0:T(8,128)(2,1)S(1)} %collective-permute-done.5.refs_0_), channel_id=1, source_target_pairs={{0,1},{1,0},{2,3},{3,2},{4,5},{5,4},{6,7},{7,6},{8,9},{9,8},{10,11... | collective-permute-start | bytes 626696 | tf_op jit(solution)/shard_map/ppermute | solution.py:182
  59.7 7.2 %collective-permute-start.25 = (bf16[48,2176]{1,0:T(8,128)(2,1)}, bf16[48,2176]{1,0:T(8,128)(2,1)}, u32[]{:S(2)}, u32[]{:S(2)}) collective-permute-start(bf16[48,2176]{1,0:T(8,128)(2,1)} %collective-permute-done.11.refs_1_), channel_id=1, source_target_pairs={{0,1},{1,0},{2,3},{3,2},{4,5},{5,4},{6,7},{7,6},{8,9},{9,8},{10,11... | collective-permute-start | bytes 626696 | tf_op jit(solution)/shard_map/ppermute | solution.py:182
  62.4 12.3 %collective-permute-start.6 = (bf16[48,2176]{1,0:T(8,128)(2,1)}, bf16[48,2176]{1,0:T(8,128)(2,1)}, u32[]{:S(2)}, u32[]{:S(2)}) collective-permute-start(bf16[48,2176]{1,0:T(8,128)(2,1)} %get-tuple-element.31.refs_0_), channel_id=1, source_target_pairs={{0,1},{1,0},{2,3},{3,2},{4,5},{5,4},{6,7},{7,6},{8,9},{9,8},{10,11... | collective-permute-start | bytes 626696 | tf_op jit(solution)/shard_map/ppermute | solution.py:182
  65.6 9.3 %collective-permute-start.7 = (bf16[48,2176]{1,0:T(8,128)(2,1)}, bf16[48,2176]{1,0:T(8,128)(2,1)}, u32[]{:S(2)}, u32[]{:S(2)}) collective-permute-start(bf16[48,2176]{1,0:T(8,128)(2,1)} %collective-permute-done.4.refs_1_), channel_id=1, source_target_pairs={{0,1},{1,0},{2,3},{3,2},{4,5},{5,4},{6,7},{7,6},{8,9},{9,8},{10,11... | collective-permute-start | bytes 626696 | tf_op jit(solution)/shard_map/ppermute | solution.py:182
  66.3 8.9 %collective-permute-start.15 = (bf16[48,2176]{1,0:T(8,128)(2,1)S(1)}, bf16[48,2176]{1,0:T(8,128)(2,1)}, u32[]{:S(2)}, u32[]{:S(2)}) collective-permute-start(bf16[48,2176]{1,0:T(8,128)(2,1)S(1)} %collective-permute-done.14.refs_0_), channel_id=1, source_target_pairs={{0,2},{1,3},{2,0},{3,1},{4,6},{5,7},{6,4},{7,5},{8,10},{9,11},{10,... | collective-permute-start | bytes 626696 | tf_op jit(solution)/shard_map/ppermute | solution.py:182
  74.1 10.7 %collective-permute-start.26 = (bf16[96,2048]{1,0:T(8,128)(2,1)S(1)}, bf16[96,2048]{1,0:T(8,128)(2,1)S(1)}, u32[]{:S(2)}, u32[]{:S(2)}) collective-permute-start(bf16[96,2048]{1,0:T(8,128)(2,1)S(1)} %get-tuple-element.48), channel_id=1, source_target_pairs={{0,1},{1,0},{2,3},{3,2},{4,5},{5,4},{6,7},{7,6},{8,9},{9,8},{10,11... | collective-permute-start | bytes 1179656 | tf_op jit(solution)/shard_map/ppermute | solution.py:182
  74.4 3.9 %collective-permute-start.20 = (bf16[48,2176]{1,0:T(8,128)(2,1)S(1)}, bf16[48,2176]{1,0:T(8,128)(2,1)S(1)}, u32[]{:S(2)}, u32[]{:S(2)}) collective-permute-start(bf16[48,2176]{1,0:T(8,128)(2,1)S(1)} %copy-done.8), channel_id=1, source_target_pairs={{0,1},{1,0},{2,3},{3,2},{4,5},{5,4},{6,7},{7,6},{8,9},{9,8},{10,11... | collective-permute-start | bytes 626696 | tf_op jit(solution)/shard_map/ppermute | solution.py:182
  74.7 4.0 %collective-permute-start.21 = (bf16[48,2176]{1,0:T(8,128)(2,1)S(1)}, bf16[48,2176]{1,0:T(8,128)(2,1)S(1)}, u32[]{:S(2)}, u32[]{:S(2)}) collective-permute-start(bf16[48,2176]{1,0:T(8,128)(2,1)S(1)} %copy-done.10), channel_id=1, source_target_pairs={{0,1},{1,0},{2,3},{3,2},{4,5},{5,4},{6,7},{7,6},{8,9},{9,8},{10,11... | collective-permute-start | bytes 626696 | tf_op jit(solution)/shard_map/ppermute | solution.py:182
  74.9 6.7 %collective-permute-start.16 = (bf16[48,2176]{1,0:T(8,128)(2,1)S(1)}, bf16[48,2176]{1,0:T(8,128)(2,1)S(1)}, u32[]{:S(2)}, u32[]{:S(2)}) collective-permute-start(bf16[48,2176]{1,0:T(8,128)(2,1)S(1)} %collective-permute-done.14.refs_0_), channel_id=1, source_target_pairs={{0,1},{1,0},{2,3},{3,2},{4,5},{5,4},{6,7},{7,6},{8,9},{9,8},{10,11... | collective-permute-start | bytes 626696 | tf_op jit(solution)/shard_map/ppermute | solution.py:182
  75.2 6.4 %collective-permute-start.17 = (bf16[48,2176]{1,0:T(8,128)(2,1)}, bf16[48,2176]{1,0:T(8,128)(2,1)S(1)}, u32[]{:S(2)}, u32[]{:S(2)}) collective-permute-start(bf16[48,2176]{1,0:T(8,128)(2,1)} %collective-permute-done.15.refs_1_), channel_id=1, source_target_pairs={{0,1},{1,0},{2,3},{3,2},{4,5},{5,4},{6,7},{7,6},{8,9},{9,8},{10,11... | collective-permute-start | bytes 626696 | tf_op jit(solution)/shard_map/ppermute | solution.py:182
  78.3 6.6 %collective-permute-start.10 = (bf16[96,2048]{1,0:T(8,128)(2,1)S(1)}, bf16[96,2048]{1,0:T(8,128)(2,1)S(1)}, u32[]{:S(2)}, u32[]{:S(2)}) collective-permute-start(bf16[96,2048]{1,0:T(8,128)(2,1)S(1)} %get-tuple-element.36), channel_id=1, source_target_pairs={{0,1},{1,0},{2,3},{3,2},{4,5},{5,4},{6,7},{7,6},{8,9},{9,8},{10,11... | collective-permute-start | bytes 1179656 | tf_op jit(solution)/shard_map/ppermute | solution.py:182
  81.3 6.6 %collective-permute-start.22 = (bf16[96,2048]{1,0:T(8,128)(2,1)S(1)}, bf16[96,2048]{1,0:T(8,128)(2,1)S(1)}, u32[]{:S(2)}, u32[]{:S(2)}) collective-permute-start(bf16[96,2048]{1,0:T(8,128)(2,1)S(1)} %get-tuple-element.44), channel_id=1, source_target_pairs={{0,1},{1,0},{2,3},{3,2},{4,5},{5,4},{6,7},{7,6},{8,9},{9,8},{10,11... | collective-permute-start | bytes 1179656 | tf_op jit(solution)/shard_map/ppermute | solution.py:182
  86.4 7.2 %collective-permute-start.19 = (bf16[48,2048]{1,0:T(8,128)(2,1)S(1)}, bf16[48,2048]{1,0:T(8,128)(2,1)S(1)}, u32[]{:S(2)}, u32[]{:S(2)}) collective-permute-start(bf16[48,2048]{1,0:T(8,128)(2,1)S(1)} %slice.33), channel_id=1, source_target_pairs={{0,2},{1,3},{2,0},{3,1},{4,6},{5,7},{6,4},{7,5},{8,10},{9,11},{10,... | collective-permute-start | bytes 589832 | tf_op jit(solution)/shard_map/ppermute | solution.py:182
  93.5 6.3 %collective-permute-start.23 = (bf16[48,2048]{1,0:T(8,128)(2,1)S(1)}, bf16[48,2048]{1,0:T(8,128)(2,1)S(1)}, u32[]{:S(2)}, u32[]{:S(2)}) collective-permute-start(bf16[48,2048]{1,0:T(8,128)(2,1)S(1)} %slice.34), channel_id=1, source_target_pairs={{0,2},{1,3},{2,0},{3,1},{4,6},{5,7},{6,4},{7,5},{8,10},{9,11},{10,... | collective-permute-start | bytes 589832 | tf_op jit(solution)/shard_map/ppermute | solution.py:182
  95.1 14.6 %collective-permute-start.31 = (bf16[48,2048]{1,0:T(8,128)(2,1)S(1)}, bf16[48,2048]{1,0:T(8,128)(2,1)S(1)}, u32[]{:S(2)}, u32[]{:S(2)}) collective-permute-start(bf16[48,2048]{1,0:T(8,128)(2,1)S(1)} %add_convert_fusion.5), channel_id=1, source_target_pairs={{0,24},{4,28},{8,16},{12,20},{16,8},{20,12},{24,0},{28,4},{1,25},{... | collective-permute-start | bytes 589832 | tf_op jit(solution)/shard_map/ppermute | solution.py:182
  99.8 5.7 %collective-permute-start.27 = (bf16[48,2048]{1,0:T(8,128)(2,1)S(1)}, bf16[48,2048]{1,0:T(8,128)(2,1)S(1)}, u32[]{:S(2)}, u32[]{:S(2)}) collective-permute-start(bf16[48,2048]{1,0:T(8,128)(2,1)S(1)} %slice.35), channel_id=1, source_target_pairs={{0,2},{1,3},{2,0},{3,1},{4,6},{5,7},{6,4},{7,5},{8,10},{9,11},{10,... | collective-permute-start | bytes 589832 | tf_op jit(solution)/shard_map/ppermute | solution.py:182
  101.3 14.6 %collective-permute-start.30 = (bf16[48,2048]{1,0:T(8,128)(2,1)S(1)}, bf16[48,2048]{1,0:T(8,128)(2,1)S(1)}, u32[]{:S(2)}, u32[]{:S(2)}) collective-permute-start(bf16[48,2048]{1,0:T(8,128)(2,1)S(1)} %add_convert_fusion.6), channel_id=1, source_target_pairs={{0,16},{4,20},{8,24},{12,28},{16,0},{20,4},{24,8},{28,12},{1,17},{... | collective-permute-start | bytes 589832 | tf_op jit(solution)/shard_map/ppermute | solution.py:182
  105.5 10.5 %collective-permute-start.29 = (bf16[48,2048]{1,0:T(8,128)(2,1)S(1)}, bf16[48,2048]{1,0:T(8,128)(2,1)S(1)}, u32[]{:S(2)}, u32[]{:S(2)}) collective-permute-start(bf16[48,2048]{1,0:T(8,128)(2,1)S(1)} %add_convert_fusion.7), channel_id=1, source_target_pairs={{0,8},{4,12},{8,0},{12,4},{16,24},{20,28},{24,16},{28,20},{1,9},{5... | collective-permute-start | bytes 589832 | tf_op jit(solution)/shard_map/ppermute | solution.py:182
  108.2 7.9 %collective-permute-start.28 = (bf16[48,2048]{1,0:T(8,128)(2,1)S(1)}, bf16[48,2048]{1,0:T(8,128)(2,1)S(1)}, u32[]{:S(2)}, u32[]{:S(2)}) collective-permute-start(bf16[48,2048]{1,0:T(8,128)(2,1)S(1)} %slice.36), channel_id=1, source_target_pairs={{0,2},{1,3},{2,0},{3,1},{4,6},{5,7},{6,4},{7,5},{8,10},{9,11},{10,... | collective-permute-start | bytes 589832 | tf_op jit(solution)/shard_map/ppermute | solution.py:182
  (23 other events, 90.3 us)

commit v4 on v3

--- a/solution.py
+++ b/solution.py
@@ -182,68 +182,62 @@
     return lax.ppermute(value, axis, [(source, source ^ mask) for source in range(count)])
 
 
-def attention_kernel(share, index_ref, spectrum_ref, pos_ref, q_ref, *refs):
-    before_ref, own_k, own_v, out_ref, cos_ref, sin_ref, pos_col = refs
-    heads, rows, size = out_ref.shape
-    block = own_k.shape[0]
-    start = pl.multiple_of(index_ref[0] * rows, 16)
+def attention_kernel(order, index_ref, pos_ref, q_ref, before_ref, own_ref, weight_ref, *refs):
+    outputs, (cos_ref, sin_ref, mixed) = refs[:-3], refs[-3:]
+    block, size = q_ref.shape
+    rows = block // len(order)
     pos_row = pos_ref[...].astype(jnp.float32)
     along = lax.broadcasted_iota(jnp.int32, (block, block), 0)
     across = lax.broadcasted_iota(jnp.int32, (block, block), 1)
-    pos_col[...] = jnp.sum(jnp.where(along == across, pos_row, 0.0), axis=1, keepdims=True)
+    pos_col = jnp.sum(jnp.where(along == across, pos_row, 0.0), axis=1, keepdims=True)
     opening = jnp.sum(jnp.where(across[:1] == 0, pos_row, 0.0), axis=1, keepdims=True)
     earlier = opening - block + along[:, :1].astype(jnp.float32)
     lane = lax.broadcasted_iota(jnp.int32, (1, size), 1)
     lower = lane < size // 2
     phase = jnp.where(lower, 0.0, math.pi / 2)
-    for half, at in enumerate((earlier, pos_col[...])):
-        turn = jnp.cos(at * spectrum_ref[...] - phase)
+    turn_of = jnp.where(lower, lane, lane - size // 2).astype(jnp.float32)
+    spectrum = jnp.exp(turn_of * (-2.0 * math.log(theta) / size))
+    for half, at in enumerate((earlier, pos_col)):
+        turn = jnp.cos(at * spectrum - phase)
         swap = pltpu.roll(turn, size // 2, 1)
         cos_ref[half * block : (half + 1) * block, :] = jnp.where(lower, turn, swap)
         sin_ref[half * block : (half + 1) * block, :] = jnp.where(lower, -swap, turn)
 
-    def turned(vectors, cosine, sine):
+    def turned(vectors, start):
         wide = vectors.astype(jnp.float32)
         wide = wide * lax.rsqrt(jnp.mean(wide * wide, axis=1, keepdims=True) + eps)
+        cosine, sine = cos_ref[start : start + block, :], sin_ref[start : start + block, :]
         return (wide * cosine + pltpu.roll(wide, size // 2, 1) * sine).astype(jnp.bfloat16)
 
-    own = pl.ds(block + start, rows)
-    query_at = start + lax.broadcasted_iota(jnp.int32, (rows, 2 * block), 0)
-    key_at = lax.broadcasted_iota(jnp.int32, (rows, 2 * block), 1) - block
-    reach = pos_col[pl.ds(start, rows), :].astype(jnp.int32)
-    allowed = (key_at <= query_at) & (key_at >= query_at - reach)
-    for group in range(heads // share):
-        columns = slice(group * size, (group + 1) * size)
-        keys = jnp.concatenate(
-            [
-                turned(before_ref[:, columns], cos_ref[:block, :], sin_ref[:block, :]),
-                turned(own_k[:, columns], cos_ref[block:, :], sin_ref[block:, :]),
-            ],
-            axis=0,
-        )
-        values = jnp.concatenate([before_ref[:, own_k.shape[1] + group * size :][:, :size], own_v[:, columns]], axis=0)
-        for h in range(group * share, (group + 1) * share):
-            query = turned(q_ref[:, h * size : (h + 1) * size], cos_ref[own, :], sin_ref[own, :])
-            scores = lax.dot_general(
-                query, keys, (((1,), (1,)), ((), ())), preferred_element_type=jnp.float32
-            ) * (1.0 / math.sqrt(size))
-            raw = jnp.where(allowed, jnp.exp(scores), 0.0)
-            weights = (raw / jnp.sum(raw, axis=1, keepdims=True)).astype(jnp.bfloat16)
-            out_ref[h] = jnp.dot(weights, values, preferred_element_type=jnp.float32).astype(
-                jnp.bfloat16
-            )
-
-
-def router_kernel(order, index_ref, heads_ref, *refs):
-    parts, refs = refs[: len(order)], refs[len(order) :]
-    hidden_ref, gain_ref, router_ref, routes_ref, rollout_ref, attended_ref, payload_ref, kl_ref = refs
+    query_at = lax.broadcasted_iota(jnp.int32, (block, 2 * block), 0)
+    key_at = lax.broadcasted_iota(jnp.int32, (block, 2 * block), 1) - block
+    allowed = (key_at <= query_at) & (key_at >= query_at - pos_col.astype(jnp.int32))
+    keys = jnp.concatenate([turned(before_ref[:, :size], 0), turned(own_ref[:, :size], block)], axis=0)
+    values = jnp.concatenate([before_ref[:, size:], own_ref[:, size:]], axis=0)
+    query = turned(q_ref[...], block)
+    scores = lax.dot_general(
+        query, keys, (((1,), (1,)), ((), ())), preferred_element_type=jnp.float32
+    ) * (1.0 / math.sqrt(size))
+    raw = jnp.where(allowed, jnp.exp(scores), 0.0)
+    weights = (raw / jnp.sum(raw, axis=1, keepdims=True)).astype(jnp.bfloat16)
+    mixed[...] = jnp.dot(weights, values, preferred_element_type=jnp.float32).astype(jnp.bfloat16)
+    picked = [
+        mixed[pl.ds(pl.multiple_of((index_ref[0] ^ owner) * rows, 16), rows), :] for owner in order
+    ]
+    term = jnp.dot(
+        jnp.concatenate(picked, axis=0), weight_ref[...], preferred_element_type=jnp.float32
+    ).astype(jnp.bfloat16)
+    for i, output in enumerate(outputs):
+        output[...] = term[i * rows : (i + 1) * rows]
+
+
+def router_kernel(heads, index_ref, *refs):
+    terms, refs = refs[:heads], refs[heads:]
+    hidden_ref, gain_ref, router_ref, routes_ref, rollout_ref = refs[:5]
+    attended_ref, payload_ref, kl_ref = refs[5:]
     width = hidden_ref.shape[1]
     experts, rows = rollout_ref.shape
-    total = hidden_ref[...].astype(jnp.float32)
-    for part, h in zip(parts, order):
-        total = total + jnp.dot(
-            heads_ref[index_ref[0] ^ h], part[...], preferred_element_type=jnp.float32
-        )
+    total = sum(term[...].astype(jnp.float32) for term in terms) + hidden_ref[...].astype(jnp.float32)
     attended = total.astype(jnp.bfloat16)
     attended_ref[...] = attended
     wide = attended.astype(jnp.float32)
@@ -280,6 +274,7 @@
 
 
 HBM = pl.BlockSpec(memory_space=pltpu.HBM)
+GRANT = 60 * 1024 * 1024
 
 
 def fetching(kernel, count, stored, index_ref, *refs):
@@ -324,57 +319,109 @@
             pltpu.SemaphoreType.DMA((max(1, len(sent)),)),
             *scratch,
         ],
-        compiler_params=pltpu.CompilerParams(vmem_limit_bytes=16 * 1024 * 1024),
-        cost_estimate=pl.CostEstimate(flops=flops, bytes_accessed=1 << 20, transcendentals=0),
+        compiler_params=pltpu.CompilerParams(vmem_limit_bytes=GRANT),
+        cost_estimate=pl.CostEstimate(flops=0, bytes_accessed=0, transcendentals=0),
     )(*inputs)
 
 
-def expert_kernel(parts, width, index_ref, *refs):
-    token_refs, refs = refs[:parts], refs[parts:]
-    own_in, other_in, own_out, other_out, keep_ref, send_ref, tokens, arrived = refs
-    rows = token_refs[0].shape[0]
-    lanes = token_refs[0].shape[1] - width
+def fetched(sources, targets, arrived):
     copies = [
-        pltpu.make_async_copy(ref, tokens.at[pl.ds(p * rows, rows), :], arrived.at[p])
-        for p, ref in enumerate(token_refs)
+        pltpu.make_async_copy(source, target, arrived.at[i])
+        for i, (source, target) in enumerate(zip(sources, targets))
     ]
     for copy in copies:
         copy.start()
+    return copies
+
+
+def hidden_kernel(width, *refs):
+    parts = len(refs) - 8
+    sources, refs = refs[: parts + 2], refs[parts + 2 :]
+    inner_ref, spare_ref, own, other, tokens, arrived = refs
+    rows = sources[2].shape[0]
+    targets = [own, other] + [tokens.at[pl.ds(p * rows, rows), :] for p in range(parts)]
+    copies = fetched(sources, targets, arrived)
+    for copy in copies[:1] + copies[2:]:
+        copy.wait()
+    half = own.shape[1] // 2
+    inner_ref[:, :half] = activate(
+        jnp.dot(tokens[:, :width], own[...], preferred_element_type=jnp.float32)
+    )
+    spare_ref[...] = tokens[:, width:]
+    copies[1].wait()
+    inner_ref[:, half:] = activate(
+        jnp.dot(tokens[:, :width], other[...], preferred_element_type=jnp.float32)
+    )
+
+
+def hidden_blocks(tokens, own_in, other_in):
+    width, inner = own_in.shape
+    rows, total = tokens[0].shape
+    parts = len(tokens)
+    return pl.pallas_call(
+        functools.partial(hidden_kernel, width),
+        out_shape=(
+            jax.ShapeDtypeStruct((parts * rows, inner), jnp.bfloat16),
+            jax.ShapeDtypeStruct((parts * rows, total - width), jnp.bfloat16),
+        ),
+        in_specs=[HBM] * (parts + 2),
+        out_specs=(VMEM, VMEM),
+        scratch_shapes=[
+            pltpu.VMEM(own_in.shape, own_in.dtype),
+            pltpu.VMEM(own_in.shape, own_in.dtype),
+            pltpu.VMEM((parts * rows, total), jnp.bfloat16),
+            pltpu.SemaphoreType.DMA((parts + 2,)),
+        ],
+        compiler_params=pltpu.CompilerParams(vmem_limit_bytes=GRANT),
+        cost_estimate=pl.CostEstimate(flops=0, bytes_accessed=9 << 20, transcendentals=0),
+    )(own_in, other_in, *tokens)
+
+
+def output_kernel(index_ref, inner_ref, spare_ref, own_ref, other_ref, *refs):
+    outputs, (inner, spare, weight, ready, arrived, left) = refs[:-6], refs[-6:]
+    depth = own_ref.shape[0]
+    targets = [weight.at[pl.ds(0, depth), :], weight.at[pl.ds(depth, depth), :], inner, spare]
+    for copy in fetched([own_ref, other_ref, inner_ref, spare_ref], targets, arrived):
+        copy.wait()
+    part = outputs[0].shape[0]
+    step = 4 * part
+    copies = []
+    for start in reversed(range(0, inner.shape[0], step)):
+        block = slice(start, start + step)
+        chosen = spare[block, :].astype(jnp.float32)
+        picked = lax.broadcasted_iota(jnp.int32, chosen.shape, 1) == index_ref[0]
+        gate = jnp.sum(jnp.where(picked, chosen, 0.0), axis=1, keepdims=True)
+        out = jnp.dot(inner[block, :], weight[...], preferred_element_type=jnp.float32)
+        ready[block, :] = (out * gate).astype(jnp.bfloat16)
+        for i in reversed(range(start // part, (start + step) // part)):
+            source = ready.at[pl.ds(i * part, part), :]
+            copies.append(pltpu.make_async_copy(source, outputs[i], left.at[i]))
+            copies[-1].start()
     for copy in copies:
         copy.wait()
-    picked = lax.broadcasted_iota(jnp.int32, (parts * rows, lanes), 1) == index_ref[0]
-    gate = jnp.sum(
-        jnp.where(picked, tokens[:, width:].astype(jnp.float32), 0.0), axis=1, keepdims=True
-    )
-    own = jnp.dot(tokens[:, :width], own_in[...], preferred_element_type=jnp.float32)
-    other = jnp.dot(tokens[:, :width], other_in[...], preferred_element_type=jnp.float32)
-    out = jnp.dot(activate(own), own_out[...], preferred_element_type=jnp.float32) + jnp.dot(
-        activate(other), other_out[...], preferred_element_type=jnp.float32
-    )
-    out = (out * gate).astype(jnp.bfloat16)
-    half = keep_ref.shape[0]
-    keep_ref[...] = out[:half]
-    send_ref[...] = out[half:]
-
-
-def expert_block(index, tokens, own_in, own_out, other_in, other_out, width):
-    parts = len(tokens)
-    rows = parts * tokens[0].shape[0]
-    half = jax.ShapeDtypeStruct((rows // 2, width), jnp.bfloat16)
-    return pl.pallas_call(
-        functools.partial(expert_kernel, parts, width),
-        out_shape=(half, half),
-        in_specs=[SMEM] + [HBM] * parts + [VMEM] * 4,
-        out_specs=(VMEM, VMEM),
+
+
+def output_blocks(count, index, inner, spare, own_out, other_out):
+    width = own_out.shape[1]
+    rows = inner.shape[0]
+    half = jax.ShapeDtypeStruct((rows // count // 2, width), jnp.bfloat16)
+    flat = pl.pallas_call(
+        output_kernel,
+        out_shape=(half,) * (2 * count),
+        in_specs=[SMEM] + [HBM] * 4,
+        out_specs=(HBM,) * (2 * count),
         scratch_shapes=[
-            pltpu.VMEM((rows, tokens[0].shape[1]), jnp.bfloat16),
-            pltpu.SemaphoreType.DMA((parts,)),
+            pltpu.VMEM(inner.shape, inner.dtype),
+            pltpu.VMEM(spare.shape, spare.dtype),
+            pltpu.VMEM((inner.shape[1], width), jnp.bfloat16),
+            pltpu.VMEM((rows, width), jnp.bfloat16),
+            pltpu.SemaphoreType.DMA((4,)),
+            pltpu.SemaphoreType.DMA((2 * count,)),
         ],
-        compiler_params=pltpu.CompilerParams(vmem_limit_bytes=16 * 1024 * 1024),
-        cost_estimate=pl.CostEstimate(
-            flops=2 * rows * 3 * width * own_in.shape[1], bytes_accessed=8 << 20, transcendentals=0
-        ),
-    )(index, *tokens, own_in, other_in, own_out, other_out)
+        compiler_params=pltpu.CompilerParams(vmem_limit_bytes=GRANT),
+        cost_estimate=pl.CostEstimate(flops=0, bytes_accessed=0, transcendentals=0),
+    )(index, inner, spare, own_out, other_out)
+    return [flat[2 * k : 2 * k + 2] for k in range(count)]
 
 
 def dense_body(
@@ -410,75 +457,90 @@
 
     weight_in = expert_in[0, 0]
     weight_out = expert_out[0, 0]
-    before = passed_along(jnp.concatenate([keys, values], axis=1), "ctx", 1)
-    query_rows = lax.all_to_all(queries, "exp", split_axis=0, concat_axis=1, tiled=True)
-    before, weight_in, weight_out = lax.optimization_barrier((before, weight_in, weight_out))
-    other_out = swapped(weight_out, "ctx", 1)
-    other_in = swapped(weight_in, "ctx", 1)
+    kv_group = exp_index // share
+    kv_own = jnp.concatenate(
+        [lax.dynamic_slice_in_dim(array, kv_group * head_dim, head_dim, 1) for array in (keys, values)],
+        axis=1,
+    )
+    before = passed_along(kv_own, "ctx", 1)
+    before, weight_in_sent, weight_out_sent = lax.optimization_barrier((before, weight_in, weight_out))
+    other_out = swapped(weight_out_sent, "ctx", 1)
+    other_in = swapped(weight_in_sent, "ctx", 1)
 
     index = exp_index.reshape(1).astype(jnp.int32)
-    spectrum = np.float32(theta) ** (-np.arange(head_dim // 2, dtype=np.float32) * 2.0 / head_dim)
-    spectrum = jnp.asarray(np.concatenate([spectrum, spectrum])[None, :].astype(np.float32))
+    owners = [0]
+    for bit in bits:
+        owners = owners + [owner ^ bit for owner in owners]
     table = pltpu.VMEM((2 * block_rows, head_dim), jnp.float32)
-    (head_out,) = small_kernel(
-        functools.partial(attention_kernel, exp_count // kv_heads),
-        (jax.ShapeDtypeStruct((exp_count, token_rows, head_dim), jnp.bfloat16),),
-        (index, spectrum, positions[None, :], query_rows, before, keys, values),
-        (True,),
-        (table, table, pltpu.VMEM((block_rows, 1), jnp.float32)),
-        8 * block_rows * token_rows * queries.shape[1],
-    )
-    out_parts, head_order = [out_weight], [0]
-    for bit in bits[:-1]:
-        out_parts = out_parts + [swapped(part, "exp", bit) for part in out_parts]
-        head_order = head_order + [h ^ bit for h in head_order]
-    head_out, *late = lax.optimization_barrier((head_out, *out_parts[1:]))
-    out_parts = out_parts[:1] + late
-    out_parts = out_parts + [swapped(part, "exp", bits[-1]) for part in out_parts]
-    head_order = head_order + [h ^ bits[-1] for h in head_order]
+    term = jax.ShapeDtypeStruct((token_rows, width), jnp.bfloat16)
+    terms = small_kernel(
+        functools.partial(attention_kernel, tuple(owners)),
+        (term,) * exp_count,
+        (index, positions[None, :], queries, before, kv_own, out_weight),
+        (True,) * exp_count,
+        (table, table, pltpu.VMEM((block_rows, head_dim), jnp.bfloat16)),
+        0,
+    )
+    terms = [terms[0]] + [swapped(term, "exp", owner) for term, owner in zip(terms[1:], owners[1:])]
     lanes = -(-experts_total // 128) * 128
     attended, payload, router_kl = small_kernel(
-        functools.partial(router_kernel, tuple(head_order)),
+        functools.partial(router_kernel, exp_count),
         (
             jax.ShapeDtypeStruct((token_rows, width), jnp.bfloat16),
             jax.ShapeDtypeStruct((token_rows, width + lanes), jnp.bfloat16),
             jax.ShapeDtypeStruct((1, token_rows), jnp.float32),
         ),
-        (index, head_out, *out_parts, hidden, ffn_gain[None, :], router_weight.T, routes.T, rollout_logits.T),
+        (
+            index,
+            *terms,
+            hidden,
+            ffn_gain[None, :],
+            router_weight.T,
+            routes.T,
+            rollout_logits.T,
+        ),
         (False, True, False),
         (),
-        2 * token_rows * width * out_weight.shape[0] * exp_count,
+        2 * token_rows * width * experts_total,
     )
     router_kl = router_kl[0]
-    blocks = [payload] + [swapped(payload, "ctx", 2 * k) for k in range(1, per_column)]
-    gathered, passed = [], None
-    for block in blocks:
+    blocks, sent = [payload], payload
+    for k in range(1, per_column):
+        if k > 2:
+            blocks[-1], sent = lax.optimization_barrier((blocks[-1], payload))
+        blocks.append(swapped(sent, "ctx", 2 * k))
+    crossed = []
+    for turn, block in enumerate(blocks):
         parts = [block]
-        for bit in bits:
-            if passed is not None and bit != bits[-1]:
-                passed, *parts = lax.optimization_barrier((passed, *parts))
-                gathered[-1][1] = passed
+        for bit in bits[:-1]:
+            if turn > 0:
+                crossed[turn - 1][-1], *parts = lax.optimization_barrier((crossed[turn - 1][-1], *parts))
             parts = parts + [swapped(part, "exp", bit) for part in parts]
-            if bit == bits[0]:
-                passed = parts[-1]
-        gathered.append(parts)
+        crossed.append(parts)
     expert_index = (exp_index * per_column + ctx_index // 2).reshape(1).astype(jnp.int32)
-    returned, passed = {}, None
-    for k in sorted(range(per_column), key=lambda k: -min(k, 2.5)):
-        keep, send = expert_block(
-            expert_index, gathered[k], weight_in, weight_out, other_in, other_out, width
-        )
+    groups, pairs, tokens = 1, [], []
+    for turn, parts in enumerate(crossed):
+        stack = jnp.concatenate(parts, axis=0)
+        tokens = tokens + [stack, swapped(stack, "exp", bits[-1])]
+        if (turn + 1) % (per_column // groups) == 0:
+            pairs.append(hidden_blocks(tokens, weight_in, other_in))
+            tokens = []
+    inner, spare = pairs[0]
+    inner, other_out = lax.optimization_barrier((inner, other_out))
+    partials = output_blocks(per_column, expert_index, inner, spare, weight_out, other_out)
+    returned = {}
+    for k in reversed(range(per_column)):
+        keep, send = partials[k]
         for bit in reversed(bits):
-            if passed is not None and bit == bits[0]:
-                passed, send = lax.optimization_barrier((passed, send))
+            if bit == bits[0] and k == 0:
+                send, returned[2] = lax.optimization_barrier((send, returned[2]))
             received = swapped(send, "exp", bit)
-            if bit == bits[0]:
-                passed = received
             total = keep.astype(jnp.float32) + received.astype(jnp.float32)
             total = total.astype(jnp.bfloat16)
-            half = total.shape[0] // 2
-            keep, send = total[:half], total[half:]
-        returned[k] = total if k == 0 else swapped(total, "ctx", 2 * k)
+            middle = total.shape[0] // 2
+            keep, send = total[:middle], total[middle:]
+        returned[k] = total
+    returned = {k: total if k == 0 else swapped(total, "ctx", 2 * k) for k, total in returned.items()}
     moe_out = sum(returned[k].astype(jnp.float32) for k in range(per_column))
     layer_out = (attended.astype(jnp.float32) + moe_out).astype(jnp.bfloat16)
     return (layer_out, router_kl)

time: 118 us -> 110 us (0.932)
  local copies, waits for them, and re-layouts: 14.5 us -> 5.67 us
  starting transfers between devices: 42.5 us -> 39.7 us
  waiting for transfers between devices: 39.1 us -> 41.1 us
  Pallas kernels: 17.6 us -> 19.3 us
    unnamed x44 -> x34, local copies, waits for them, and re-layouts: 14.4 us -> 4.69 us
    ppermute x31 -> x27, waiting for transfers between devices: 31.7 us -> 38.9 us  [swapped(): lax.ppermute(value, axis, [(source, source ^ mask) for source in range(co...]
    all_to_all x1 -> x0, waiting for transfers between devices: 3.53 us -> none  [dense_body(): lax.all_to_all(queries, 'exp', split_axis=0, concat_axis=1, tiled=True)]
    all_to_all x1 -> x0, starting transfers between devices: 3.41 us -> none  [dense_body(): lax.all_to_all(queries, 'exp', split_axis=0, concat_axis=1, tiled=True)]
    ppermute x1, waiting for transfers between devices: 3.85 us -> 2.19 us  [passed_along(): lax.ppermute(value, axis, [(source, source + steps) for source in range(i...]
    ppermute x1, starting transfers between devices: 3.44 us -> 4.88 us  [passed_along(): lax.ppermute(value, axis, [(source, source + steps) for source in range(i...]
    pallas_call x4 -> x2, Pallas kernels: 11.4 us -> 12.2 us  [the longest x1 7.6 us: hidden_blocks(): pl.pallas_call(functools.partial(hidden_kernel, width), out_shape=(jax.Sh...]
    ppermute x31 -> x27, starting transfers between devices: 35.7 us -> 34.8 us  [swapped(): lax.ppermute(value, axis, [(source, source ^ mask) for source in range(co...]
  transfers between devices with their start and end apart: 33 -> 28, of which waited for: 15 -> 17; matrix products, arithmetic and copies ran while one was open for 1% -> 3% of each run, Pallas kernels for 15% -> 10%
where the time goes in v4:
time: 110 us; the launch traced here: 109 us
  waiting for transfers between devices  41.1 us (37%)
  starting transfers between devices  39.7 us (36%)
  Pallas kernels  19.3 us (18%)
  local copies, waits for them, and re-layouts  5.67 us (5%)
  other arithmetic  2.42 us (2%)
    ppermute x27, waiting for transfers between devices, swapped(): lax.ppermute(value, axis, [(source, source ^ mask) for source in range(co...  38.9 us
    ppermute x27, starting transfers between devices, swapped(): lax.ppermute(value, axis, [(source, source ^ mask) for source in range(co...  34.8 us
    pallas_call x1, Pallas kernels, hidden_blocks(): pl.pallas_call(functools.partial(hidden_kernel, width), out_shape=(jax.Sh...  7.6 us
    pallas_call x2, Pallas kernels, small_kernel(): pl.pallas_call(functools.partial(fetching, kernel, len(held), stored), ou...  7.08 us
    ppermute x1, starting transfers between devices, passed_along(): lax.ppermute(value, axis, [(source, source + steps) for source in range(i...  4.88 us
    unnamed x34, local copies, waits for them, and re-layouts  4.69 us
    pallas_call x1, Pallas kernels, output_blocks(): pl.pallas_call(output_kernel, out_shape=(half,) * (2 * count), in_specs=[...  4.65 us
  transfers between devices with their start and end apart: 28, of which 17 were waited for; matrix products, arithmetic and copies ran while one was open for 3% of the time, Pallas kernels for 10%

profile of v4, /device:TPU:0, one launch (start us, length us, event | category | flops | bytes accessed | tf_op | source)
XLA Modules:
  0.0 109.2 jit_solution(737707302798235447)
XLA Ops:
  1.5 4.9 %collective-permute-start = (bf16[192,256]{1,0:T(8,128)(2,1)S(1)}, bf16[192,256]{1,0:T(8,128)(2,1)S(1)}, u32[]{:S(2)}, u32[]{:S(2)}) collective-permute-start(bf16[192,256]{1,0:T(8,128)(2,1)S(1)} %pad_maximum_fusion.refs_3_), channel_id=1, source_target_pairs={{0,4},{4,8},{8,12},{12,16},{16,20},{20,24},{24,28},{1,5},{5,9},{9,... | collective-permute-start | bytes 294920 | tf_op jit(solution)/shard_map/ppermute | solution.py:19
  6.4 2.2 %collective-permute-done.refs_2_ = bf16[192,256]{1,0:T(8,128)(2,1)S(1)} collective-permute-done((bf16[192,256]{1,0:T(8,128)(2,1)S(1)}, bf16[192,256]{1,0:T(8,128)(2,1)S(1)}, u32[]{:S(2)}, u32[]{:S(2)}) %collective-permute-start) | collective-permute-done | bytes 98336 | tf_op jit(solution)/shard_map/ppermute | solution.py:19
  9.2 3.7 %shard_map.131 = (bf16[48,2048]{1,0:T(8,128)(2,1)}, bf16[48,2048]{1,0:T(8,128)(2,1)}, bf16[48,2048]{1,0:T(8,128)(2,1)}, bf16[48,2048]{1,0:T(8,128)(2,1)}) custom-call(s32[1]{0:T(128)} %bitcast.index_ref, s32[1,192]{1,0:T(1,128)} %bitcast.18, bf16[192,128]{1,0:T(8,128)(2,1)} %refs_1_.1, bf16[192,256]{1,0:T(8,128)(2,1)} %copy-done.14, ...), custom_call_target="tpu_custom_call" | custom-call | tf_op jit(solution)/shard_map/pallas_call | solution.py:310
  13.0 1.6 %collective-permute-start.1 = (bf16[48,2048]{1,0:T(8,128)(2,1)}, bf16[48,2048]{1,0:T(8,128)(2,1)S(1)}, u32[]{:S(2)}, u32[]{:S(2)}) collective-permute-start(bf16[48,2048]{1,0:T(8,128)(2,1)} %get-tuple-element.36), channel_id=1, source_target_pairs={{0,2},{1,3},{2,0},{3,1},{4,6},{5,7},{6,4},{7,5},{8,10},{9,11},{10,... | collective-permute-start | bytes 589832 | tf_op jit(solution)/shard_map/ppermute | solution.py:182
  15.2 2.4 %collective-permute-start.4 = (bf16[2048,384]{1,0:T(8,128)(2,1)}, bf16[2048,384]{1,0:T(8,128)(2,1)S(1)}, u32[]{:S(2)}, u32[]{:S(2)}) collective-permute-start(bf16[2048,384]{1,0:T(8,128)(2,1)} %bitcast.10), channel_id=1, source_target_pairs={{0,4},{4,0},{8,12},{12,8},{16,20},{20,16},{24,28},{28,24},{1,5},{5... | collective-permute-start | bytes 4718600 | tf_op jit(solution)/shard_map/ppermute | solution.py:182
  17.6 2.8 %collective-permute-done.1.refs_1_ = bf16[48,2048]{1,0:T(8,128)(2,1)S(1)} collective-permute-done((bf16[48,2048]{1,0:T(8,128)(2,1)}, bf16[48,2048]{1,0:T(8,128)(2,1)S(1)}, u32[]{:S(2)}, u32[]{:S(2)}) %collective-permute-start.1) | collective-permute-done | bytes 196640 | tf_op jit(solution)/shard_map/ppermute | solution.py:182
  20.4 2.0 %collective-permute-done.3.refs_3_ = bf16[48,2048]{1,0:T(8,128)(2,1)S(1)} collective-permute-done((bf16[48,2048]{1,0:T(8,128)(2,1)}, bf16[48,2048]{1,0:T(8,128)(2,1)S(1)}, u32[]{:S(2)}, u32[]{:S(2)}) %collective-permute-start.3) | collective-permute-done | bytes 196640 | tf_op jit(solution)/shard_map/ppermute | solution.py:182
  23.0 3.3 %shard_map.132 = (bf16[48,2048]{1,0:T(8,128)(2,1)}, bf16[48,2176]{1,0:T(8,128)(2,1)}, f32[1,48]{1,0:T(1,128)}) custom-call(s32[1]{0:T(128)} %bitcast.index_ref, bf16[48,2048]{1,0:T(8,128)(2,1)} %get-tuple-element.35.refs_0_, bf16[48,2048]{1,0:T(8,128)(2,1)} %copy-done.11, bf16[48,2048]{1,0:T(8,128)(2,1)} %copy-done.12, bf16[48,2048]{1,0:T(8,128)(2,1)} %copy-done.13, ...), custom_call_target="tpu_custom_call" | custom-call | tf_op jit(solution)/shard_map/pallas_call | solution.py:310
  27.0 3.2 %collective-permute-start.6 = (bf16[48,2176]{1,0:T(8,128)(2,1)}, bf16[48,2176]{1,0:T(8,128)(2,1)S(1)}, u32[]{:S(2)}, u32[]{:S(2)}) collective-permute-start(bf16[48,2176]{1,0:T(8,128)(2,1)} %get-tuple-element.47), channel_id=1, source_target_pairs={{0,8},{4,12},{8,0},{12,4},{16,24},{20,28},{24,16},{28,20},{1,9},{5... | collective-permute-start | bytes 626696 | tf_op jit(solution)/shard_map/ppermute | solution.py:182
  30.2 2.6 %collective-permute-start.9 = (bf16[48,2176]{1,0:T(8,128)(2,1)}, bf16[48,2176]{1,0:T(8,128)(2,1)S(1)}, u32[]{:S(2)}, u32[]{:S(2)}) collective-permute-start(bf16[48,2176]{1,0:T(8,128)(2,1)} %get-tuple-element.47), channel_id=1, source_target_pairs={{0,16},{4,20},{8,24},{12,28},{16,0},{20,4},{24,8},{28,12},{1,17},{... | collective-permute-start | bytes 626696 | tf_op jit(solution)/shard_map/ppermute | solution.py:182
  34.7 4.8 %collective-permute-done.6 = bf16[48,2176]{1,0:T(8,128)(2,1)S(1)} collective-permute-done((bf16[48,2176]{1,0:T(8,128)(2,1)}, bf16[48,2176]{1,0:T(8,128)(2,1)S(1)}, u32[]{:S(2)}, u32[]{:S(2)}) %collective-permute-start.6) | collective-permute-done | bytes 208928 | tf_op jit(solution)/shard_map/ppermute | solution.py:182
  39.5 1.3 %collective-permute-start.7 = (bf16[96,2176]{1,0:T(8,128)(2,1)S(1)}, bf16[96,2176]{1,0:T(8,128)(2,1)S(1)}, u32[]{:S(2)}, u32[]{:S(2)}) collective-permute-start(bf16[96,2176]{1,0:T(8,128)(2,1)S(1)} %constant_dynamic-update-slice_fusion.refs_2_), channel_id=1, source_target_pairs={{0,1},{1,0},{2,3},{3,2},{4,5},{5,4},{6,7},{7,6},{8,9},{9,8},{10,11... | collective-permute-start | bytes 1253384 | tf_op jit(solution)/shard_map/ppermute | solution.py:182
  40.8 1.7 %collective-permute-start.8 = (bf16[48,2176]{1,0:T(8,128)(2,1)S(1)}, bf16[48,2176]{1,0:T(8,128)(2,1)S(1)}, u32[]{:S(2)}, u32[]{:S(2)}) collective-permute-start(bf16[48,2176]{1,0:T(8,128)(2,1)S(1)} %collective-permute-done.6), channel_id=1, source_target_pairs={{0,2},{1,3},{2,0},{3,1},{4,6},{5,7},{6,4},{7,5},{8,10},{9,11},{10,... | collective-permute-start | bytes 626696 | tf_op jit(solution)/shard_map/ppermute | solution.py:182
  43.6 2.5 %collective-permute-start.12 = (bf16[48,2176]{1,0:T(8,128)(2,1)}, bf16[48,2176]{1,0:T(8,128)(2,1)S(1)}, u32[]{:S(2)}, u32[]{:S(2)}) collective-permute-start(bf16[48,2176]{1,0:T(8,128)(2,1)} %get-tuple-element.47), channel_id=1, source_target_pairs={{0,24},{4,28},{8,16},{12,20},{16,8},{20,12},{24,0},{28,4},{1,25},{... | collective-permute-start | bytes 626696 | tf_op jit(solution)/shard_map/ppermute | solution.py:182
  46.1 2.1 %collective-permute-done.8 = bf16[48,2176]{1,0:T(8,128)(2,1)S(1)} collective-permute-done((bf16[48,2176]{1,0:T(8,128)(2,1)S(1)}, bf16[48,2176]{1,0:T(8,128)(2,1)S(1)}, u32[]{:S(2)}, u32[]{:S(2)}) %collective-permute-start.8) | collective-permute-done | bytes 208928 | tf_op jit(solution)/shard_map/ppermute | solution.py:182
  48.2 1.8 %collective-permute-start.11 = (bf16[48,2176]{1,0:T(8,128)(2,1)S(1)}, bf16[48,2176]{1,0:T(8,128)(2,1)S(1)}, u32[]{:S(2)}, u32[]{:S(2)}) collective-permute-start(bf16[48,2176]{1,0:T(8,128)(2,1)S(1)} %collective-permute-done.9), channel_id=1, source_target_pairs={{0,2},{1,3},{2,0},{3,1},{4,6},{5,7},{6,4},{7,5},{8,10},{9,11},{10,... | collective-permute-start | bytes 626696 | tf_op jit(solution)/shard_map/ppermute | solution.py:182
  50.0 2.9 %collective-permute-done.12 = bf16[48,2176]{1,0:T(8,128)(2,1)S(1)} collective-permute-done((bf16[48,2176]{1,0:T(8,128)(2,1)}, bf16[48,2176]{1,0:T(8,128)(2,1)S(1)}, u32[]{:S(2)}, u32[]{:S(2)}) %collective-permute-start.12) | collective-permute-done | bytes 208928 | tf_op jit(solution)/shard_map/ppermute | solution.py:182
  52.9 1.9 %collective-permute-done.11 = bf16[48,2176]{1,0:T(8,128)(2,1)S(1)} collective-permute-done((bf16[48,2176]{1,0:T(8,128)(2,1)S(1)}, bf16[48,2176]{1,0:T(8,128)(2,1)S(1)}, u32[]{:S(2)}, u32[]{:S(2)}) %collective-permute-start.11) | collective-permute-done | bytes 208928 | tf_op jit(solution)/shard_map/ppermute | solution.py:182
  54.8 1.7 %collective-permute-start.14 = (bf16[48,2176]{1,0:T(8,128)(2,1)S(1)}, bf16[48,2176]{1,0:T(8,128)(2,1)S(1)}, u32[]{:S(2)}, u32[]{:S(2)}) collective-permute-start(bf16[48,2176]{1,0:T(8,128)(2,1)S(1)} %collective-permute-done.12), channel_id=1, source_target_pairs={{0,2},{1,3},{2,0},{3,1},{4,6},{5,7},{6,4},{7,5},{8,10},{9,11},{10,... | collective-permute-start | bytes 626696 | tf_op jit(solution)/shard_map/ppermute | solution.py:182
  56.6 4.0 %collective-permute-done.14 = bf16[48,2176]{1,0:T(8,128)(2,1)S(1)} collective-permute-done((bf16[48,2176]{1,0:T(8,128)(2,1)S(1)}, bf16[48,2176]{1,0:T(8,128)(2,1)S(1)}, u32[]{:S(2)}, u32[]{:S(2)}) %collective-permute-start.14) | collective-permute-done | bytes 208928 | tf_op jit(solution)/shard_map/ppermute | solution.py:182
  63.5 1.2 %copy-done = bf16[2048,384]{1,0:T(8,128)(2,1)} copy-done((bf16[2048,384]{1,0:T(8,128)(2,1)}, bf16[2048,384]{1,0:T(8,128)(2,1)S(1)}, u32[]{:S(2)}) %copy-start) | copy-done | bytes 1572888
  64.7 7.6 %shard_map.133 = (bf16[768,384]{1,0:T(8,128)(2,1)}, bf16[768,128]{1,0:T(8,128)(2,1)}) custom-call(bf16[2048,384]{1,0:T(8,128)(2,1)} %bitcast.11, bf16[2048,384]{1,0:T(8,128)(2,1)} %copy-done, bf16[96,2176]{1,0:T(8,128)(2,1)} %copy-done.4, bf16[96,2176]{1,0:T(8,128)(2,1)} %copy-done.5, bf16[96,2176]{1,0:T(8,128)(2,1)} %copy-done.3, ...), custom_call_target="tpu_custom_call" | custom-call | bytes 9437184 | tf_op jit(solution)/shard_map/pallas_call | solution.py:361
  72.3 4.6 %shard_map.134 = (bf16[96,2048]{1,0:T(8,128)(2,1)}, bf16[96,2048]{1,0:T(8,128)(2,1)}, bf16[96,2048]{1,0:T(8,128)(2,1)}, bf16[96,2048]{1,0:T(8,128)(2,1)}, bf16[9...) custom-call(s32[1]{0:T(128)} %bitcast.8.index_ref, ...), custom_call_target="tpu_custom_call" | custom-call | tf_op jit(solution)/shard_map/pallas_call | solution.py:408
  79.0 1.1 %add_convert_fusion = bf16[96,2048]{1,0:T(8,128)(2,1)S(1)} fusion(bf16[96,2048]{1,0:T(8,128)(2,1)S(1)} %collective-permute-done.25, bf16[96,2048]{1,0:T(8,128)(2,1)} %get-tuple-element.63), kind=kLoop, calls=%fused_computation | loop fusion | flops 786432 | bytes 1179648 | tf_op jit(solution)/shard_map/convert_element_type | solution.py:539
  80.1 1.8 %collective-permute-start.26 = (bf16[48,2048]{1,0:T(8,128)(2,1)S(1)}, bf16[48,2048]{1,0:T(8,128)(2,1)S(1)}, u32[]{:S(2)}, u32[]{:S(2)}) collective-permute-start(bf16[48,2048]{1,0:T(8,128)(2,1)S(1)} %slice.39), channel_id=1, source_target_pairs={{0,2},{1,3},{2,0},{3,1},{4,6},{5,7},{6,4},{7,5},{8,10},{9,11},{10,... | collective-permute-start | bytes 589832 | tf_op jit(solution)/shard_map/ppermute | solution.py:182
  83.1 1.4 %collective-permute-start.22 = (bf16[48,2048]{1,0:T(8,128)(2,1)S(1)}, bf16[48,2048]{1,0:T(8,128)(2,1)S(1)}, u32[]{:S(2)}, u32[]{:S(2)}) collective-permute-start(bf16[48,2048]{1,0:T(8,128)(2,1)S(1)} %slice.37), channel_id=1, source_target_pairs={{0,2},{1,3},{2,0},{3,1},{4,6},{5,7},{6,4},{7,5},{8,10},{9,11},{10,... | collective-permute-start | bytes 589832 | tf_op jit(solution)/shard_map/ppermute | solution.py:182
  84.5 3.4 %collective-permute-done.26 = bf16[48,2048]{1,0:T(8,128)(2,1)S(1)} collective-permute-done((bf16[48,2048]{1,0:T(8,128)(2,1)S(1)}, bf16[48,2048]{1,0:T(8,128)(2,1)S(1)}, u32[]{:S(2)}, u32[]{:S(2)}) %collective-permute-start.26) | collective-permute-done | bytes 196640 | tf_op jit(solution)/shard_map/ppermute | solution.py:182
  88.0 3.0 %collective-permute-start.27 = (bf16[48,2048]{1,0:T(8,128)(2,1)S(1)}, bf16[48,2048]{1,0:T(8,128)(2,1)S(1)}, u32[]{:S(2)}, u32[]{:S(2)}) collective-permute-start(bf16[48,2048]{1,0:T(8,128)(2,1)S(1)} %add_convert_fusion.5), channel_id=1, source_target_pairs={{0,24},{4,28},{8,16},{12,20},{16,8},{20,12},{24,0},{28,4},{1,25},{... | collective-permute-start | bytes 589832 | tf_op jit(solution)/shard_map/ppermute | solution.py:182
  92.2 2.6 %collective-permute-start.24 = (bf16[48,2048]{1,0:T(8,128)(2,1)S(1)}, bf16[48,2048]{1,0:T(8,128)(2,1)S(1)}, u32[]{:S(2)}, u32[]{:S(2)}) collective-permute-start(bf16[48,2048]{1,0:T(8,128)(2,1)S(1)} %add_convert_fusion.8), channel_id=1, source_target_pairs={{0,16},{4,20},{8,24},{12,28},{16,0},{20,4},{24,8},{28,12},{1,17},{... | collective-permute-start | bytes 589832 | tf_op jit(solution)/shard_map/ppermute | solution.py:182
  95.9 2.7 %collective-permute-start.23 = (bf16[48,2048]{1,0:T(8,128)(2,1)S(1)}, bf16[48,2048]{1,0:T(8,128)(2,1)S(1)}, u32[]{:S(2)}, u32[]{:S(2)}) collective-permute-start(bf16[48,2048]{1,0:T(8,128)(2,1)S(1)} %add_convert_fusion.6), channel_id=1, source_target_pairs={{0,8},{4,12},{8,0},{12,4},{16,24},{20,28},{24,16},{28,20},{1,9},{5... | collective-permute-start | bytes 589832 | tf_op jit(solution)/shard_map/ppermute | solution.py:182
  98.5 1.3 %collective-permute-start.20 = (bf16[48,2048]{1,0:T(8,128)(2,1)S(1)}, bf16[48,2048]{1,0:T(8,128)(2,1)S(1)}, u32[]{:S(2)}, u32[]{:S(2)}) collective-permute-start(bf16[48,2048]{1,0:T(8,128)(2,1)S(1)} %slice.33), channel_id=1, source_target_pairs={{0,2},{1,3},{2,0},{3,1},{4,6},{5,7},{6,4},{7,5},{8,10},{9,11},{10,... | collective-permute-start | bytes 589832 | tf_op jit(solution)/shard_map/ppermute | solution.py:182
  99.8 8.5 %collective-permute-done.24 = bf16[48,2048]{1,0:T(8,128)(2,1)S(1)} collective-permute-done((bf16[48,2048]{1,0:T(8,128)(2,1)S(1)}, bf16[48,2048]{1,0:T(8,128)(2,1)S(1)}, u32[]{:S(2)}, u32[]{:S(2)}) %collective-permute-start.24) | collective-permute-done | bytes 196640 | tf_op jit(solution)/shard_map/ppermute | solution.py:182
  (80 shorter events, 15.6 us)
Async XLA Ops:
  1.5 7.1 %copy-start.9 = (bf16[192,256]{1,0:T(8,128)(2,1)}, bf16[192,256]{1,0:T(8,128)(2,1)S(1)}, u32[]{:S(2)}) copy-start(bf16[192,256]{1,0:T(8,128)(2,1)S(1)} %pad_maximum_fusion.refs_3_) | copy-start | bytes 294916
  1.5 7.1 %collective-permute-start = (bf16[192,256]{1,0:T(8,128)(2,1)S(1)}, bf16[192,256]{1,0:T(8,128)(2,1)S(1)}, u32[]{:S(2)}, u32[]{:S(2)}) collective-permute-start(bf16[192,256]{1,0:T(8,128)(2,1)S(1)} %pad_maximum_fusion.refs_3_), channel_id=1, source_target_pairs={{0,4},{4,8},{8,12},{12,16},{16,20},{20,24},{24,28},{1,5},{5,9},{9,... | collective-permute-start | bytes 294920 | tf_op jit(solution)/shard_map/ppermute | solution.py:19
  13.0 7.4 %collective-permute-start.1 = (bf16[48,2048]{1,0:T(8,128)(2,1)}, bf16[48,2048]{1,0:T(8,128)(2,1)S(1)}, u32[]{:S(2)}, u32[]{:S(2)}) collective-permute-start(bf16[48,2048]{1,0:T(8,128)(2,1)} %get-tuple-element.36), channel_id=1, source_target_pairs={{0,2},{1,3},{2,0},{3,1},{4,6},{5,7},{6,4},{7,5},{8,10},{9,11},{10,... | collective-permute-start | bytes 589832 | tf_op jit(solution)/shard_map/ppermute | solution.py:182
  14.5 5.8 %collective-permute-start.2 = (bf16[48,2048]{1,0:T(8,128)(2,1)}, bf16[48,2048]{1,0:T(8,128)(2,1)S(1)}, u32[]{:S(2)}, u32[]{:S(2)}) collective-permute-start(bf16[48,2048]{1,0:T(8,128)(2,1)} %get-tuple-element.37), channel_id=1, source_target_pairs={{0,1},{1,0},{2,3},{3,2},{4,5},{5,4},{6,7},{7,6},{8,9},{9,8},{10,11... | collective-permute-start | bytes 589832 | tf_op jit(solution)/shard_map/ppermute | solution.py:182
  14.5 7.8 %collective-permute-start.3 = (bf16[48,2048]{1,0:T(8,128)(2,1)}, bf16[48,2048]{1,0:T(8,128)(2,1)S(1)}, u32[]{:S(2)}, u32[]{:S(2)}) collective-permute-start(bf16[48,2048]{1,0:T(8,128)(2,1)} %get-tuple-element.38), channel_id=1, source_target_pairs={{0,3},{1,2},{2,1},{3,0},{4,7},{5,6},{6,5},{7,4},{8,11},{9,10},{10,... | collective-permute-start | bytes 589832 | tf_op jit(solution)/shard_map/ppermute | solution.py:182
  15.2 48.3 %collective-permute-start.4 = (bf16[2048,384]{1,0:T(8,128)(2,1)}, bf16[2048,384]{1,0:T(8,128)(2,1)S(1)}, u32[]{:S(2)}, u32[]{:S(2)}) collective-permute-start(bf16[2048,384]{1,0:T(8,128)(2,1)} %bitcast.10), channel_id=1, source_target_pairs={{0,4},{4,0},{8,12},{12,8},{16,20},{20,16},{24,28},{28,24},{1,5},{5... | collective-permute-start | bytes 4718600 | tf_op jit(solution)/shard_map/ppermute | solution.py:182
  17.6 54.7 %collective-permute-start.16 = (bf16[192,2048]{1,0:T(8,128)(2,1)}, bf16[192,2048]{1,0:T(8,128)(2,1)}, u32[]{:S(2)}, u32[]{:S(2)}) collective-permute-start(bf16[192,2048]{1,0:T(8,128)(2,1)} %bitcast.12), channel_id=1, source_target_pairs={{0,4},{4,0},{8,12},{12,8},{16,20},{20,16},{24,28},{28,24},{1,5},{5... | collective-permute-start | bytes 2359304 | tf_op jit(solution)/shard_map/ppermute | solution.py:182
  26.4 8.3 %collective-permute-start.5 = (bf16[48,2176]{1,0:T(8,128)(2,1)}, bf16[48,2176]{1,0:T(8,128)(2,1)S(1)}, u32[]{:S(2)}, u32[]{:S(2)}) collective-permute-start(bf16[48,2176]{1,0:T(8,128)(2,1)} %get-tuple-element.47), channel_id=1, source_target_pairs={{0,2},{1,3},{2,0},{3,1},{4,6},{5,7},{6,4},{7,5},{8,10},{9,11},{10,... | collective-permute-start | bytes 626696 | tf_op jit(solution)/shard_map/ppermute | solution.py:182
  27.0 12.5 %collective-permute-start.6 = (bf16[48,2176]{1,0:T(8,128)(2,1)}, bf16[48,2176]{1,0:T(8,128)(2,1)S(1)}, u32[]{:S(2)}, u32[]{:S(2)}) collective-permute-start(bf16[48,2176]{1,0:T(8,128)(2,1)} %get-tuple-element.47), channel_id=1, source_target_pairs={{0,8},{4,12},{8,0},{12,4},{16,24},{20,28},{24,16},{28,20},{1,9},{5... | collective-permute-start | bytes 626696 | tf_op jit(solution)/shard_map/ppermute | solution.py:182
  30.2 13.3 %collective-permute-start.9 = (bf16[48,2176]{1,0:T(8,128)(2,1)}, bf16[48,2176]{1,0:T(8,128)(2,1)S(1)}, u32[]{:S(2)}, u32[]{:S(2)}) collective-permute-start(bf16[48,2176]{1,0:T(8,128)(2,1)} %get-tuple-element.47), channel_id=1, source_target_pairs={{0,16},{4,20},{8,24},{12,28},{16,0},{20,4},{24,8},{28,12},{1,17},{... | collective-permute-start | bytes 626696 | tf_op jit(solution)/shard_map/ppermute | solution.py:182
  39.5 24.0 %copy-start.4 = (bf16[96,2176]{1,0:T(8,128)(2,1)}, bf16[96,2176]{1,0:T(8,128)(2,1)S(1)}, u32[]{:S(2)}) copy-start(bf16[96,2176]{1,0:T(8,128)(2,1)S(1)} %constant_dynamic-update-slice_fusion.refs_2_) | copy-start | bytes 1253380
  39.5 21.1 %collective-permute-start.7 = (bf16[96,2176]{1,0:T(8,128)(2,1)S(1)}, bf16[96,2176]{1,0:T(8,128)(2,1)S(1)}, u32[]{:S(2)}, u32[]{:S(2)}) collective-permute-start(bf16[96,2176]{1,0:T(8,128)(2,1)S(1)} %constant_dynamic-update-slice_fusion.refs_2_), channel_id=1, source_target_pairs={{0,1},{1,0},{2,3},{3,2},{4,5},{5,4},{6,7},{7,6},{8,9},{9,8},{10,11... | collective-permute-start | bytes 1253384 | tf_op jit(solution)/shard_map/ppermute | solution.py:182
  40.8 7.4 %collective-permute-start.8 = (bf16[48,2176]{1,0:T(8,128)(2,1)S(1)}, bf16[48,2176]{1,0:T(8,128)(2,1)S(1)}, u32[]{:S(2)}, u32[]{:S(2)}) collective-permute-start(bf16[48,2176]{1,0:T(8,128)(2,1)S(1)} %collective-permute-done.6), channel_id=1, source_target_pairs={{0,2},{1,3},{2,0},{3,1},{4,6},{5,7},{6,4},{7,5},{8,10},{9,11},{10,... | collective-permute-start | bytes 626696 | tf_op jit(solution)/shard_map/ppermute | solution.py:182
  43.6 9.3 %collective-permute-start.12 = (bf16[48,2176]{1,0:T(8,128)(2,1)}, bf16[48,2176]{1,0:T(8,128)(2,1)S(1)}, u32[]{:S(2)}, u32[]{:S(2)}) collective-permute-start(bf16[48,2176]{1,0:T(8,128)(2,1)} %get-tuple-element.47), channel_id=1, source_target_pairs={{0,24},{4,28},{8,16},{12,20},{16,8},{20,12},{24,0},{28,4},{1,25},{... | collective-permute-start | bytes 626696 | tf_op jit(solution)/shard_map/ppermute | solution.py:182
  48.2 6.7 %collective-permute-start.11 = (bf16[48,2176]{1,0:T(8,128)(2,1)S(1)}, bf16[48,2176]{1,0:T(8,128)(2,1)S(1)}, u32[]{:S(2)}, u32[]{:S(2)}) collective-permute-start(bf16[48,2176]{1,0:T(8,128)(2,1)S(1)} %collective-permute-done.9), channel_id=1, source_target_pairs={{0,2},{1,3},{2,0},{3,1},{4,6},{5,7},{6,4},{7,5},{8,10},{9,11},{10,... | collective-permute-start | bytes 626696 | tf_op jit(solution)/shard_map/ppermute | solution.py:182
  50.0 13.5 %copy-start.3 = (bf16[96,2176]{1,0:T(8,128)(2,1)}, bf16[96,2176]{1,0:T(8,128)(2,1)S(1)}, u32[]{:S(2)}) copy-start(bf16[96,2176]{1,0:T(8,128)(2,1)S(1)} %constant_dynamic-update-slice_fusion.2.refs_4_) | copy-start | bytes 1253380
  52.9 9.1 %collective-permute-start.10 = (bf16[96,2176]{1,0:T(8,128)(2,1)S(1)}, bf16[96,2176]{1,0:T(8,128)(2,1)}, u32[]{:S(2)}, u32[]{:S(2)}) collective-permute-start(bf16[96,2176]{1,0:T(8,128)(2,1)S(1)} %constant_dynamic-update-slice_fusion.2.refs_4_), channel_id=1, source_target_pairs={{0,1},{1,0},{2,3},{3,2},{4,5},{5,4},{6,7},{7,6},{8,9},{9,8},{10,11... | collective-permute-start | bytes 1253384 | tf_op jit(solution)/shard_map/ppermute | solution.py:182
  54.8 5.8 %collective-permute-start.14 = (bf16[48,2176]{1,0:T(8,128)(2,1)S(1)}, bf16[48,2176]{1,0:T(8,128)(2,1)S(1)}, u32[]{:S(2)}, u32[]{:S(2)}) collective-permute-start(bf16[48,2176]{1,0:T(8,128)(2,1)S(1)} %collective-permute-done.12), channel_id=1, source_target_pairs={{0,2},{1,3},{2,0},{3,1},{4,6},{5,7},{6,4},{7,5},{8,10},{9,11},{10,... | collective-permute-start | bytes 626696 | tf_op jit(solution)/shard_map/ppermute | solution.py:182
  60.6 1.9 %collective-permute-start.13 = (bf16[96,2176]{1,0:T(8,128)(2,1)S(1)}, bf16[96,2176]{1,0:T(8,128)(2,1)}, u32[]{:S(2)}, u32[]{:S(2)}) collective-permute-start(bf16[96,2176]{1,0:T(8,128)(2,1)S(1)} %constant_dynamic-update-slice_fusion.4.refs_6_), channel_id=1, source_target_pairs={{0,1},{1,0},{2,3},{3,2},{4,5},{5,4},{6,7},{7,6},{8,9},{9,8},{10,11... | collective-permute-start | bytes 1253384 | tf_op jit(solution)/shard_map/ppermute | solution.py:182
  61.5 2.0 %collective-permute-start.15 = (bf16[96,2176]{1,0:T(8,128)(2,1)S(1)}, bf16[96,2176]{1,0:T(8,128)(2,1)}, u32[]{:S(2)}, u32[]{:S(2)}) collective-permute-start(bf16[96,2176]{1,0:T(8,128)(2,1)S(1)} %constant_dynamic-update-slice_fusion.6.refs_8_), channel_id=1, source_target_pairs={{0,1},{1,0},{2,3},{3,2},{4,5},{5,4},{6,7},{7,6},{8,9},{9,8},{10,11... | collective-permute-start | bytes 1253384 | tf_op jit(solution)/shard_map/ppermute | solution.py:182
  77.0 2.0 %collective-permute-start.25 = (bf16[96,2048]{1,0:T(8,128)(2,1)}, bf16[96,2048]{1,0:T(8,128)(2,1)S(1)}, u32[]{:S(2)}, u32[]{:S(2)}) collective-permute-start(bf16[96,2048]{1,0:T(8,128)(2,1)} %get-tuple-element.64), channel_id=1, source_target_pairs={{0,1},{1,0},{2,3},{3,2},{4,5},{5,4},{6,7},{7,6},{8,9},{9,8},{10,11... | collective-permute-start | bytes 1179656 | tf_op jit(solution)/shard_map/ppermute | solution.py:182
  77.4 4.6 %collective-permute-start.17 = (bf16[96,2048]{1,0:T(8,128)(2,1)}, bf16[96,2048]{1,0:T(8,128)(2,1)S(1)}, u32[]{:S(2)}, u32[]{:S(2)}) collective-permute-start(bf16[96,2048]{1,0:T(8,128)(2,1)} %get-tuple-element.56), channel_id=1, source_target_pairs={{0,1},{1,0},{2,3},{3,2},{4,5},{5,4},{6,7},{7,6},{8,9},{9,8},{10,11... | collective-permute-start | bytes 1179656 | tf_op jit(solution)/shard_map/ppermute | solution.py:182
  77.5 4.6 %collective-permute-start.18 = (bf16[96,2048]{1,0:T(8,128)(2,1)}, bf16[96,2048]{1,0:T(8,128)(2,1)S(1)}, u32[]{:S(2)}, u32[]{:S(2)}) collective-permute-start(bf16[96,2048]{1,0:T(8,128)(2,1)} %get-tuple-element.58), channel_id=1, source_target_pairs={{0,1},{1,0},{2,3},{3,2},{4,5},{5,4},{6,7},{7,6},{8,9},{9,8},{10,11... | collective-permute-start | bytes 1179656 | tf_op jit(solution)/shard_map/ppermute | solution.py:182
  77.9 4.7 %collective-permute-start.21 = (bf16[96,2048]{1,0:T(8,128)(2,1)}, bf16[96,2048]{1,0:T(8,128)(2,1)S(1)}, u32[]{:S(2)}, u32[]{:S(2)}) collective-permute-start(bf16[96,2048]{1,0:T(8,128)(2,1)} %get-tuple-element.61), channel_id=1, source_target_pairs={{0,1},{1,0},{2,3},{3,2},{4,5},{5,4},{6,7},{7,6},{8,9},{9,8},{10,11... | collective-permute-start | bytes 1179656 | tf_op jit(solution)/shard_map/ppermute | solution.py:182
  80.1 7.8 %collective-permute-start.26 = (bf16[48,2048]{1,0:T(8,128)(2,1)S(1)}, bf16[48,2048]{1,0:T(8,128)(2,1)S(1)}, u32[]{:S(2)}, u32[]{:S(2)}) collective-permute-start(bf16[48,2048]{1,0:T(8,128)(2,1)S(1)} %slice.39), channel_id=1, source_target_pairs={{0,2},{1,3},{2,0},{3,1},{4,6},{5,7},{6,4},{7,5},{8,10},{9,11},{10,... | collective-permute-start | bytes 589832 | tf_op jit(solution)/shard_map/ppermute | solution.py:182
  82.3 9.9 %collective-permute-start.19 = (bf16[48,2048]{1,0:T(8,128)(2,1)S(1)}, bf16[48,2048]{1,0:T(8,128)(2,1)S(1)}, u32[]{:S(2)}, u32[]{:S(2)}) collective-permute-start(bf16[48,2048]{1,0:T(8,128)(2,1)S(1)} %slice.35), channel_id=1, source_target_pairs={{0,2},{1,3},{2,0},{3,1},{4,6},{5,7},{6,4},{7,5},{8,10},{9,11},{10,... | collective-permute-start | bytes 589832 | tf_op jit(solution)/shard_map/ppermute | solution.py:182
  83.0 25.3 %copy-start.10 = (bf16[48,2048]{1,0:T(8,128)(2,1)S(1)}, bf16[48,2048]{1,0:T(8,128)(2,1)}, u32[]{:S(2)}) copy-start(bf16[48,2048]{1,0:T(8,128)(2,1)} %get-tuple-element.39) | copy-start | bytes 589828
  83.1 12.7 %collective-permute-start.22 = (bf16[48,2048]{1,0:T(8,128)(2,1)S(1)}, bf16[48,2048]{1,0:T(8,128)(2,1)S(1)}, u32[]{:S(2)}, u32[]{:S(2)}) collective-permute-start(bf16[48,2048]{1,0:T(8,128)(2,1)S(1)} %slice.37), channel_id=1, source_target_pairs={{0,2},{1,3},{2,0},{3,1},{4,6},{5,7},{6,4},{7,5},{8,10},{9,11},{10,... | collective-permute-start | bytes 589832 | tf_op jit(solution)/shard_map/ppermute | solution.py:182
  88.0 11.8 %collective-permute-start.27 = (bf16[48,2048]{1,0:T(8,128)(2,1)S(1)}, bf16[48,2048]{1,0:T(8,128)(2,1)S(1)}, u32[]{:S(2)}, u32[]{:S(2)}) collective-permute-start(bf16[48,2048]{1,0:T(8,128)(2,1)S(1)} %add_convert_fusion.5), channel_id=1, source_target_pairs={{0,24},{4,28},{8,16},{12,20},{16,8},{20,12},{24,0},{28,4},{1,25},{... | collective-permute-start | bytes 589832 | tf_op jit(solution)/shard_map/ppermute | solution.py:182
  92.2 16.1 %collective-permute-start.24 = (bf16[48,2048]{1,0:T(8,128)(2,1)S(1)}, bf16[48,2048]{1,0:T(8,128)(2,1)S(1)}, u32[]{:S(2)}, u32[]{:S(2)}) collective-permute-start(bf16[48,2048]{1,0:T(8,128)(2,1)S(1)} %add_convert_fusion.8), channel_id=1, source_target_pairs={{0,16},{4,20},{8,24},{12,28},{16,0},{20,4},{24,8},{28,12},{1,17},{... | collective-permute-start | bytes 589832 | tf_op jit(solution)/shard_map/ppermute | solution.py:182
  95.9 12.4 %collective-permute-start.23 = (bf16[48,2048]{1,0:T(8,128)(2,1)S(1)}, bf16[48,2048]{1,0:T(8,128)(2,1)S(1)}, u32[]{:S(2)}, u32[]{:S(2)}) collective-permute-start(bf16[48,2048]{1,0:T(8,128)(2,1)S(1)} %add_convert_fusion.6), channel_id=1, source_target_pairs={{0,8},{4,12},{8,0},{12,4},{16,24},{20,28},{24,16},{28,20},{1,9},{5... | collective-permute-start | bytes 589832 | tf_op jit(solution)/shard_map/ppermute | solution.py:182
  98.5 9.8 %collective-permute-start.20 = (bf16[48,2048]{1,0:T(8,128)(2,1)S(1)}, bf16[48,2048]{1,0:T(8,128)(2,1)S(1)}, u32[]{:S(2)}, u32[]{:S(2)}) collective-permute-start(bf16[48,2048]{1,0:T(8,128)(2,1)S(1)} %slice.33), channel_id=1, source_target_pairs={{0,2},{1,3},{2,0},{3,1},{4,6},{5,7},{6,4},{7,5},{8,10},{9,11},{10,... | collective-permute-start | bytes 589832 | tf_op jit(solution)/shard_map/ppermute | solution.py:182
  (11 other events, 26.2 us)

commit v5 on v4

--- a/solution.py
+++ b/solution.py
@@ -504,23 +504,26 @@
         2 * token_rows * width * experts_total,
     )
     router_kl = router_kl[0]
-    blocks, sent = [payload], payload
-    for k in range(1, per_column):
-        if k > 2:
-            blocks[-1], sent = lax.optimization_barrier((blocks[-1], payload))
-        blocks.append(swapped(sent, "ctx", 2 * k))
-    crossed = []
-    for turn, block in enumerate(blocks):
-        parts = [block]
+    crossed, passed = {}, None
+    for k in sorted(range(per_column), key=lambda k: (k.bit_count(), -k)):
+        low = k & -k
+        if k != low:
+            crossed[k] = [swapped(part, "ctx", 2 * low) for part in crossed[k ^ low]]
+            continue
+        parts = [payload if k == 0 else swapped(payload, "ctx", 2 * k)]
         for bit in bits[:-1]:
-            if turn > 0:
-                crossed[turn - 1][-1], *parts = lax.optimization_barrier((crossed[turn - 1][-1], *parts))
+            if k > 0:
+                passed, *parts = lax.optimization_barrier((passed, *parts))
             parts = parts + [swapped(part, "exp", bit) for part in parts]
-        crossed.append(parts)
+        passed = parts[-1]
+        crossed[k] = parts
+    crossed = [crossed[k] for k in range(per_column)]
     expert_index = (exp_index * per_column + ctx_index // 2).reshape(1).astype(jnp.int32)
     groups, pairs, tokens = 1, [], []
     for turn, parts in enumerate(crossed):
         stack = jnp.concatenate(parts, axis=0)
+        if turn == per_column // 2:
+            stack, other_in = lax.optimization_barrier((stack, other_in))
         tokens = tokens + [stack, swapped(stack, "exp", bits[-1])]
         if (turn + 1) % (per_column // groups) == 0:
             pairs.append(hidden_blocks(tokens, weight_in, other_in))
@@ -532,7 +535,7 @@
     for k in reversed(range(per_column)):
         keep, send = partials[k]
         for bit in reversed(bits):
-            if bit == bits[0] and k == 0:
+            if bit == bits[0] and k == 0 and per_column > 2:
                 send, returned[2] = lax.optimization_barrier((send, returned[2]))
             received = swapped(send, "exp", bit)
             total = keep.astype(jnp.float32) + received.astype(jnp.float32)

time: 110 us -> 106 us (0.964)
  local copies, waits for them, and re-layouts: 5.67 us -> 3.44 us
    unnamed x34 -> x31, local copies, waits for them, and re-layouts: 4.69 us -> 2.48 us
  transfers between devices with their start and end apart: 28 -> 28, of which waited for: 17 -> 15; matrix products, arithmetic and copies ran while one was open for 3% -> 3% of each run, Pallas kernels for 10% -> 10%
where the time goes in v5:
time: 106 us
  waiting for transfers between devices  41 us (39%)
  starting transfers between devices  38.8 us (37%)
  Pallas kernels  19.3 us (18%)
  local copies, waits for them, and re-layouts  3.44 us (3%)
  other arithmetic  2.46 us (2%)
    ppermute x27, waiting for transfers between devices, swapped(): lax.ppermute(value, axis, [(source, source ^ mask) for source in range(co...  38.8 us
    ppermute x27, starting transfers between devices, swapped(): lax.ppermute(value, axis, [(source, source ^ mask) for source in range(co...  33.9 us
    pallas_call x1, Pallas kernels, hidden_blocks(): pl.pallas_call(functools.partial(hidden_kernel, width), out_shape=(jax.Sh...  7.61 us
    pallas_call x2, Pallas kernels, small_kernel(): pl.pallas_call(functools.partial(fetching, kernel, len(held), stored), ou...  7.1 us
    ppermute x1, starting transfers between devices, passed_along(): lax.ppermute(value, axis, [(source, source + steps) for source in range(i...  4.88 us
    pallas_call x1, Pallas kernels, output_blocks(): pl.pallas_call(output_kernel, out_shape=(half,) * (2 * count), in_specs=[...  4.64 us
    unnamed x31, local copies, waits for them, and re-layouts  2.48 us
    ppermute x1, waiting for transfers between devices, passed_along(): lax.ppermute(value, axis, [(source, source + steps) for source in range(i...  2.19 us
  transfers between devices with their start and end apart: 28, of which 15 were waited for; matrix products, arithmetic and copies ran while one was open for 3% of the time, Pallas kernels for 10%

profile of v5, /device:TPU:0, one launch (start us, length us, event | category | flops | bytes accessed | tf_op | source)
XLA Modules:
  0.0 106.0 jit_solution(13094459724585725633)
XLA Ops:
  1.5 4.9 %collective-permute-start = (bf16[192,256]{1,0:T(8,128)(2,1)S(1)}, bf16[192,256]{1,0:T(8,128)(2,1)S(1)}, u32[]{:S(2)}, u32[]{:S(2)}) collective-permute-start(bf16[192,256]{1,0:T(8,128)(2,1)S(1)} %pad_maximum_fusion.1.refs_3_), channel_id=1, source_target_pairs={{0,4},{4,8},{8,12},{12,16},{16,20},{20,24},{24,28},{1,5},{5,9},{9,... | collective-permute-start | bytes 294920 | tf_op jit(solution)/shard_map/ppermute | solution.py:19
  6.4 2.2 %collective-permute-done.refs_2_ = bf16[192,256]{1,0:T(8,128)(2,1)S(1)} collective-permute-done((bf16[192,256]{1,0:T(8,128)(2,1)S(1)}, bf16[192,256]{1,0:T(8,128)(2,1)S(1)}, u32[]{:S(2)}, u32[]{:S(2)}) %collective-permute-start) | collective-permute-done | bytes 98336 | tf_op jit(solution)/shard_map/ppermute | solution.py:19
  9.2 3.7 %shard_map.131 = (bf16[48,2048]{1,0:T(8,128)(2,1)}, bf16[48,2048]{1,0:T(8,128)(2,1)}, bf16[48,2048]{1,0:T(8,128)(2,1)}, bf16[48,2048]{1,0:T(8,128)(2,1)}) custom-call(s32[1]{0:T(128)} %bitcast.index_ref, s32[1,192]{1,0:T(1,128)} %bitcast.18, bf16[192,128]{1,0:T(8,128)(2,1)} %refs_1_.1, bf16[192,256]{1,0:T(8,128)(2,1)} %copy-done.13, ...), custom_call_target="tpu_custom_call" | custom-call | tf_op jit(solution)/shard_map/pallas_call | solution.py:310
  13.0 1.6 %collective-permute-start.1 = (bf16[48,2048]{1,0:T(8,128)(2,1)}, bf16[48,2048]{1,0:T(8,128)(2,1)S(1)}, u32[]{:S(2)}, u32[]{:S(2)}) collective-permute-start(bf16[48,2048]{1,0:T(8,128)(2,1)} %get-tuple-element.32), channel_id=1, source_target_pairs={{0,2},{1,3},{2,0},{3,1},{4,6},{5,7},{6,4},{7,5},{8,10},{9,11},{10,... | collective-permute-start | bytes 589832 | tf_op jit(solution)/shard_map/ppermute | solution.py:182
  15.2 2.4 %collective-permute-start.7 = (bf16[2048,384]{1,0:T(8,128)(2,1)}, bf16[2048,384]{1,0:T(8,128)(2,1)S(1)}, u32[]{:S(2)}, u32[]{:S(2)}) collective-permute-start(bf16[2048,384]{1,0:T(8,128)(2,1)} %bitcast.10), channel_id=1, source_target_pairs={{0,4},{4,0},{8,12},{12,8},{16,20},{20,16},{24,28},{28,24},{1,5},{5... | collective-permute-start | bytes 4718600 | tf_op jit(solution)/shard_map/ppermute | solution.py:182
  17.6 2.7 %collective-permute-done.1.refs_1_ = bf16[48,2048]{1,0:T(8,128)(2,1)S(1)} collective-permute-done((bf16[48,2048]{1,0:T(8,128)(2,1)}, bf16[48,2048]{1,0:T(8,128)(2,1)S(1)}, u32[]{:S(2)}, u32[]{:S(2)}) %collective-permute-start.1) | collective-permute-done | bytes 196640 | tf_op jit(solution)/shard_map/ppermute | solution.py:182
  20.3 2.0 %collective-permute-done.3.refs_3_ = bf16[48,2048]{1,0:T(8,128)(2,1)S(1)} collective-permute-done((bf16[48,2048]{1,0:T(8,128)(2,1)}, bf16[48,2048]{1,0:T(8,128)(2,1)S(1)}, u32[]{:S(2)}, u32[]{:S(2)}) %collective-permute-start.3) | collective-permute-done | bytes 196640 | tf_op jit(solution)/shard_map/ppermute | solution.py:182
  23.0 3.4 %shard_map.132 = (bf16[48,2048]{1,0:T(8,128)(2,1)}, bf16[48,2176]{1,0:T(8,128)(2,1)}, f32[1,48]{1,0:T(1,128)}) custom-call(s32[1]{0:T(128)} %bitcast.index_ref, bf16[48,2048]{1,0:T(8,128)(2,1)} %get-tuple-element.31.refs_0_, bf16[48,2048]{1,0:T(8,128)(2,1)} %copy-done.10, bf16[48,2048]{1,0:T(8,128)(2,1)} %copy-done.11, bf16[48,2048]{1,0:T(8,128)(2,1)} %copy-done.12, ...), custom_call_target="tpu_custom_call" | custom-call | tf_op jit(solution)/shard_map/pallas_call | solution.py:310
  27.0 4.3 %collective-permute-start.5 = (bf16[48,2176]{1,0:T(8,128)(2,1)}, bf16[48,2176]{1,0:T(8,128)(2,1)S(1)}, u32[]{:S(2)}, u32[]{:S(2)}) collective-permute-start(bf16[48,2176]{1,0:T(8,128)(2,1)} %get-tuple-element.36), channel_id=1, source_target_pairs={{0,16},{4,20},{8,24},{12,28},{16,0},{20,4},{24,8},{28,12},{1,17},{... | collective-permute-start | bytes 626696 | tf_op jit(solution)/shard_map/ppermute | solution.py:182
  31.3 1.6 %collective-permute-start.9 = (bf16[48,2176]{1,0:T(8,128)(2,1)}, bf16[48,2176]{1,0:T(8,128)(2,1)S(1)}, u32[]{:S(2)}, u32[]{:S(2)}) collective-permute-start(bf16[48,2176]{1,0:T(8,128)(2,1)} %get-tuple-element.36), channel_id=1, source_target_pairs={{0,8},{4,12},{8,0},{12,4},{16,24},{20,28},{24,16},{28,20},{1,9},{5... | collective-permute-start | bytes 626696 | tf_op jit(solution)/shard_map/ppermute | solution.py:182
  32.9 1.0 constant_dynamic-update-slice_fusion.1
  34.7 6.5 %collective-permute-done.5 = bf16[48,2176]{1,0:T(8,128)(2,1)S(1)} collective-permute-done((bf16[48,2176]{1,0:T(8,128)(2,1)}, bf16[48,2176]{1,0:T(8,128)(2,1)S(1)}, u32[]{:S(2)}, u32[]{:S(2)}) %collective-permute-start.5) | collective-permute-done | bytes 208928 | tf_op jit(solution)/shard_map/ppermute | solution.py:182
  41.2 2.3 %collective-permute-start.6 = (bf16[48,2176]{1,0:T(8,128)(2,1)S(1)}, bf16[48,2176]{1,0:T(8,128)(2,1)S(1)}, u32[]{:S(2)}, u32[]{:S(2)}) collective-permute-start(bf16[48,2176]{1,0:T(8,128)(2,1)S(1)} %collective-permute-done.5), channel_id=1, source_target_pairs={{0,2},{1,3},{2,0},{3,1},{4,6},{5,7},{6,4},{7,5},{8,10},{9,11},{10,... | collective-permute-start | bytes 626696 | tf_op jit(solution)/shard_map/ppermute | solution.py:182
  44.5 4.6 %collective-permute-done.6 = bf16[48,2176]{1,0:T(8,128)(2,1)S(1)} collective-permute-done((bf16[48,2176]{1,0:T(8,128)(2,1)S(1)}, bf16[48,2176]{1,0:T(8,128)(2,1)S(1)}, u32[]{:S(2)}, u32[]{:S(2)}) %collective-permute-start.6) | collective-permute-done | bytes 208928 | tf_op jit(solution)/shard_map/ppermute | solution.py:182
  49.0 1.6 %collective-permute-start.10 = (bf16[48,2176]{1,0:T(8,128)(2,1)S(1)}, bf16[48,2176]{1,0:T(8,128)(2,1)S(1)}, u32[]{:S(2)}, u32[]{:S(2)}) collective-permute-start(bf16[48,2176]{1,0:T(8,128)(2,1)S(1)} %collective-permute-done.9), channel_id=1, source_target_pairs={{0,2},{1,3},{2,0},{3,1},{4,6},{5,7},{6,4},{7,5},{8,10},{9,11},{10,... | collective-permute-start | bytes 626696 | tf_op jit(solution)/shard_map/ppermute | solution.py:182
  50.7 0.9 collective-permute-start.14
  51.7 4.1 %collective-permute-done.10 = bf16[48,2176]{1,0:T(8,128)(2,1)S(1)} collective-permute-done((bf16[48,2176]{1,0:T(8,128)(2,1)S(1)}, bf16[48,2176]{1,0:T(8,128)(2,1)S(1)}, u32[]{:S(2)}, u32[]{:S(2)}) %collective-permute-start.10) | collective-permute-done | bytes 208928 | tf_op jit(solution)/shard_map/ppermute | solution.py:182
  55.9 0.9 collective-permute-done.14
  57.8 1.0 collective-permute-done.15.refs_9_
  59.4 7.6 %shard_map.133 = (bf16[768,384]{1,0:T(8,128)(2,1)}, bf16[768,128]{1,0:T(8,128)(2,1)}) custom-call(bf16[2048,384]{1,0:T(8,128)(2,1)} %bitcast.11, bf16[2048,384]{1,0:T(8,128)(2,1)} %copy-done.1, bf16[96,2176]{1,0:T(8,128)(2,1)} %copy-done.3, bf16[96,2176]{1,0:T(8,128)(2,1)} %collective-permute-done.8.refs_3_, bf16[96,2176]{1,0:T(8,128)(2,1)} %copy-done.4, ...), custom_call_target="tpu_custom_call" | custom-call | bytes 9437184 | tf_op jit(solution)/shard_map/pallas_call | solution.py:361
  67.0 2.3 %collective-permute-done.16.other_ref = bf16[192,2048]{1,0:T(8,128)(2,1)} collective-permute-done((bf16[192,2048]{1,0:T(8,128)(2,1)}, bf16[192,2048]{1,0:T(8,128)(2,1)}, u32[]{:S(2)}, u32[]{:S(2)}) %collective-permute-start.16) | collective-permute-done | bytes 786464 | tf_op jit(solution)/shard_map/ppermute | solution.py:182
  69.3 4.6 %shard_map.134 = (bf16[96,2048]{1,0:T(8,128)(2,1)}, bf16[96,2048]{1,0:T(8,128)(2,1)}, bf16[96,2048]{1,0:T(8,128)(2,1)}, bf16[96,2048]{1,0:T(8,128)(2,1)}, bf16[9...) custom-call(s32[1]{0:T(128)} %bitcast.8.index_ref, ...), custom_call_target="tpu_custom_call" | custom-call | tf_op jit(solution)/shard_map/pallas_call | solution.py:408
  75.0 0.9 collective-permute-done.25
  76.0 1.1 %add_convert_fusion = bf16[96,2048]{1,0:T(8,128)(2,1)S(1)} fusion(bf16[96,2048]{1,0:T(8,128)(2,1)S(1)} %collective-permute-done.25, bf16[96,2048]{1,0:T(8,128)(2,1)} %get-tuple-element.55), kind=kLoop, calls=%fused_computation | loop fusion | flops 786432 | bytes 1179648 | tf_op jit(solution)/shard_map/convert_element_type | solution.py:542
  77.1 1.6 %collective-permute-start.26 = (bf16[48,2048]{1,0:T(8,128)(2,1)S(1)}, bf16[48,2048]{1,0:T(8,128)(2,1)S(1)}, u32[]{:S(2)}, u32[]{:S(2)}) collective-permute-start(bf16[48,2048]{1,0:T(8,128)(2,1)S(1)} %slice.39), channel_id=1, source_target_pairs={{0,2},{1,3},{2,0},{3,1},{4,6},{5,7},{6,4},{7,5},{8,10},{9,11},{10,... | collective-permute-start | bytes 589832 | tf_op jit(solution)/shard_map/ppermute | solution.py:182
  79.8 1.4 %collective-permute-start.22 = (bf16[48,2048]{1,0:T(8,128)(2,1)S(1)}, bf16[48,2048]{1,0:T(8,128)(2,1)S(1)}, u32[]{:S(2)}, u32[]{:S(2)}) collective-permute-start(bf16[48,2048]{1,0:T(8,128)(2,1)S(1)} %slice.37), channel_id=1, source_target_pairs={{0,2},{1,3},{2,0},{3,1},{4,6},{5,7},{6,4},{7,5},{8,10},{9,11},{10,... | collective-permute-start | bytes 589832 | tf_op jit(solution)/shard_map/ppermute | solution.py:182
  81.3 3.7 %collective-permute-done.26 = bf16[48,2048]{1,0:T(8,128)(2,1)S(1)} collective-permute-done((bf16[48,2048]{1,0:T(8,128)(2,1)S(1)}, bf16[48,2048]{1,0:T(8,128)(2,1)S(1)}, u32[]{:S(2)}, u32[]{:S(2)}) %collective-permute-start.26) | collective-permute-done | bytes 196640 | tf_op jit(solution)/shard_map/ppermute | solution.py:182
  85.0 4.8 %collective-permute-start.27 = (bf16[48,2048]{1,0:T(8,128)(2,1)S(1)}, bf16[48,2048]{1,0:T(8,128)(2,1)S(1)}, u32[]{:S(2)}, u32[]{:S(2)}) collective-permute-start(bf16[48,2048]{1,0:T(8,128)(2,1)S(1)} %add_convert_fusion.5), channel_id=1, source_target_pairs={{0,24},{4,28},{8,16},{12,20},{16,8},{20,12},{24,0},{28,4},{1,25},{... | collective-permute-start | bytes 589832 | tf_op jit(solution)/shard_map/ppermute | solution.py:182
  89.8 3.1 %collective-permute-start.24 = (bf16[48,2048]{1,0:T(8,128)(2,1)S(1)}, bf16[48,2048]{1,0:T(8,128)(2,1)S(1)}, u32[]{:S(2)}, u32[]{:S(2)}) collective-permute-start(bf16[48,2048]{1,0:T(8,128)(2,1)S(1)} %add_convert_fusion.8), channel_id=1, source_target_pairs={{0,16},{4,20},{8,24},{12,28},{16,0},{20,4},{24,8},{28,12},{1,17},{... | collective-permute-start | bytes 589832 | tf_op jit(solution)/shard_map/ppermute | solution.py:182
  93.0 2.3 %collective-permute-start.23 = (bf16[48,2048]{1,0:T(8,128)(2,1)S(1)}, bf16[48,2048]{1,0:T(8,128)(2,1)S(1)}, u32[]{:S(2)}, u32[]{:S(2)}) collective-permute-start(bf16[48,2048]{1,0:T(8,128)(2,1)S(1)} %add_convert_fusion.6), channel_id=1, source_target_pairs={{0,8},{4,12},{8,0},{12,4},{16,24},{20,28},{24,16},{28,20},{1,9},{5... | collective-permute-start | bytes 589832 | tf_op jit(solution)/shard_map/ppermute | solution.py:182
  95.4 1.5 %collective-permute-start.20 = (bf16[48,2048]{1,0:T(8,128)(2,1)S(1)}, bf16[48,2048]{1,0:T(8,128)(2,1)S(1)}, u32[]{:S(2)}, u32[]{:S(2)}) collective-permute-start(bf16[48,2048]{1,0:T(8,128)(2,1)S(1)} %slice.33), channel_id=1, source_target_pairs={{0,2},{1,3},{2,0},{3,1},{4,6},{5,7},{6,4},{7,5},{8,10},{9,11},{10,... | collective-permute-start | bytes 589832 | tf_op jit(solution)/shard_map/ppermute | solution.py:182
  96.9 8.3 %collective-permute-done.24 = bf16[48,2048]{1,0:T(8,128)(2,1)S(1)} collective-permute-done((bf16[48,2048]{1,0:T(8,128)(2,1)S(1)}, bf16[48,2048]{1,0:T(8,128)(2,1)S(1)}, u32[]{:S(2)}, u32[]{:S(2)}) %collective-permute-start.24) | collective-permute-done | bytes 196640 | tf_op jit(solution)/shard_map/ppermute | solution.py:182
  (77 shorter events, 10.1 us)
Async XLA Ops:
  1.5 7.1 %copy-start.8 = (bf16[192,256]{1,0:T(8,128)(2,1)}, bf16[192,256]{1,0:T(8,128)(2,1)S(1)}, u32[]{:S(2)}) copy-start(bf16[192,256]{1,0:T(8,128)(2,1)S(1)} %pad_maximum_fusion.1.refs_3_) | copy-start | bytes 294916
  1.5 7.1 %collective-permute-start = (bf16[192,256]{1,0:T(8,128)(2,1)S(1)}, bf16[192,256]{1,0:T(8,128)(2,1)S(1)}, u32[]{:S(2)}, u32[]{:S(2)}) collective-permute-start(bf16[192,256]{1,0:T(8,128)(2,1)S(1)} %pad_maximum_fusion.1.refs_3_), channel_id=1, source_target_pairs={{0,4},{4,8},{8,12},{12,16},{16,20},{20,24},{24,28},{1,5},{5,9},{9,... | collective-permute-start | bytes 294920 | tf_op jit(solution)/shard_map/ppermute | solution.py:19
  13.0 7.4 %collective-permute-start.1 = (bf16[48,2048]{1,0:T(8,128)(2,1)}, bf16[48,2048]{1,0:T(8,128)(2,1)S(1)}, u32[]{:S(2)}, u32[]{:S(2)}) collective-permute-start(bf16[48,2048]{1,0:T(8,128)(2,1)} %get-tuple-element.32), channel_id=1, source_target_pairs={{0,2},{1,3},{2,0},{3,1},{4,6},{5,7},{6,4},{7,5},{8,10},{9,11},{10,... | collective-permute-start | bytes 589832 | tf_op jit(solution)/shard_map/ppermute | solution.py:182
  14.5 5.8 %collective-permute-start.2 = (bf16[48,2048]{1,0:T(8,128)(2,1)}, bf16[48,2048]{1,0:T(8,128)(2,1)S(1)}, u32[]{:S(2)}, u32[]{:S(2)}) collective-permute-start(bf16[48,2048]{1,0:T(8,128)(2,1)} %get-tuple-element.33), channel_id=1, source_target_pairs={{0,1},{1,0},{2,3},{3,2},{4,5},{5,4},{6,7},{7,6},{8,9},{9,8},{10,11... | collective-permute-start | bytes 589832 | tf_op jit(solution)/shard_map/ppermute | solution.py:182
  14.5 7.8 %collective-permute-start.3 = (bf16[48,2048]{1,0:T(8,128)(2,1)}, bf16[48,2048]{1,0:T(8,128)(2,1)S(1)}, u32[]{:S(2)}, u32[]{:S(2)}) collective-permute-start(bf16[48,2048]{1,0:T(8,128)(2,1)} %get-tuple-element.34), channel_id=1, source_target_pairs={{0,3},{1,2},{2,1},{3,0},{4,7},{5,6},{6,5},{7,4},{8,11},{9,10},{10,... | collective-permute-start | bytes 589832 | tf_op jit(solution)/shard_map/ppermute | solution.py:182
  15.2 41.7 %collective-permute-start.7 = (bf16[2048,384]{1,0:T(8,128)(2,1)}, bf16[2048,384]{1,0:T(8,128)(2,1)S(1)}, u32[]{:S(2)}, u32[]{:S(2)}) collective-permute-start(bf16[2048,384]{1,0:T(8,128)(2,1)} %bitcast.10), channel_id=1, source_target_pairs={{0,4},{4,0},{8,12},{12,8},{16,20},{20,16},{24,28},{28,24},{1,5},{5... | collective-permute-start | bytes 4718600 | tf_op jit(solution)/shard_map/ppermute | solution.py:182
  17.6 51.7 %collective-permute-start.16 = (bf16[192,2048]{1,0:T(8,128)(2,1)}, bf16[192,2048]{1,0:T(8,128)(2,1)}, u32[]{:S(2)}, u32[]{:S(2)}) collective-permute-start(bf16[192,2048]{1,0:T(8,128)(2,1)} %bitcast.12), channel_id=1, source_target_pairs={{0,4},{4,0},{8,12},{12,8},{16,20},{20,16},{24,28},{28,24},{1,5},{5... | collective-permute-start | bytes 2359304 | tf_op jit(solution)/shard_map/ppermute | solution.py:182
  26.4 8.3 %collective-permute-start.4 = (bf16[48,2176]{1,0:T(8,128)(2,1)}, bf16[48,2176]{1,0:T(8,128)(2,1)S(1)}, u32[]{:S(2)}, u32[]{:S(2)}) collective-permute-start(bf16[48,2176]{1,0:T(8,128)(2,1)} %get-tuple-element.36), channel_id=1, source_target_pairs={{0,2},{1,3},{2,0},{3,1},{4,6},{5,7},{6,4},{7,5},{8,10},{9,11},{10,... | collective-permute-start | bytes 626696 | tf_op jit(solution)/shard_map/ppermute | solution.py:182
  27.0 14.2 %collective-permute-start.5 = (bf16[48,2176]{1,0:T(8,128)(2,1)}, bf16[48,2176]{1,0:T(8,128)(2,1)S(1)}, u32[]{:S(2)}, u32[]{:S(2)}) collective-permute-start(bf16[48,2176]{1,0:T(8,128)(2,1)} %get-tuple-element.36), channel_id=1, source_target_pairs={{0,16},{4,20},{8,24},{12,28},{16,0},{20,4},{24,8},{28,12},{1,17},{... | collective-permute-start | bytes 626696 | tf_op jit(solution)/shard_map/ppermute | solution.py:182
  31.3 13.1 %collective-permute-start.9 = (bf16[48,2176]{1,0:T(8,128)(2,1)}, bf16[48,2176]{1,0:T(8,128)(2,1)S(1)}, u32[]{:S(2)}, u32[]{:S(2)}) collective-permute-start(bf16[48,2176]{1,0:T(8,128)(2,1)} %get-tuple-element.36), channel_id=1, source_target_pairs={{0,8},{4,12},{8,0},{12,4},{16,24},{20,28},{24,16},{28,20},{1,9},{5... | collective-permute-start | bytes 626696 | tf_op jit(solution)/shard_map/ppermute | solution.py:182
  41.2 7.8 %collective-permute-start.6 = (bf16[48,2176]{1,0:T(8,128)(2,1)S(1)}, bf16[48,2176]{1,0:T(8,128)(2,1)S(1)}, u32[]{:S(2)}, u32[]{:S(2)}) collective-permute-start(bf16[48,2176]{1,0:T(8,128)(2,1)S(1)} %collective-permute-done.5), channel_id=1, source_target_pairs={{0,2},{1,3},{2,0},{3,1},{4,6},{5,7},{6,4},{7,5},{8,10},{9,11},{10,... | collective-permute-start | bytes 626696 | tf_op jit(solution)/shard_map/ppermute | solution.py:182
  43.5 7.2 %collective-permute-start.13 = (bf16[48,2176]{1,0:T(8,128)(2,1)S(1)}, bf16[48,2176]{1,0:T(8,128)(2,1)S(1)}, u32[]{:S(2)}, u32[]{:S(2)}) collective-permute-start(bf16[48,2176]{1,0:T(8,128)(2,1)S(1)} %collective-permute-done.5), channel_id=1, source_target_pairs={{0,8},{4,12},{8,0},{12,4},{16,24},{20,28},{24,16},{28,20},{1,9},{5... | collective-permute-start | bytes 626696 | tf_op jit(solution)/shard_map/ppermute | solution.py:182
  44.4 15.0 %copy-start.3 = (bf16[96,2176]{1,0:T(8,128)(2,1)}, bf16[96,2176]{1,0:T(8,128)(2,1)S(1)}, u32[]{:S(2)}) copy-start(bf16[96,2176]{1,0:T(8,128)(2,1)S(1)} %constant_dynamic-update-slice_fusion.refs_2_) | copy-start | bytes 1253380
  44.4 13.0 %collective-permute-start.8 = (bf16[96,2176]{1,0:T(8,128)(2,1)S(1)}, bf16[96,2176]{1,0:T(8,128)(2,1)}, u32[]{:S(2)}, u32[]{:S(2)}) collective-permute-start(bf16[96,2176]{1,0:T(8,128)(2,1)S(1)} %constant_dynamic-update-slice_fusion.refs_2_), channel_id=1, source_target_pairs={{0,1},{1,0},{2,3},{3,2},{4,5},{5,4},{6,7},{7,6},{8,9},{9,8},{10,11... | collective-permute-start | bytes 1253384 | tf_op jit(solution)/shard_map/ppermute | solution.py:182
  49.0 6.8 %collective-permute-start.10 = (bf16[48,2176]{1,0:T(8,128)(2,1)S(1)}, bf16[48,2176]{1,0:T(8,128)(2,1)S(1)}, u32[]{:S(2)}, u32[]{:S(2)}) collective-permute-start(bf16[48,2176]{1,0:T(8,128)(2,1)S(1)} %collective-permute-done.9), channel_id=1, source_target_pairs={{0,2},{1,3},{2,0},{3,1},{4,6},{5,7},{6,4},{7,5},{8,10},{9,11},{10,... | collective-permute-start | bytes 626696 | tf_op jit(solution)/shard_map/ppermute | solution.py:182
  50.7 8.7 %copy-start = (bf16[96,2176]{1,0:T(8,128)(2,1)}, bf16[96,2176]{1,0:T(8,128)(2,1)S(1)}, u32[]{:S(2)}) copy-start(bf16[96,2176]{1,0:T(8,128)(2,1)S(1)} %pad_maximum_fusion.refs_6_) | copy-start | bytes 1253380
  50.7 6.1 %collective-permute-start.14 = (bf16[48,2176]{1,0:T(8,128)(2,1)S(1)}, bf16[48,2176]{1,0:T(8,128)(2,1)S(1)}, u32[]{:S(2)}, u32[]{:S(2)}) collective-permute-start(bf16[48,2176]{1,0:T(8,128)(2,1)S(1)} %collective-permute-done.6), channel_id=1, source_target_pairs={{0,8},{4,12},{8,0},{12,4},{16,24},{20,28},{24,16},{28,20},{1,9},{5... | collective-permute-start | bytes 626696 | tf_op jit(solution)/shard_map/ppermute | solution.py:182
  55.8 2.0 %collective-permute-start.11 = (bf16[96,2176]{1,0:T(8,128)(2,1)S(1)}, bf16[96,2176]{1,0:T(8,128)(2,1)}, u32[]{:S(2)}, u32[]{:S(2)}) collective-permute-start(bf16[96,2176]{1,0:T(8,128)(2,1)S(1)} %constant_dynamic-update-slice_fusion.2.refs_4_), channel_id=1, source_target_pairs={{0,1},{1,0},{2,3},{3,2},{4,5},{5,4},{6,7},{7,6},{8,9},{9,8},{10,11... | collective-permute-start | bytes 1253384 | tf_op jit(solution)/shard_map/ppermute | solution.py:182
  56.8 2.0 %collective-permute-start.15 = (bf16[96,2176]{1,0:T(8,128)(2,1)S(1)}, bf16[96,2176]{1,0:T(8,128)(2,1)}, u32[]{:S(2)}, u32[]{:S(2)}) collective-permute-start(bf16[96,2176]{1,0:T(8,128)(2,1)S(1)} %constant_dynamic-update-slice_fusion.4.refs_8_), channel_id=1, source_target_pairs={{0,1},{1,0},{2,3},{3,2},{4,5},{5,4},{6,7},{7,6},{8,9},{9,8},{10,11... | collective-permute-start | bytes 1253384 | tf_op jit(solution)/shard_map/ppermute | solution.py:182
  56.9 2.5 %collective-permute-start.12 = (bf16[96,2176]{1,0:T(8,128)(2,1)S(1)}, bf16[96,2176]{1,0:T(8,128)(2,1)}, u32[]{:S(2)}, u32[]{:S(2)}) collective-permute-start(bf16[96,2176]{1,0:T(8,128)(2,1)S(1)} %pad_maximum_fusion.refs_6_), channel_id=1, source_target_pairs={{0,1},{1,0},{2,3},{3,2},{4,5},{5,4},{6,7},{7,6},{8,9},{9,8},{10,11... | collective-permute-start | bytes 1253384 | tf_op jit(solution)/shard_map/ppermute | solution.py:182
  74.0 2.0 %collective-permute-start.25 = (bf16[96,2048]{1,0:T(8,128)(2,1)}, bf16[96,2048]{1,0:T(8,128)(2,1)S(1)}, u32[]{:S(2)}, u32[]{:S(2)}) collective-permute-start(bf16[96,2048]{1,0:T(8,128)(2,1)} %get-tuple-element.56), channel_id=1, source_target_pairs={{0,1},{1,0},{2,3},{3,2},{4,5},{5,4},{6,7},{7,6},{8,9},{9,8},{10,11... | collective-permute-start | bytes 1179656 | tf_op jit(solution)/shard_map/ppermute | solution.py:182
  74.0 4.7 %collective-permute-start.17 = (bf16[96,2048]{1,0:T(8,128)(2,1)}, bf16[96,2048]{1,0:T(8,128)(2,1)S(1)}, u32[]{:S(2)}, u32[]{:S(2)}) collective-permute-start(bf16[96,2048]{1,0:T(8,128)(2,1)} %get-tuple-element.48), channel_id=1, source_target_pairs={{0,1},{1,0},{2,3},{3,2},{4,5},{5,4},{6,7},{7,6},{8,9},{9,8},{10,11... | collective-permute-start | bytes 1179656 | tf_op jit(solution)/shard_map/ppermute | solution.py:182
  74.5 4.3 %collective-permute-start.18 = (bf16[96,2048]{1,0:T(8,128)(2,1)}, bf16[96,2048]{1,0:T(8,128)(2,1)S(1)}, u32[]{:S(2)}, u32[]{:S(2)}) collective-permute-start(bf16[96,2048]{1,0:T(8,128)(2,1)} %get-tuple-element.50), channel_id=1, source_target_pairs={{0,1},{1,0},{2,3},{3,2},{4,5},{5,4},{6,7},{7,6},{8,9},{9,8},{10,11... | collective-permute-start | bytes 1179656 | tf_op jit(solution)/shard_map/ppermute | solution.py:182
  74.6 5.0 %collective-permute-start.21 = (bf16[96,2048]{1,0:T(8,128)(2,1)}, bf16[96,2048]{1,0:T(8,128)(2,1)S(1)}, u32[]{:S(2)}, u32[]{:S(2)}) collective-permute-start(bf16[96,2048]{1,0:T(8,128)(2,1)} %get-tuple-element.53), channel_id=1, source_target_pairs={{0,1},{1,0},{2,3},{3,2},{4,5},{5,4},{6,7},{7,6},{8,9},{9,8},{10,11... | collective-permute-start | bytes 1179656 | tf_op jit(solution)/shard_map/ppermute | solution.py:182
  77.1 7.8 %collective-permute-start.26 = (bf16[48,2048]{1,0:T(8,128)(2,1)S(1)}, bf16[48,2048]{1,0:T(8,128)(2,1)S(1)}, u32[]{:S(2)}, u32[]{:S(2)}) collective-permute-start(bf16[48,2048]{1,0:T(8,128)(2,1)S(1)} %slice.39), channel_id=1, source_target_pairs={{0,2},{1,3},{2,0},{3,1},{4,6},{5,7},{6,4},{7,5},{8,10},{9,11},{10,... | collective-permute-start | bytes 589832 | tf_op jit(solution)/shard_map/ppermute | solution.py:182
  79.0 10.8 %collective-permute-start.19 = (bf16[48,2048]{1,0:T(8,128)(2,1)S(1)}, bf16[48,2048]{1,0:T(8,128)(2,1)S(1)}, u32[]{:S(2)}, u32[]{:S(2)}) collective-permute-start(bf16[48,2048]{1,0:T(8,128)(2,1)S(1)} %slice.35), channel_id=1, source_target_pairs={{0,2},{1,3},{2,0},{3,1},{4,6},{5,7},{6,4},{7,5},{8,10},{9,11},{10,... | collective-permute-start | bytes 589832 | tf_op jit(solution)/shard_map/ppermute | solution.py:182
  79.7 25.5 %copy-start.9 = (bf16[48,2048]{1,0:T(8,128)(2,1)S(1)}, bf16[48,2048]{1,0:T(8,128)(2,1)}, u32[]{:S(2)}) copy-start(bf16[48,2048]{1,0:T(8,128)(2,1)} %get-tuple-element.35) | copy-start | bytes 589828
  79.8 13.2 %collective-permute-start.22 = (bf16[48,2048]{1,0:T(8,128)(2,1)S(1)}, bf16[48,2048]{1,0:T(8,128)(2,1)S(1)}, u32[]{:S(2)}, u32[]{:S(2)}) collective-permute-start(bf16[48,2048]{1,0:T(8,128)(2,1)S(1)} %slice.37), channel_id=1, source_target_pairs={{0,2},{1,3},{2,0},{3,1},{4,6},{5,7},{6,4},{7,5},{8,10},{9,11},{10,... | collective-permute-start | bytes 589832 | tf_op jit(solution)/shard_map/ppermute | solution.py:182
  85.0 11.9 %collective-permute-start.27 = (bf16[48,2048]{1,0:T(8,128)(2,1)S(1)}, bf16[48,2048]{1,0:T(8,128)(2,1)S(1)}, u32[]{:S(2)}, u32[]{:S(2)}) collective-permute-start(bf16[48,2048]{1,0:T(8,128)(2,1)S(1)} %add_convert_fusion.5), channel_id=1, source_target_pairs={{0,24},{4,28},{8,16},{12,20},{16,8},{20,12},{24,0},{28,4},{1,25},{... | collective-permute-start | bytes 589832 | tf_op jit(solution)/shard_map/ppermute | solution.py:182
  89.8 15.3 %collective-permute-start.24 = (bf16[48,2048]{1,0:T(8,128)(2,1)S(1)}, bf16[48,2048]{1,0:T(8,128)(2,1)S(1)}, u32[]{:S(2)}, u32[]{:S(2)}) collective-permute-start(bf16[48,2048]{1,0:T(8,128)(2,1)S(1)} %add_convert_fusion.8), channel_id=1, source_target_pairs={{0,16},{4,20},{8,24},{12,28},{16,0},{20,4},{24,8},{28,12},{1,17},{... | collective-permute-start | bytes 589832 | tf_op jit(solution)/shard_map/ppermute | solution.py:182
  93.0 12.1 %collective-permute-start.23 = (bf16[48,2048]{1,0:T(8,128)(2,1)S(1)}, bf16[48,2048]{1,0:T(8,128)(2,1)S(1)}, u32[]{:S(2)}, u32[]{:S(2)}) collective-permute-start(bf16[48,2048]{1,0:T(8,128)(2,1)S(1)} %add_convert_fusion.6), channel_id=1, source_target_pairs={{0,8},{4,12},{8,0},{12,4},{16,24},{20,28},{24,16},{28,20},{1,9},{5... | collective-permute-start | bytes 589832 | tf_op jit(solution)/shard_map/ppermute | solution.py:182
  95.4 9.8 %collective-permute-start.20 = (bf16[48,2048]{1,0:T(8,128)(2,1)S(1)}, bf16[48,2048]{1,0:T(8,128)(2,1)S(1)}, u32[]{:S(2)}, u32[]{:S(2)}) collective-permute-start(bf16[48,2048]{1,0:T(8,128)(2,1)S(1)} %slice.33), channel_id=1, source_target_pairs={{0,2},{1,3},{2,0},{3,1},{4,6},{5,7},{6,4},{7,5},{8,10},{9,11},{10,... | collective-permute-start | bytes 589832 | tf_op jit(solution)/shard_map/ppermute | solution.py:182
  (10 other events, 22.7 us)

commit v6 on v5

--- a/solution.py
+++ b/solution.py
@@ -182,41 +182,57 @@
     return lax.ppermute(value, axis, [(source, source ^ mask) for source in range(count)])
 
 
-def attention_kernel(order, index_ref, pos_ref, q_ref, before_ref, own_ref, weight_ref, *refs):
-    outputs, (cos_ref, sin_ref, mixed) = refs[:-3], refs[-3:]
+def column_of(row):
+    count = row.shape[1]
+    along = lax.broadcasted_iota(jnp.int32, (count, count), 0)
+    across = lax.broadcasted_iota(jnp.int32, (count, count), 1)
+    return jnp.sum(jnp.where(along == across, row, 0.0), axis=1, keepdims=True)
+
+
+def turned(vectors, cosine, sine):
+    wide = vectors.astype(jnp.float32)
+    wide = wide * lax.rsqrt(jnp.mean(wide * wide, axis=1, keepdims=True) + eps)
+    return (wide * cosine + pltpu.roll(wide, wide.shape[1] // 2, 1) * sine).astype(jnp.bfloat16)
+
+
+def rotation_kernel(index_ref, pos_ref, q_ref, own_ref, query_ref, key_ref, cos_ref, sin_ref):
     block, size = q_ref.shape
-    rows = block // len(order)
     pos_row = pos_ref[...].astype(jnp.float32)
-    along = lax.broadcasted_iota(jnp.int32, (block, block), 0)
-    across = lax.broadcasted_iota(jnp.int32, (block, block), 1)
-    pos_col = jnp.sum(jnp.where(along == across, pos_row, 0.0), axis=1, keepdims=True)
-    opening = jnp.sum(jnp.where(across[:1] == 0, pos_row, 0.0), axis=1, keepdims=True)
-    earlier = opening - block + along[:, :1].astype(jnp.float32)
+    pos_col = column_of(pos_row)
+    first = lax.broadcasted_iota(jnp.int32, (1, block), 1) == 0
+    opening = jnp.sum(jnp.where(first, pos_row, 0.0), axis=1, keepdims=True)
+    earlier = opening - block + lax.broadcasted_iota(jnp.int32, (block, 1), 0).astype(jnp.float32)
     lane = lax.broadcasted_iota(jnp.int32, (1, size), 1)
     lower = lane < size // 2
     phase = jnp.where(lower, 0.0, math.pi / 2)
     turn_of = jnp.where(lower, lane, lane - size // 2).astype(jnp.float32)
     spectrum = jnp.exp(turn_of * (-2.0 * math.log(theta) / size))
-    for half, at in enumerate((earlier, pos_col)):
+
+    def table(at):
         turn = jnp.cos(at * spectrum - phase)
         swap = pltpu.roll(turn, size // 2, 1)
-        cos_ref[half * block : (half + 1) * block, :] = jnp.where(lower, turn, swap)
-        sin_ref[half * block : (half + 1) * block, :] = jnp.where(lower, -swap, turn)
-
-    def turned(vectors, start):
-        wide = vectors.astype(jnp.float32)
-        wide = wide * lax.rsqrt(jnp.mean(wide * wide, axis=1, keepdims=True) + eps)
-        cosine, sine = cos_ref[start : start + block, :], sin_ref[start : start + block, :]
-        return (wide * cosine + pltpu.roll(wide, size // 2, 1) * sine).astype(jnp.bfloat16)
-
+        return jnp.where(lower, turn, swap), jnp.where(lower, -swap, turn)
+
+    cosine, sine = table(pos_col)
+    query_ref[...] = turned(q_ref[...], cosine, sine)
+    key_ref[...] = turned(own_ref[:, :size], cosine, sine)
+    cos_ref[...], sin_ref[...] = table(earlier)
+
+
+def attention_kernel(order, index_ref, pos_ref, query_ref, key_ref, cos_ref, sin_ref, before_ref, own_ref, *refs):
+    weight_ref, outputs, mixed = refs[0], refs[1:-1], refs[-1]
+    block, size = query_ref.shape
+    rows = block // len(order)
+    pos_col = column_of(pos_ref[...].astype(jnp.float32))
     query_at = lax.broadcasted_iota(jnp.int32, (block, 2 * block), 0)
     key_at = lax.broadcasted_iota(jnp.int32, (block, 2 * block), 1) - block
     allowed = (key_at <= query_at) & (key_at >= query_at - pos_col.astype(jnp.int32))
-    keys = jnp.concatenate([turned(before_ref[:, :size], 0), turned(own_ref[:, :size], block)], axis=0)
+    keys = jnp.concatenate(
+        [turned(before_ref[:, :size], cos_ref[...], sin_ref[...]), key_ref[...]], axis=0
+    )
     values = jnp.concatenate([before_ref[:, size:], own_ref[:, size:]], axis=0)
-    query = turned(q_ref[...], block)
     scores = lax.dot_general(
-        query, keys, (((1,), (1,)), ((), ())), preferred_element_type=jnp.float32
+        query_ref[...], keys, (((1,), (1,)), ((), ())), preferred_element_type=jnp.float32
     ) * (1.0 / math.sqrt(size))
     raw = jnp.where(allowed, jnp.exp(scores), 0.0)
     weights = (raw / jnp.sum(raw, axis=1, keepdims=True)).astype(jnp.bfloat16)
@@ -275,6 +291,7 @@
 
 HBM = pl.BlockSpec(memory_space=pltpu.HBM)
 GRANT = 60 * 1024 * 1024
+LEAN_GRANT = 24 * 1024 * 1024
 
 
 def fetching(kernel, count, stored, index_ref, *refs):
@@ -304,7 +321,7 @@
         copy.wait()
 
 
-def small_kernel(kernel, out_shape, inputs, stored, scratch=(), flops=0):
+def small_kernel(kernel, out_shape, inputs, stored, scratch=(), moved=0):
     held = [pltpu.VMEM(array.shape, array.dtype) for array in inputs[1:]]
     sent = [pltpu.VMEM(leaf.shape, leaf.dtype) for leaf, far in zip(out_shape, stored) if far]
     return pl.pallas_call(
@@ -320,7 +337,7 @@
             *scratch,
         ],
         compiler_params=pltpu.CompilerParams(vmem_limit_bytes=GRANT),
-        cost_estimate=pl.CostEstimate(flops=0, bytes_accessed=0, transcendentals=0),
+        cost_estimate=pl.CostEstimate(flops=0, bytes_accessed=moved, transcendentals=0),
     )(*inputs)
 
 
@@ -364,7 +381,7 @@
             jax.ShapeDtypeStruct((parts * rows, inner), jnp.bfloat16),
             jax.ShapeDtypeStruct((parts * rows, total - width), jnp.bfloat16),
         ),
-        in_specs=[HBM] * (parts + 2),
+        in_specs=[pl.BlockSpec(memory_space=pl.ANY)] * (parts + 2),
         out_specs=(VMEM, VMEM),
         scratch_shapes=[
             pltpu.VMEM(own_in.shape, own_in.dtype),
@@ -372,33 +389,28 @@
             pltpu.VMEM((parts * rows, total), jnp.bfloat16),
             pltpu.SemaphoreType.DMA((parts + 2,)),
         ],
-        compiler_params=pltpu.CompilerParams(vmem_limit_bytes=GRANT),
+        compiler_params=pltpu.CompilerParams(vmem_limit_bytes=LEAN_GRANT),
         cost_estimate=pl.CostEstimate(flops=0, bytes_accessed=9 << 20, transcendentals=0),
     )(own_in, other_in, *tokens)
 
 
 def output_kernel(index_ref, inner_ref, spare_ref, own_ref, other_ref, *refs):
-    outputs, (inner, spare, weight, ready, arrived, left) = refs[:-6], refs[-6:]
+    outputs, (inner, spare, weight, arrived) = refs[:-4], refs[-4:]
     depth = own_ref.shape[0]
     targets = [weight.at[pl.ds(0, depth), :], weight.at[pl.ds(depth, depth), :], inner, spare]
     for copy in fetched([own_ref, other_ref, inner_ref, spare_ref], targets, arrived):
         copy.wait()
     part = outputs[0].shape[0]
     step = 4 * part
-    copies = []
     for start in reversed(range(0, inner.shape[0], step)):
         block = slice(start, start + step)
         chosen = spare[block, :].astype(jnp.float32)
         picked = lax.broadcasted_iota(jnp.int32, chosen.shape, 1) == index_ref[0]
         gate = jnp.sum(jnp.where(picked, chosen, 0.0), axis=1, keepdims=True)
         out = jnp.dot(inner[block, :], weight[...], preferred_element_type=jnp.float32)
-        ready[block, :] = (out * gate).astype(jnp.bfloat16)
-        for i in reversed(range(start // part, (start + step) // part)):
-            source = ready.at[pl.ds(i * part, part), :]
-            copies.append(pltpu.make_async_copy(source, outputs[i], left.at[i]))
-            copies[-1].start()
-    for copy in copies:
-        copy.wait()
+        out = (out * gate).astype(jnp.bfloat16)
+        for i in range(start // part, (start + step) // part):
+            outputs[i][...] = out[i * part - start : (i + 1) * part - start]
 
 
 def output_blocks(count, index, inner, spare, own_out, other_out):
@@ -408,17 +420,15 @@
     flat = pl.pallas_call(
         output_kernel,
         out_shape=(half,) * (2 * count),
-        in_specs=[SMEM] + [HBM] * 4,
-        out_specs=(HBM,) * (2 * count),
+        in_specs=[SMEM] + [pl.BlockSpec(memory_space=pl.ANY)] * 4,
+        out_specs=(VMEM,) * (2 * count),
         scratch_shapes=[
             pltpu.VMEM(inner.shape, inner.dtype),
             pltpu.VMEM(spare.shape, spare.dtype),
             pltpu.VMEM((inner.shape[1], width), jnp.bfloat16),
-            pltpu.VMEM((rows, width), jnp.bfloat16),
             pltpu.SemaphoreType.DMA((4,)),
-            pltpu.SemaphoreType.DMA((2 * count,)),
         ],
-        compiler_params=pltpu.CompilerParams(vmem_limit_bytes=GRANT),
+        compiler_params=pltpu.CompilerParams(vmem_limit_bytes=LEAN_GRANT),
         cost_estimate=pl.CostEstimate(flops=0, bytes_accessed=0, transcendentals=0),
     )(index, inner, spare, own_out, other_out)
     return [flat[2 * k : 2 * k + 2] for k in range(count)]
@@ -471,15 +481,22 @@
     owners = [0]
     for bit in bits:
         owners = owners + [owner ^ bit for owner in owners]
-    table = pltpu.VMEM((2 * block_rows, head_dim), jnp.float32)
+    turned_head = jax.ShapeDtypeStruct((block_rows, head_dim), jnp.bfloat16)
+    table = jax.ShapeDtypeStruct((block_rows, head_dim), jnp.float32)
+    rotated = small_kernel(
+        rotation_kernel,
+        (turned_head, turned_head, table, table),
+        (index, positions[None, :], queries, kv_own),
+        (True,) * 4,
+        moved=20 << 20,
+    )
     term = jax.ShapeDtypeStruct((token_rows, width), jnp.bfloat16)
     terms = small_kernel(
         functools.partial(attention_kernel, tuple(owners)),
         (term,) * exp_count,
-        (index, positions[None, :], queries, before, kv_own, out_weight),
+        (index, positions[None, :], *rotated, before, kv_own, out_weight),
         (True,) * exp_count,
-        (table, table, pltpu.VMEM((block_rows, head_dim), jnp.bfloat16)),
-        0,
+        (pltpu.VMEM((block_rows, head_dim), jnp.bfloat16),),
     )
     terms = [terms[0]] + [swapped(term, "exp", owner) for term, owner in zip(terms[1:], owners[1:])]
     lanes = -(-experts_total // 128) * 128
@@ -500,8 +517,6 @@
             rollout_logits.T,
         ),
         (False, True, False),
-        (),
-        2 * token_rows * width * experts_total,
     )
     router_kl = router_kl[0]
     crossed, passed = {}, None

time: 106 us -> 103 us (0.972)
  Pallas kernels: 19.3 us -> 18.2 us
    ppermute x1, waiting for transfers between devices: 2.19 us -> 0.01 us  [passed_along(): lax.ppermute(value, axis, [(source, source + steps) for source in range(i...]
    pallas_call x2 -> x3, Pallas kernels: 7.1 us -> 9.08 us  [small_kernel(): pl.pallas_call(functools.partial(fetching, kernel, len(held), stored), ou...]
    ppermute x27, waiting for transfers between devices: 38.8 us -> 40.6 us  [swapped(): lax.ppermute(value, axis, [(source, source ^ mask) for source in range(co...]
    pallas_call x1, Pallas kernels: 4.64 us -> 3.02 us  [output_blocks(): pl.pallas_call(output_kernel, out_shape=(half,) * (2 * count), in_specs=[...]
    pallas_call x1, Pallas kernels: 7.61 us -> 6.13 us  [hidden_blocks(): pl.pallas_call(functools.partial(hidden_kernel, width), out_shape=(jax.Sh...]
    unnamed x31 -> x19, local copies, waits for them, and re-layouts: 2.48 us -> 2.32 us
  transfers between devices with their start and end apart: 28 -> 28, of which waited for: 15 -> 14; matrix products, arithmetic and copies ran while one was open for 3% -> 2% of each run, Pallas kernels for 10% -> 12%
where the time goes in v6:
time: 103 us; the launch traced here: 102 us
  waiting for transfers between devices  40.6 us (39%)
  starting transfers between devices  37.9 us (37%)
  Pallas kernels  18.2 us (18%)
  local copies, waits for them, and re-layouts  3.39 us (3%)
  other arithmetic  1.41 us (1%)
    ppermute x27, waiting for transfers between devices, swapped(): lax.ppermute(value, axis, [(source, source ^ mask) for source in range(co...  40.6 us
    ppermute x27, starting transfers between devices, swapped(): lax.ppermute(value, axis, [(source, source ^ mask) for source in range(co...  33.1 us
    pallas_call x3, Pallas kernels, small_kernel(): pl.pallas_call(functools.partial(fetching, kernel, len(held), stored), ou...  9.08 us
    pallas_call x1, Pallas kernels, hidden_blocks(): pl.pallas_call(functools.partial(hidden_kernel, width), out_shape=(jax.Sh...  6.13 us
    ppermute x1, starting transfers between devices, passed_along(): lax.ppermute(value, axis, [(source, source + steps) for source in range(i...  4.88 us
    pallas_call x1, Pallas kernels, output_blocks(): pl.pallas_call(output_kernel, out_shape=(half,) * (2 * count), in_specs=[...  3.02 us
    unnamed x19, local copies, waits for them, and re-layouts  2.32 us
  transfers between devices with their start and end apart: 28, of which 14 were waited for; matrix products, arithmetic and copies ran while one was open for 2% of the time, Pallas kernels for 12%

profile of v6, /device:TPU:0, one launch (start us, length us, event | category | flops | bytes accessed | tf_op | source)
XLA Modules:
  0.0 102.5 jit_solution(631699535871603440)
XLA Ops:
  0.7 0.9 constant_dynamic-slice_fusion
  1.6 4.9 %collective-permute-start = (bf16[192,256]{1,0:T(8,128)(2,1)S(1)}, bf16[192,256]{1,0:T(8,128)(2,1)S(1)}, u32[]{:S(2)}, u32[]{:S(2)}) collective-permute-start(bf16[192,256]{1,0:T(8,128)(2,1)S(1)} %pad_maximum_fusion.1.refs_2_.refs_6_), channel_id=1, source_target_pairs={{0,4},{4,8},{8,12},{12,16},{16,20},{20,24},{24,28},{1,5},{5,9},{9,... | collective-permute-start | bytes 294920 | tf_op jit(solution)/shard_map/ppermute | solution.py:19
  6.5 2.5 %shard_map.131 = (bf16[192,128]{1,0:T(8,128)(2,1)}, bf16[192,128]{1,0:T(8,128)(2,1)}, f32[192,128]{1,0:T(8,128)}, f32[192,128]{1,0:T(8,128)}) custom-call(s32[1]{0:T(128)} %bitcast.index_ref, s32[1,192]{1,0:T(1,128)} %bitcast.18, bf16[192,128]{1,0:T(8,128)(2,1)} %refs_1_.1, bf16[192,256]{1,0:T(8,128)(2,1)} %copy-done.2), custom_call_target="tpu_custom_call" | custom-call | bytes 20971520 | tf_op jit(solution)/shard_map/pallas_call | solution.py:327
  9.7 3.2 %shard_map.132 = (bf16[48,2048]{1,0:T(8,128)(2,1)}, bf16[48,2048]{1,0:T(8,128)(2,1)}, bf16[48,2048]{1,0:T(8,128)(2,1)}, bf16[48,2048]{1,0:T(8,128)(2,1)}) custom-call(s32[1]{0:T(128)} %bitcast.index_ref, s32[1,192]{1,0:T(1,128)} %bitcast.19, bf16[192,128]{1,0:T(8,128)(2,1)} %get-tuple-element.34.refs_1_, bf16[192,128]{1,0:T(8,128)(2,1)} %get-tuple-element.35.refs_2_, ...), custom_call_target="tpu_custom_call" | custom-call | tf_op jit(solution)/shard_map/pallas_call | solution.py:327
  12.9 1.6 %collective-permute-start.1 = (bf16[48,2048]{1,0:T(8,128)(2,1)}, bf16[48,2048]{1,0:T(8,128)(2,1)S(1)}, u32[]{:S(2)}, u32[]{:S(2)}) collective-permute-start(bf16[48,2048]{1,0:T(8,128)(2,1)} %get-tuple-element.40), channel_id=1, source_target_pairs={{0,2},{1,3},{2,0},{3,1},{4,6},{5,7},{6,4},{7,5},{8,10},{9,11},{10,... | collective-permute-start | bytes 589832 | tf_op jit(solution)/shard_map/ppermute | solution.py:182
  15.1 2.0 %collective-permute-start.7 = (bf16[2048,384]{1,0:T(8,128)(2,1)S(1)}, bf16[2048,384]{1,0:T(8,128)(2,1)}, u32[]{:S(2)}, u32[]{:S(2)}) collective-permute-start(bf16[2048,384]{1,0:T(8,128)(2,1)S(1)} %bitcast.10), channel_id=1, source_target_pairs={{0,4},{4,0},{8,12},{12,8},{16,20},{20,16},{24,28},{28,24},{1,5},{5... | collective-permute-start | bytes 4718600 | tf_op jit(solution)/shard_map/ppermute | solution.py:182
  17.2 3.8 %collective-permute-done.1.refs_1_ = bf16[48,2048]{1,0:T(8,128)(2,1)S(1)} collective-permute-done((bf16[48,2048]{1,0:T(8,128)(2,1)}, bf16[48,2048]{1,0:T(8,128)(2,1)S(1)}, u32[]{:S(2)}, u32[]{:S(2)}) %collective-permute-start.1) | collective-permute-done | bytes 196640 | tf_op jit(solution)/shard_map/ppermute | solution.py:182
  21.0 1.9 %collective-permute-done.3.refs_3_ = bf16[48,2048]{1,0:T(8,128)(2,1)S(1)} collective-permute-done((bf16[48,2048]{1,0:T(8,128)(2,1)}, bf16[48,2048]{1,0:T(8,128)(2,1)S(1)}, u32[]{:S(2)}, u32[]{:S(2)}) %collective-permute-start.3) | collective-permute-done | bytes 196640 | tf_op jit(solution)/shard_map/ppermute | solution.py:182
  23.6 3.3 %shard_map.133 = (bf16[48,2048]{1,0:T(8,128)(2,1)}, bf16[48,2176]{1,0:T(8,128)(2,1)}, f32[1,48]{1,0:T(1,128)}) custom-call(s32[1]{0:T(128)} %bitcast.index_ref, bf16[48,2048]{1,0:T(8,128)(2,1)} %get-tuple-element.39.refs_0_, bf16[48,2048]{1,0:T(8,128)(2,1)} %copy-done.4, bf16[48,2048]{1,0:T(8,128)(2,1)} %copy-done.5, bf16[48,2048]{1,0:T(8,128)(2,1)} %copy-done.6, ...), custom_call_target="tpu_custom_call" | custom-call | tf_op jit(solution)/shard_map/pallas_call | solution.py:327
  26.9 1.0 collective-permute-start.4
  27.9 2.9 %collective-permute-start.5 = (bf16[48,2176]{1,0:T(8,128)(2,1)}, bf16[48,2176]{1,0:T(8,128)(2,1)S(1)}, u32[]{:S(2)}, u32[]{:S(2)}) collective-permute-start(bf16[48,2176]{1,0:T(8,128)(2,1)} %get-tuple-element.44), channel_id=1, source_target_pairs={{0,16},{4,20},{8,24},{12,28},{16,0},{20,4},{24,8},{28,12},{1,17},{... | collective-permute-start | bytes 626696 | tf_op jit(solution)/shard_map/ppermute | solution.py:182
  30.8 1.6 %collective-permute-start.9 = (bf16[48,2176]{1,0:T(8,128)(2,1)}, bf16[48,2176]{1,0:T(8,128)(2,1)S(1)}, u32[]{:S(2)}, u32[]{:S(2)}) collective-permute-start(bf16[48,2176]{1,0:T(8,128)(2,1)} %get-tuple-element.44), channel_id=1, source_target_pairs={{0,8},{4,12},{8,0},{12,4},{16,24},{20,28},{24,16},{28,20},{1,9},{5... | collective-permute-start | bytes 626696 | tf_op jit(solution)/shard_map/ppermute | solution.py:182
  32.4 1.0 constant_dynamic-update-slice_fusion.1
  33.4 1.7 %collective-permute-done.4 = bf16[48,2176]{1,0:T(8,128)(2,1)S(1)} collective-permute-done((bf16[48,2176]{1,0:T(8,128)(2,1)}, bf16[48,2176]{1,0:T(8,128)(2,1)S(1)}, u32[]{:S(2)}, u32[]{:S(2)}) %collective-permute-start.4) | collective-permute-done | bytes 208928 | tf_op jit(solution)/shard_map/ppermute | solution.py:182
  35.1 5.5 %collective-permute-done.5 = bf16[48,2176]{1,0:T(8,128)(2,1)S(1)} collective-permute-done((bf16[48,2176]{1,0:T(8,128)(2,1)}, bf16[48,2176]{1,0:T(8,128)(2,1)S(1)}, u32[]{:S(2)}, u32[]{:S(2)}) %collective-permute-start.5) | collective-permute-done | bytes 208928 | tf_op jit(solution)/shard_map/ppermute | solution.py:182
  40.6 2.3 %collective-permute-start.6 = (bf16[48,2176]{1,0:T(8,128)(2,1)S(1)}, bf16[48,2176]{1,0:T(8,128)(2,1)S(1)}, u32[]{:S(2)}, u32[]{:S(2)}) collective-permute-start(bf16[48,2176]{1,0:T(8,128)(2,1)S(1)} %collective-permute-done.5), channel_id=1, source_target_pairs={{0,2},{1,3},{2,0},{3,1},{4,6},{5,7},{6,4},{7,5},{8,10},{9,11},{10,... | collective-permute-start | bytes 626696 | tf_op jit(solution)/shard_map/ppermute | solution.py:182
  42.9 1.0 %collective-permute-start.13 = (bf16[48,2176]{1,0:T(8,128)(2,1)S(1)}, bf16[48,2176]{1,0:T(8,128)(2,1)S(1)}, u32[]{:S(2)}, u32[]{:S(2)}) collective-permute-start(bf16[48,2176]{1,0:T(8,128)(2,1)S(1)} %collective-permute-done.5), channel_id=1, source_target_pairs={{0,8},{4,12},{8,0},{12,4},{16,24},{20,28},{24,16},{28,20},{1,9},{5... | collective-permute-start | bytes 626696 | tf_op jit(solution)/shard_map/ppermute | solution.py:182
  44.1 4.5 %collective-permute-done.6 = bf16[48,2176]{1,0:T(8,128)(2,1)S(1)} collective-permute-done((bf16[48,2176]{1,0:T(8,128)(2,1)S(1)}, bf16[48,2176]{1,0:T(8,128)(2,1)S(1)}, u32[]{:S(2)}, u32[]{:S(2)}) %collective-permute-start.6) | collective-permute-done | bytes 208928 | tf_op jit(solution)/shard_map/ppermute | solution.py:182
  48.5 1.5 %collective-permute-start.10 = (bf16[48,2176]{1,0:T(8,128)(2,1)S(1)}, bf16[48,2176]{1,0:T(8,128)(2,1)S(1)}, u32[]{:S(2)}, u32[]{:S(2)}) collective-permute-start(bf16[48,2176]{1,0:T(8,128)(2,1)S(1)} %collective-permute-done.9), channel_id=1, source_target_pairs={{0,2},{1,3},{2,0},{3,1},{4,6},{5,7},{6,4},{7,5},{8,10},{9,11},{10,... | collective-permute-start | bytes 626696 | tf_op jit(solution)/shard_map/ppermute | solution.py:182
  50.1 1.2 %collective-permute-start.14 = (bf16[48,2176]{1,0:T(8,128)(2,1)S(1)}, bf16[48,2176]{1,0:T(8,128)(2,1)S(1)}, u32[]{:S(2)}, u32[]{:S(2)}) collective-permute-start(bf16[48,2176]{1,0:T(8,128)(2,1)S(1)} %collective-permute-done.6), channel_id=1, source_target_pairs={{0,8},{4,12},{8,0},{12,4},{16,24},{20,28},{24,16},{28,20},{1,9},{5... | collective-permute-start | bytes 626696 | tf_op jit(solution)/shard_map/ppermute | solution.py:182
  51.3 4.2 %collective-permute-done.10 = bf16[48,2176]{1,0:T(8,128)(2,1)S(1)} collective-permute-done((bf16[48,2176]{1,0:T(8,128)(2,1)S(1)}, bf16[48,2176]{1,0:T(8,128)(2,1)S(1)}, u32[]{:S(2)}, u32[]{:S(2)}) %collective-permute-start.10) | collective-permute-done | bytes 208928 | tf_op jit(solution)/shard_map/ppermute | solution.py:182
  58.9 6.1 %shard_map.134 = (bf16[768,384]{1,0:T(8,128)(2,1)S(1)}, bf16[768,128]{1,0:T(8,128)(2,1)S(1)}) custom-call(bf16[2048,384]{1,0:T(8,128)(2,1)S(1)} %bitcast.11, bf16[2048,384]{1,0:T(8,128)(2,1)} %collective-permute-done.7.refs_1_, bf16[96,2176]{1,0:T(8,128)(2,1)S(1)} %constant_dynamic-update-slice_fusion.refs_2_, ...), custom_call_target="tpu_custom_call" | custom-call | bytes 9437184 | tf_op jit(solution)/shard_map/pallas_call | solution.py:378
  65.0 3.6 %collective-permute-done.16.other_ref = bf16[192,2048]{1,0:T(8,128)(2,1)} collective-permute-done((bf16[192,2048]{1,0:T(8,128)(2,1)}, bf16[192,2048]{1,0:T(8,128)(2,1)}, u32[]{:S(2)}, u32[]{:S(2)}) %collective-permute-start.16) | collective-permute-done | bytes 786464 | tf_op jit(solution)/shard_map/ppermute | solution.py:182
  68.7 3.0 %shard_map.135 = (bf16[96,2048]{1,0:T(8,128)(2,1)S(1)}, bf16[96,2048]{1,0:T(8,128)(2,1)S(1)}, bf16[96,2048]{1,0:T(8,128)(2,1)S(1)}, bf16[96,2048]{1,0:T(8,128)(2...) custom-call(s32[1]{0:T(128)} %bitcast.8.index_ref, ...), custom_call_target="tpu_custom_call" | custom-call | tf_op jit(solution)/shard_map/pallas_call | solution.py:420
  73.6 1.6 %collective-permute-start.26 = (bf16[48,2048]{1,0:T(8,128)(2,1)S(1)}, bf16[48,2048]{1,0:T(8,128)(2,1)S(1)}, u32[]{:S(2)}, u32[]{:S(2)}) collective-permute-start(bf16[48,2048]{1,0:T(8,128)(2,1)S(1)} %slice.39), channel_id=1, source_target_pairs={{0,2},{1,3},{2,0},{3,1},{4,6},{5,7},{6,4},{7,5},{8,10},{9,11},{10,... | collective-permute-start | bytes 589832 | tf_op jit(solution)/shard_map/ppermute | solution.py:182
  76.4 1.3 %collective-permute-start.22 = (bf16[48,2048]{1,0:T(8,128)(2,1)S(1)}, bf16[48,2048]{1,0:T(8,128)(2,1)S(1)}, u32[]{:S(2)}, u32[]{:S(2)}) collective-permute-start(bf16[48,2048]{1,0:T(8,128)(2,1)S(1)} %slice.37), channel_id=1, source_target_pairs={{0,2},{1,3},{2,0},{3,1},{4,6},{5,7},{6,4},{7,5},{8,10},{9,11},{10,... | collective-permute-start | bytes 589832 | tf_op jit(solution)/shard_map/ppermute | solution.py:182
  77.7 3.7 %collective-permute-done.26 = bf16[48,2048]{1,0:T(8,128)(2,1)S(1)} collective-permute-done((bf16[48,2048]{1,0:T(8,128)(2,1)S(1)}, bf16[48,2048]{1,0:T(8,128)(2,1)S(1)}, u32[]{:S(2)}, u32[]{:S(2)}) %collective-permute-start.26) | collective-permute-done | bytes 196640 | tf_op jit(solution)/shard_map/ppermute | solution.py:182
  81.5 4.8 %collective-permute-start.27 = (bf16[48,2048]{1,0:T(8,128)(2,1)S(1)}, bf16[48,2048]{1,0:T(8,128)(2,1)S(1)}, u32[]{:S(2)}, u32[]{:S(2)}) collective-permute-start(bf16[48,2048]{1,0:T(8,128)(2,1)S(1)} %add_convert_fusion.5), channel_id=1, source_target_pairs={{0,24},{4,28},{8,16},{12,20},{16,8},{20,12},{24,0},{28,4},{1,25},{... | collective-permute-start | bytes 589832 | tf_op jit(solution)/shard_map/ppermute | solution.py:182
  86.3 3.1 %collective-permute-start.24 = (bf16[48,2048]{1,0:T(8,128)(2,1)S(1)}, bf16[48,2048]{1,0:T(8,128)(2,1)S(1)}, u32[]{:S(2)}, u32[]{:S(2)}) collective-permute-start(bf16[48,2048]{1,0:T(8,128)(2,1)S(1)} %add_convert_fusion.8), channel_id=1, source_target_pairs={{0,16},{4,20},{8,24},{12,28},{16,0},{20,4},{24,8},{28,12},{1,17},{... | collective-permute-start | bytes 589832 | tf_op jit(solution)/shard_map/ppermute | solution.py:182
  89.5 2.3 %collective-permute-start.23 = (bf16[48,2048]{1,0:T(8,128)(2,1)S(1)}, bf16[48,2048]{1,0:T(8,128)(2,1)S(1)}, u32[]{:S(2)}, u32[]{:S(2)}) collective-permute-start(bf16[48,2048]{1,0:T(8,128)(2,1)S(1)} %add_convert_fusion.6), channel_id=1, source_target_pairs={{0,8},{4,12},{8,0},{12,4},{16,24},{20,28},{24,16},{28,20},{1,9},{5... | collective-permute-start | bytes 589832 | tf_op jit(solution)/shard_map/ppermute | solution.py:182
  91.9 1.5 %collective-permute-start.20 = (bf16[48,2048]{1,0:T(8,128)(2,1)S(1)}, bf16[48,2048]{1,0:T(8,128)(2,1)S(1)}, u32[]{:S(2)}, u32[]{:S(2)}) collective-permute-start(bf16[48,2048]{1,0:T(8,128)(2,1)S(1)} %slice.33), channel_id=1, source_target_pairs={{0,2},{1,3},{2,0},{3,1},{4,6},{5,7},{6,4},{7,5},{8,10},{9,11},{10,... | collective-permute-start | bytes 589832 | tf_op jit(solution)/shard_map/ppermute | solution.py:182
  93.4 8.3 %collective-permute-done.24 = bf16[48,2048]{1,0:T(8,128)(2,1)S(1)} collective-permute-done((bf16[48,2048]{1,0:T(8,128)(2,1)S(1)}, bf16[48,2048]{1,0:T(8,128)(2,1)S(1)}, u32[]{:S(2)}, u32[]{:S(2)}) %collective-permute-start.24) | collective-permute-done | bytes 196640 | tf_op jit(solution)/shard_map/ppermute | solution.py:182
  (66 shorter events, 9.6 us)
Async XLA Ops:
  0.6 14.5 %copy-start = (bf16[1,1,2048,384]{3,2,1,0:T(8,128)(2,1)S(1)}, bf16[1,1,2048,384]{3,2,1,0:T(8,128)(2,1)}, u32[]{:S(2)}) copy-start(bf16[1,1,2048,384]{3,2,1,0:T(8,128)(2,1)} %param.21) | copy-start | bytes 4718596
  1.6 4.9 %copy-start.2 = (bf16[192,256]{1,0:T(8,128)(2,1)}, bf16[192,256]{1,0:T(8,128)(2,1)S(1)}, u32[]{:S(2)}) copy-start(bf16[192,256]{1,0:T(8,128)(2,1)S(1)} %pad_maximum_fusion.1.refs_2_.refs_6_) | copy-start | bytes 294916
  1.6 7.5 %collective-permute-start = (bf16[192,256]{1,0:T(8,128)(2,1)S(1)}, bf16[192,256]{1,0:T(8,128)(2,1)S(1)}, u32[]{:S(2)}, u32[]{:S(2)}) collective-permute-start(bf16[192,256]{1,0:T(8,128)(2,1)S(1)} %pad_maximum_fusion.1.refs_2_.refs_6_), channel_id=1, source_target_pairs={{0,4},{4,8},{8,12},{12,16},{16,20},{20,24},{24,28},{1,5},{5,9},{9,... | collective-permute-start | bytes 294920 | tf_op jit(solution)/shard_map/ppermute | solution.py:19
  12.9 8.1 %collective-permute-start.1 = (bf16[48,2048]{1,0:T(8,128)(2,1)}, bf16[48,2048]{1,0:T(8,128)(2,1)S(1)}, u32[]{:S(2)}, u32[]{:S(2)}) collective-permute-start(bf16[48,2048]{1,0:T(8,128)(2,1)} %get-tuple-element.40), channel_id=1, source_target_pairs={{0,2},{1,3},{2,0},{3,1},{4,6},{5,7},{6,4},{7,5},{8,10},{9,11},{10,... | collective-permute-start | bytes 589832 | tf_op jit(solution)/shard_map/ppermute | solution.py:182
  14.5 6.6 %collective-permute-start.2 = (bf16[48,2048]{1,0:T(8,128)(2,1)}, bf16[48,2048]{1,0:T(8,128)(2,1)S(1)}, u32[]{:S(2)}, u32[]{:S(2)}) collective-permute-start(bf16[48,2048]{1,0:T(8,128)(2,1)} %get-tuple-element.41), channel_id=1, source_target_pairs={{0,1},{1,0},{2,3},{3,2},{4,5},{5,4},{6,7},{7,6},{8,9},{9,8},{10,11... | collective-permute-start | bytes 589832 | tf_op jit(solution)/shard_map/ppermute | solution.py:182
  14.5 8.4 %collective-permute-start.3 = (bf16[48,2048]{1,0:T(8,128)(2,1)}, bf16[48,2048]{1,0:T(8,128)(2,1)S(1)}, u32[]{:S(2)}, u32[]{:S(2)}) collective-permute-start(bf16[48,2048]{1,0:T(8,128)(2,1)} %get-tuple-element.42), channel_id=1, source_target_pairs={{0,3},{1,2},{2,1},{3,0},{4,7},{5,6},{6,5},{7,4},{8,11},{9,10},{10,... | collective-permute-start | bytes 589832 | tf_op jit(solution)/shard_map/ppermute | solution.py:182
  15.1 41.3 %collective-permute-start.7 = (bf16[2048,384]{1,0:T(8,128)(2,1)S(1)}, bf16[2048,384]{1,0:T(8,128)(2,1)}, u32[]{:S(2)}, u32[]{:S(2)}) collective-permute-start(bf16[2048,384]{1,0:T(8,128)(2,1)S(1)} %bitcast.10), channel_id=1, source_target_pairs={{0,4},{4,0},{8,12},{12,8},{16,20},{20,16},{24,28},{28,24},{1,5},{5... | collective-permute-start | bytes 4718600 | tf_op jit(solution)/shard_map/ppermute | solution.py:182
  17.2 51.5 %collective-permute-start.16 = (bf16[192,2048]{1,0:T(8,128)(2,1)}, bf16[192,2048]{1,0:T(8,128)(2,1)}, u32[]{:S(2)}, u32[]{:S(2)}) collective-permute-start(bf16[192,2048]{1,0:T(8,128)(2,1)} %bitcast.12), channel_id=1, source_target_pairs={{0,4},{4,0},{8,12},{12,8},{16,20},{20,16},{24,28},{28,24},{1,5},{5... | collective-permute-start | bytes 2359304 | tf_op jit(solution)/shard_map/ppermute | solution.py:182
  26.9 8.2 %collective-permute-start.4 = (bf16[48,2176]{1,0:T(8,128)(2,1)}, bf16[48,2176]{1,0:T(8,128)(2,1)S(1)}, u32[]{:S(2)}, u32[]{:S(2)}) collective-permute-start(bf16[48,2176]{1,0:T(8,128)(2,1)} %get-tuple-element.44), channel_id=1, source_target_pairs={{0,2},{1,3},{2,0},{3,1},{4,6},{5,7},{6,4},{7,5},{8,10},{9,11},{10,... | collective-permute-start | bytes 626696 | tf_op jit(solution)/shard_map/ppermute | solution.py:182
  27.9 12.7 %collective-permute-start.5 = (bf16[48,2176]{1,0:T(8,128)(2,1)}, bf16[48,2176]{1,0:T(8,128)(2,1)S(1)}, u32[]{:S(2)}, u32[]{:S(2)}) collective-permute-start(bf16[48,2176]{1,0:T(8,128)(2,1)} %get-tuple-element.44), channel_id=1, source_target_pairs={{0,16},{4,20},{8,24},{12,28},{16,0},{20,4},{24,8},{28,12},{1,17},{... | collective-permute-start | bytes 626696 | tf_op jit(solution)/shard_map/ppermute | solution.py:182
  30.8 13.2 %collective-permute-start.9 = (bf16[48,2176]{1,0:T(8,128)(2,1)}, bf16[48,2176]{1,0:T(8,128)(2,1)S(1)}, u32[]{:S(2)}, u32[]{:S(2)}) collective-permute-start(bf16[48,2176]{1,0:T(8,128)(2,1)} %get-tuple-element.44), channel_id=1, source_target_pairs={{0,8},{4,12},{8,0},{12,4},{16,24},{20,28},{24,16},{28,20},{1,9},{5... | collective-permute-start | bytes 626696 | tf_op jit(solution)/shard_map/ppermute | solution.py:182
  40.6 8.0 %collective-permute-start.6 = (bf16[48,2176]{1,0:T(8,128)(2,1)S(1)}, bf16[48,2176]{1,0:T(8,128)(2,1)S(1)}, u32[]{:S(2)}, u32[]{:S(2)}) collective-permute-start(bf16[48,2176]{1,0:T(8,128)(2,1)S(1)} %collective-permute-done.5), channel_id=1, source_target_pairs={{0,2},{1,3},{2,0},{3,1},{4,6},{5,7},{6,4},{7,5},{8,10},{9,11},{10,... | collective-permute-start | bytes 626696 | tf_op jit(solution)/shard_map/ppermute | solution.py:182
  42.9 7.2 %collective-permute-start.13 = (bf16[48,2176]{1,0:T(8,128)(2,1)S(1)}, bf16[48,2176]{1,0:T(8,128)(2,1)S(1)}, u32[]{:S(2)}, u32[]{:S(2)}) collective-permute-start(bf16[48,2176]{1,0:T(8,128)(2,1)S(1)} %collective-permute-done.5), channel_id=1, source_target_pairs={{0,8},{4,12},{8,0},{12,4},{16,24},{20,28},{24,16},{28,20},{1,9},{5... | collective-permute-start | bytes 626696 | tf_op jit(solution)/shard_map/ppermute | solution.py:182
  44.0 12.9 %collective-permute-start.8 = (bf16[96,2176]{1,0:T(8,128)(2,1)S(1)}, bf16[96,2176]{1,0:T(8,128)(2,1)}, u32[]{:S(2)}, u32[]{:S(2)}) collective-permute-start(bf16[96,2176]{1,0:T(8,128)(2,1)S(1)} %constant_dynamic-update-slice_fusion.refs_2_), channel_id=1, source_target_pairs={{0,1},{1,0},{2,3},{3,2},{4,5},{5,4},{6,7},{7,6},{8,9},{9,8},{10,11... | collective-permute-start | bytes 1253384 | tf_op jit(solution)/shard_map/ppermute | solution.py:182
  48.5 7.0 %collective-permute-start.10 = (bf16[48,2176]{1,0:T(8,128)(2,1)S(1)}, bf16[48,2176]{1,0:T(8,128)(2,1)S(1)}, u32[]{:S(2)}, u32[]{:S(2)}) collective-permute-start(bf16[48,2176]{1,0:T(8,128)(2,1)S(1)} %collective-permute-done.9), channel_id=1, source_target_pairs={{0,2},{1,3},{2,0},{3,1},{4,6},{5,7},{6,4},{7,5},{8,10},{9,11},{10,... | collective-permute-start | bytes 626696 | tf_op jit(solution)/shard_map/ppermute | solution.py:182
  50.1 6.2 %collective-permute-start.14 = (bf16[48,2176]{1,0:T(8,128)(2,1)S(1)}, bf16[48,2176]{1,0:T(8,128)(2,1)S(1)}, u32[]{:S(2)}, u32[]{:S(2)}) collective-permute-start(bf16[48,2176]{1,0:T(8,128)(2,1)S(1)} %collective-permute-done.6), channel_id=1, source_target_pairs={{0,8},{4,12},{8,0},{12,4},{16,24},{20,28},{24,16},{28,20},{1,9},{5... | collective-permute-start | bytes 626696 | tf_op jit(solution)/shard_map/ppermute | solution.py:182
  55.5 2.0 %collective-permute-start.11 = (bf16[96,2176]{1,0:T(8,128)(2,1)S(1)}, bf16[96,2176]{1,0:T(8,128)(2,1)}, u32[]{:S(2)}, u32[]{:S(2)}) collective-permute-start(bf16[96,2176]{1,0:T(8,128)(2,1)S(1)} %constant_dynamic-update-slice_fusion.2.refs_4_), channel_id=1, source_target_pairs={{0,1},{1,0},{2,3},{3,2},{4,5},{5,4},{6,7},{7,6},{8,9},{9,8},{10,11... | collective-permute-start | bytes 1253384 | tf_op jit(solution)/shard_map/ppermute | solution.py:182
  56.3 2.0 %collective-permute-start.15 = (bf16[96,2176]{1,0:T(8,128)(2,1)S(1)}, bf16[96,2176]{1,0:T(8,128)(2,1)}, u32[]{:S(2)}, u32[]{:S(2)}) collective-permute-start(bf16[96,2176]{1,0:T(8,128)(2,1)S(1)} %constant_dynamic-update-slice_fusion.4.refs_8_), channel_id=1, source_target_pairs={{0,1},{1,0},{2,3},{3,2},{4,5},{5,4},{6,7},{7,6},{8,9},{9,8},{10,11... | collective-permute-start | bytes 1253384 | tf_op jit(solution)/shard_map/ppermute | solution.py:182
  56.4 2.5 %collective-permute-start.12 = (bf16[96,2176]{1,0:T(8,128)(2,1)S(1)}, bf16[96,2176]{1,0:T(8,128)(2,1)}, u32[]{:S(2)}, u32[]{:S(2)}) collective-permute-start(bf16[96,2176]{1,0:T(8,128)(2,1)S(1)} %pad_maximum_fusion.refs_6_), channel_id=1, source_target_pairs={{0,1},{1,0},{2,3},{3,2},{4,5},{5,4},{6,7},{7,6},{8,9},{9,8},{10,11... | collective-permute-start | bytes 1253384 | tf_op jit(solution)/shard_map/ppermute | solution.py:182
  56.9 11.8 %copy-start.1 = (bf16[1,1,192,2048]{3,2,1,0:T(8,128)(2,1)S(1)}, bf16[1,1,192,2048]{3,2,1,0:T(8,128)(2,1)}, u32[]{:S(2)}) copy-start(bf16[1,1,192,2048]{3,2,1,0:T(8,128)(2,1)} %param.22) | copy-start | bytes 2359300
  71.7 1.8 %collective-permute-start.25 = (bf16[96,2048]{1,0:T(8,128)(2,1)S(1)}, bf16[96,2048]{1,0:T(8,128)(2,1)S(1)}, u32[]{:S(2)}, u32[]{:S(2)}) collective-permute-start(bf16[96,2048]{1,0:T(8,128)(2,1)S(1)} %get-tuple-element.64), channel_id=1, source_target_pairs={{0,1},{1,0},{2,3},{3,2},{4,5},{5,4},{6,7},{7,6},{8,9},{9,8},{10,11... | collective-permute-start | bytes 1179656 | tf_op jit(solution)/shard_map/ppermute | solution.py:182
  71.8 3.4 %collective-permute-start.17 = (bf16[96,2048]{1,0:T(8,128)(2,1)S(1)}, bf16[96,2048]{1,0:T(8,128)(2,1)S(1)}, u32[]{:S(2)}, u32[]{:S(2)}) collective-permute-start(bf16[96,2048]{1,0:T(8,128)(2,1)S(1)} %get-tuple-element.56), channel_id=1, source_target_pairs={{0,1},{1,0},{2,3},{3,2},{4,5},{5,4},{6,7},{7,6},{8,9},{9,8},{10,11... | collective-permute-start | bytes 1179656 | tf_op jit(solution)/shard_map/ppermute | solution.py:182
  72.3 3.0 %collective-permute-start.18 = (bf16[96,2048]{1,0:T(8,128)(2,1)S(1)}, bf16[96,2048]{1,0:T(8,128)(2,1)S(1)}, u32[]{:S(2)}, u32[]{:S(2)}) collective-permute-start(bf16[96,2048]{1,0:T(8,128)(2,1)S(1)} %get-tuple-element.58), channel_id=1, source_target_pairs={{0,1},{1,0},{2,3},{3,2},{4,5},{5,4},{6,7},{7,6},{8,9},{9,8},{10,11... | collective-permute-start | bytes 1179656 | tf_op jit(solution)/shard_map/ppermute | solution.py:182
  72.4 4.0 %collective-permute-start.21 = (bf16[96,2048]{1,0:T(8,128)(2,1)S(1)}, bf16[96,2048]{1,0:T(8,128)(2,1)S(1)}, u32[]{:S(2)}, u32[]{:S(2)}) collective-permute-start(bf16[96,2048]{1,0:T(8,128)(2,1)S(1)} %get-tuple-element.61), channel_id=1, source_target_pairs={{0,1},{1,0},{2,3},{3,2},{4,5},{5,4},{6,7},{7,6},{8,9},{9,8},{10,11... | collective-permute-start | bytes 1179656 | tf_op jit(solution)/shard_map/ppermute | solution.py:182
  73.6 7.8 %collective-permute-start.26 = (bf16[48,2048]{1,0:T(8,128)(2,1)S(1)}, bf16[48,2048]{1,0:T(8,128)(2,1)S(1)}, u32[]{:S(2)}, u32[]{:S(2)}) collective-permute-start(bf16[48,2048]{1,0:T(8,128)(2,1)S(1)} %slice.39), channel_id=1, source_target_pairs={{0,2},{1,3},{2,0},{3,1},{4,6},{5,7},{6,4},{7,5},{8,10},{9,11},{10,... | collective-permute-start | bytes 589832 | tf_op jit(solution)/shard_map/ppermute | solution.py:182
  75.4 10.8 %collective-permute-start.19 = (bf16[48,2048]{1,0:T(8,128)(2,1)S(1)}, bf16[48,2048]{1,0:T(8,128)(2,1)S(1)}, u32[]{:S(2)}, u32[]{:S(2)}) collective-permute-start(bf16[48,2048]{1,0:T(8,128)(2,1)S(1)} %slice.35), channel_id=1, source_target_pairs={{0,2},{1,3},{2,0},{3,1},{4,6},{5,7},{6,4},{7,5},{8,10},{9,11},{10,... | collective-permute-start | bytes 589832 | tf_op jit(solution)/shard_map/ppermute | solution.py:182
  76.3 25.3 %copy-start.3 = (bf16[48,2048]{1,0:T(8,128)(2,1)S(1)}, bf16[48,2048]{1,0:T(8,128)(2,1)}, u32[]{:S(2)}) copy-start(bf16[48,2048]{1,0:T(8,128)(2,1)} %get-tuple-element.43) | copy-start | bytes 589828
  76.4 13.0 %collective-permute-start.22 = (bf16[48,2048]{1,0:T(8,128)(2,1)S(1)}, bf16[48,2048]{1,0:T(8,128)(2,1)S(1)}, u32[]{:S(2)}, u32[]{:S(2)}) collective-permute-start(bf16[48,2048]{1,0:T(8,128)(2,1)S(1)} %slice.37), channel_id=1, source_target_pairs={{0,2},{1,3},{2,0},{3,1},{4,6},{5,7},{6,4},{7,5},{8,10},{9,11},{10,... | collective-permute-start | bytes 589832 | tf_op jit(solution)/shard_map/ppermute | solution.py:182
  81.5 11.9 %collective-permute-start.27 = (bf16[48,2048]{1,0:T(8,128)(2,1)S(1)}, bf16[48,2048]{1,0:T(8,128)(2,1)S(1)}, u32[]{:S(2)}, u32[]{:S(2)}) collective-permute-start(bf16[48,2048]{1,0:T(8,128)(2,1)S(1)} %add_convert_fusion.5), channel_id=1, source_target_pairs={{0,24},{4,28},{8,16},{12,20},{16,8},{20,12},{24,0},{28,4},{1,25},{... | collective-permute-start | bytes 589832 | tf_op jit(solution)/shard_map/ppermute | solution.py:182
  86.3 15.3 %collective-permute-start.24 = (bf16[48,2048]{1,0:T(8,128)(2,1)S(1)}, bf16[48,2048]{1,0:T(8,128)(2,1)S(1)}, u32[]{:S(2)}, u32[]{:S(2)}) collective-permute-start(bf16[48,2048]{1,0:T(8,128)(2,1)S(1)} %add_convert_fusion.8), channel_id=1, source_target_pairs={{0,16},{4,20},{8,24},{12,28},{16,0},{20,4},{24,8},{28,12},{1,17},{... | collective-permute-start | bytes 589832 | tf_op jit(solution)/shard_map/ppermute | solution.py:182
  89.5 12.1 %collective-permute-start.23 = (bf16[48,2048]{1,0:T(8,128)(2,1)S(1)}, bf16[48,2048]{1,0:T(8,128)(2,1)S(1)}, u32[]{:S(2)}, u32[]{:S(2)}) collective-permute-start(bf16[48,2048]{1,0:T(8,128)(2,1)S(1)} %add_convert_fusion.6), channel_id=1, source_target_pairs={{0,8},{4,12},{8,0},{12,4},{16,24},{20,28},{24,16},{28,20},{1,9},{5... | collective-permute-start | bytes 589832 | tf_op jit(solution)/shard_map/ppermute | solution.py:182
  91.9 9.8 %collective-permute-start.20 = (bf16[48,2048]{1,0:T(8,128)(2,1)S(1)}, bf16[48,2048]{1,0:T(8,128)(2,1)S(1)}, u32[]{:S(2)}, u32[]{:S(2)}) collective-permute-start(bf16[48,2048]{1,0:T(8,128)(2,1)S(1)} %slice.33), channel_id=1, source_target_pairs={{0,2},{1,3},{2,0},{3,1},{4,6},{5,7},{6,4},{7,5},{8,10},{9,11},{10,... | collective-permute-start | bytes 589832 | tf_op jit(solution)/shard_map/ppermute | solution.py:182
  (4 other events, 5.0 us)

commit v7 on v6

--- a/solution.py
+++ b/solution.py
@@ -546,20 +546,29 @@
     inner, spare = pairs[0]
     inner, other_out = lax.optimization_barrier((inner, other_out))
     partials = output_blocks(per_column, expert_index, inner, spare, weight_out, other_out)
-    returned = {}
-    for k in reversed(range(per_column)):
+    returned, arrived = {}, []
+    for k in sorted(range(per_column), key=lambda k: -k):
         keep, send = partials[k]
         for bit in reversed(bits):
-            if bit == bits[0] and k == 0 and per_column > 2:
-                send, returned[2] = lax.optimization_barrier((send, returned[2]))
+            if bit == bits[0] and k < 2 and per_column > 2:
+                returned[per_column - 1], send = lax.optimization_barrier((returned[per_column - 1], send))
             received = swapped(send, "exp", bit)
             total = keep.astype(jnp.float32) + received.astype(jnp.float32)
             total = total.astype(jnp.bfloat16)
             middle = total.shape[0] // 2
             keep, send = total[:middle], total[middle:]
         returned[k] = total
-    returned = {k: total if k == 0 else swapped(total, "ctx", 2 * k) for k, total in returned.items()}
-    moe_out = sum(returned[k].astype(jnp.float32) for k in range(per_column))
+    step = 1
+    while step < per_column:
+        for k in reversed(range(0, per_column, step)):
+            if k & step:
+                came = swapped(returned[k], "ctx", 2 * step).astype(jnp.float32)
+                if k == step:
+                    arrived.append(came)
+                else:
+                    returned[k ^ step] = (returned[k ^ step].astype(jnp.float32) + came).astype(jnp.bfloat16)
+        step *= 2
+    moe_out = returned[0].astype(jnp.float32) + sum(arrived)
     layer_out = (attended.astype(jnp.float32) + moe_out).astype(jnp.bfloat16)
     return (layer_out, router_kl)
 

time: 103 us -> 100 us (0.971)
  starting transfers between devices: 37.9 us -> 34.6 us
    ppermute x27, starting transfers between devices: 33.1 us -> 29.7 us  [swapped(): lax.ppermute(value, axis, [(source, source ^ mask) for source in range(co...]
  transfers between devices with their start and end apart: 28 -> 28, of which waited for: 14 -> 18; matrix products, arithmetic and copies ran while one was open for 2% -> 2% of each run, Pallas kernels for 12% -> 12%
where the time goes in v7:
time: 100 us
  waiting for transfers between devices  41.6 us (42%)
  starting transfers between devices  34.6 us (35%)
  Pallas kernels  18.2 us (18%)
  local copies, waits for them, and re-layouts  3.39 us (3%)
  other arithmetic  1.41 us (1%)
    ppermute x27, waiting for transfers between devices, swapped(): lax.ppermute(value, axis, [(source, source ^ mask) for source in range(co...  41.6 us
    ppermute x27, starting transfers between devices, swapped(): lax.ppermute(value, axis, [(source, source ^ mask) for source in range(co...  29.7 us
    pallas_call x3, Pallas kernels, small_kernel(): pl.pallas_call(functools.partial(fetching, kernel, len(held), stored), ou...  9.08 us
    pallas_call x1, Pallas kernels, hidden_blocks(): pl.pallas_call(functools.partial(hidden_kernel, width), out_shape=(jax.Sh...  6.13 us
    ppermute x1, starting transfers between devices, passed_along(): lax.ppermute(value, axis, [(source, source + steps) for source in range(i...  4.88 us
    pallas_call x1, Pallas kernels, output_blocks(): pl.pallas_call(output_kernel, out_shape=(half,) * (2 * count), in_specs=[...  3.02 us
    unnamed x19, local copies, waits for them, and re-layouts  2.32 us
  transfers between devices with their start and end apart: 28, of which 18 were waited for; matrix products, arithmetic and copies ran while one was open for 2% of the time, Pallas kernels for 12%

profile of v7, /device:TPU:0, one launch (start us, length us, event | category | flops | bytes accessed | tf_op | source)
XLA Modules:
  0.0 100.1 jit_solution(2364470689363544287)
XLA Ops:
  1.6 4.9 %collective-permute-start = (bf16[192,256]{1,0:T(8,128)(2,1)S(1)}, bf16[192,256]{1,0:T(8,128)(2,1)S(1)}, u32[]{:S(2)}, u32[]{:S(2)}) collective-permute-start(bf16[192,256]{1,0:T(8,128)(2,1)S(1)} %pad_maximum_fusion.1.refs_2_.refs_6_), channel_id=1, source_target_pairs={{0,4},{4,8},{8,12},{12,16},{16,20},{20,24},{24,28},{1,5},{5,9},{9,... | collective-permute-start | bytes 294920 | tf_op jit(solution)/shard_map/ppermute | solution.py:19
  6.5 2.5 %shard_map.131 = (bf16[192,128]{1,0:T(8,128)(2,1)}, bf16[192,128]{1,0:T(8,128)(2,1)}, f32[192,128]{1,0:T(8,128)}, f32[192,128]{1,0:T(8,128)}) custom-call(s32[1]{0:T(128)} %bitcast.index_ref, s32[1,192]{1,0:T(1,128)} %bitcast.18, bf16[192,128]{1,0:T(8,128)(2,1)} %refs_1_.1, bf16[192,256]{1,0:T(8,128)(2,1)} %copy-done.2), custom_call_target="tpu_custom_call" | custom-call | bytes 20971520 | tf_op jit(solution)/shard_map/pallas_call | solution.py:327
  9.7 3.2 %shard_map.132 = (bf16[48,2048]{1,0:T(8,128)(2,1)}, bf16[48,2048]{1,0:T(8,128)(2,1)}, bf16[48,2048]{1,0:T(8,128)(2,1)}, bf16[48,2048]{1,0:T(8,128)(2,1)}) custom-call(s32[1]{0:T(128)} %bitcast.index_ref, s32[1,192]{1,0:T(1,128)} %bitcast.19, bf16[192,128]{1,0:T(8,128)(2,1)} %get-tuple-element.36.refs_1_, bf16[192,128]{1,0:T(8,128)(2,1)} %get-tuple-element.37.refs_2_, ...), custom_call_target="tpu_custom_call" | custom-call | tf_op jit(solution)/shard_map/pallas_call | solution.py:327
  12.9 1.6 %collective-permute-start.1 = (bf16[48,2048]{1,0:T(8,128)(2,1)}, bf16[48,2048]{1,0:T(8,128)(2,1)S(1)}, u32[]{:S(2)}, u32[]{:S(2)}) collective-permute-start(bf16[48,2048]{1,0:T(8,128)(2,1)} %get-tuple-element.42), channel_id=1, source_target_pairs={{0,2},{1,3},{2,0},{3,1},{4,6},{5,7},{6,4},{7,5},{8,10},{9,11},{10,... | collective-permute-start | bytes 589832 | tf_op jit(solution)/shard_map/ppermute | solution.py:182
  15.1 2.0 %collective-permute-start.7 = (bf16[2048,384]{1,0:T(8,128)(2,1)S(1)}, bf16[2048,384]{1,0:T(8,128)(2,1)}, u32[]{:S(2)}, u32[]{:S(2)}) collective-permute-start(bf16[2048,384]{1,0:T(8,128)(2,1)S(1)} %bitcast.10), channel_id=1, source_target_pairs={{0,4},{4,0},{8,12},{12,8},{16,20},{20,16},{24,28},{28,24},{1,5},{5... | collective-permute-start | bytes 4718600 | tf_op jit(solution)/shard_map/ppermute | solution.py:182
  17.2 3.8 %collective-permute-done.1.refs_1_ = bf16[48,2048]{1,0:T(8,128)(2,1)S(1)} collective-permute-done((bf16[48,2048]{1,0:T(8,128)(2,1)}, bf16[48,2048]{1,0:T(8,128)(2,1)S(1)}, u32[]{:S(2)}, u32[]{:S(2)}) %collective-permute-start.1) | collective-permute-done | bytes 196640 | tf_op jit(solution)/shard_map/ppermute | solution.py:182
  21.0 1.9 %collective-permute-done.3.refs_3_ = bf16[48,2048]{1,0:T(8,128)(2,1)S(1)} collective-permute-done((bf16[48,2048]{1,0:T(8,128)(2,1)}, bf16[48,2048]{1,0:T(8,128)(2,1)S(1)}, u32[]{:S(2)}, u32[]{:S(2)}) %collective-permute-start.3) | collective-permute-done | bytes 196640 | tf_op jit(solution)/shard_map/ppermute | solution.py:182
  23.6 3.3 %shard_map.133 = (bf16[48,2048]{1,0:T(8,128)(2,1)}, bf16[48,2176]{1,0:T(8,128)(2,1)}, f32[1,48]{1,0:T(1,128)}) custom-call(s32[1]{0:T(128)} %bitcast.index_ref, bf16[48,2048]{1,0:T(8,128)(2,1)} %get-tuple-element.41.refs_0_, bf16[48,2048]{1,0:T(8,128)(2,1)} %copy-done.4, bf16[48,2048]{1,0:T(8,128)(2,1)} %copy-done.5, bf16[48,2048]{1,0:T(8,128)(2,1)} %copy-done.6, ...), custom_call_target="tpu_custom_call" | custom-call | tf_op jit(solution)/shard_map/pallas_call | solution.py:327
  27.9 2.9 %collective-permute-start.5 = (bf16[48,2176]{1,0:T(8,128)(2,1)}, bf16[48,2176]{1,0:T(8,128)(2,1)S(1)}, u32[]{:S(2)}, u32[]{:S(2)}) collective-permute-start(bf16[48,2176]{1,0:T(8,128)(2,1)} %get-tuple-element.46), channel_id=1, source_target_pairs={{0,16},{4,20},{8,24},{12,28},{16,0},{20,4},{24,8},{28,12},{1,17},{... | collective-permute-start | bytes 626696 | tf_op jit(solution)/shard_map/ppermute | solution.py:182
  30.8 1.6 %collective-permute-start.9 = (bf16[48,2176]{1,0:T(8,128)(2,1)}, bf16[48,2176]{1,0:T(8,128)(2,1)S(1)}, u32[]{:S(2)}, u32[]{:S(2)}) collective-permute-start(bf16[48,2176]{1,0:T(8,128)(2,1)} %get-tuple-element.46), channel_id=1, source_target_pairs={{0,8},{4,12},{8,0},{12,4},{16,24},{20,28},{24,16},{28,20},{1,9},{5... | collective-permute-start | bytes 626696 | tf_op jit(solution)/shard_map/ppermute | solution.py:182
  32.4 1.0 constant_dynamic-update-slice_fusion.1
  33.4 1.7 %collective-permute-done.4 = bf16[48,2176]{1,0:T(8,128)(2,1)S(1)} collective-permute-done((bf16[48,2176]{1,0:T(8,128)(2,1)}, bf16[48,2176]{1,0:T(8,128)(2,1)S(1)}, u32[]{:S(2)}, u32[]{:S(2)}) %collective-permute-start.4) | collective-permute-done | bytes 208928 | tf_op jit(solution)/shard_map/ppermute | solution.py:182
  35.1 5.5 %collective-permute-done.5 = bf16[48,2176]{1,0:T(8,128)(2,1)S(1)} collective-permute-done((bf16[48,2176]{1,0:T(8,128)(2,1)}, bf16[48,2176]{1,0:T(8,128)(2,1)S(1)}, u32[]{:S(2)}, u32[]{:S(2)}) %collective-permute-start.5) | collective-permute-done | bytes 208928 | tf_op jit(solution)/shard_map/ppermute | solution.py:182
  40.6 2.3 %collective-permute-start.6 = (bf16[48,2176]{1,0:T(8,128)(2,1)S(1)}, bf16[48,2176]{1,0:T(8,128)(2,1)S(1)}, u32[]{:S(2)}, u32[]{:S(2)}) collective-permute-start(bf16[48,2176]{1,0:T(8,128)(2,1)S(1)} %collective-permute-done.5), channel_id=1, source_target_pairs={{0,2},{1,3},{2,0},{3,1},{4,6},{5,7},{6,4},{7,5},{8,10},{9,11},{10,... | collective-permute-start | bytes 626696 | tf_op jit(solution)/shard_map/ppermute | solution.py:182
  42.9 1.0 %collective-permute-start.13 = (bf16[48,2176]{1,0:T(8,128)(2,1)S(1)}, bf16[48,2176]{1,0:T(8,128)(2,1)S(1)}, u32[]{:S(2)}, u32[]{:S(2)}) collective-permute-start(bf16[48,2176]{1,0:T(8,128)(2,1)S(1)} %collective-permute-done.5), channel_id=1, source_target_pairs={{0,8},{4,12},{8,0},{12,4},{16,24},{20,28},{24,16},{28,20},{1,9},{5... | collective-permute-start | bytes 626696 | tf_op jit(solution)/shard_map/ppermute | solution.py:182
  44.1 4.5 %collective-permute-done.6 = bf16[48,2176]{1,0:T(8,128)(2,1)S(1)} collective-permute-done((bf16[48,2176]{1,0:T(8,128)(2,1)S(1)}, bf16[48,2176]{1,0:T(8,128)(2,1)S(1)}, u32[]{:S(2)}, u32[]{:S(2)}) %collective-permute-start.6) | collective-permute-done | bytes 208928 | tf_op jit(solution)/shard_map/ppermute | solution.py:182
  48.5 1.5 %collective-permute-start.10 = (bf16[48,2176]{1,0:T(8,128)(2,1)S(1)}, bf16[48,2176]{1,0:T(8,128)(2,1)S(1)}, u32[]{:S(2)}, u32[]{:S(2)}) collective-permute-start(bf16[48,2176]{1,0:T(8,128)(2,1)S(1)} %collective-permute-done.9), channel_id=1, source_target_pairs={{0,2},{1,3},{2,0},{3,1},{4,6},{5,7},{6,4},{7,5},{8,10},{9,11},{10,... | collective-permute-start | bytes 626696 | tf_op jit(solution)/shard_map/ppermute | solution.py:182
  50.1 1.2 %collective-permute-start.14 = (bf16[48,2176]{1,0:T(8,128)(2,1)S(1)}, bf16[48,2176]{1,0:T(8,128)(2,1)S(1)}, u32[]{:S(2)}, u32[]{:S(2)}) collective-permute-start(bf16[48,2176]{1,0:T(8,128)(2,1)S(1)} %collective-permute-done.6), channel_id=1, source_target_pairs={{0,8},{4,12},{8,0},{12,4},{16,24},{20,28},{24,16},{28,20},{1,9},{5... | collective-permute-start | bytes 626696 | tf_op jit(solution)/shard_map/ppermute | solution.py:182
  51.3 4.2 %collective-permute-done.10 = bf16[48,2176]{1,0:T(8,128)(2,1)S(1)} collective-permute-done((bf16[48,2176]{1,0:T(8,128)(2,1)S(1)}, bf16[48,2176]{1,0:T(8,128)(2,1)S(1)}, u32[]{:S(2)}, u32[]{:S(2)}) %collective-permute-start.10) | collective-permute-done | bytes 208928 | tf_op jit(solution)/shard_map/ppermute | solution.py:182
  58.9 6.1 %shard_map.134 = (bf16[768,384]{1,0:T(8,128)(2,1)S(1)}, bf16[768,128]{1,0:T(8,128)(2,1)S(1)}) custom-call(bf16[2048,384]{1,0:T(8,128)(2,1)S(1)} %bitcast.11, bf16[2048,384]{1,0:T(8,128)(2,1)} %collective-permute-done.7.refs_1_, bf16[96,2176]{1,0:T(8,128)(2,1)S(1)} %constant_dynamic-update-slice_fusion.refs_2_, ...), custom_call_target="tpu_custom_call" | custom-call | bytes 9437184 | tf_op jit(solution)/shard_map/pallas_call | solution.py:378
  65.0 3.6 %collective-permute-done.16.other_ref = bf16[192,2048]{1,0:T(8,128)(2,1)} collective-permute-done((bf16[192,2048]{1,0:T(8,128)(2,1)}, bf16[192,2048]{1,0:T(8,128)(2,1)}, u32[]{:S(2)}, u32[]{:S(2)}) %collective-permute-start.16) | collective-permute-done | bytes 786464 | tf_op jit(solution)/shard_map/ppermute | solution.py:182
  68.7 3.0 %shard_map.135 = (bf16[96,2048]{1,0:T(8,128)(2,1)S(1)}, bf16[96,2048]{1,0:T(8,128)(2,1)S(1)}, bf16[96,2048]{1,0:T(8,128)(2,1)S(1)}, bf16[96,2048]{1,0:T(8,128)(2...) custom-call(s32[1]{0:T(128)} %bitcast.8.index_ref, ...), custom_call_target="tpu_custom_call" | custom-call | tf_op jit(solution)/shard_map/pallas_call | solution.py:420
  73.6 1.6 %collective-permute-start.19 = (bf16[48,2048]{1,0:T(8,128)(2,1)S(1)}, bf16[48,2048]{1,0:T(8,128)(2,1)S(1)}, u32[]{:S(2)}, u32[]{:S(2)}) collective-permute-start(bf16[48,2048]{1,0:T(8,128)(2,1)S(1)} %slice.34), channel_id=1, source_target_pairs={{0,2},{1,3},{2,0},{3,1},{4,6},{5,7},{6,4},{7,5},{8,10},{9,11},{10,... | collective-permute-start | bytes 589832 | tf_op jit(solution)/shard_map/ppermute | solution.py:182
  75.6 1.3 %collective-permute-start.25 = (bf16[48,2048]{1,0:T(8,128)(2,1)S(1)}, bf16[48,2048]{1,0:T(8,128)(2,1)S(1)}, u32[]{:S(2)}, u32[]{:S(2)}) collective-permute-start(bf16[48,2048]{1,0:T(8,128)(2,1)S(1)} %slice.39), channel_id=1, source_target_pairs={{0,2},{1,3},{2,0},{3,1},{4,6},{5,7},{6,4},{7,5},{8,10},{9,11},{10,... | collective-permute-start | bytes 589832 | tf_op jit(solution)/shard_map/ppermute | solution.py:182
  76.9 4.5 %collective-permute-done.19 = bf16[48,2048]{1,0:T(8,128)(2,1)S(1)} collective-permute-done((bf16[48,2048]{1,0:T(8,128)(2,1)S(1)}, bf16[48,2048]{1,0:T(8,128)(2,1)S(1)}, u32[]{:S(2)}, u32[]{:S(2)}) %collective-permute-start.19) | collective-permute-done | bytes 196640 | tf_op jit(solution)/shard_map/ppermute | solution.py:182
  81.5 2.8 %collective-permute-start.26 = (bf16[48,2048]{1,0:T(8,128)(2,1)S(1)}, bf16[48,2048]{1,0:T(8,128)(2,1)S(1)}, u32[]{:S(2)}, u32[]{:S(2)}) collective-permute-start(bf16[48,2048]{1,0:T(8,128)(2,1)S(1)} %add_convert_fusion.9), channel_id=1, source_target_pairs={{0,8},{4,12},{8,0},{12,4},{16,24},{20,28},{24,16},{28,20},{1,9},{5... | collective-permute-start | bytes 589832 | tf_op jit(solution)/shard_map/ppermute | solution.py:182
  84.2 1.5 %collective-permute-start.22 = (bf16[48,2048]{1,0:T(8,128)(2,1)S(1)}, bf16[48,2048]{1,0:T(8,128)(2,1)S(1)}, u32[]{:S(2)}, u32[]{:S(2)}) collective-permute-start(bf16[48,2048]{1,0:T(8,128)(2,1)S(1)} %slice.35), channel_id=1, source_target_pairs={{0,2},{1,3},{2,0},{3,1},{4,6},{5,7},{6,4},{7,5},{8,10},{9,11},{10,... | collective-permute-start | bytes 589832 | tf_op jit(solution)/shard_map/ppermute | solution.py:182
  86.3 1.6 %collective-permute-done.26 = bf16[48,2048]{1,0:T(8,128)(2,1)S(1)} collective-permute-done((bf16[48,2048]{1,0:T(8,128)(2,1)S(1)}, bf16[48,2048]{1,0:T(8,128)(2,1)S(1)}, u32[]{:S(2)}, u32[]{:S(2)}) %collective-permute-start.26) | collective-permute-done | bytes 196640 | tf_op jit(solution)/shard_map/ppermute | solution.py:182
  88.0 3.1 %collective-permute-start.27 = (bf16[48,2048]{1,0:T(8,128)(2,1)S(1)}, bf16[48,2048]{1,0:T(8,128)(2,1)S(1)}, u32[]{:S(2)}, u32[]{:S(2)}) collective-permute-start(bf16[48,2048]{1,0:T(8,128)(2,1)S(1)} %add_convert_fusion.5), channel_id=1, source_target_pairs={{0,16},{4,20},{8,24},{12,28},{16,0},{20,4},{24,8},{28,12},{1,17},{... | collective-permute-start | bytes 589832 | tf_op jit(solution)/shard_map/ppermute | solution.py:182
  91.4 1.3 %collective-permute-start.23 = (bf16[48,2048]{1,0:T(8,128)(2,1)S(1)}, bf16[48,2048]{1,0:T(8,128)(2,1)S(1)}, u32[]{:S(2)}, u32[]{:S(2)}) collective-permute-start(bf16[48,2048]{1,0:T(8,128)(2,1)S(1)} %add_convert_fusion.7), channel_id=1, source_target_pairs={{0,8},{4,12},{8,0},{12,4},{16,24},{20,28},{24,16},{28,20},{1,9},{5... | collective-permute-start | bytes 589832 | tf_op jit(solution)/shard_map/ppermute | solution.py:182
  93.5 4.6 %collective-permute-done.27 = bf16[48,2048]{1,0:T(8,128)(2,1)S(1)} collective-permute-done((bf16[48,2048]{1,0:T(8,128)(2,1)S(1)}, bf16[48,2048]{1,0:T(8,128)(2,1)S(1)}, u32[]{:S(2)}, u32[]{:S(2)}) %collective-permute-start.27) | collective-permute-done | bytes 196640 | tf_op jit(solution)/shard_map/ppermute | solution.py:182
  98.1 1.2 %collective-permute-done.23 = bf16[48,2048]{1,0:T(8,128)(2,1)S(1)} collective-permute-done((bf16[48,2048]{1,0:T(8,128)(2,1)S(1)}, bf16[48,2048]{1,0:T(8,128)(2,1)S(1)}, u32[]{:S(2)}, u32[]{:S(2)}) %collective-permute-start.23) | collective-permute-done | bytes 196640 | tf_op jit(solution)/shard_map/ppermute | solution.py:182
  (66 shorter events, 12.2 us)
Async XLA Ops:
  0.6 14.5 %copy-start = (bf16[1,1,2048,384]{3,2,1,0:T(8,128)(2,1)S(1)}, bf16[1,1,2048,384]{3,2,1,0:T(8,128)(2,1)}, u32[]{:S(2)}) copy-start(bf16[1,1,2048,384]{3,2,1,0:T(8,128)(2,1)} %param.21) | copy-start | bytes 4718596
  1.6 4.9 %copy-start.2 = (bf16[192,256]{1,0:T(8,128)(2,1)}, bf16[192,256]{1,0:T(8,128)(2,1)S(1)}, u32[]{:S(2)}) copy-start(bf16[192,256]{1,0:T(8,128)(2,1)S(1)} %pad_maximum_fusion.1.refs_2_.refs_6_) | copy-start | bytes 294916
  1.6 7.5 %collective-permute-start = (bf16[192,256]{1,0:T(8,128)(2,1)S(1)}, bf16[192,256]{1,0:T(8,128)(2,1)S(1)}, u32[]{:S(2)}, u32[]{:S(2)}) collective-permute-start(bf16[192,256]{1,0:T(8,128)(2,1)S(1)} %pad_maximum_fusion.1.refs_2_.refs_6_), channel_id=1, source_target_pairs={{0,4},{4,8},{8,12},{12,16},{16,20},{20,24},{24,28},{1,5},{5,9},{9,... | collective-permute-start | bytes 294920 | tf_op jit(solution)/shard_map/ppermute | solution.py:19
  12.9 8.1 %collective-permute-start.1 = (bf16[48,2048]{1,0:T(8,128)(2,1)}, bf16[48,2048]{1,0:T(8,128)(2,1)S(1)}, u32[]{:S(2)}, u32[]{:S(2)}) collective-permute-start(bf16[48,2048]{1,0:T(8,128)(2,1)} %get-tuple-element.42), channel_id=1, source_target_pairs={{0,2},{1,3},{2,0},{3,1},{4,6},{5,7},{6,4},{7,5},{8,10},{9,11},{10,... | collective-permute-start | bytes 589832 | tf_op jit(solution)/shard_map/ppermute | solution.py:182
  14.5 6.6 %collective-permute-start.2 = (bf16[48,2048]{1,0:T(8,128)(2,1)}, bf16[48,2048]{1,0:T(8,128)(2,1)S(1)}, u32[]{:S(2)}, u32[]{:S(2)}) collective-permute-start(bf16[48,2048]{1,0:T(8,128)(2,1)} %get-tuple-element.43), channel_id=1, source_target_pairs={{0,1},{1,0},{2,3},{3,2},{4,5},{5,4},{6,7},{7,6},{8,9},{9,8},{10,11... | collective-permute-start | bytes 589832 | tf_op jit(solution)/shard_map/ppermute | solution.py:182
  14.5 8.4 %collective-permute-start.3 = (bf16[48,2048]{1,0:T(8,128)(2,1)}, bf16[48,2048]{1,0:T(8,128)(2,1)S(1)}, u32[]{:S(2)}, u32[]{:S(2)}) collective-permute-start(bf16[48,2048]{1,0:T(8,128)(2,1)} %get-tuple-element.44), channel_id=1, source_target_pairs={{0,3},{1,2},{2,1},{3,0},{4,7},{5,6},{6,5},{7,4},{8,11},{9,10},{10,... | collective-permute-start | bytes 589832 | tf_op jit(solution)/shard_map/ppermute | solution.py:182
  15.1 41.3 %collective-permute-start.7 = (bf16[2048,384]{1,0:T(8,128)(2,1)S(1)}, bf16[2048,384]{1,0:T(8,128)(2,1)}, u32[]{:S(2)}, u32[]{:S(2)}) collective-permute-start(bf16[2048,384]{1,0:T(8,128)(2,1)S(1)} %bitcast.10), channel_id=1, source_target_pairs={{0,4},{4,0},{8,12},{12,8},{16,20},{20,16},{24,28},{28,24},{1,5},{5... | collective-permute-start | bytes 4718600 | tf_op jit(solution)/shard_map/ppermute | solution.py:182
  17.2 51.5 %collective-permute-start.16 = (bf16[192,2048]{1,0:T(8,128)(2,1)}, bf16[192,2048]{1,0:T(8,128)(2,1)}, u32[]{:S(2)}, u32[]{:S(2)}) collective-permute-start(bf16[192,2048]{1,0:T(8,128)(2,1)} %bitcast.12), channel_id=1, source_target_pairs={{0,4},{4,0},{8,12},{12,8},{16,20},{20,16},{24,28},{28,24},{1,5},{5... | collective-permute-start | bytes 2359304 | tf_op jit(solution)/shard_map/ppermute | solution.py:182
  26.9 8.2 %collective-permute-start.4 = (bf16[48,2176]{1,0:T(8,128)(2,1)}, bf16[48,2176]{1,0:T(8,128)(2,1)S(1)}, u32[]{:S(2)}, u32[]{:S(2)}) collective-permute-start(bf16[48,2176]{1,0:T(8,128)(2,1)} %get-tuple-element.46), channel_id=1, source_target_pairs={{0,2},{1,3},{2,0},{3,1},{4,6},{5,7},{6,4},{7,5},{8,10},{9,11},{10,... | collective-permute-start | bytes 626696 | tf_op jit(solution)/shard_map/ppermute | solution.py:182
  27.9 12.7 %collective-permute-start.5 = (bf16[48,2176]{1,0:T(8,128)(2,1)}, bf16[48,2176]{1,0:T(8,128)(2,1)S(1)}, u32[]{:S(2)}, u32[]{:S(2)}) collective-permute-start(bf16[48,2176]{1,0:T(8,128)(2,1)} %get-tuple-element.46), channel_id=1, source_target_pairs={{0,16},{4,20},{8,24},{12,28},{16,0},{20,4},{24,8},{28,12},{1,17},{... | collective-permute-start | bytes 626696 | tf_op jit(solution)/shard_map/ppermute | solution.py:182
  30.8 13.2 %collective-permute-start.9 = (bf16[48,2176]{1,0:T(8,128)(2,1)}, bf16[48,2176]{1,0:T(8,128)(2,1)S(1)}, u32[]{:S(2)}, u32[]{:S(2)}) collective-permute-start(bf16[48,2176]{1,0:T(8,128)(2,1)} %get-tuple-element.46), channel_id=1, source_target_pairs={{0,8},{4,12},{8,0},{12,4},{16,24},{20,28},{24,16},{28,20},{1,9},{5... | collective-permute-start | bytes 626696 | tf_op jit(solution)/shard_map/ppermute | solution.py:182
  40.6 8.0 %collective-permute-start.6 = (bf16[48,2176]{1,0:T(8,128)(2,1)S(1)}, bf16[48,2176]{1,0:T(8,128)(2,1)S(1)}, u32[]{:S(2)}, u32[]{:S(2)}) collective-permute-start(bf16[48,2176]{1,0:T(8,128)(2,1)S(1)} %collective-permute-done.5), channel_id=1, source_target_pairs={{0,2},{1,3},{2,0},{3,1},{4,6},{5,7},{6,4},{7,5},{8,10},{9,11},{10,... | collective-permute-start | bytes 626696 | tf_op jit(solution)/shard_map/ppermute | solution.py:182
  42.9 7.2 %collective-permute-start.13 = (bf16[48,2176]{1,0:T(8,128)(2,1)S(1)}, bf16[48,2176]{1,0:T(8,128)(2,1)S(1)}, u32[]{:S(2)}, u32[]{:S(2)}) collective-permute-start(bf16[48,2176]{1,0:T(8,128)(2,1)S(1)} %collective-permute-done.5), channel_id=1, source_target_pairs={{0,8},{4,12},{8,0},{12,4},{16,24},{20,28},{24,16},{28,20},{1,9},{5... | collective-permute-start | bytes 626696 | tf_op jit(solution)/shard_map/ppermute | solution.py:182
  44.0 12.9 %collective-permute-start.8 = (bf16[96,2176]{1,0:T(8,128)(2,1)S(1)}, bf16[96,2176]{1,0:T(8,128)(2,1)}, u32[]{:S(2)}, u32[]{:S(2)}) collective-permute-start(bf16[96,2176]{1,0:T(8,128)(2,1)S(1)} %constant_dynamic-update-slice_fusion.refs_2_), channel_id=1, source_target_pairs={{0,1},{1,0},{2,3},{3,2},{4,5},{5,4},{6,7},{7,6},{8,9},{9,8},{10,11... | collective-permute-start | bytes 1253384 | tf_op jit(solution)/shard_map/ppermute | solution.py:182
  48.5 7.0 %collective-permute-start.10 = (bf16[48,2176]{1,0:T(8,128)(2,1)S(1)}, bf16[48,2176]{1,0:T(8,128)(2,1)S(1)}, u32[]{:S(2)}, u32[]{:S(2)}) collective-permute-start(bf16[48,2176]{1,0:T(8,128)(2,1)S(1)} %collective-permute-done.9), channel_id=1, source_target_pairs={{0,2},{1,3},{2,0},{3,1},{4,6},{5,7},{6,4},{7,5},{8,10},{9,11},{10,... | collective-permute-start | bytes 626696 | tf_op jit(solution)/shard_map/ppermute | solution.py:182
  50.1 6.2 %collective-permute-start.14 = (bf16[48,2176]{1,0:T(8,128)(2,1)S(1)}, bf16[48,2176]{1,0:T(8,128)(2,1)S(1)}, u32[]{:S(2)}, u32[]{:S(2)}) collective-permute-start(bf16[48,2176]{1,0:T(8,128)(2,1)S(1)} %collective-permute-done.6), channel_id=1, source_target_pairs={{0,8},{4,12},{8,0},{12,4},{16,24},{20,28},{24,16},{28,20},{1,9},{5... | collective-permute-start | bytes 626696 | tf_op jit(solution)/shard_map/ppermute | solution.py:182
  55.5 2.0 %collective-permute-start.11 = (bf16[96,2176]{1,0:T(8,128)(2,1)S(1)}, bf16[96,2176]{1,0:T(8,128)(2,1)}, u32[]{:S(2)}, u32[]{:S(2)}) collective-permute-start(bf16[96,2176]{1,0:T(8,128)(2,1)S(1)} %constant_dynamic-update-slice_fusion.2.refs_4_), channel_id=1, source_target_pairs={{0,1},{1,0},{2,3},{3,2},{4,5},{5,4},{6,7},{7,6},{8,9},{9,8},{10,11... | collective-permute-start | bytes 1253384 | tf_op jit(solution)/shard_map/ppermute | solution.py:182
  56.3 2.0 %collective-permute-start.15 = (bf16[96,2176]{1,0:T(8,128)(2,1)S(1)}, bf16[96,2176]{1,0:T(8,128)(2,1)}, u32[]{:S(2)}, u32[]{:S(2)}) collective-permute-start(bf16[96,2176]{1,0:T(8,128)(2,1)S(1)} %constant_dynamic-update-slice_fusion.4.refs_8_), channel_id=1, source_target_pairs={{0,1},{1,0},{2,3},{3,2},{4,5},{5,4},{6,7},{7,6},{8,9},{9,8},{10,11... | collective-permute-start | bytes 1253384 | tf_op jit(solution)/shard_map/ppermute | solution.py:182
  56.4 2.5 %collective-permute-start.12 = (bf16[96,2176]{1,0:T(8,128)(2,1)S(1)}, bf16[96,2176]{1,0:T(8,128)(2,1)}, u32[]{:S(2)}, u32[]{:S(2)}) collective-permute-start(bf16[96,2176]{1,0:T(8,128)(2,1)S(1)} %pad_maximum_fusion.refs_6_), channel_id=1, source_target_pairs={{0,1},{1,0},{2,3},{3,2},{4,5},{5,4},{6,7},{7,6},{8,9},{9,8},{10,11... | collective-permute-start | bytes 1253384 | tf_op jit(solution)/shard_map/ppermute | solution.py:182
  56.9 11.8 %copy-start.1 = (bf16[1,1,192,2048]{3,2,1,0:T(8,128)(2,1)S(1)}, bf16[1,1,192,2048]{3,2,1,0:T(8,128)(2,1)}, u32[]{:S(2)}) copy-start(bf16[1,1,192,2048]{3,2,1,0:T(8,128)(2,1)} %param.22) | copy-start | bytes 2359300
  71.7 1.8 %collective-permute-start.18 = (bf16[96,2048]{1,0:T(8,128)(2,1)S(1)}, bf16[96,2048]{1,0:T(8,128)(2,1)S(1)}, u32[]{:S(2)}, u32[]{:S(2)}) collective-permute-start(bf16[96,2048]{1,0:T(8,128)(2,1)S(1)} %get-tuple-element.60), channel_id=1, source_target_pairs={{0,1},{1,0},{2,3},{3,2},{4,5},{5,4},{6,7},{7,6},{8,9},{9,8},{10,11... | collective-permute-start | bytes 1179656 | tf_op jit(solution)/shard_map/ppermute | solution.py:182
  71.8 3.4 %collective-permute-start.20 = (bf16[96,2048]{1,0:T(8,128)(2,1)S(1)}, bf16[96,2048]{1,0:T(8,128)(2,1)S(1)}, u32[]{:S(2)}, u32[]{:S(2)}) collective-permute-start(bf16[96,2048]{1,0:T(8,128)(2,1)S(1)} %get-tuple-element.62), channel_id=1, source_target_pairs={{0,1},{1,0},{2,3},{3,2},{4,5},{5,4},{6,7},{7,6},{8,9},{9,8},{10,11... | collective-permute-start | bytes 1179656 | tf_op jit(solution)/shard_map/ppermute | solution.py:182
  72.3 3.0 %collective-permute-start.17 = (bf16[96,2048]{1,0:T(8,128)(2,1)S(1)}, bf16[96,2048]{1,0:T(8,128)(2,1)S(1)}, u32[]{:S(2)}, u32[]{:S(2)}) collective-permute-start(bf16[96,2048]{1,0:T(8,128)(2,1)S(1)} %get-tuple-element.58), channel_id=1, source_target_pairs={{0,1},{1,0},{2,3},{3,2},{4,5},{5,4},{6,7},{7,6},{8,9},{9,8},{10,11... | collective-permute-start | bytes 1179656 | tf_op jit(solution)/shard_map/ppermute | solution.py:182
  72.4 3.0 %collective-permute-start.24 = (bf16[96,2048]{1,0:T(8,128)(2,1)S(1)}, bf16[96,2048]{1,0:T(8,128)(2,1)S(1)}, u32[]{:S(2)}, u32[]{:S(2)}) collective-permute-start(bf16[96,2048]{1,0:T(8,128)(2,1)S(1)} %get-tuple-element.67), channel_id=1, source_target_pairs={{0,1},{1,0},{2,3},{3,2},{4,5},{5,4},{6,7},{7,6},{8,9},{9,8},{10,11... | collective-permute-start | bytes 1179656 | tf_op jit(solution)/shard_map/ppermute | solution.py:182
  73.6 7.8 %collective-permute-start.19 = (bf16[48,2048]{1,0:T(8,128)(2,1)S(1)}, bf16[48,2048]{1,0:T(8,128)(2,1)S(1)}, u32[]{:S(2)}, u32[]{:S(2)}) collective-permute-start(bf16[48,2048]{1,0:T(8,128)(2,1)S(1)} %slice.34), channel_id=1, source_target_pairs={{0,2},{1,3},{2,0},{3,1},{4,6},{5,7},{6,4},{7,5},{8,10},{9,11},{10,... | collective-permute-start | bytes 589832 | tf_op jit(solution)/shard_map/ppermute | solution.py:182
  75.5 23.8 %copy-start.3 = (bf16[48,2048]{1,0:T(8,128)(2,1)S(1)}, bf16[48,2048]{1,0:T(8,128)(2,1)}, u32[]{:S(2)}) copy-start(bf16[48,2048]{1,0:T(8,128)(2,1)} %get-tuple-element.45) | copy-start | bytes 589828
  75.6 10.7 %collective-permute-start.25 = (bf16[48,2048]{1,0:T(8,128)(2,1)S(1)}, bf16[48,2048]{1,0:T(8,128)(2,1)S(1)}, u32[]{:S(2)}, u32[]{:S(2)}) collective-permute-start(bf16[48,2048]{1,0:T(8,128)(2,1)S(1)} %slice.39), channel_id=1, source_target_pairs={{0,2},{1,3},{2,0},{3,1},{4,6},{5,7},{6,4},{7,5},{8,10},{9,11},{10,... | collective-permute-start | bytes 589832 | tf_op jit(solution)/shard_map/ppermute | solution.py:182
  81.5 6.4 %collective-permute-start.26 = (bf16[48,2048]{1,0:T(8,128)(2,1)S(1)}, bf16[48,2048]{1,0:T(8,128)(2,1)S(1)}, u32[]{:S(2)}, u32[]{:S(2)}) collective-permute-start(bf16[48,2048]{1,0:T(8,128)(2,1)S(1)} %add_convert_fusion.9), channel_id=1, source_target_pairs={{0,8},{4,12},{8,0},{12,4},{16,24},{20,28},{24,16},{28,20},{1,9},{5... | collective-permute-start | bytes 589832 | tf_op jit(solution)/shard_map/ppermute | solution.py:182
  84.2 7.1 %collective-permute-start.22 = (bf16[48,2048]{1,0:T(8,128)(2,1)S(1)}, bf16[48,2048]{1,0:T(8,128)(2,1)S(1)}, u32[]{:S(2)}, u32[]{:S(2)}) collective-permute-start(bf16[48,2048]{1,0:T(8,128)(2,1)S(1)} %slice.35), channel_id=1, source_target_pairs={{0,2},{1,3},{2,0},{3,1},{4,6},{5,7},{6,4},{7,5},{8,10},{9,11},{10,... | collective-permute-start | bytes 589832 | tf_op jit(solution)/shard_map/ppermute | solution.py:182
  85.7 7.8 %collective-permute-start.21 = (bf16[48,2048]{1,0:T(8,128)(2,1)S(1)}, bf16[48,2048]{1,0:T(8,128)(2,1)S(1)}, u32[]{:S(2)}, u32[]{:S(2)}) collective-permute-start(bf16[48,2048]{1,0:T(8,128)(2,1)S(1)} %slice.36), channel_id=1, source_target_pairs={{0,2},{1,3},{2,0},{3,1},{4,6},{5,7},{6,4},{7,5},{8,10},{9,11},{10,... | collective-permute-start | bytes 589832 | tf_op jit(solution)/shard_map/ppermute | solution.py:182
  88.0 10.1 %collective-permute-start.27 = (bf16[48,2048]{1,0:T(8,128)(2,1)S(1)}, bf16[48,2048]{1,0:T(8,128)(2,1)S(1)}, u32[]{:S(2)}, u32[]{:S(2)}) collective-permute-start(bf16[48,2048]{1,0:T(8,128)(2,1)S(1)} %add_convert_fusion.5), channel_id=1, source_target_pairs={{0,16},{4,20},{8,24},{12,28},{16,0},{20,4},{24,8},{28,12},{1,17},{... | collective-permute-start | bytes 589832 | tf_op jit(solution)/shard_map/ppermute | solution.py:182
  91.4 7.9 %collective-permute-start.23 = (bf16[48,2048]{1,0:T(8,128)(2,1)S(1)}, bf16[48,2048]{1,0:T(8,128)(2,1)S(1)}, u32[]{:S(2)}, u32[]{:S(2)}) collective-permute-start(bf16[48,2048]{1,0:T(8,128)(2,1)S(1)} %add_convert_fusion.7), channel_id=1, source_target_pairs={{0,8},{4,12},{8,0},{12,4},{16,24},{20,28},{24,16},{28,20},{1,9},{5... | collective-permute-start | bytes 589832 | tf_op jit(solution)/shard_map/ppermute | solution.py:182
  (4 other events, 5.0 us)

commit v8 on v7

--- a/solution.py
+++ b/solution.py
@@ -195,8 +195,9 @@
     return (wide * cosine + pltpu.roll(wide, wide.shape[1] // 2, 1) * sine).astype(jnp.bfloat16)
 
 
-def rotation_kernel(index_ref, pos_ref, q_ref, own_ref, query_ref, key_ref, cos_ref, sin_ref):
+def rotation_kernel(share, index_ref, pos_ref, q_ref, own_ref, query_ref, key_ref, cos_ref, sin_ref):
     block, size = q_ref.shape
+    group = pl.ds(pl.multiple_of(index_ref[0] // share * size, size), size)
     pos_row = pos_ref[...].astype(jnp.float32)
     pos_col = column_of(pos_row)
     first = lax.broadcasted_iota(jnp.int32, (1, block), 1) == 0
@@ -215,11 +216,11 @@
 
     cosine, sine = table(pos_col)
     query_ref[...] = turned(q_ref[...], cosine, sine)
-    key_ref[...] = turned(own_ref[:, :size], cosine, sine)
+    key_ref[...] = turned(own_ref[:, group], cosine, sine)
     cos_ref[...], sin_ref[...] = table(earlier)
 
 
-def attention_kernel(order, index_ref, pos_ref, query_ref, key_ref, cos_ref, sin_ref, before_ref, own_ref, *refs):
+def attention_kernel(share, order, weight_ready, index_ref, pos_ref, query_ref, key_ref, cos_ref, sin_ref, before_ref, own_ref, *refs):
     weight_ref, outputs, mixed = refs[0], refs[1:-1], refs[-1]
     block, size = query_ref.shape
     rows = block // len(order)
@@ -230,7 +231,8 @@
     keys = jnp.concatenate(
         [turned(before_ref[:, :size], cos_ref[...], sin_ref[...]), key_ref[...]], axis=0
     )
-    values = jnp.concatenate([before_ref[:, size:], own_ref[:, size:]], axis=0)
+    group = pl.ds(pl.multiple_of(index_ref[0] // share * size, size), size)
+    values = jnp.concatenate([before_ref[:, size:], own_ref[:, group]], axis=0)
     scores = lax.dot_general(
         query_ref[...], keys, (((1,), (1,)), ((), ())), preferred_element_type=jnp.float32
     ) * (1.0 / math.sqrt(size))
@@ -240,6 +242,7 @@
     picked = [
         mixed[pl.ds(pl.multiple_of((index_ref[0] ^ owner) * rows, 16), rows), :] for owner in order
     ]
+    weight_ready()
     term = jnp.dot(
         jnp.concatenate(picked, axis=0), weight_ref[...], preferred_element_type=jnp.float32
     ).astype(jnp.bfloat16)
@@ -294,7 +297,7 @@
 LEAN_GRANT = 24 * 1024 * 1024
 
 
-def fetching(kernel, count, stored, index_ref, *refs):
+def fetching(kernel, count, stored, late, index_ref, *refs):
     inputs, refs = refs[:count], refs[count:]
     outputs, refs = refs[: len(stored)], refs[len(stored) :]
     held, refs = refs[:count], refs[count:]
@@ -306,26 +309,27 @@
     ]
     for copy in copies:
         copy.start()
-    for copy in copies:
+    for copy in copies[: count - late]:
         copy.wait()
+    awaited = [copy.wait for copy in copies[count - late :]]
     sent = iter(sent)
     built, copies = [], []
     for output, far in zip(outputs, stored):
         built.append(next(sent) if far else output)
         if far:
             copies.append(pltpu.make_async_copy(built[-1], output, left.at[len(copies)]))
-    kernel(index_ref, *held, *built, *scratch)
+    kernel(*awaited, index_ref, *held, *built, *scratch)
     for copy in copies:
         copy.start()
     for copy in copies:
         copy.wait()
 
 
-def small_kernel(kernel, out_shape, inputs, stored, scratch=(), moved=0):
+def small_kernel(kernel, out_shape, inputs, stored, scratch=(), moved=0, late=0):
     held = [pltpu.VMEM(array.shape, array.dtype) for array in inputs[1:]]
     sent = [pltpu.VMEM(leaf.shape, leaf.dtype) for leaf, far in zip(out_shape, stored) if far]
     return pl.pallas_call(
-        functools.partial(fetching, kernel, len(held), stored),
+        functools.partial(fetching, kernel, len(held), stored, late),
         out_shape=out_shape,
         in_specs=[SMEM] + [HBM] * len(held),
         out_specs=tuple(HBM if far else VMEM for far in stored),
@@ -484,19 +488,20 @@
     turned_head = jax.ShapeDtypeStruct((block_rows, head_dim), jnp.bfloat16)
     table = jax.ShapeDtypeStruct((block_rows, head_dim), jnp.float32)
     rotated = small_kernel(
-        rotation_kernel,
+        functools.partial(rotation_kernel, share),
         (turned_head, turned_head, table, table),
-        (index, positions[None, :], queries, kv_own),
+        (index, positions[None, :], queries, keys),
         (True,) * 4,
         moved=20 << 20,
     )
     term = jax.ShapeDtypeStruct((token_rows, width), jnp.bfloat16)
     terms = small_kernel(
-        functools.partial(attention_kernel, tuple(owners)),
+        functools.partial(attention_kernel, share, tuple(owners)),
         (term,) * exp_count,
-        (index, positions[None, :], *rotated, before, kv_own, out_weight),
+        (index, positions[None, :], *rotated, before, values, out_weight),
         (True,) * exp_count,
         (pltpu.VMEM((block_rows, head_dim), jnp.bfloat16),),
+        late=1,
     )
     terms = [terms[0]] + [swapped(term, "exp", owner) for term, owner in zip(terms[1:], owners[1:])]
     lanes = -(-experts_total // 128) * 128

time: 100 us -> 100 us (level)
    unnamed x19 -> x17, local copies, waits for them, and re-layouts: 2.32 us -> 2.32 us
where the time goes in v8:
time: 100 us; the launch traced here: 99.9 us
  waiting for transfers between devices  41.5 us (42%)
  starting transfers between devices  34.6 us (35%)
  Pallas kernels  18.1 us (18%)
  local copies, waits for them, and re-layouts  3.39 us (3%)
  other arithmetic  1.41 us (1%)
    ppermute x27, waiting for transfers between devices, swapped(): lax.ppermute(value, axis, [(source, source ^ mask) for source in range(co...  41.5 us
    ppermute x27, starting transfers between devices, swapped(): lax.ppermute(value, axis, [(source, source ^ mask) for source in range(co...  29.7 us
    pallas_call x3, Pallas kernels, small_kernel(): pl.pallas_call(functools.partial(fetching, kernel, len(held), stored, lat...  8.94 us
    pallas_call x1, Pallas kernels, hidden_blocks(): pl.pallas_call(functools.partial(hidden_kernel, width), out_shape=(jax.Sh...  6.13 us
    ppermute x1, starting transfers between devices, passed_along(): lax.ppermute(value, axis, [(source, source + steps) for source in range(i...  4.88 us
    pallas_call x1, Pallas kernels, output_blocks(): pl.pallas_call(output_kernel, out_shape=(half,) * (2 * count), in_specs=[...  3.02 us
    unnamed x17, local copies, waits for them, and re-layouts  2.32 us
  transfers between devices with their start and end apart: 28, of which 18 were waited for; matrix products, arithmetic and copies ran while one was open for 2% of the time, Pallas kernels for 12%

profile of v8, /device:TPU:0, one launch (start us, length us, event | category | flops | bytes accessed | tf_op | source)
XLA Modules:
  0.0 99.9 jit_solution(16775834754772096359)
XLA Ops:
  1.6 4.9 %collective-permute-start = (bf16[192,256]{1,0:T(8,128)(2,1)S(1)}, bf16[192,256]{1,0:T(8,128)(2,1)S(1)}, u32[]{:S(2)}, u32[]{:S(2)}) collective-permute-start(bf16[192,256]{1,0:T(8,128)(2,1)S(1)} %pad_maximum_fusion.1), channel_id=1, source_target_pairs={{0,4},{4,8},{8,12},{12,16},{16,20},{20,24},{24,28},{1,5},{5,9},{9,... | collective-permute-start | bytes 294920 | tf_op jit(solution)/shard_map/ppermute | solution.py:19
  6.5 2.5 %shard_map.131 = (bf16[192,128]{1,0:T(8,128)(2,1)}, bf16[192,128]{1,0:T(8,128)(2,1)}, f32[192,128]{1,0:T(8,128)}, f32[192,128]{1,0:T(8,128)}) custom-call(s32[1]{0:T(128)} %bitcast.index_ref, s32[1,192]{1,0:T(1,128)} %bitcast.18, bf16[192,128]{1,0:T(8,128)(2,1)} %refs_1_.1, bf16[192,256]{1,0:T(8,128)(2,1)} %refs_2_.1), custom_call_target="tpu_custom_call" | custom-call | bytes 20971520 | tf_op jit(solution)/shard_map/pallas_call | solution.py:331
  9.7 3.0 %shard_map.132 = (bf16[48,2048]{1,0:T(8,128)(2,1)}, bf16[48,2048]{1,0:T(8,128)(2,1)}, bf16[48,2048]{1,0:T(8,128)(2,1)}, bf16[48,2048]{1,0:T(8,128)(2,1)}) custom-call(s32[1]{0:T(128)} %bitcast.index_ref, s32[1,192]{1,0:T(1,128)} %bitcast.19, bf16[192,128]{1,0:T(8,128)(2,1)} %get-tuple-element.36.refs_1_, bf16[192,128]{1,0:T(8,128)(2,1)} %get-tuple-element.37.refs_2_, ...), custom_call_target="tpu_custom_call" | custom-call | tf_op jit(solution)/shard_map/pallas_call | solution.py:331
  12.7 1.6 %collective-permute-start.1 = (bf16[48,2048]{1,0:T(8,128)(2,1)}, bf16[48,2048]{1,0:T(8,128)(2,1)S(1)}, u32[]{:S(2)}, u32[]{:S(2)}) collective-permute-start(bf16[48,2048]{1,0:T(8,128)(2,1)} %get-tuple-element.42), channel_id=1, source_target_pairs={{0,2},{1,3},{2,0},{3,1},{4,6},{5,7},{6,4},{7,5},{8,10},{9,11},{10,... | collective-permute-start | bytes 589832 | tf_op jit(solution)/shard_map/ppermute | solution.py:182
  15.0 2.0 %collective-permute-start.7 = (bf16[2048,384]{1,0:T(8,128)(2,1)S(1)}, bf16[2048,384]{1,0:T(8,128)(2,1)}, u32[]{:S(2)}, u32[]{:S(2)}) collective-permute-start(bf16[2048,384]{1,0:T(8,128)(2,1)S(1)} %bitcast.10), channel_id=1, source_target_pairs={{0,4},{4,0},{8,12},{12,8},{16,20},{20,16},{24,28},{28,24},{1,5},{5... | collective-permute-start | bytes 4718600 | tf_op jit(solution)/shard_map/ppermute | solution.py:182
  17.0 3.8 %collective-permute-done.1.refs_1_ = bf16[48,2048]{1,0:T(8,128)(2,1)S(1)} collective-permute-done((bf16[48,2048]{1,0:T(8,128)(2,1)}, bf16[48,2048]{1,0:T(8,128)(2,1)S(1)}, u32[]{:S(2)}, u32[]{:S(2)}) %collective-permute-start.1) | collective-permute-done | bytes 196640 | tf_op jit(solution)/shard_map/ppermute | solution.py:182
  20.9 1.9 %collective-permute-done.3.refs_3_ = bf16[48,2048]{1,0:T(8,128)(2,1)S(1)} collective-permute-done((bf16[48,2048]{1,0:T(8,128)(2,1)}, bf16[48,2048]{1,0:T(8,128)(2,1)S(1)}, u32[]{:S(2)}, u32[]{:S(2)}) %collective-permute-start.3) | collective-permute-done | bytes 196640 | tf_op jit(solution)/shard_map/ppermute | solution.py:182
  23.4 3.4 %shard_map.133 = (bf16[48,2048]{1,0:T(8,128)(2,1)}, bf16[48,2176]{1,0:T(8,128)(2,1)}, f32[1,48]{1,0:T(1,128)}) custom-call(s32[1]{0:T(128)} %bitcast.index_ref, bf16[48,2048]{1,0:T(8,128)(2,1)} %get-tuple-element.41.refs_0_, bf16[48,2048]{1,0:T(8,128)(2,1)} %copy-done.3, bf16[48,2048]{1,0:T(8,128)(2,1)} %copy-done.4, bf16[48,2048]{1,0:T(8,128)(2,1)} %copy-done.5, ...), custom_call_target="tpu_custom_call" | custom-call | tf_op jit(solution)/shard_map/pallas_call | solution.py:331
  27.7 2.9 %collective-permute-start.5 = (bf16[48,2176]{1,0:T(8,128)(2,1)}, bf16[48,2176]{1,0:T(8,128)(2,1)S(1)}, u32[]{:S(2)}, u32[]{:S(2)}) collective-permute-start(bf16[48,2176]{1,0:T(8,128)(2,1)} %get-tuple-element.46), channel_id=1, source_target_pairs={{0,16},{4,20},{8,24},{12,28},{16,0},{20,4},{24,8},{28,12},{1,17},{... | collective-permute-start | bytes 626696 | tf_op jit(solution)/shard_map/ppermute | solution.py:182
  30.7 1.6 %collective-permute-start.9 = (bf16[48,2176]{1,0:T(8,128)(2,1)}, bf16[48,2176]{1,0:T(8,128)(2,1)S(1)}, u32[]{:S(2)}, u32[]{:S(2)}) collective-permute-start(bf16[48,2176]{1,0:T(8,128)(2,1)} %get-tuple-element.46), channel_id=1, source_target_pairs={{0,8},{4,12},{8,0},{12,4},{16,24},{20,28},{24,16},{28,20},{1,9},{5... | collective-permute-start | bytes 626696 | tf_op jit(solution)/shard_map/ppermute | solution.py:182
  32.2 1.0 constant_dynamic-update-slice_fusion.1
  33.2 1.7 %collective-permute-done.4 = bf16[48,2176]{1,0:T(8,128)(2,1)S(1)} collective-permute-done((bf16[48,2176]{1,0:T(8,128)(2,1)}, bf16[48,2176]{1,0:T(8,128)(2,1)S(1)}, u32[]{:S(2)}, u32[]{:S(2)}) %collective-permute-start.4) | collective-permute-done | bytes 208928 | tf_op jit(solution)/shard_map/ppermute | solution.py:182
  34.9 5.5 %collective-permute-done.5 = bf16[48,2176]{1,0:T(8,128)(2,1)S(1)} collective-permute-done((bf16[48,2176]{1,0:T(8,128)(2,1)}, bf16[48,2176]{1,0:T(8,128)(2,1)S(1)}, u32[]{:S(2)}, u32[]{:S(2)}) %collective-permute-start.5) | collective-permute-done | bytes 208928 | tf_op jit(solution)/shard_map/ppermute | solution.py:182
  40.4 2.3 %collective-permute-start.6 = (bf16[48,2176]{1,0:T(8,128)(2,1)S(1)}, bf16[48,2176]{1,0:T(8,128)(2,1)S(1)}, u32[]{:S(2)}, u32[]{:S(2)}) collective-permute-start(bf16[48,2176]{1,0:T(8,128)(2,1)S(1)} %collective-permute-done.5), channel_id=1, source_target_pairs={{0,2},{1,3},{2,0},{3,1},{4,6},{5,7},{6,4},{7,5},{8,10},{9,11},{10,... | collective-permute-start | bytes 626696 | tf_op jit(solution)/shard_map/ppermute | solution.py:182
  42.8 1.0 %collective-permute-start.13 = (bf16[48,2176]{1,0:T(8,128)(2,1)S(1)}, bf16[48,2176]{1,0:T(8,128)(2,1)S(1)}, u32[]{:S(2)}, u32[]{:S(2)}) collective-permute-start(bf16[48,2176]{1,0:T(8,128)(2,1)S(1)} %collective-permute-done.5), channel_id=1, source_target_pairs={{0,8},{4,12},{8,0},{12,4},{16,24},{20,28},{24,16},{28,20},{1,9},{5... | collective-permute-start | bytes 626696 | tf_op jit(solution)/shard_map/ppermute | solution.py:182
  43.9 4.5 %collective-permute-done.6 = bf16[48,2176]{1,0:T(8,128)(2,1)S(1)} collective-permute-done((bf16[48,2176]{1,0:T(8,128)(2,1)S(1)}, bf16[48,2176]{1,0:T(8,128)(2,1)S(1)}, u32[]{:S(2)}, u32[]{:S(2)}) %collective-permute-start.6) | collective-permute-done | bytes 208928 | tf_op jit(solution)/shard_map/ppermute | solution.py:182
  48.4 1.5 %collective-permute-start.10 = (bf16[48,2176]{1,0:T(8,128)(2,1)S(1)}, bf16[48,2176]{1,0:T(8,128)(2,1)S(1)}, u32[]{:S(2)}, u32[]{:S(2)}) collective-permute-start(bf16[48,2176]{1,0:T(8,128)(2,1)S(1)} %collective-permute-done.9), channel_id=1, source_target_pairs={{0,2},{1,3},{2,0},{3,1},{4,6},{5,7},{6,4},{7,5},{8,10},{9,11},{10,... | collective-permute-start | bytes 626696 | tf_op jit(solution)/shard_map/ppermute | solution.py:182
  50.0 1.2 %collective-permute-start.14 = (bf16[48,2176]{1,0:T(8,128)(2,1)S(1)}, bf16[48,2176]{1,0:T(8,128)(2,1)S(1)}, u32[]{:S(2)}, u32[]{:S(2)}) collective-permute-start(bf16[48,2176]{1,0:T(8,128)(2,1)S(1)} %collective-permute-done.6), channel_id=1, source_target_pairs={{0,8},{4,12},{8,0},{12,4},{16,24},{20,28},{24,16},{28,20},{1,9},{5... | collective-permute-start | bytes 626696 | tf_op jit(solution)/shard_map/ppermute | solution.py:182
  51.2 4.2 %collective-permute-done.10 = bf16[48,2176]{1,0:T(8,128)(2,1)S(1)} collective-permute-done((bf16[48,2176]{1,0:T(8,128)(2,1)S(1)}, bf16[48,2176]{1,0:T(8,128)(2,1)S(1)}, u32[]{:S(2)}, u32[]{:S(2)}) %collective-permute-start.10) | collective-permute-done | bytes 208928 | tf_op jit(solution)/shard_map/ppermute | solution.py:182
  58.7 6.1 %shard_map.134 = (bf16[768,384]{1,0:T(8,128)(2,1)S(1)}, bf16[768,128]{1,0:T(8,128)(2,1)S(1)}) custom-call(bf16[2048,384]{1,0:T(8,128)(2,1)S(1)} %bitcast.11, bf16[2048,384]{1,0:T(8,128)(2,1)} %collective-permute-done.7.refs_1_, bf16[96,2176]{1,0:T(8,128)(2,1)S(1)} %constant_dynamic-update-slice_fusion.refs_2_, ...), custom_call_target="tpu_custom_call" | custom-call | bytes 9437184 | tf_op jit(solution)/shard_map/pallas_call | solution.py:382
  64.9 3.6 %collective-permute-done.16.other_ref = bf16[192,2048]{1,0:T(8,128)(2,1)} collective-permute-done((bf16[192,2048]{1,0:T(8,128)(2,1)}, bf16[192,2048]{1,0:T(8,128)(2,1)}, u32[]{:S(2)}, u32[]{:S(2)}) %collective-permute-start.16) | collective-permute-done | bytes 786464 | tf_op jit(solution)/shard_map/ppermute | solution.py:182
  68.5 3.0 %shard_map.135 = (bf16[96,2048]{1,0:T(8,128)(2,1)S(1)}, bf16[96,2048]{1,0:T(8,128)(2,1)S(1)}, bf16[96,2048]{1,0:T(8,128)(2,1)S(1)}, bf16[96,2048]{1,0:T(8,128)(2...) custom-call(s32[1]{0:T(128)} %bitcast.8.index_ref, ...), custom_call_target="tpu_custom_call" | custom-call | tf_op jit(solution)/shard_map/pallas_call | solution.py:424
  73.4 1.6 %collective-permute-start.19 = (bf16[48,2048]{1,0:T(8,128)(2,1)S(1)}, bf16[48,2048]{1,0:T(8,128)(2,1)S(1)}, u32[]{:S(2)}, u32[]{:S(2)}) collective-permute-start(bf16[48,2048]{1,0:T(8,128)(2,1)S(1)} %slice.34), channel_id=1, source_target_pairs={{0,2},{1,3},{2,0},{3,1},{4,6},{5,7},{6,4},{7,5},{8,10},{9,11},{10,... | collective-permute-start | bytes 589832 | tf_op jit(solution)/shard_map/ppermute | solution.py:182
  75.4 1.3 %collective-permute-start.25 = (bf16[48,2048]{1,0:T(8,128)(2,1)S(1)}, bf16[48,2048]{1,0:T(8,128)(2,1)S(1)}, u32[]{:S(2)}, u32[]{:S(2)}) collective-permute-start(bf16[48,2048]{1,0:T(8,128)(2,1)S(1)} %slice.39), channel_id=1, source_target_pairs={{0,2},{1,3},{2,0},{3,1},{4,6},{5,7},{6,4},{7,5},{8,10},{9,11},{10,... | collective-permute-start | bytes 589832 | tf_op jit(solution)/shard_map/ppermute | solution.py:182
  76.8 4.5 %collective-permute-done.19 = bf16[48,2048]{1,0:T(8,128)(2,1)S(1)} collective-permute-done((bf16[48,2048]{1,0:T(8,128)(2,1)S(1)}, bf16[48,2048]{1,0:T(8,128)(2,1)S(1)}, u32[]{:S(2)}, u32[]{:S(2)}) %collective-permute-start.19) | collective-permute-done | bytes 196640 | tf_op jit(solution)/shard_map/ppermute | solution.py:182
  81.3 2.8 %collective-permute-start.26 = (bf16[48,2048]{1,0:T(8,128)(2,1)S(1)}, bf16[48,2048]{1,0:T(8,128)(2,1)S(1)}, u32[]{:S(2)}, u32[]{:S(2)}) collective-permute-start(bf16[48,2048]{1,0:T(8,128)(2,1)S(1)} %add_convert_fusion.9), channel_id=1, source_target_pairs={{0,8},{4,12},{8,0},{12,4},{16,24},{20,28},{24,16},{28,20},{1,9},{5... | collective-permute-start | bytes 589832 | tf_op jit(solution)/shard_map/ppermute | solution.py:182
  84.1 1.5 %collective-permute-start.22 = (bf16[48,2048]{1,0:T(8,128)(2,1)S(1)}, bf16[48,2048]{1,0:T(8,128)(2,1)S(1)}, u32[]{:S(2)}, u32[]{:S(2)}) collective-permute-start(bf16[48,2048]{1,0:T(8,128)(2,1)S(1)} %slice.35), channel_id=1, source_target_pairs={{0,2},{1,3},{2,0},{3,1},{4,6},{5,7},{6,4},{7,5},{8,10},{9,11},{10,... | collective-permute-start | bytes 589832 | tf_op jit(solution)/shard_map/ppermute | solution.py:182
  86.1 1.6 %collective-permute-done.26 = bf16[48,2048]{1,0:T(8,128)(2,1)S(1)} collective-permute-done((bf16[48,2048]{1,0:T(8,128)(2,1)S(1)}, bf16[48,2048]{1,0:T(8,128)(2,1)S(1)}, u32[]{:S(2)}, u32[]{:S(2)}) %collective-permute-start.26) | collective-permute-done | bytes 196640 | tf_op jit(solution)/shard_map/ppermute | solution.py:182
  87.8 3.1 %collective-permute-start.27 = (bf16[48,2048]{1,0:T(8,128)(2,1)S(1)}, bf16[48,2048]{1,0:T(8,128)(2,1)S(1)}, u32[]{:S(2)}, u32[]{:S(2)}) collective-permute-start(bf16[48,2048]{1,0:T(8,128)(2,1)S(1)} %add_convert_fusion.5), channel_id=1, source_target_pairs={{0,16},{4,20},{8,24},{12,28},{16,0},{20,4},{24,8},{28,12},{1,17},{... | collective-permute-start | bytes 589832 | tf_op jit(solution)/shard_map/ppermute | solution.py:182
  91.3 1.3 %collective-permute-start.23 = (bf16[48,2048]{1,0:T(8,128)(2,1)S(1)}, bf16[48,2048]{1,0:T(8,128)(2,1)S(1)}, u32[]{:S(2)}, u32[]{:S(2)}) collective-permute-start(bf16[48,2048]{1,0:T(8,128)(2,1)S(1)} %add_convert_fusion.7), channel_id=1, source_target_pairs={{0,8},{4,12},{8,0},{12,4},{16,24},{20,28},{24,16},{28,20},{1,9},{5... | collective-permute-start | bytes 589832 | tf_op jit(solution)/shard_map/ppermute | solution.py:182
  93.3 4.5 %collective-permute-done.27 = bf16[48,2048]{1,0:T(8,128)(2,1)S(1)} collective-permute-done((bf16[48,2048]{1,0:T(8,128)(2,1)S(1)}, bf16[48,2048]{1,0:T(8,128)(2,1)S(1)}, u32[]{:S(2)}, u32[]{:S(2)}) %collective-permute-start.27) | collective-permute-done | bytes 196640 | tf_op jit(solution)/shard_map/ppermute | solution.py:182
  97.9 1.3 %collective-permute-done.23 = bf16[48,2048]{1,0:T(8,128)(2,1)S(1)} collective-permute-done((bf16[48,2048]{1,0:T(8,128)(2,1)S(1)}, bf16[48,2048]{1,0:T(8,128)(2,1)S(1)}, u32[]{:S(2)}, u32[]{:S(2)}) %collective-permute-start.23) | collective-permute-done | bytes 196640 | tf_op jit(solution)/shard_map/ppermute | solution.py:182
  (64 shorter events, 12.2 us)
Async XLA Ops:
  0.6 14.3 %copy-start = (bf16[1,1,2048,384]{3,2,1,0:T(8,128)(2,1)S(1)}, bf16[1,1,2048,384]{3,2,1,0:T(8,128)(2,1)}, u32[]{:S(2)}) copy-start(bf16[1,1,2048,384]{3,2,1,0:T(8,128)(2,1)} %param.21) | copy-start | bytes 4718596
  1.6 7.4 %collective-permute-start = (bf16[192,256]{1,0:T(8,128)(2,1)S(1)}, bf16[192,256]{1,0:T(8,128)(2,1)S(1)}, u32[]{:S(2)}, u32[]{:S(2)}) collective-permute-start(bf16[192,256]{1,0:T(8,128)(2,1)S(1)} %pad_maximum_fusion.1), channel_id=1, source_target_pairs={{0,4},{4,8},{8,12},{12,16},{16,20},{20,24},{24,28},{1,5},{5,9},{9,... | collective-permute-start | bytes 294920 | tf_op jit(solution)/shard_map/ppermute | solution.py:19
  12.7 8.1 %collective-permute-start.1 = (bf16[48,2048]{1,0:T(8,128)(2,1)}, bf16[48,2048]{1,0:T(8,128)(2,1)S(1)}, u32[]{:S(2)}, u32[]{:S(2)}) collective-permute-start(bf16[48,2048]{1,0:T(8,128)(2,1)} %get-tuple-element.42), channel_id=1, source_target_pairs={{0,2},{1,3},{2,0},{3,1},{4,6},{5,7},{6,4},{7,5},{8,10},{9,11},{10,... | collective-permute-start | bytes 589832 | tf_op jit(solution)/shard_map/ppermute | solution.py:182
  14.3 6.6 %collective-permute-start.2 = (bf16[48,2048]{1,0:T(8,128)(2,1)}, bf16[48,2048]{1,0:T(8,128)(2,1)S(1)}, u32[]{:S(2)}, u32[]{:S(2)}) collective-permute-start(bf16[48,2048]{1,0:T(8,128)(2,1)} %get-tuple-element.43), channel_id=1, source_target_pairs={{0,1},{1,0},{2,3},{3,2},{4,5},{5,4},{6,7},{7,6},{8,9},{9,8},{10,11... | collective-permute-start | bytes 589832 | tf_op jit(solution)/shard_map/ppermute | solution.py:182
  14.3 8.4 %collective-permute-start.3 = (bf16[48,2048]{1,0:T(8,128)(2,1)}, bf16[48,2048]{1,0:T(8,128)(2,1)S(1)}, u32[]{:S(2)}, u32[]{:S(2)}) collective-permute-start(bf16[48,2048]{1,0:T(8,128)(2,1)} %get-tuple-element.44), channel_id=1, source_target_pairs={{0,3},{1,2},{2,1},{3,0},{4,7},{5,6},{6,5},{7,4},{8,11},{9,10},{10,... | collective-permute-start | bytes 589832 | tf_op jit(solution)/shard_map/ppermute | solution.py:182
  15.0 41.3 %collective-permute-start.7 = (bf16[2048,384]{1,0:T(8,128)(2,1)S(1)}, bf16[2048,384]{1,0:T(8,128)(2,1)}, u32[]{:S(2)}, u32[]{:S(2)}) collective-permute-start(bf16[2048,384]{1,0:T(8,128)(2,1)S(1)} %bitcast.10), channel_id=1, source_target_pairs={{0,4},{4,0},{8,12},{12,8},{16,20},{20,16},{24,28},{28,24},{1,5},{5... | collective-permute-start | bytes 4718600 | tf_op jit(solution)/shard_map/ppermute | solution.py:182
  17.0 51.5 %collective-permute-start.16 = (bf16[192,2048]{1,0:T(8,128)(2,1)}, bf16[192,2048]{1,0:T(8,128)(2,1)}, u32[]{:S(2)}, u32[]{:S(2)}) collective-permute-start(bf16[192,2048]{1,0:T(8,128)(2,1)} %bitcast.12), channel_id=1, source_target_pairs={{0,4},{4,0},{8,12},{12,8},{16,20},{20,16},{24,28},{28,24},{1,5},{5... | collective-permute-start | bytes 2359304 | tf_op jit(solution)/shard_map/ppermute | solution.py:182
  20.8 1.9 %copy-start.3 = (bf16[48,2048]{1,0:T(8,128)(2,1)}, bf16[48,2048]{1,0:T(8,128)(2,1)S(1)}, u32[]{:S(2)}) copy-start(bf16[48,2048]{1,0:T(8,128)(2,1)S(1)} %collective-permute-done.1.refs_1_) | copy-start | bytes 589828
  26.7 8.2 %collective-permute-start.4 = (bf16[48,2176]{1,0:T(8,128)(2,1)}, bf16[48,2176]{1,0:T(8,128)(2,1)S(1)}, u32[]{:S(2)}, u32[]{:S(2)}) collective-permute-start(bf16[48,2176]{1,0:T(8,128)(2,1)} %get-tuple-element.46), channel_id=1, source_target_pairs={{0,2},{1,3},{2,0},{3,1},{4,6},{5,7},{6,4},{7,5},{8,10},{9,11},{10,... | collective-permute-start | bytes 626696 | tf_op jit(solution)/shard_map/ppermute | solution.py:182
  27.7 12.7 %collective-permute-start.5 = (bf16[48,2176]{1,0:T(8,128)(2,1)}, bf16[48,2176]{1,0:T(8,128)(2,1)S(1)}, u32[]{:S(2)}, u32[]{:S(2)}) collective-permute-start(bf16[48,2176]{1,0:T(8,128)(2,1)} %get-tuple-element.46), channel_id=1, source_target_pairs={{0,16},{4,20},{8,24},{12,28},{16,0},{20,4},{24,8},{28,12},{1,17},{... | collective-permute-start | bytes 626696 | tf_op jit(solution)/shard_map/ppermute | solution.py:182
  30.7 13.2 %collective-permute-start.9 = (bf16[48,2176]{1,0:T(8,128)(2,1)}, bf16[48,2176]{1,0:T(8,128)(2,1)S(1)}, u32[]{:S(2)}, u32[]{:S(2)}) collective-permute-start(bf16[48,2176]{1,0:T(8,128)(2,1)} %get-tuple-element.46), channel_id=1, source_target_pairs={{0,8},{4,12},{8,0},{12,4},{16,24},{20,28},{24,16},{28,20},{1,9},{5... | collective-permute-start | bytes 626696 | tf_op jit(solution)/shard_map/ppermute | solution.py:182
  40.4 8.0 %collective-permute-start.6 = (bf16[48,2176]{1,0:T(8,128)(2,1)S(1)}, bf16[48,2176]{1,0:T(8,128)(2,1)S(1)}, u32[]{:S(2)}, u32[]{:S(2)}) collective-permute-start(bf16[48,2176]{1,0:T(8,128)(2,1)S(1)} %collective-permute-done.5), channel_id=1, source_target_pairs={{0,2},{1,3},{2,0},{3,1},{4,6},{5,7},{6,4},{7,5},{8,10},{9,11},{10,... | collective-permute-start | bytes 626696 | tf_op jit(solution)/shard_map/ppermute | solution.py:182
  42.8 7.2 %collective-permute-start.13 = (bf16[48,2176]{1,0:T(8,128)(2,1)S(1)}, bf16[48,2176]{1,0:T(8,128)(2,1)S(1)}, u32[]{:S(2)}, u32[]{:S(2)}) collective-permute-start(bf16[48,2176]{1,0:T(8,128)(2,1)S(1)} %collective-permute-done.5), channel_id=1, source_target_pairs={{0,8},{4,12},{8,0},{12,4},{16,24},{20,28},{24,16},{28,20},{1,9},{5... | collective-permute-start | bytes 626696 | tf_op jit(solution)/shard_map/ppermute | solution.py:182
  43.9 12.9 %collective-permute-start.8 = (bf16[96,2176]{1,0:T(8,128)(2,1)S(1)}, bf16[96,2176]{1,0:T(8,128)(2,1)}, u32[]{:S(2)}, u32[]{:S(2)}) collective-permute-start(bf16[96,2176]{1,0:T(8,128)(2,1)S(1)} %constant_dynamic-update-slice_fusion.refs_2_), channel_id=1, source_target_pairs={{0,1},{1,0},{2,3},{3,2},{4,5},{5,4},{6,7},{7,6},{8,9},{9,8},{10,11... | collective-permute-start | bytes 1253384 | tf_op jit(solution)/shard_map/ppermute | solution.py:182
  48.4 7.0 %collective-permute-start.10 = (bf16[48,2176]{1,0:T(8,128)(2,1)S(1)}, bf16[48,2176]{1,0:T(8,128)(2,1)S(1)}, u32[]{:S(2)}, u32[]{:S(2)}) collective-permute-start(bf16[48,2176]{1,0:T(8,128)(2,1)S(1)} %collective-permute-done.9), channel_id=1, source_target_pairs={{0,2},{1,3},{2,0},{3,1},{4,6},{5,7},{6,4},{7,5},{8,10},{9,11},{10,... | collective-permute-start | bytes 626696 | tf_op jit(solution)/shard_map/ppermute | solution.py:182
  50.0 6.2 %collective-permute-start.14 = (bf16[48,2176]{1,0:T(8,128)(2,1)S(1)}, bf16[48,2176]{1,0:T(8,128)(2,1)S(1)}, u32[]{:S(2)}, u32[]{:S(2)}) collective-permute-start(bf16[48,2176]{1,0:T(8,128)(2,1)S(1)} %collective-permute-done.6), channel_id=1, source_target_pairs={{0,8},{4,12},{8,0},{12,4},{16,24},{20,28},{24,16},{28,20},{1,9},{5... | collective-permute-start | bytes 626696 | tf_op jit(solution)/shard_map/ppermute | solution.py:182
  55.4 2.0 %collective-permute-start.11 = (bf16[96,2176]{1,0:T(8,128)(2,1)S(1)}, bf16[96,2176]{1,0:T(8,128)(2,1)}, u32[]{:S(2)}, u32[]{:S(2)}) collective-permute-start(bf16[96,2176]{1,0:T(8,128)(2,1)S(1)} %constant_dynamic-update-slice_fusion.2.refs_4_), channel_id=1, source_target_pairs={{0,1},{1,0},{2,3},{3,2},{4,5},{5,4},{6,7},{7,6},{8,9},{9,8},{10,11... | collective-permute-start | bytes 1253384 | tf_op jit(solution)/shard_map/ppermute | solution.py:182
  56.2 2.0 %collective-permute-start.15 = (bf16[96,2176]{1,0:T(8,128)(2,1)S(1)}, bf16[96,2176]{1,0:T(8,128)(2,1)}, u32[]{:S(2)}, u32[]{:S(2)}) collective-permute-start(bf16[96,2176]{1,0:T(8,128)(2,1)S(1)} %constant_dynamic-update-slice_fusion.4.refs_8_), channel_id=1, source_target_pairs={{0,1},{1,0},{2,3},{3,2},{4,5},{5,4},{6,7},{7,6},{8,9},{9,8},{10,11... | collective-permute-start | bytes 1253384 | tf_op jit(solution)/shard_map/ppermute | solution.py:182
  56.3 2.5 %collective-permute-start.12 = (bf16[96,2176]{1,0:T(8,128)(2,1)S(1)}, bf16[96,2176]{1,0:T(8,128)(2,1)}, u32[]{:S(2)}, u32[]{:S(2)}) collective-permute-start(bf16[96,2176]{1,0:T(8,128)(2,1)S(1)} %pad_maximum_fusion.refs_6_), channel_id=1, source_target_pairs={{0,1},{1,0},{2,3},{3,2},{4,5},{5,4},{6,7},{7,6},{8,9},{9,8},{10,11... | collective-permute-start | bytes 1253384 | tf_op jit(solution)/shard_map/ppermute | solution.py:182
  56.8 11.7 %copy-start.1 = (bf16[1,1,192,2048]{3,2,1,0:T(8,128)(2,1)S(1)}, bf16[1,1,192,2048]{3,2,1,0:T(8,128)(2,1)}, u32[]{:S(2)}) copy-start(bf16[1,1,192,2048]{3,2,1,0:T(8,128)(2,1)} %param.22) | copy-start | bytes 2359300
  71.5 1.8 %collective-permute-start.18 = (bf16[96,2048]{1,0:T(8,128)(2,1)S(1)}, bf16[96,2048]{1,0:T(8,128)(2,1)S(1)}, u32[]{:S(2)}, u32[]{:S(2)}) collective-permute-start(bf16[96,2048]{1,0:T(8,128)(2,1)S(1)} %get-tuple-element.60), channel_id=1, source_target_pairs={{0,1},{1,0},{2,3},{3,2},{4,5},{5,4},{6,7},{7,6},{8,9},{9,8},{10,11... | collective-permute-start | bytes 1179656 | tf_op jit(solution)/shard_map/ppermute | solution.py:182
  71.6 3.4 %collective-permute-start.20 = (bf16[96,2048]{1,0:T(8,128)(2,1)S(1)}, bf16[96,2048]{1,0:T(8,128)(2,1)S(1)}, u32[]{:S(2)}, u32[]{:S(2)}) collective-permute-start(bf16[96,2048]{1,0:T(8,128)(2,1)S(1)} %get-tuple-element.62), channel_id=1, source_target_pairs={{0,1},{1,0},{2,3},{3,2},{4,5},{5,4},{6,7},{7,6},{8,9},{9,8},{10,11... | collective-permute-start | bytes 1179656 | tf_op jit(solution)/shard_map/ppermute | solution.py:182
  72.1 3.0 %collective-permute-start.17 = (bf16[96,2048]{1,0:T(8,128)(2,1)S(1)}, bf16[96,2048]{1,0:T(8,128)(2,1)S(1)}, u32[]{:S(2)}, u32[]{:S(2)}) collective-permute-start(bf16[96,2048]{1,0:T(8,128)(2,1)S(1)} %get-tuple-element.58), channel_id=1, source_target_pairs={{0,1},{1,0},{2,3},{3,2},{4,5},{5,4},{6,7},{7,6},{8,9},{9,8},{10,11... | collective-permute-start | bytes 1179656 | tf_op jit(solution)/shard_map/ppermute | solution.py:182
  72.2 3.1 %collective-permute-start.24 = (bf16[96,2048]{1,0:T(8,128)(2,1)S(1)}, bf16[96,2048]{1,0:T(8,128)(2,1)S(1)}, u32[]{:S(2)}, u32[]{:S(2)}) collective-permute-start(bf16[96,2048]{1,0:T(8,128)(2,1)S(1)} %get-tuple-element.67), channel_id=1, source_target_pairs={{0,1},{1,0},{2,3},{3,2},{4,5},{5,4},{6,7},{7,6},{8,9},{9,8},{10,11... | collective-permute-start | bytes 1179656 | tf_op jit(solution)/shard_map/ppermute | solution.py:182
  73.4 7.8 %collective-permute-start.19 = (bf16[48,2048]{1,0:T(8,128)(2,1)S(1)}, bf16[48,2048]{1,0:T(8,128)(2,1)S(1)}, u32[]{:S(2)}, u32[]{:S(2)}) collective-permute-start(bf16[48,2048]{1,0:T(8,128)(2,1)S(1)} %slice.34), channel_id=1, source_target_pairs={{0,2},{1,3},{2,0},{3,1},{4,6},{5,7},{6,4},{7,5},{8,10},{9,11},{10,... | collective-permute-start | bytes 589832 | tf_op jit(solution)/shard_map/ppermute | solution.py:182
  75.4 23.8 %copy-start.2 = (bf16[48,2048]{1,0:T(8,128)(2,1)S(1)}, bf16[48,2048]{1,0:T(8,128)(2,1)}, u32[]{:S(2)}) copy-start(bf16[48,2048]{1,0:T(8,128)(2,1)} %get-tuple-element.45) | copy-start | bytes 589828
  75.4 10.7 %collective-permute-start.25 = (bf16[48,2048]{1,0:T(8,128)(2,1)S(1)}, bf16[48,2048]{1,0:T(8,128)(2,1)S(1)}, u32[]{:S(2)}, u32[]{:S(2)}) collective-permute-start(bf16[48,2048]{1,0:T(8,128)(2,1)S(1)} %slice.39), channel_id=1, source_target_pairs={{0,2},{1,3},{2,0},{3,1},{4,6},{5,7},{6,4},{7,5},{8,10},{9,11},{10,... | collective-permute-start | bytes 589832 | tf_op jit(solution)/shard_map/ppermute | solution.py:182
  81.3 6.4 %collective-permute-start.26 = (bf16[48,2048]{1,0:T(8,128)(2,1)S(1)}, bf16[48,2048]{1,0:T(8,128)(2,1)S(1)}, u32[]{:S(2)}, u32[]{:S(2)}) collective-permute-start(bf16[48,2048]{1,0:T(8,128)(2,1)S(1)} %add_convert_fusion.9), channel_id=1, source_target_pairs={{0,8},{4,12},{8,0},{12,4},{16,24},{20,28},{24,16},{28,20},{1,9},{5... | collective-permute-start | bytes 589832 | tf_op jit(solution)/shard_map/ppermute | solution.py:182
  84.1 7.1 %collective-permute-start.22 = (bf16[48,2048]{1,0:T(8,128)(2,1)S(1)}, bf16[48,2048]{1,0:T(8,128)(2,1)S(1)}, u32[]{:S(2)}, u32[]{:S(2)}) collective-permute-start(bf16[48,2048]{1,0:T(8,128)(2,1)S(1)} %slice.35), channel_id=1, source_target_pairs={{0,2},{1,3},{2,0},{3,1},{4,6},{5,7},{6,4},{7,5},{8,10},{9,11},{10,... | collective-permute-start | bytes 589832 | tf_op jit(solution)/shard_map/ppermute | solution.py:182
  85.6 7.8 %collective-permute-start.21 = (bf16[48,2048]{1,0:T(8,128)(2,1)S(1)}, bf16[48,2048]{1,0:T(8,128)(2,1)S(1)}, u32[]{:S(2)}, u32[]{:S(2)}) collective-permute-start(bf16[48,2048]{1,0:T(8,128)(2,1)S(1)} %slice.36), channel_id=1, source_target_pairs={{0,2},{1,3},{2,0},{3,1},{4,6},{5,7},{6,4},{7,5},{8,10},{9,11},{10,... | collective-permute-start | bytes 589832 | tf_op jit(solution)/shard_map/ppermute | solution.py:182
  87.8 10.1 %collective-permute-start.27 = (bf16[48,2048]{1,0:T(8,128)(2,1)S(1)}, bf16[48,2048]{1,0:T(8,128)(2,1)S(1)}, u32[]{:S(2)}, u32[]{:S(2)}) collective-permute-start(bf16[48,2048]{1,0:T(8,128)(2,1)S(1)} %add_convert_fusion.5), channel_id=1, source_target_pairs={{0,16},{4,20},{8,24},{12,28},{16,0},{20,4},{24,8},{28,12},{1,17},{... | collective-permute-start | bytes 589832 | tf_op jit(solution)/shard_map/ppermute | solution.py:182
  91.3 7.9 %collective-permute-start.23 = (bf16[48,2048]{1,0:T(8,128)(2,1)S(1)}, bf16[48,2048]{1,0:T(8,128)(2,1)S(1)}, u32[]{:S(2)}, u32[]{:S(2)}) collective-permute-start(bf16[48,2048]{1,0:T(8,128)(2,1)S(1)} %add_convert_fusion.7), channel_id=1, source_target_pairs={{0,8},{4,12},{8,0},{12,4},{16,24},{20,28},{24,16},{28,20},{1,9},{5... | collective-permute-start | bytes 589832 | tf_op jit(solution)/shard_map/ppermute | solution.py:182
  (3 other events, 3.2 us)
